TPU v7x, 32 devices: a whole 2x2x4 slice. The times are simulated.
32 devices in a mesh: wide: 8 (over y, x, core), narrow: 4 (over z).
Axes of the slice: x: 2, y: 2, z: 4, core: 2. Of those that a mesh axis runs over, the one named last changes fastest.
Arguments:
- tokens: bfloat16 [12288, 2048], P(('wide', 'narrow')), may hold values from -6 to 6
- cotangent: bfloat16 [12288, 2048], P(('wide', 'narrow')), may hold values from -6 to 6
- lengths: int32 [8], replicated, may hold values from 768 to 1536, as said below
- owners: int32 [116], replicated, may hold values from 0 to 7, as said below
- master: float32 [208, 4, 1024, 128], P('wide', 'narrow'), as said below
- moment_one: float32 [208, 4, 1024, 128], P('wide', 'narrow'), as said below
- moment_two: float32 [208, 4, 1024, 128], P('wide', 'narrow'), as said below
- norm_gains: float32 [2, 2048], replicated, may hold values from 0.5 to 1.5
- gain_first: float32 [2, 2048], replicated, may hold values from -640 to 640
- gain_second: float32 [2, 2048], replicated, may hold values from 12288 to 49152
Outputs:
- output: bfloat16 [12288, 2048], P(('wide', 'narrow'))
- input_grad: bfloat16 [12288, 2048], P(('wide', 'narrow'))
- weight_grads: float32 [208, 4, 1024, 128], P('wide', 'narrow')
- new_master: float32 [208, 4, 1024, 128], P('wide', 'narrow')
- new_copy: bfloat16 [208, 4, 1024, 128], P('wide', 'narrow')
- new_first: float32 [208, 4, 1024, 128], P('wide', 'narrow')
- new_second: float32 [208, 4, 1024, 128], P('wide', 'narrow')
- gain_grads: float32 [2, 2048], replicated
- gain_second_new: float32 [2, 2048], replicated
- new_gains: float32 [2, 2048], replicated
Inputs may be any that keep to these rules, and one draw needn't show every extreme that they name: `owners`: each owner holds at most 26 units and some owner holds exactly 26. `lengths`: some sequence has length exactly 1536. `master`: slots that hold no unit are zero. `moment_one`: slots that hold no unit are zero. `moment_two`: slots that hold no unit are zero, the others positive.
All inputs are finite; a program needn't handle non-finite values.
Results may differ from a plain program's by a relative error of at most 0.025.
Values may be sent and summed in bfloat16 or wider, within the bound.
A program may use at most 704 MiB of HBM per device.

v0:
```python
import jax
import jax.numpy as jnp
from jax import lax
from jax.sharding import PartitionSpec as P

D = 2048
H = 32
KV = 8
HD = 64
FF = 8192
STEP = 5


def rotate(values, cos_table, sin_table):
    middle = values.shape[-1] // 2
    turned = jnp.concatenate([-values[..., middle:], values[..., :middle]], axis=-1)
    return values * cos_table + turned * sin_table


def unrotate(gradient, cos_table, sin_table):
    middle = gradient.shape[-1] // 2
    weighted = gradient * sin_table
    turned = jnp.concatenate([weighted[..., middle:], -weighted[..., :middle]], axis=-1)
    return gradient * cos_table + turned


def tables(length_all, head_size):
    inverse = 500000.0 ** (-jnp.arange(0, head_size, 2, dtype=jnp.float32) / head_size)
    angles = jnp.arange(length_all, dtype=jnp.float32)[:, None] * inverse[None, :]
    angles = jnp.concatenate([angles, angles], axis=1)
    return (jnp.cos(angles), jnp.sin(angles))


def rmsnorm(values, weight_gain):
    return (
        values * lax.rsqrt(jnp.mean(values * values, axis=-1, keepdims=True) + 1e-05) * weight_gain
    )


def positions(owners, wide_count, capacity):
    onehot = (owners[:, None] == jnp.arange(wide_count, dtype=jnp.int32)[None, :]).astype(jnp.int32)
    before = jnp.cumsum(onehot, axis=0) - onehot
    return owners * capacity + jnp.sum(before * onehot, axis=1)


def matmul_rows(first_op, second_op):
    return lax.dot_general(
        first_op, second_op, (((0,), (0,)), ((), ())), preferred_element_type=jnp.float32
    )


def matmul_cols(first_op, second_op):
    return lax.dot_general(
        first_op, second_op, (((1,), (1,)), ((), ())), preferred_element_type=jnp.float32
    )


def adamw(weight, gradient, moment_one, moment_two, rate, decay):
    moment_one = 0.5 * moment_one + 0.5 * gradient
    moment_two = 0.5 * moment_two + 0.5 * gradient * gradient
    correct = 1.0 - 0.5**STEP
    update = moment_one / correct / (jnp.sqrt(moment_two / correct) + 1e-08)
    return (weight - rate * (update + decay * weight), moment_one, moment_two)


def project(normed_all, w_qkv, cos_heads, sin_heads, heads_here, kv_here):
    seq_len = normed_all.shape[0]
    projected = jnp.dot(normed_all, w_qkv, preferred_element_type=jnp.float32)
    query_width = heads_here * HD
    kv_width = kv_here * HD
    group_size = heads_here // kv_here
    query_heads = rotate(
        projected[:, :query_width].reshape(seq_len, heads_here, HD), cos_heads, sin_heads
    )
    key_heads = rotate(
        projected[:, query_width : query_width + kv_width].reshape(seq_len, kv_here, HD),
        cos_heads,
        sin_heads,
    )
    value_heads = projected[:, query_width + kv_width :].reshape(seq_len, kv_here, HD)
    query_heads = jnp.transpose(query_heads.astype(jnp.bfloat16), (1, 0, 2)).reshape(
        kv_here, group_size, seq_len, HD
    )
    key_heads = jnp.transpose(key_heads.astype(jnp.bfloat16), (1, 0, 2))
    value_heads = jnp.transpose(value_heads.astype(jnp.bfloat16), (1, 0, 2))
    return (query_heads, key_heads, value_heads)


def masked_scores(query_block, key_heads, row_start, length):
    block_rows = query_block.shape[2]
    seq_len = key_heads.shape[1]
    scores = jnp.einsum(
        "kgqd,ksd->kgqs", query_block, key_heads, preferred_element_type=jnp.float32
    ) * HD ** (-0.5)
    row_pos = row_start + jnp.arange(block_rows, dtype=jnp.int32)
    key_pos = jnp.arange(seq_len, dtype=jnp.int32)
    allowed = (key_pos[None, :] <= row_pos[:, None]) & (key_pos[None, :] < length)
    return jnp.where(allowed, scores, -1e30)


def attend_forward(query_heads, key_heads, value_heads, length, block_rows):
    seq_len = query_heads.shape[2]
    outputs = []
    log_sums = []
    for row_start in range(0, seq_len, block_rows):
        query_block = query_heads[:, :, row_start : row_start + block_rows]
        scores = masked_scores(query_block, key_heads, row_start, length)
        row_peak = jnp.max(scores, axis=-1, keepdims=True)
        raised = jnp.exp(scores - row_peak)
        row_total = jnp.sum(raised, axis=-1, keepdims=True)
        attn_probs = (raised / row_total).astype(jnp.bfloat16)
        outputs.append(
            jnp.einsum(
                "kgqs,ksd->kgqd", attn_probs, value_heads, preferred_element_type=jnp.float32
            )
        )
        log_sums.append((row_peak + jnp.log(row_total))[..., 0])
    return (jnp.concatenate(outputs, axis=2), jnp.concatenate(log_sums, axis=2))


def attend_backward(query_heads, key_heads, value_heads, out_back, log_sums, length, block_rows):
    seq_len = query_heads.shape[2]
    query_grads = []
    key_grad = jnp.zeros(key_heads.shape, jnp.float32)
    value_grad = jnp.zeros(value_heads.shape, jnp.float32)
    for row_start in range(0, seq_len, block_rows):
        query_block = query_heads[:, :, row_start : row_start + block_rows]
        back_block = out_back[:, :, row_start : row_start + block_rows]
        scores = masked_scores(query_block, key_heads, row_start, length)
        attn_probs = jnp.exp(scores - log_sums[:, :, row_start : row_start + block_rows, None])
        probs_back = jnp.einsum(
            "kgqd,ksd->kgqs", back_block, value_heads, preferred_element_type=jnp.float32
        )
        row_shift = jnp.sum(attn_probs * probs_back, axis=-1, keepdims=True)
        scores_back = (HD ** (-0.5) * attn_probs * (probs_back - row_shift)).astype(jnp.bfloat16)
        query_grads.append(
            jnp.einsum("kgqs,ksd->kgqd", scores_back, key_heads, preferred_element_type=jnp.float32)
        )
        key_grad = key_grad + jnp.einsum(
            "kgqs,kgqd->ksd", scores_back, query_block, preferred_element_type=jnp.float32
        )
        value_grad = value_grad + jnp.einsum(
            "kgqs,kgqd->ksd",
            attn_probs.astype(jnp.bfloat16),
            back_block,
            preferred_element_type=jnp.float32,
        )
    return (jnp.concatenate(query_grads, axis=2), key_grad, value_grad)


def local(
    tokens,
    cotangent,
    lengths,
    owners,
    master,
    moment_one,
    moment_two,
    norm_gains,
    gain_first,
    gain_second,
):
    wide_count = lax.axis_size("wide")
    narrow_count = lax.axis_size("narrow")
    capacity = master.shape[0]
    unit_rows = master.shape[2]
    unit_cols = master.shape[3]
    unit_count = owners.shape[0]
    row_count = tokens.shape[0]
    seq_len = row_count * narrow_count
    slot_place = positions(owners, wide_count, capacity)
    own_slots = master[:, 0].astype(jnp.bfloat16)
    all_slots = lax.all_gather(own_slots, "wide", axis=0, tiled=True)
    unit_data = jnp.take(all_slots, slot_place, axis=0)
    row_blocks = D // unit_rows
    col_blocks = unit_count // row_blocks
    packed = jnp.transpose(
        unit_data.reshape(row_blocks, col_blocks, unit_rows, unit_cols), (0, 2, 1, 3)
    ).reshape(D, col_blocks * unit_cols)
    heads_here = H // narrow_count
    kv_here = KV // narrow_count
    group_size = heads_here // kv_here
    query_width = heads_here * HD
    kv_width = kv_here * HD
    ff_width = FF // narrow_count
    qkv_end = query_width + 2 * kv_width
    out_end = qkv_end + query_width
    gate_end = out_end + 2 * ff_width
    w_qkv = packed[:, :qkv_end]
    w_out_t = packed[:, qkv_end:out_end]
    w_gate_up = packed[:, out_end:gate_end]
    w_down_t = packed[:, gate_end:]
    cos_table, sin_table = tables(seq_len, HD)
    cos_heads = cos_table[:, None, :]
    sin_heads = sin_table[:, None, :]
    block_rows = min(512, seq_len)
    wide_index = lax.axis_index("wide")
    length = lengths[wide_index]
    inputs = tokens.astype(jnp.float32)
    normed = rmsnorm(inputs, norm_gains[0]).astype(jnp.bfloat16)
    normed_all = lax.all_gather(normed, "narrow", axis=0, tiled=True)
    query_heads, key_heads, value_heads = project(
        normed_all, w_qkv, cos_heads, sin_heads, heads_here, kv_here
    )
    attended, log_sums = attend_forward(query_heads, key_heads, value_heads, length, block_rows)
    attended = (
        jnp.transpose(attended.reshape(heads_here, seq_len, HD), (1, 0, 2))
        .reshape(seq_len, query_width)
        .astype(jnp.bfloat16)
    )
    residual = inputs + lax.psum_scatter(
        matmul_cols(attended, w_out_t), "narrow", scatter_dimension=0, tiled=True
    )
    normed_two = rmsnorm(residual, norm_gains[1]).astype(jnp.bfloat16)
    mlp_input = lax.all_gather(normed_two, "narrow", axis=0, tiled=True)
    gate_up = jnp.dot(mlp_input, w_gate_up, preferred_element_type=jnp.float32)
    hidden = (jax.nn.silu(gate_up[:, :ff_width]) * gate_up[:, ff_width:]).astype(jnp.bfloat16)
    output = residual + lax.psum_scatter(
        matmul_cols(hidden, w_down_t).astype(jnp.bfloat16),
        "narrow",
        scatter_dimension=0,
        tiled=True,
    ).astype(jnp.float32)
    down_back = lax.all_gather(cotangent, "narrow", axis=0, tiled=True)
    mlp_again = lax.all_gather(normed_two, "narrow", axis=0, tiled=True)
    gate_up = jnp.dot(mlp_again, w_gate_up, preferred_element_type=jnp.float32)
    hidden_back = jnp.dot(down_back, w_down_t, preferred_element_type=jnp.float32)
    grad_down_t = matmul_rows(down_back, hidden)
    _, swiglu_pull = jax.vjp(
        lambda gate_in, upper_in: jax.nn.silu(gate_in) * upper_in,
        gate_up[:, :ff_width],
        gate_up[:, ff_width:],
    )
    gate_back, upper_back = swiglu_pull(hidden_back)
    gate_up_back = jnp.concatenate([gate_back, upper_back], axis=1).astype(jnp.bfloat16)
    grad_gate_up = matmul_rows(mlp_again, gate_up_back)
    norm_two_back = lax.psum_scatter(
        matmul_cols(gate_up_back, w_gate_up).astype(jnp.bfloat16),
        "narrow",
        scatter_dimension=0,
        tiled=True,
    ).astype(jnp.float32)
    _, norm_two_pull = jax.vjp(rmsnorm, residual, norm_gains[1])
    resid_part, gain_two = norm_two_pull(norm_two_back)
    resid_back = cotangent.astype(jnp.float32) + resid_part
    attn_back = lax.all_gather(resid_back.astype(jnp.bfloat16), "narrow", axis=0, tiled=True)
    normed_again = lax.all_gather(normed, "narrow", axis=0, tiled=True)
    query_heads, key_heads, value_heads = project(
        normed_again, w_qkv, cos_heads, sin_heads, heads_here, kv_here
    )
    out_back = jnp.dot(attn_back, w_out_t, preferred_element_type=jnp.float32).astype(jnp.bfloat16)
    grad_out_t = matmul_rows(attn_back, attended)
    out_back = jnp.transpose(out_back.reshape(seq_len, heads_here, HD), (1, 0, 2)).reshape(
        kv_here, group_size, seq_len, HD
    )
    query_grad, key_grad, value_grad = attend_backward(
        query_heads, key_heads, value_heads, out_back, log_sums, length, block_rows
    )
    query_grad = jnp.transpose(query_grad.reshape(heads_here, seq_len, HD), (1, 0, 2))
    query_grad = unrotate(query_grad, cos_heads, sin_heads).reshape(seq_len, query_width)
    key_grad = unrotate(jnp.transpose(key_grad, (1, 0, 2)), cos_heads, sin_heads).reshape(
        seq_len, kv_width
    )
    value_grad = jnp.transpose(value_grad, (1, 0, 2)).reshape(seq_len, kv_width)
    qkv_back = jnp.concatenate([query_grad, key_grad, value_grad], axis=1).astype(jnp.bfloat16)
    grad_qkv = matmul_rows(normed_again, qkv_back)
    norm_one_back = lax.psum_scatter(
        matmul_cols(qkv_back, w_qkv).astype(jnp.bfloat16), "narrow", scatter_dimension=0, tiled=True
    ).astype(jnp.float32)
    _, norm_one_pull = jax.vjp(rmsnorm, inputs, norm_gains[0])
    input_part, gain_one = norm_one_pull(norm_one_back)
    input_grad = (resid_back + input_part).astype(jnp.bfloat16)
    grad_packed = jnp.concatenate([grad_qkv, grad_out_t, grad_gate_up, grad_down_t], axis=1)
    grad_units = jnp.transpose(
        grad_packed.reshape(row_blocks, unit_rows, col_blocks, unit_cols), (0, 2, 1, 3)
    ).reshape(unit_count, unit_rows, unit_cols)
    grad_slots = (
        jnp.zeros((wide_count * capacity, unit_rows, unit_cols), jnp.float32)
        .at[slot_place]
        .set(grad_units)
    )
    owned_grads = lax.psum_scatter(
        grad_slots.astype(jnp.bfloat16), "wide", scatter_dimension=0, tiled=True
    ).astype(jnp.float32)[:, None]
    new_master, new_first, new_second = adamw(
        master, owned_grads, moment_one, moment_two, 0.02, 0.1
    )
    gain_grads = lax.psum(jnp.stack([gain_one, gain_two]), ("wide", "narrow"))
    new_gains, unused, gain_second_new = adamw(
        norm_gains, gain_grads, gain_first, gain_second, 0.5, 0.0
    )
    return (
        output.astype(jnp.bfloat16),
        input_grad,
        owned_grads,
        new_master,
        new_master.astype(jnp.bfloat16),
        new_first,
        new_second,
        gain_grads,
        gain_second_new,
        new_gains,
    )


def solution(mesh):
    placed = (
        P(("wide", "narrow"), None),
        P(("wide", "narrow"), None),
        P(),
        P(),
        P("wide", "narrow", None, None),
        P("wide", "narrow", None, None),
        P("wide", "narrow", None, None),
        P(),
        P(),
        P(),
    )
    return jax.shard_map(
        local,
        mesh=mesh,
        in_specs=placed,
        out_specs=(
            P(("wide", "narrow"), None),
            P(("wide", "narrow"), None),
            P("wide", "narrow", None, None),
            P("wide", "narrow", None, None),
            P("wide", "narrow", None, None),
            P("wide", "narrow", None, None),
            P("wide", "narrow", None, None),
            P(),
            P(),
            P(),
        ),
        check_vma=False,
    )
```

profile of v0, /device:TPU:0, one launch (start us, length us, event | category | flops | bytes accessed | tf_op | source)
XLA Modules:
  0.0 2400.0 jit_solution(9072217437414351259)
XLA Ops:
  27.0 241.7 %all-gather.15.cloned.1.call-done = bf16[208,1,1024,128]{3,2,1,0:T(8,128)(2,1)} async-done(((bf16[26,1,1024,128]{3,2,1,0:T(8,128)(2,1)}), bf16[208,1,1024,128]{3,2,1,0:T(8,128)(2,1)}) %all-gather.15.cloned.1.call-update) | async-done | bytes 54525968 | tf_op jit(solution)/shard_map/all_gather | solution.py:173
  268.7 22.4 gather_fusion
  291.1 73.8 %copy.56 = bf16[2,58,1024,128]{2,0,3,1:T(2,128)(2,1)} copy(bf16[2,58,1024,128]{3,2,1,0:T(8,128)(2,1)} %bitcast.197) | data formatting | bytes 60817408 | tf_op jit(solution)/shard_map/jit(_take)/gather | solution.py:174
  364.9 33.5 %broadcast_select_fusion = bf16[2,58,1024,128]{2,0,3,1:T(2,128)(2,1)} fusion(bf16[2,58,1024,128]{2,0,3,1:T(2,128)(2,1)} %copy.56, pred[2,58]{0,1:T(8,128)(4,1)S(1)} %copy.55), kind=kLoop, calls=%fused_computation.3 | loop fusion | flops 15204352 | bytes 60817524 | tf_op jit(solution)/shard_map/jit(_take)/select_n | solution.py:174
  547.2 212.0 %reduce-scatter.8.cloned.1.call-done = f32[384,2048]{1,0:T(8,128)} async-done(((f32[1536,2048]{1,0:T(8,128)}), f32[384,2048]{1,0:T(8,128)}) %reduce-scatter.8.cloned.1.call-update) | async-done | bytes 3145744 | tf_op jit(solution)/shard_map/reduce_scatter | solution.py:211
  765.3 115.9 %all-gather.9.cloned.1.call-done = bf16[1536,2048]{1,0:T(8,128)(2,1)} async-done(((bf16[384,2048]{1,0:T(8,128)(2,1)}), bf16[1536,2048]{1,0:T(8,128)(2,1)}) %all-gather.9.cloned.1.call-update) | async-done | bytes 6291472 | tf_op jit(solution)/shard_map/all_gather | solution.py:215
  881.2 33.7 %fusion.9 = f32[1536,4096]{1,0:T(8,128)} fusion(bf16[1536,2048]{1,0:T(8,128)(2,1)} %all-gather.9.cloned.1.call-done, bf16[2048,7424]{0,1:T(8,128)(2,1)} %bitcast.201), kind=kOutput, calls=%fused_computation.35 | convolution fusion | flops 25769803776 | bytes 48234496 | tf_op jit(solution)/shard_map/dot_general | solution.py:216
  914.9 81.3 %all-gather.11.cloned.1.call-done = bf16[1536,2048]{1,0:T(8,128)(2,1)} async-done(((bf16[384,2048]{1,0:T(8,128)(2,1)}), bf16[1536,2048]{1,0:T(8,128)(2,1)}) %all-gather.11.cloned.1.call-update) | async-done | bytes 6291472 | tf_op jit(solution)/shard_map/all_gather | solution.py:224
  996.2 28.4 %fusion.18 = (bf16[1536,2048]{1,0:T(8,128)(2,1)}, bf16[1536,2048]{1,0:T(8,128)(2,1)}, bf16[1536,2048]{1,0:T(8,128)(2,1)}) fusion(f32[1536,4096]{1,0:T(8,128)} %fusion.9, bf16[1536,2048]{1,0:T(8,128)(2,1)} %all-gather.11.cloned.1.call-done, bf16[2048,7424]{0,1:T(8,128)(2,1)} %bitcast.202), kind=kOutput, calls=%fused_computation.48 | convolution fusion | flops 12935233536 | bytes 58720256 | tf_op jit(solution)/shard_map/dot_general | solution.py:227
  1024.6 34.9 %fusion.34 = bf16[1536,2048]{1,0:T(8,128)(2,1)} fusion(bf16[2048,7424]{0,1:T(8,128)(2,1)} %bitcast.203, bf16[1536,2048]{1,0:T(8,128)(2,1)} %get-tuple-element.63, bf16[1536,2048]{1,0:T(8,128)(2,1)} %get-tuple-element.62), kind=kOutput, calls=%fused_computation.68 | convolution fusion | flops 25798115328 | bytes 35651584 | tf_op jit(solution)/shard_map/dot_general | solution.py:53
  1059.7 109.0 %reduce-scatter.12.cloned.1.call-done = bf16[384,2048]{1,0:T(8,128)(2,1)} async-done(((bf16[1536,2048]{1,0:T(8,128)(2,1)}), bf16[384,2048]{1,0:T(8,128)(2,1)}) %reduce-scatter.12.cloned.1.call-update) | async-done | bytes 1572880 | tf_op jit(solution)/shard_map/reduce_scatter | solution.py:237
  1176.5 115.9 %all-gather.13.cloned.1.call-done = bf16[1536,2048]{1,0:T(8,128)(2,1)} async-done(((bf16[384,2048]{1,0:T(8,128)(2,1)}), bf16[1536,2048]{1,0:T(8,128)(2,1)}) %all-gather.13.cloned.1.call-update) | async-done | bytes 6291472 | tf_op jit(solution)/shard_map/all_gather | solution.py:246
  1440.6 22.1 multiply_convert_fusion
  1540.9 34.7 %fusion.33 = f32[2048,4096]{1,0:T(8,128)} fusion(bf16[1536,2048]{1,0:T(8,128)(2,1)} %all-gather.9.cloned.1.call-done, bf16[1536,2048]{1,0:T(8,128)(2,1)} %get-tuple-element.63, bf16[1536,2048]{1,0:T(8,128)(2,1)} %get-tuple-element.62), kind=kOutput, calls=%fused_computation.66 | convolution fusion | flops 25794969600 | bytes 52428800 | tf_op jit(solution)/shard_map/dot_general | solution.py:47
  1588.3 39.5 %pad_maximum_fusion = f32[2048,7424]{1,0:T(8,128)} fusion(f32[2048,2048]{1,0:T(8,128)} %convolution_bitcast_fusion, f32[2048,4096]{1,0:T(8,128)} %fusion.33, f32[2048,512]{1,0:T(8,128)} %fusion.133, f32[2048,768]{1,0:T(8,128)S(1)} %fusion.90), kind=kLoop, calls=%fused_computation.2 | loop fusion | flops 45613056 | bytes 121634816 | tf_op jit(solution)/shard_map/concatenate | solution.py:273
  1627.8 63.3 %reshape.255 = f32[2,1024,58,128]{3,2,1,0:T(8,128)} reshape(f32[2048,7424]{1,0:T(8,128)} %pad_maximum_fusion) | data formatting | bytes 121634816 | tf_op jit(solution)/shard_map/reshape | solution.py:275
  1691.1 75.0 %copy.84 = f32[2,1024,58,128]{1,0,3,2:T(2,128)} copy(f32[2,1024,58,128]{3,2,1,0:T(8,128)} %reshape.255) | data formatting | bytes 121634816 | tf_op jit(solution)/shard_map/reshape | solution.py:275
  1766.2 87.2 %copy.62 = f32[2,58,1024,128]{3,2,1,0:T(8,128)} copy(f32[2,58,1024,128]{2,0,3,1:T(2,128)} %bitcast.195) | data formatting | bytes 121634816 | tf_op jit(solution)/shard_map/transpose | solution.py:274
  1853.3 33.6 %broadcast_in_dim.96 = f32[208,1024,128]{2,1,0:T(8,128)} broadcast(f32[]{:T(128)} %constant.22.clone.1), dimensions={} | broadcast | bytes 109051904 | tf_op jit(solution)/shard_map/broadcast_in_dim | solution.py:278
  1886.9 108.2 %scatter_fusion = f32[208,1024,128]{2,1,0:T(8,128)} fusion(f32[208,1024,128]{2,1,0:T(8,128)} %broadcast_in_dim.96, s32[116]{0:T(128)S(1)} %copy-done.65, f32[116,1024,128]{2,1,0:T(8,128)} %bitcast.196), kind=kCustom, calls=%fused_computation.1 | custom fusion | bytes 182452688 | tf_op jit(solution)/shard_map/scatter | solution.py:280
  1995.1 52.0 %convert_element_type.148 = bf16[208,1024,128]{2,1,0:T(8,128)(2,1)} convert(f32[208,1024,128]{2,1,0:T(8,128)} %scatter_fusion) | non-fusion elementwise | flops 27262976 | bytes 163577856 | tf_op jit(solution)/shard_map/convert_element_type | solution.py:283
  2051.3 37.8 %psum.7 = f32[2,2048]{1,0:T(2,128)S(1)} all-reduce(f32[2,2048]{1,0:T(2,128)S(1)} %pad_maximum_fusion.12), channel_id=1, replica_groups=mesh['wide'=8,'narrow'=4] {'wide','narrow'}, use_global_device_ids=true, to_apply=%region_23.24 | all-reduce | flops 4096 | bytes 32768 | tf_op jit(solution)/shard_map/psum | solution.py:288
  2097.6 255.8 %reduce-scatter.16.cloned.1.call-done = bf16[26,1024,128]{2,1,0:T(8,128)(2,1)} async-done(((bf16[208,1024,128]{2,1,0:T(8,128)(2,1)}), bf16[26,1024,128]{2,1,0:T(8,128)(2,1)}) %reduce-scatter.16.cloned.1.call-update) | async-done | bytes 6815760
  2363.2 29.5 %convert_bitcast_fusion.1 = (bf16[26,1,1024,128]{3,2,1,0:T(8,128)(2,1)}, f32[26,1,1024,128]{3,2,0,1:T(8,128)}, f32[26,1,1024,128]{3,2,1,0:T(8,128)}, f32[26,1,1024,128]{3,2,1,0:T(8,128)}) fusion(f32[26,1,1024,128]{3,2,1,0:T(8,128)} %param.16, bf16[26,1024,128]{2,1,0:T(8,128)(2,1)S(1)} %copy-done.6, f32[26,1,1024,128]{3,2,1,0:T(8,128)} %param.15, ...), kind=kLoop, calls=%fused_computation.73 | loop fusion | flops 54525952 | bytes 95420416
  (243 shorter events, 443.1 us)
Async XLA Ops:
  7.2 261.6 %all-gather.15.cloned.1.call-start = ((), (), s32[]{:S(2)}) async-start(), calls=%async_computation.13 | async-start | bytes 61341696 | tf_op jit(solution)/shard_map/all_gather | solution.py:173
  16.1 403.0 %all-gather.7.cloned.1.call-start = ((), (), s32[]{:S(2)}) async-start(), calls=%async_computation.5 | async-start | bytes 7864320 | tf_op jit(solution)/shard_map/all_gather | solution.py:201
  20.7 738.4 %reduce-scatter.8.cloned.1.call-start = ((), (), s32[]{:S(2)}) async-start(), calls=%async_computation.6 | async-start | bytes 15728640 | tf_op jit(solution)/shard_map/reduce_scatter | solution.py:211
  24.2 403.9 %copy-start.11 = (f32[1536,64]{0,1:T(8,128)}, f32[1536,64]{0,1:T(8,128)S(1)}, u32[]{:S(2)}) copy-start(f32[1536,64]{0,1:T(8,128)S(1)} %get-tuple-element.77) | copy-start | bytes 1179652
  24.3 403.9 %copy-start.13 = (f32[1536,64]{0,1:T(8,128)}, f32[1536,64]{0,1:T(8,128)S(1)}, u32[]{:S(2)}) copy-start(f32[1536,64]{0,1:T(8,128)S(1)} %get-tuple-element.78) | copy-start | bytes 1179652
  547.1 212.1 %copy-start.5 = (bf16[384,2048]{1,0:T(8,128)(2,1)S(1)}, bf16[384,2048]{1,0:T(8,128)(2,1)}, u32[]{:S(2)}) copy-start(bf16[384,2048]{1,0:T(8,128)(2,1)} %param.10) | copy-start | bytes 4718596
  547.1 216.0 %copy-start.28 = (f32[1,2048]{1,0:T(1,128)S(1)}, f32[1,2048]{1,0:T(1,128)}, u32[]{:S(2)}) copy-start(f32[1,2048]{1,0:T(1,128)} %get-tuple-element.79) | copy-start | bytes 24580
  547.1 334.1 %all-gather.9.cloned.1.call-start = ((), (), s32[]{:S(2)}) async-start(), calls=%async_computation.7 | async-start | bytes 7864320 | tf_op jit(solution)/shard_map/all_gather | solution.py:215
  764.6 231.6 %all-gather.11.cloned.1.call-start = ((), (), s32[]{:S(2)}) async-start(), calls=%async_computation.9 | async-start | bytes 7864320 | tf_op jit(solution)/shard_map/all_gather | solution.py:224
  765.2 403.5 %reduce-scatter.12.cloned.1.call-start = ((), (), s32[]{:S(2)}) async-start(), calls=%async_computation.10 | async-start | bytes 7864320 | tf_op jit(solution)/shard_map/reduce_scatter | solution.py:237
  1024.6 144.1 %copy-start.29 = (f32[1,2048]{1,0:T(1,128)S(1)}, f32[1,2048]{1,0:T(1,128)}, u32[]{:S(2)}) copy-start(f32[1,2048]{1,0:T(1,128)} %get-tuple-element.79) | copy-start | bytes 24580
  1024.6 144.1 %copy-start.50 = (f32[384]{0:T(512)S(1)}, f32[384]{0:T(512)}, u32[]{:S(2)}) copy-start(f32[384]{0:T(512)} %copy-done.49) | copy-start | bytes 4612
  1059.6 112.1 %copy-start.58 = (f32[384]{0:T(512)S(1)}, f32[384]{0:T(512)}, u32[]{:S(2)}) copy-start(f32[384]{0:T(512)} %copy-done.57) | copy-start | bytes 4612
  1059.6 116.8 %copy-start.32 = (f32[2,4,512]{2,1,0:T(4,128)S(1)}, f32[2,4,512]{2,1,0:T(4,128)}, u32[]{:S(2)}) copy-start(f32[2,4,512]{2,1,0:T(4,128)} %copy-done.31) | copy-start | bytes 49156
  1059.6 116.8 %copy-start.41 = (f32[2,4,512]{2,1,0:T(4,128)S(1)}, f32[2,4,512]{2,1,0:T(4,128)}, u32[]{:S(2)}) copy-start(f32[2,4,512]{2,1,0:T(4,128)} %copy-done.40) | copy-start | bytes 49156
  1059.6 116.8 %copy-start.34 = (f32[2,4,512]{2,1,0:T(4,128)S(1)}, f32[2,4,512]{2,1,0:T(4,128)}, u32[]{:S(2)}) copy-start(f32[2,4,512]{2,1,0:T(4,128)} %copy-done.33) | copy-start | bytes 49156
  1059.6 116.8 %copy-start.43 = (f32[2,4,512]{2,1,0:T(4,128)S(1)}, f32[2,4,512]{2,1,0:T(4,128)}, u32[]{:S(2)}) copy-start(f32[2,4,512]{2,1,0:T(4,128)} %copy-done.42) | copy-start | bytes 49156
  1059.6 116.8 %copy-start.36 = (f32[2,4,512]{2,1,0:T(4,128)S(1)}, f32[2,4,512]{2,1,0:T(4,128)}, u32[]{:S(2)}) copy-start(f32[2,4,512]{2,1,0:T(4,128)} %copy-done.35) | copy-start | bytes 49156
  1059.7 116.8 %copy-start.45 = (f32[2,4,512]{2,1,0:T(4,128)S(1)}, f32[2,4,512]{2,1,0:T(4,128)}, u32[]{:S(2)}) copy-start(f32[2,4,512]{2,1,0:T(4,128)} %copy-done.44) | copy-start | bytes 49156
  1059.7 232.7 %all-gather.13.cloned.1.call-start = ((), (), s32[]{:S(2)}) async-start(), calls=%async_computation.11 | async-start | bytes 7864320 | tf_op jit(solution)/shard_map/all_gather | solution.py:246
  1176.4 870.9 %reduce-scatter.14.cloned.1.call-start = ((), (), s32[]{:S(2)}) async-start(), calls=%async_computation.12 | async-start | bytes 7864320 | tf_op jit(solution)/shard_map/reduce_scatter | solution.py:267
  1176.4 159.9 %copy-start.26 = (f32[1,8,512]{2,1,0:T(8,128)}, f32[1,8,512]{2,1,0:T(8,128)S(1)}, u32[]{:S(2)}) copy-start(f32[1,8,512]{2,1,0:T(8,128)S(1)} %log_add_fusion) | copy-start | bytes 49156
  1501.1 588.7 %reduce-scatter.10.cloned.1.call-start = ((), (), s32[]{:S(2)}) async-start(), calls=%async_computation.8 | async-start | bytes 7864320 | tf_op jit(solution)/shard_map/reduce_scatter | solution.py:218
  1520.2 833.2 %reduce-scatter.16.cloned.1.call-start = ((), (), s32[]{:S(2)}) async-start(), calls=%async_computation.14 | async-start | bytes 61341696
  (55 other events, 1092.4 us)
Sparse Core Ops, SparseCore 0:
  16.3 252.4 all-gather.14
  270.9 115.3 all-gather.6
  547.2 211.8 reduce-scatter.7
  764.7 116.3 all-gather.8
  882.6 113.5 all-gather.10
  1059.7 108.9 reduce-scatter.11
  1176.5 115.8 all-gather.12
  1501.2 108.9 reduce-scatter.13
  1613.1 111.2 reduce-scatter.9
  2047.4 305.9 reduce-scatter.15
where the time goes:
time: 2420 us; the launch traced here: 2400 us
  waiting for transfers between devices  1130 us (47%)
  local copies, waits for them, and re-layouts  497 us (21%)
  matrix products  416 us (17%)
  other arithmetic  301 us (12%)
  blocking collectives  37.8 us (2%)
    unnamed x11, waiting for transfers between devices  256 us
    all_gather x1, waiting for transfers between devices, local(): all_slots = lax.all_gather(own_slots, 'wide', axis=0, tiled=True)  242 us
    reduce_scatter x1, waiting for transfers between devices, local(): lax.psum_scatter(matmul_cols(attended, w_out_t), 'narrow', scatter_dimens...  212 us
    reshape x2, local copies, waits for them, and re-layouts, local(): grad_packed.reshape(row_blocks, unit_rows, col_blocks, unit_cols)  138 us
    all_gather x1, waiting for transfers between devices, local(): mlp_input = lax.all_gather(normed_two, 'narrow', axis=0, tiled=True)  116 us
    all_gather x1, waiting for transfers between devices, local(): lax.all_gather(resid_back.astype(jnp.bfloat16), 'narrow', axis=0, tiled=T...  116 us
    reduce_scatter x1, waiting for transfers between devices, local(): lax.psum_scatter(matmul_cols(gate_up_back, w_gate_up).astype(jnp.bfloat16...  109 us
    scatter x1, local copies, waits for them, and re-layouts, local(): grad_slots = jnp.zeros((wide_count * capacity, unit_rows, unit_cols), jnp...  108 us
  transfers between devices with their start and end apart: 10, of which 7 were waited for; matrix products, arithmetic and copies ran while one was open for 31% of the time, Pallas kernels for 0%

commit v1 on v0

v1 whole, which is shorter than its diff:
```python
import functools

import jax
import jax.numpy as jnp
from jax import lax
from jax.experimental import pallas as pl
from jax.experimental.pallas import tpu as pltpu
from jax.sharding import PartitionSpec as P

D = 2048
H = 32
KV = 8
HD = 64
FF = 8192
STEP = 5
LANES = 128
MIB = 1 << 20

f32 = jnp.float32
bf16 = jnp.bfloat16


def dot(first_op, second_op, first_dim, second_dim):
    return lax.dot_general(
        first_op,
        second_op,
        (((first_dim,), (second_dim,)), ((), ())),
        preferred_element_type=f32,
    )


def params(mib):
    return pltpu.CompilerParams(vmem_limit_bytes=mib * MIB)


def cost(flops, moved, transcendentals=0):
    return pl.CostEstimate(
        flops=int(flops), bytes_accessed=int(moved), transcendentals=int(transcendentals)
    )


def tables(length_all, head_size):
    inverse = 500000.0 ** (-jnp.arange(0, head_size, 2, dtype=f32) / head_size)
    angles = jnp.arange(length_all, dtype=f32)[:, None] * inverse[None, :]
    angles = jnp.concatenate([angles, angles], axis=1)
    return (jnp.cos(angles), jnp.sin(angles))


def rmsnorm(values, weight_gain):
    return (
        values * lax.rsqrt(jnp.mean(values * values, axis=-1, keepdims=True) + 1e-05) * weight_gain
    )


def positions(owners, wide_count, capacity):
    onehot = (owners[:, None] == jnp.arange(wide_count, dtype=jnp.int32)[None, :]).astype(jnp.int32)
    before = jnp.cumsum(onehot, axis=0) - onehot
    return (owners * capacity + jnp.sum(before * onehot, axis=1), jnp.sum(onehot, axis=0))


def adamw(weight, gradient, moment_one, moment_two, rate, decay):
    moment_one = 0.5 * moment_one + 0.5 * gradient
    moment_two = 0.5 * moment_two + 0.5 * gradient * gradient
    correct = 1.0 - 0.5**STEP
    update = moment_one / correct / (jnp.sqrt(moment_two / correct) + 1e-08)
    return (weight - rate * (update + decay * weight), moment_one, moment_two)


def turn_kernel(unit_ref, out_ref):
    for k in range(out_ref.shape[0]):
        out_ref[k] = jnp.transpose(unit_ref[k, 0], (1, 0)).astype(bf16)


def turn_units(master):
    capacity, _, unit_rows, unit_cols = master.shape
    step = 2 if capacity % 2 == 0 else 1
    return pl.pallas_call(
        turn_kernel,
        grid=(capacity // step,),
        in_specs=[pl.BlockSpec((step, 1, unit_rows, unit_cols), lambda s: (s, 0, 0, 0))],
        out_specs=pl.BlockSpec((step, unit_cols, unit_rows), lambda s: (s, 0, 0)),
        out_shape=jax.ShapeDtypeStruct((capacity, unit_cols, unit_rows), bf16),
        compiler_params=params(32),
        cost_estimate=cost(0, master.size * 6),
        name="turn_units",
    )(master)


def pick_kernel(place_ref, got_ref, out_ref, sem, *, col_blocks, piece, unit_rows):
    def start(unit, carry):
        half = unit // col_blocks
        block = unit - half * col_blocks
        pltpu.make_async_copy(
            got_ref.at[place_ref[unit]],
            out_ref.at[
                pl.ds(pl.multiple_of(block * piece, piece), piece),
                pl.ds(pl.multiple_of(half * unit_rows, unit_rows), unit_rows),
            ],
            sem,
        ).start()
        return carry

    lax.fori_loop(0, place_ref.shape[0], start, 0)
    pltpu.make_async_copy(out_ref, out_ref, sem).wait()


def pick_units(got, slot_place, row_blocks):
    _, piece, unit_rows = got.shape
    unit_count = slot_place.shape[0]
    col_blocks = unit_count // row_blocks
    if piece % 16 == 0:
        return pl.pallas_call(
            functools.partial(
                pick_kernel, col_blocks=col_blocks, piece=piece, unit_rows=unit_rows
            ),
            in_specs=[
                pl.BlockSpec(memory_space=pltpu.SMEM),
                pl.BlockSpec(memory_space=pl.ANY),
            ],
            out_specs=pl.BlockSpec(memory_space=pl.ANY),
            out_shape=jax.ShapeDtypeStruct((col_blocks * piece, row_blocks * unit_rows), bf16),
            scratch_shapes=[pltpu.SemaphoreType.DMA],
            cost_estimate=cost(0, unit_count * piece * unit_rows * 4),
            name="pick_units",
        )(slot_place, got)
    units = jnp.take(got, slot_place, axis=0).reshape(row_blocks, col_blocks, piece, unit_rows)
    return jnp.transpose(units, (1, 2, 0, 3)).reshape(col_blocks * piece, row_blocks * unit_rows)


def unpick_kernel(unit_ref, rows_ref, out_ref, sem, *, col_blocks, piece, unit_rows):
    def start(slot, carry):
        unit = unit_ref[slot]
        half = unit // col_blocks
        block = unit - half * col_blocks
        pltpu.make_async_copy(
            rows_ref.at[
                pl.ds(pl.multiple_of(block * piece, piece), piece),
                pl.ds(pl.multiple_of(half * unit_rows, unit_rows), unit_rows),
            ],
            out_ref.at[slot],
            sem,
        ).start()
        return carry

    lax.fori_loop(0, unit_ref.shape[0], start, 0)
    pltpu.make_async_copy(out_ref, out_ref, sem).wait()


def unpick_units(rows, unit_of, unit_count, piece, unit_rows):
    row_blocks = rows.shape[1] // unit_rows
    col_blocks = unit_count // row_blocks
    slots = unit_of.shape[0]
    if piece % 16 == 0:
        return pl.pallas_call(
            functools.partial(
                unpick_kernel, col_blocks=col_blocks, piece=piece, unit_rows=unit_rows
            ),
            in_specs=[
                pl.BlockSpec(memory_space=pltpu.SMEM),
                pl.BlockSpec(memory_space=pl.ANY),
            ],
            out_specs=pl.BlockSpec(memory_space=pl.ANY),
            out_shape=jax.ShapeDtypeStruct((slots, piece, unit_rows), bf16),
            scratch_shapes=[pltpu.SemaphoreType.DMA],
            cost_estimate=cost(0, slots * piece * unit_rows * 4),
            name="unpick_units",
        )(unit_of, rows)
    units = jnp.transpose(
        rows.reshape(col_blocks, piece, row_blocks, unit_rows), (2, 0, 1, 3)
    ).reshape(unit_count, piece, unit_rows)
    return jnp.take(units, unit_of, axis=0)


def update_kernel(
    count_ref, grad_ref, master_ref, one_ref, two_ref,
    grad_out, master_out, copy_out, one_out, two_out,
):
    filled = pl.program_id(0) < count_ref[0]
    parts, _, piece, unit_rows = grad_ref.shape
    turned = grad_ref[:, 0].astype(f32).reshape(parts * piece, unit_rows)
    gradient = jnp.where(filled, jnp.transpose(turned, (1, 0)), 0.0)
    weight, one, two = adamw(master_ref[0, 0], gradient, one_ref[0, 0], two_ref[0, 0], 0.02, 0.1)
    grad_out[0, 0] = gradient
    master_out[0, 0] = weight
    copy_out[0, 0] = weight.astype(bf16)
    one_out[0, 0] = one
    two_out[0, 0] = two


def update_units(count, grads, master, moment_one, moment_two):
    capacity, _, unit_rows, unit_cols = master.shape
    parts, _, piece, _ = grads.shape
    unit = pl.BlockSpec((1, 1, unit_rows, unit_cols), lambda s: (s, 0, 0, 0))
    whole = jax.ShapeDtypeStruct(master.shape, f32)
    return pl.pallas_call(
        update_kernel,
        grid=(capacity,),
        in_specs=[
            pl.BlockSpec(memory_space=pltpu.SMEM),
            pl.BlockSpec((parts, 1, piece, unit_rows), lambda s: (0, s, 0, 0)),
            unit,
            unit,
            unit,
        ],
        out_specs=[unit] * 5,
        out_shape=[whole, whole, jax.ShapeDtypeStruct(master.shape, bf16), whole, whole],
        compiler_params=params(40),
        cost_estimate=cost(master.size * 12, master.size * 32),
        name="update_units",
    )(count, grads, master, moment_one, moment_two)


def lane_index(shape):
    return lax.broadcasted_iota(jnp.int32, shape, 1)


def rope(tile, cos_tile, sin_tile):
    lower = lane_index(tile.shape) % HD < HD // 2
    ahead = pltpu.roll(tile, LANES - HD // 2, 1)
    behind = pltpu.roll(tile, HD // 2, 1)
    return tile * cos_tile + jnp.where(lower, -ahead, behind) * sin_tile


def unrope(tile, cos_tile, sin_tile):
    lower = lane_index(tile.shape) % HD < HD // 2
    weighted = tile * sin_tile
    ahead = pltpu.roll(weighted, LANES - HD // 2, 1)
    behind = pltpu.roll(weighted, HD // 2, 1)
    return tile * cos_tile + jnp.where(lower, ahead, -behind)


def project_kernel(rows_ref, w_ref, cos_ref, sin_ref, out_ref, *, query_width, kv_width):
    product = dot(rows_ref[...], w_ref[...], 1, 1)
    roped_end = query_width + kv_width
    for start in range(0, out_ref.shape[1], LANES):
        tile = product[:, start : start + LANES]
        if start < roped_end:
            turned = rope(tile, cos_ref[...], sin_ref[...])
            if start + LANES > roped_end:
                tile = jnp.where(lane_index(tile.shape) < roped_end - start, turned, tile)
            else:
                tile = turned
        tile = tile.astype(bf16)
        if start < query_width:
            tile = tile * HD ** (-0.5)
        out_ref[:, start : start + LANES] = tile


def project(rows, w_qkv, cos_rows, sin_rows, query_width, kv_width):
    count = rows.shape[0]
    width = w_qkv.shape[0]
    return pl.pallas_call(
        functools.partial(project_kernel, query_width=query_width, kv_width=kv_width),
        out_shape=jax.ShapeDtypeStruct((count, width), bf16),
        compiler_params=params(40),
        cost_estimate=cost(2 * count * width * D, 2 * (count + width) * D),
        name="project",
    )(rows, w_qkv, cos_rows, sin_rows)


def extend(tile_ref, offset, out_ref):
    tile = tile_ref[...].astype(f32)
    other = pltpu.roll(tile, HD, 1)
    low = lane_index(tile.shape) < HD
    at_low = offset == 0
    out_ref[0] = jnp.where(low, jnp.where(at_low, tile, other), 0.0).astype(bf16)
    out_ref[1] = jnp.where(low, 0.0, jnp.where(at_low, other, tile)).astype(bf16)


def forward_kernel(
    length_ref, q_ref, k_ref, v_ref, out_ref, log_ref, kx, vx, *, block, pairs_per, k_start, v_start
):
    pair = pl.program_id(0)
    kv_head = pair // pairs_per
    length = length_ref[0]
    seq_len = q_ref.shape[0]

    @pl.when(pair % pairs_per == 0)
    def _():
        extend(k_ref, (k_start + kv_head * HD) % LANES, kx)
        extend(v_ref, (v_start + kv_head * HD) % LANES, vx)

    row = lax.broadcasted_iota(jnp.int32, (block, block), 0)
    col = lax.broadcasted_iota(jnp.int32, (block, block), 1)
    causal = col <= row
    key_row = lax.broadcasted_iota(jnp.int32, (1, seq_len), 1)
    bias = jnp.where(key_row < length, 0.0, -1e30).astype(f32)
    low = lane_index((block, LANES)) < HD
    for start in range(0, seq_len, block):
        query = q_ref[start : start + block, :]
        total = None
        logs = []
        for half in range(2):
            diagonal = dot(query, kx[half, start : start + block, :], 1, 1)
            diagonal = jnp.where(causal, diagonal + bias[:, start : start + block], -1e30)
            peak = jnp.max(diagonal, axis=1, keepdims=True)
            if start:
                before = dot(query, kx[half, :start, :], 1, 1) + bias[:, :start]
                peak = jnp.maximum(peak, jnp.max(before, axis=1, keepdims=True))
                before = jnp.exp(before - peak)
            diagonal = jnp.exp(diagonal - peak)
            row_sum = jnp.sum(diagonal, axis=1, keepdims=True)
            part = dot(diagonal.astype(bf16), vx[half, start : start + block, :], 1, 0)
            if start:
                row_sum = row_sum + jnp.sum(before, axis=1, keepdims=True)
                part = part + dot(before.astype(bf16), vx[half, :start, :], 1, 0)
            part = part / row_sum
            total = part if total is None else total + part
            logs.append(peak + jnp.log(row_sum))
        out_ref[start : start + block, :] = total.astype(bf16)
        tile = jnp.transpose(jnp.where(low, logs[0], logs[1]), (1, 0))
        log_ref[0, 0:1, start : start + block] = tile[0:1]
        log_ref[0, 1:2, start : start + block] = tile[HD : HD + 1]


def attend_forward(length, qkv, query_width, kv_width, block):
    seq_len = qkv.shape[0]
    pairs = query_width // LANES
    pairs_per = H // KV // 2
    k_start = query_width
    v_start = query_width + kv_width
    column = functools.partial(pl.BlockSpec, (seq_len, LANES))
    return pl.pallas_call(
        functools.partial(
            forward_kernel, block=block, pairs_per=pairs_per, k_start=k_start, v_start=v_start
        ),
        grid=(pairs,),
        in_specs=[
            pl.BlockSpec(memory_space=pltpu.SMEM),
            column(lambda p: (0, p)),
            column(lambda p: (0, (k_start + p // pairs_per * HD) // LANES)),
            column(lambda p: (0, (v_start + p // pairs_per * HD) // LANES)),
        ],
        out_specs=[
            column(lambda p: (0, p)),
            pl.BlockSpec((1, 8, seq_len), lambda p: (p, 0, 0)),
        ],
        out_shape=[
            jax.ShapeDtypeStruct((seq_len, query_width), bf16),
            jax.ShapeDtypeStruct((pairs, 8, seq_len), f32),
        ],
        scratch_shapes=[
            pltpu.VMEM((2, seq_len, LANES), bf16),
            pltpu.VMEM((2, seq_len, LANES), bf16),
        ],
        compiler_params=params(56),
        cost_estimate=cost(pairs * seq_len * seq_len * 1024, seq_len * 768 * 4),
        name="attend_forward",
    )(length, qkv, qkv, qkv)


def backward_kernel(
    length_ref, q_ref, k_ref, v_ref, back_ref, out_ref, log_ref, cos_ref, sin_ref, grad_ref,
    kx, vx, dk, dv, *, block, pairs_per, k_start, v_start,
):
    pair = pl.program_id(0)
    kv_head = pair // pairs_per
    length = length_ref[0]
    seq_len = q_ref.shape[0]
    k_offset = (k_start + kv_head * HD) % LANES
    v_offset = (v_start + kv_head * HD) % LANES

    @pl.when(pair == 0)
    def _():
        grad_ref[:, k_start // LANES * LANES :] = jnp.zeros(
            (seq_len, grad_ref.shape[1] - k_start // LANES * LANES), bf16
        )

    @pl.when(pair % pairs_per == 0)
    def _():
        extend(k_ref, k_offset, kx)
        extend(v_ref, v_offset, vx)
        dk[...] = jnp.zeros(dk.shape, f32)
        dv[...] = jnp.zeros(dv.shape, f32)

    key = lax.broadcasted_iota(jnp.int32, (block, block), 0)
    row = lax.broadcasted_iota(jnp.int32, (block, block), 1)
    causal = key <= row
    for start in range(0, seq_len, block):
        here = slice(start, start + block)
        query = q_ref[here, :]
        back = back_ref[here, :]
        turned = jnp.transpose(back.astype(f32) * out_ref[here, :].astype(f32), (1, 0))
        query_grad = None
        for half in range(2):
            log_row = log_ref[0, half : half + 1, here]
            shift = jnp.sum(turned[half * HD : half * HD + HD], axis=0, keepdims=True)
            for first in range(0, start + block, block):
                keys = slice(first, first + block)
                scores = dot(kx[half, keys, :], query, 1, 1)
                probs = jnp.exp(scores - log_row)
                if first + block > seq_len // 2:
                    probs = jnp.where(key + first < length, probs, 0.0)
                if first == start:
                    probs = jnp.where(causal, probs, 0.0)
                probs_back = dot(vx[half, keys, :], back, 1, 1)
                scores_back = (probs * (probs_back - shift)).astype(bf16)
                dv[half, keys, :] += dot(probs.astype(bf16), back, 1, 0)
                dk[half, keys, :] += dot(scores_back, query, 1, 0)
                part = dot(scores_back, kx[half, keys, :], 0, 0)
                query_grad = part if query_grad is None else query_grad + part
        query_grad = unrope(query_grad * HD ** (-0.5), cos_ref[here, :], sin_ref[here, :])
        grad_ref[here, pl.ds(pl.multiple_of(pair * LANES, LANES), LANES)] = query_grad.astype(bf16)

    @pl.when(pair % pairs_per == pairs_per - 1)
    def _():
        low = lane_index((seq_len, LANES)) < HD

        def place(sums, offset, start, roped):
            joined = jnp.where(low, sums[0], 0.0) + pltpu.roll(
                jnp.where(low, 0.0, sums[1]), HD, 1
            )
            if roped:
                joined = unrope(joined, cos_ref[...], sin_ref[...])
            joined = jnp.where(offset == 0, joined, pltpu.roll(joined, HD, 1))
            tile = pl.ds(
                pl.multiple_of((start + kv_head * HD) // LANES * LANES, LANES), LANES
            )
            grad_ref[:, tile] = (grad_ref[:, tile].astype(f32) + joined).astype(bf16)

        place(dk[...], k_offset, k_start, True)
        place(dv[...], v_offset, v_start, False)


def attend_backward(length, qkv, back, out, logs, cos_all, sin_all, query_width, kv_width, block):
    seq_len, width = qkv.shape
    pairs = query_width // LANES
    pairs_per = H // KV // 2
    k_start = query_width
    v_start = query_width + kv_width
    column = functools.partial(pl.BlockSpec, (seq_len, LANES))
    return pl.pallas_call(
        functools.partial(
            backward_kernel, block=block, pairs_per=pairs_per, k_start=k_start, v_start=v_start
        ),
        grid=(pairs,),
        in_specs=[
            pl.BlockSpec(memory_space=pltpu.SMEM),
            column(lambda p: (0, p)),
            column(lambda p: (0, (k_start + p // pairs_per * HD) // LANES)),
            column(lambda p: (0, (v_start + p // pairs_per * HD) // LANES)),
            column(lambda p: (0, p)),
            column(lambda p: (0, p)),
            pl.BlockSpec((1, 8, seq_len), lambda p: (p, 0, 0)),
            column(lambda p: (0, 0)),
            column(lambda p: (0, 0)),
        ],
        out_specs=pl.BlockSpec((seq_len, width), lambda p: (0, 0)),
        out_shape=jax.ShapeDtypeStruct((seq_len, width), bf16),
        scratch_shapes=[
            pltpu.VMEM((2, seq_len, LANES), bf16),
            pltpu.VMEM((2, seq_len, LANES), bf16),
            pltpu.VMEM((2, seq_len, LANES), f32),
            pltpu.VMEM((2, seq_len, LANES), f32),
        ],
        compiler_params=params(56),
        cost_estimate=cost(pairs * seq_len * seq_len * 2560, seq_len * 768 * 6),
        name="attend_backward",
    )(length, qkv, qkv, qkv, back, out, logs, cos_all, sin_all)


def hidden_kernel(rows_ref, back_ref, wg_ref, wu_ref, wd_ref, hid_ref, dgate_ref, dup_ref):
    gate = dot(rows_ref[...], wg_ref[...], 1, 1)
    up = dot(rows_ref[...], wu_ref[...], 1, 1)
    hidden_back = dot(back_ref[...], wd_ref[...], 1, 1)
    sig = 1.0 / (1.0 + jnp.exp(-gate))
    silu = gate * sig
    hid_ref[...] = (silu * up).astype(bf16)
    dgate_ref[...] = (hidden_back * up * (sig * (1.0 + gate * (1.0 - sig)))).astype(bf16)
    dup_ref[...] = (hidden_back * silu).astype(bf16)


def hidden_pass(rows, back, wg, wu, wd):
    count = rows.shape[0]
    ff_width = wg.shape[0]
    step = 256
    resident = pl.BlockSpec((count, D), lambda i: (0, 0))
    weight = pl.BlockSpec((step, D), lambda i: (i, 0))
    given = pl.BlockSpec((count, step), lambda i: (0, i))
    shape = jax.ShapeDtypeStruct((count, ff_width), bf16)
    return pl.pallas_call(
        hidden_kernel,
        grid=(ff_width // step,),
        in_specs=[resident, resident, weight, weight, weight],
        out_specs=[given] * 3,
        out_shape=[shape] * 3,
        compiler_params=params(48),
        cost_estimate=cost(6 * count * ff_width * D, 6 * ff_width * D, count * ff_width),
        name="hidden_pass",
    )(rows, back, wg, wu, wd)


def outer_kernel(*refs):
    out_ref = refs[-1]
    count = (len(refs) - 1) // 2
    total = None
    for k in range(count):
        part = dot(refs[k][...], refs[count + k][...], 0, 0)
        total = part if total is None else total + part
    out_ref[...] = total.astype(bf16)


def outer(firsts, seconds):
    rows, height = firsts[0].shape
    width = seconds[0].shape[1]
    step = 512 if height % 512 == 0 else 256 if height % 256 == 0 else LANES
    chunks = len(firsts)
    return pl.pallas_call(
        outer_kernel,
        grid=(height // step,),
        in_specs=[pl.BlockSpec((rows, step), lambda i: (0, i))] * chunks
        + [pl.BlockSpec((rows, width), lambda i: (0, 0))] * chunks,
        out_specs=pl.BlockSpec((step, width), lambda i: (i, 0)),
        out_shape=jax.ShapeDtypeStruct((height, width), bf16),
        compiler_params=params(56),
        cost_estimate=cost(
            2 * chunks * rows * height * width,
            2 * (chunks * rows * (height + width) + height * width),
        ),
        name="outer",
    )(*firsts, *seconds)


def cycle(count, step=1):
    return [(i, (i + step) % count) for i in range(count)]


def ring_gather(own, count):
    blocks = [own]
    for _ in range(count - 1):
        blocks.append(lax.ppermute(blocks[-1], "narrow", cycle(count)))
    return blocks


def ring_reduce(parts, count):
    total = parts[1]().astype(bf16)
    for s in range(2, count):
        total = (parts[s]() + lax.ppermute(total, "narrow", cycle(count)).astype(f32)).astype(bf16)
    return parts[0]() + lax.ppermute(total, "narrow", cycle(count)).astype(f32)


def square_pairs(step):
    order = (0, 1, 3, 2)
    pairs = []
    for place, chip in enumerate(order):
        target = order[(place + step) % 4]
        pairs += [(chip * 2 + core, target * 2 + core) for core in range(2)]
    return pairs


def swap_pairs():
    return [(i, i ^ 1) for i in range(8)]


def plane_gather(halves):
    first, second = halves
    blocks = [first, second]
    for _ in range(3):
        first = lax.ppermute(first, "wide", square_pairs(1))
        second = lax.ppermute(second, "wide", square_pairs(-1))
        blocks += [first, second]
    return blocks + [lax.ppermute(block, "wide", swap_pairs()) for block in blocks]


def plane_reduce(grad):
    half = grad.shape[0] // 2
    own = grad[:half].astype(f32) + lax.ppermute(grad[half:], "wide", swap_pairs()).astype(f32)
    own = own.astype(bf16)
    size = half // 8
    blocks = [own[k * size : (k + 1) * size] for k in range(8)]
    ends = []
    for side, step in ((0, 1), (1, -1)):
        total = blocks[2 + side]
        for s in (2, 3, 0):
            total = (
                blocks[2 * s + side].astype(f32)
                + lax.ppermute(total, "wide", square_pairs(step)).astype(f32)
            ).astype(bf16)
        ends.append(total)
    return ends


def local(
    tokens, cotangent, lengths, owners, master, moment_one, moment_two, norm_gains, gain_first,
    gain_second,
):
    wide_count = lax.axis_size("wide")
    narrow_count = lax.axis_size("narrow")
    capacity, _, unit_rows, unit_cols = master.shape
    unit_count = owners.shape[0]
    row_count = tokens.shape[0]
    seq_len = row_count * narrow_count
    row_blocks = D // unit_rows
    piece = unit_cols // wide_count
    query_width = H // narrow_count * HD
    kv_width = KV // narrow_count * HD
    ff_width = FF // narrow_count
    qkv_width = query_width + 2 * kv_width
    wide_index = lax.axis_index("wide")
    narrow_index = lax.axis_index("narrow")
    length = lax.dynamic_slice(lengths, (wide_index,), (1,))
    block = min(256, seq_len)

    inputs = tokens.astype(f32)
    normed = rmsnorm(inputs, norm_gains[0]).astype(bf16)
    normed_blocks = ring_gather(normed, narrow_count)

    slot_place, counts = positions(owners, wide_count, capacity)
    turned = turn_units(master).reshape(capacity, wide_count, piece, unit_rows)
    got = lax.all_to_all(turned, "wide", split_axis=1, concat_axis=0)
    got = got.reshape(wide_count * capacity, piece, unit_rows)
    rows = pick_units(got, slot_place, row_blocks)
    qkv_end = qkv_width // wide_count
    out_end = qkv_end + query_width // wide_count
    ff_rows = ff_width // wide_count

    def plane_all(part, width):
        gathered = lax.all_gather(part, "wide", axis=0)
        gathered = gathered.reshape(wide_count, width // unit_cols, piece, D)
        return jnp.transpose(gathered, (1, 0, 2, 3)).reshape(width, D)

    w_qkv = plane_all(rows[:qkv_end], qkv_width)
    out_part = lax.all_gather(rows[qkv_end:out_end], "narrow", axis=0)
    w_out = lax.all_gather(out_part, "wide", axis=0)
    w_out = jnp.transpose(
        w_out.reshape(wide_count, narrow_count, query_width // unit_cols, piece, D),
        (1, 2, 0, 3, 4),
    ).reshape(D, D)
    ff_parts = [rows[out_end + k * ff_rows : out_end + (k + 1) * ff_rows] for k in range(3)]
    if wide_count == 8:
        half = ff_rows // 2
        halves = [
            jnp.concatenate([part[:half] for part in ff_parts], axis=0),
            jnp.concatenate([part[half:] for part in ff_parts], axis=0),
        ]
        ff_blocks = plane_gather(halves)
        w_gate, w_upper, w_down = [
            jnp.concatenate([b[k * half : (k + 1) * half] for b in ff_blocks], axis=0)
            for k in range(3)
        ]
    else:
        w_gate, w_upper, w_down = [
            lax.all_gather(part, "wide", axis=0, tiled=True) for part in ff_parts
        ]

    cos_table, sin_table = tables(seq_len, HD)
    cos_all = jnp.concatenate([cos_table] * (LANES // HD), axis=1)
    sin_all = jnp.concatenate([sin_table] * (LANES // HD), axis=1)
    projected = []
    for s in range(narrow_count):
        first_row = (narrow_index - s) % narrow_count * row_count
        projected.append(
            project(
                normed_blocks[s],
                w_qkv,
                lax.dynamic_slice(cos_all, (first_row, 0), (row_count, LANES)),
                lax.dynamic_slice(sin_all, (first_row, 0), (row_count, LANES)),
                query_width,
                kv_width,
            )
        )
    back_by = (narrow_index - jnp.arange(narrow_count, dtype=jnp.int32)) % narrow_count
    qkv = jnp.take(jnp.stack(projected), back_by, axis=0).reshape(seq_len, qkv_width)
    attended, logs = attend_forward(length, qkv, query_width, kv_width, block)
    attended_rows = lax.all_to_all(
        attended.reshape(narrow_count, row_count, query_width), "narrow", 0, 0
    )
    attended_rows = jnp.transpose(attended_rows, (1, 0, 2)).reshape(row_count, D)
    residual = inputs + dot(attended_rows, w_out, 1, 0)

    normed_two = rmsnorm(residual, norm_gains[1]).astype(bf16)
    mlp_blocks = ring_gather(normed_two, narrow_count)
    back_blocks = ring_gather(cotangent, narrow_count)
    passes = [
        hidden_pass(mlp_blocks[s], back_blocks[s], w_gate, w_upper, w_down)
        for s in range(narrow_count)
    ]

    def norm_back_part(s):
        return lambda: dot(passes[s][1], w_gate, 1, 0) + dot(passes[s][2], w_upper, 1, 0)

    norm_two_back = ring_reduce([norm_back_part(s) for s in range(narrow_count)], narrow_count)
    output = residual + ring_reduce(
        [functools.partial(dot, passes[s][0], w_down, 1, 0) for s in range(narrow_count)],
        narrow_count,
    )
    ff_grads = [
        outer([p[1] for p in passes], mlp_blocks),
        outer([p[2] for p in passes], mlp_blocks),
        outer([p[0] for p in passes], back_blocks),
    ]

    def plane_sum(grad):
        if wide_count == 8:
            return plane_reduce(grad)
        return [lax.psum_scatter(grad, "wide", scatter_dimension=0, tiled=True)]

    ff_sums = [part for grad in ff_grads for part in plane_sum(grad)]

    _, norm_two_pull = jax.vjp(rmsnorm, residual, norm_gains[1])
    resid_part, gain_two = norm_two_pull(norm_two_back)
    resid_back = cotangent.astype(f32) + resid_part
    attn_back = resid_back.astype(bf16)
    out_back = dot(attn_back, w_out, 1, 1).astype(bf16)
    out_back = jnp.transpose(out_back.reshape(row_count, narrow_count, query_width), (1, 0, 2))
    out_back = lax.all_to_all(out_back, "narrow", 0, 0).reshape(seq_len, query_width)
    grad_out = outer([attended_rows], [attn_back])
    qkv_back = attend_backward(
        length, qkv, out_back, attended, logs, cos_all, sin_all, query_width, kv_width, block
    )
    qkv_blocks = [
        lax.dynamic_slice(
            qkv_back, ((narrow_index - s) % narrow_count * row_count, 0), (row_count, qkv_width)
        )
        for s in range(narrow_count)
    ]
    grad_qkv = outer(qkv_blocks, normed_blocks)

    def plane_split(grad, width, lead):
        shaped = grad.reshape(lead, width // unit_cols, wide_count, piece, D)
        shaped = jnp.transpose(shaped, (2, 0, 1, 3, 4)).reshape(wide_count * lead * width // wide_count, D)
        return lax.psum_scatter(shaped, "wide", scatter_dimension=0, tiled=True)

    grad_out = plane_split(grad_out, query_width, narrow_count)
    grad_out = lax.psum_scatter(grad_out, "narrow", scatter_dimension=0, tiled=True)
    grad_qkv = plane_split(grad_qkv, qkv_width, 1)

    grad_rows = jnp.concatenate([grad_qkv, grad_out] + ff_sums, axis=0)
    slots = wide_count * capacity
    unit_of = jnp.zeros((slots,), jnp.int32).at[slot_place].set(
        jnp.arange(unit_count, dtype=jnp.int32)
    )
    sent = unpick_units(grad_rows, unit_of, unit_count, piece, unit_rows)
    sent = sent.reshape(wide_count, capacity, piece, unit_rows)
    owned = lax.all_to_all(sent, "wide", split_axis=0, concat_axis=0)
    count = lax.dynamic_slice(counts, (wide_index,), (1,))
    owned_grads, new_master, new_copy, new_first, new_second = update_units(
        count, owned, master, moment_one, moment_two
    )

    norm_one_back = ring_reduce(
        [functools.partial(dot, qkv_blocks[s], w_qkv, 1, 0) for s in range(narrow_count)],
        narrow_count,
    )
    _, norm_one_pull = jax.vjp(rmsnorm, inputs, norm_gains[0])
    input_part, gain_one = norm_one_pull(norm_one_back)
    input_grad = (resid_back + input_part).astype(bf16)
    gain_grads = lax.psum(jnp.stack([gain_one, gain_two]), ("wide", "narrow"))
    new_gains, _, gain_second_new = adamw(
        norm_gains, gain_grads, gain_first, gain_second, 0.5, 0.0
    )
    return (
        output.astype(bf16),
        input_grad,
        owned_grads,
        new_master,
        new_copy,
        new_first,
        new_second,
        gain_grads,
        gain_second_new,
        new_gains,
    )


def solution(mesh):
    rows = P(("wide", "narrow"), None)
    units = P("wide", "narrow", None, None)
    return jax.shard_map(
        local,
        mesh=mesh,
        in_specs=(rows, rows, P(), P(), units, units, units, P(), P(), P()),
        out_specs=(rows, rows, units, units, units, units, units, P(), P(), P()),
        check_vma=False,
    )
```

time: 2420 us -> 1580 us (0.65)
  Pallas kernels: 0 us -> 625 us
  waiting for transfers between devices: 1130 us -> 540 us
  local copies, waits for them, and re-layouts: 497 us -> 109 us
  matrix products: 416 us -> 115 us
  other arithmetic: 301 us -> 73.5 us
  starting transfers between devices: 0.41 us -> 49.3 us
    pallas_call x0 -> x19, Pallas kernels: none -> 625 us  [the longest x1 208 us: unpick_units(): pl.pallas_call(functools.partial(unpick_kernel, col_blocks=col_blocks, pi...]
    all_gather x5 -> x3, waiting for transfers between devices: 555 us -> 26.3 us  [the longest x1 26.3 us: local(): out_part = lax.all_gather(rows[qkv_end:out_end], 'narrow', axis=0)]
    ppermute x0 -> x53, waiting for transfers between devices: none -> 408 us  [the longest x9 184 us: ring_gather(): blocks.append(lax.ppermute(blocks[-1], 'narrow', cycle(count)))]
    reduce_scatter x4 -> x3, waiting for transfers between devices: 321 us -> 5.77 us  [the longest x1 5.77 us: local(): lax.psum_scatter(grad_out, 'narrow', scatter_dimension=0, tiled=True)]
    dot_general x30 -> x18, matrix products: 416 us -> 115 us  [dot(): lax.dot_general(first_op, second_op, (((first_dim,), (second_dim,)), ((),...]
    unnamed x11 -> x6, waiting for transfers between devices: 256 us -> 0.1 us
    reshape x2 -> x5, local copies, waits for them, and re-layouts: 138 us -> 17.3 us  [the longest x2 12.4 us: plane_split(): shaped = grad.reshape(lead, width // unit_cols, wide_count, piece, D)]
    scatter x1, local copies, waits for them, and re-layouts: 108 us -> 2.06 us  [local(): jnp.zeros((slots,), jnp.int32).at[slot_place]]
  transfers between devices with their start and end apart: 10 -> 63, of which waited for: 7 -> 28; matrix products, arithmetic and copies ran while one was open for 31% -> 16% of each run, Pallas kernels for 0% -> 29%
where the time goes in v1:
time: 1580 us; the launch traced here: 1570 us
  Pallas kernels  625 us (40%)
  waiting for transfers between devices  540 us (34%)
  matrix products  115 us (7%)
  local copies, waits for them, and re-layouts  109 us (7%)
  other arithmetic  73.5 us (5%)
  starting transfers between devices  49.3 us (3%)
  blocking collectives  38.3 us (2%)
    pallas_call x1, Pallas kernels, unpick_units(): pl.pallas_call(functools.partial(unpick_kernel, col_blocks=col_blocks, pi...  208 us
    ppermute x9, waiting for transfers between devices, ring_gather(): blocks.append(lax.ppermute(blocks[-1], 'narrow', cycle(count)))  184 us
    pallas_call x1, Pallas kernels, pick_units(): pl.pallas_call(functools.partial(pick_kernel, col_blocks=col_blocks, piec...  117 us
    dot_general x18, matrix products, dot(): lax.dot_general(first_op, second_op, (((first_dim,), (second_dim,)), ((),...  115 us
    pallas_call x5, Pallas kernels, outer(): pl.pallas_call(outer_kernel, grid=(height // step,), in_specs=[pl.BlockSp...  89.4 us
    ppermute x18, waiting for transfers between devices, plane_reduce(): lax.ppermute(total, 'wide', square_pairs(step)).astype(f32)  86.1 us
    all_to_all x1, waiting for transfers between devices, local(): got = lax.all_to_all(turned, 'wide', split_axis=1, concat_axis=0)  76.1 us
    ppermute x3, waiting for transfers between devices, ring_reduce(): return parts[0]() + lax.ppermute(total, 'narrow', cycle(count)).astype(f32)  71.3 us
  transfers between devices with their start and end apart: 63, of which 28 were waited for; matrix products, arithmetic and copies ran while one was open for 16% of the time, Pallas kernels for 29%

profile of v1, /device:TPU:0, one launch (start us, length us, event | category | flops | bytes accessed | tf_op | source)
XLA Modules:
  0.0 1565.2 jit_solution(2942631972624926126)
XLA Ops:
  25.2 76.1 %all-to-all-done = bf16[1,26,8,16,1024]{4,3,1,0,2:T(8,128)(2,1)} async-done(((bf16[1,26,8,16,1024]{4,3,1,0,2:T(8,128)(2,1)}), bf16[1,26,8,16,1024]{4,3,1,0,2:T(8,128)(2,1)}, u32[]{:S(2)}, u32[]{:S(2)}) %all-to-all-start) | async-done | bytes 6815776 | tf_op jit(solution)/shard_map/all_to_all | solution.py:610
  101.3 116.9 %pick_units.1 = bf16[928,2048]{1,0:T(8,128)(2,1)} custom-call(s32[116]{0:T(128)} %get-tuple-element.57.place_ref, bf16[208,16,1024]{2,1,0:T(8,128)(2,1)} %bitcast.4.got_ref), custom_call_target="tpu_custom_call" | custom-call | bytes 7602176 | tf_op jit(solution)/shard_map/pick_units/pallas_call | solution.py:112
  222.0 26.3 %all-gather.9.cloned.1.call-done = bf16[256,2048]{1,0:T(8,128)(2,1)} async-done(((bf16[64,2048]{1,0:T(8,128)(2,1)}), bf16[256,2048]{1,0:T(8,128)(2,1)}) %all-gather.9.cloned.1.call-update) | async-done | bytes 1048592 | tf_op jit(solution)/shard_map/all_gather | solution.py:623
  255.5 33.5 %collective-permute-done.rows_ref.refs_5_ = bf16[384,2048]{1,0:T(8,128)(2,1)S(1)} collective-permute-done((bf16[384,2048]{1,0:T(8,128)(2,1)S(1)}, bf16[384,2048]{1,0:T(8,128)(2,1)S(1)}, u32[]{:S(2)}, u32[]{:S(2)}) %collective-permute-start) | collective-permute-done | bytes 1572896 | tf_op jit(solution)/shard_map/ppermute | solution.py:531
  289.0 33.8 %collective-permute-done.20.back_ref.refs_5_ = bf16[384,2048]{1,0:T(8,128)(2,1)} collective-permute-done((bf16[384,2048]{1,0:T(8,128)(2,1)}, bf16[384,2048]{1,0:T(8,128)(2,1)}, u32[]{:S(2)}, u32[]{:S(2)}) %collective-permute-start.20) | collective-permute-done | bytes 1572896 | tf_op jit(solution)/shard_map/ppermute | solution.py:531
  332.7 23.8 %collective-permute-done.1.rows_ref.refs_6_ = bf16[384,2048]{1,0:T(8,128)(2,1)} collective-permute-done((bf16[384,2048]{1,0:T(8,128)(2,1)S(1)}, bf16[384,2048]{1,0:T(8,128)(2,1)}, u32[]{:S(2)}, u32[]{:S(2)}) %collective-permute-start.1) | collective-permute-done | bytes 1572896 | tf_op jit(solution)/shard_map/ppermute | solution.py:531
  356.5 33.7 %collective-permute-done.21.back_ref.refs_6_ = bf16[384,2048]{1,0:T(8,128)(2,1)} collective-permute-done((bf16[384,2048]{1,0:T(8,128)(2,1)}, bf16[384,2048]{1,0:T(8,128)(2,1)}, u32[]{:S(2)}, u32[]{:S(2)}) %collective-permute-start.21) | collective-permute-done | bytes 1572896 | tf_op jit(solution)/shard_map/ppermute | solution.py:531
  401.6 22.7 %collective-permute-done.6 = bf16[384,2048]{1,0:T(8,128)(2,1)} collective-permute-done((bf16[384,2048]{1,0:T(8,128)(2,1)}, bf16[384,2048]{1,0:T(8,128)(2,1)}, u32[]{:S(2)}, u32[]{:S(2)}) %collective-permute-start.6) | collective-permute-done | bytes 1572896 | tf_op jit(solution)/shard_map/ppermute | solution.py:560
  452.6 27.3 %attend_forward.1 = (bf16[1536,512]{1,0:T(8,128)(2,1)}, f32[4,8,1536]{2,1,0:T(8,128)}) custom-call(s32[1]{0:T(128)} %dynamic_slice.42.length_ref, bf16[1536,768]{1,0:T(8,128)(2,1)} %bitcast_select_fusion.q_ref.k_ref.v_ref, bf16[1536,768]{1,0:T(8,128)(2,1)} %bitcast_select_fusion.q_ref.k_ref.v_ref, bf16[1536,768]{1,0:T(8,128)(2,1)} %bitcast_select_fusion.q_ref.k_ref.v_ref), custom_call_target="tpu_custom_call" | custom-call | flops 9663676416 | bytes 4718592 | tf_op jit(solution)/shard_map/attend_forward/pallas_call | solution.py:323
  498.1 23.6 %all-to-all-done.1 = bf16[4,384,512]{2,1,0:T(8,128)(2,1)S(1)} async-done(((bf16[4,384,512]{2,1,0:T(8,128)(2,1)}), bf16[4,384,512]{2,1,0:T(8,128)(2,1)S(1)}, u32[]{:S(2)}, u32[]{:S(2)}) %all-to-all-start.1) | async-done | bytes 1572896 | tf_op jit(solution)/shard_map/all_to_all | solution.py:665
  549.6 25.8 %collective-permute-done.17.rows_ref.refs_5_ = bf16[384,2048]{1,0:T(8,128)(2,1)S(1)} collective-permute-done((bf16[384,2048]{1,0:T(8,128)(2,1)S(1)}, bf16[384,2048]{1,0:T(8,128)(2,1)S(1)}, u32[]{:S(2)}, u32[]{:S(2)}) %collective-permute-start.17) | collective-permute-done | bytes 1572896 | tf_op jit(solution)/shard_map/ppermute | solution.py:531
  651.3 30.3 %collective-permute-done.19.rows_ref.refs_7_ = bf16[384,2048]{1,0:T(8,128)(2,1)} collective-permute-done((bf16[384,2048]{1,0:T(8,128)(2,1)}, bf16[384,2048]{1,0:T(8,128)(2,1)}, u32[]{:S(2)}, u32[]{:S(2)}) %collective-permute-start.19) | collective-permute-done | bytes 1572896 | tf_op jit(solution)/shard_map/ppermute | solution.py:531
  719.9 16.6 %hidden_pass.4 = (bf16[384,2048]{1,0:T(8,128)(2,1)S(1)}, bf16[384,2048]{1,0:T(8,128)(2,1)S(1)}, bf16[384,2048]{1,0:T(8,128)(2,1)S(1)}) custom-call(bf16[384,2048]{1,0:T(8,128)(2,1)} %copy-done.44, bf16[384,2048]{1,0:T(8,128)(2,1)} %refs_4_.1, bf16[2048,2048]{1,0:T(8,128)(2,1)} %get-tuple-element.85.wg_ref, bf16[2048,2048]{1,0:T(8,128)(2,1)} %get-tuple-element.84.wu_ref, ...), custom_call_target="tpu_custom_call" | custom-call | flops 9663676416 | bytes 25165824 | tf_op jit(solution)/shard_map/hidden_pass/pallas_call | solution.py:481
  797.8 28.3 %collective-permute-done.23 = bf16[384,2048]{1,0:T(8,128)(2,1)S(1)} collective-permute-done((bf16[384,2048]{1,0:T(8,128)(2,1)}, bf16[384,2048]{1,0:T(8,128)(2,1)S(1)}, u32[]{:S(2)}, u32[]{:S(2)}) %collective-permute-start.23) | collective-permute-done | bytes 1572896 | tf_op jit(solution)/shard_map/ppermute | solution.py:538
  834.0 23.7 %outer.7 = bf16[2048,2048]{1,0:T(8,128)(2,1)} custom-call(bf16[384,2048]{1,0:T(8,128)(2,1)} %copy-done.11, bf16[384,2048]{1,0:T(8,128)(2,1)} %copy-done.19, bf16[384,2048]{1,0:T(8,128)(2,1)} %copy-done.20, bf16[384,2048]{1,0:T(8,128)(2,1)} %copy-done.23, bf16[384,2048]{1,0:T(8,128)(2,1)} %copy-done.44, bf16[384,2048]{1,0:T(8,128)(2,1)} %copy-done.70, ...), custom_call_target="tpu_custom_call" | custom-call | flops 12884901888 | bytes 20971520 | tf_op jit(solution)/shard_map/outer/pallas_call | solution.py:508
  874.4 23.1 %outer.8 = bf16[2048,2048]{1,0:T(8,128)(2,1)} custom-call(bf16[384,2048]{1,0:T(8,128)(2,1)} %copy-done.22, bf16[384,2048]{1,0:T(8,128)(2,1)} %copy-done.17, bf16[384,2048]{1,0:T(8,128)(2,1)} %copy-done.18, bf16[384,2048]{1,0:T(8,128)(2,1)} %copy-done.21, bf16[384,2048]{1,0:T(8,128)(2,1)} %copy-done.44, bf16[384,2048]{1,0:T(8,128)(2,1)} %copy-done.70, ...), custom_call_target="tpu_custom_call" | custom-call | flops 12884901888 | bytes 20971520 | tf_op jit(solution)/shard_map/outer/pallas_call | solution.py:508
  902.7 23.1 %outer.9 = bf16[2048,2048]{1,0:T(8,128)(2,1)} custom-call(bf16[384,2048]{1,0:T(8,128)(2,1)} %copy-done.12, bf16[384,2048]{1,0:T(8,128)(2,1)} %copy-done.15, bf16[384,2048]{1,0:T(8,128)(2,1)} %copy-done.16, bf16[384,2048]{1,0:T(8,128)(2,1)} %copy-done.14, bf16[384,2048]{1,0:T(8,128)(2,1)} %refs_4_.1, ...), custom_call_target="tpu_custom_call" | custom-call | flops 12884901888 | bytes 20971520 | tf_op jit(solution)/shard_map/outer/pallas_call | solution.py:508
  931.8 58.9 %attend_backward.1 = bf16[1536,768]{1,0:T(8,128)(2,1)} custom-call(s32[1]{0:T(128)} %dynamic_slice.42.length_ref, bf16[1536,768]{1,0:T(8,128)(2,1)} %bitcast_select_fusion.q_ref.k_ref.v_ref, bf16[1536,768]{1,0:T(8,128)(2,1)} %bitcast_select_fusion.q_ref.k_ref.v_ref, bf16[1536,768]{1,0:T(8,128)(2,1)} %bitcast_select_fusion.q_ref.k_ref.v_ref, ...), custom_call_target="tpu_custom_call" | custom-call | flops 24159191040 | bytes 7077888 | tf_op jit(solution)/shard_map/attend_backward/pallas_call | solution.py:432
  1035.3 18.5 %collective-permute-done.43 = bf16[128,2048]{1,0:T(8,128)(2,1)S(1)} collective-permute-done((bf16[128,2048]{1,0:T(8,128)(2,1)S(1)}, bf16[128,2048]{1,0:T(8,128)(2,1)S(1)}, u32[]{:S(2)}, u32[]{:S(2)}) %collective-permute-start.43) | collective-permute-done | bytes 524320 | tf_op jit(solution)/shard_map/ppermute | solution.py:577
  1169.4 208.3 %unpick_units.1 = bf16[208,16,1024]{2,1,0:T(8,128)(2,1)} custom-call(s32[208]{0:T(256)} %scatter_custom_fusion.unit_ref, bf16[928,2048]{1,0:T(8,128)(2,1)} %fusion.16.rows_ref), custom_call_target="tpu_custom_call" | custom-call | bytes 13631488 | tf_op jit(solution)/shard_map/unpick_units/pallas_call | solution.py:154
  1394.6 34.7 %collective-permute-done.25 = bf16[384,2048]{1,0:T(8,128)(2,1)S(1)} collective-permute-done((bf16[384,2048]{1,0:T(8,128)(2,1)S(1)}, bf16[384,2048]{1,0:T(8,128)(2,1)S(1)}, u32[]{:S(2)}, u32[]{:S(2)}) %collective-permute-start.25) | collective-permute-done | bytes 1572896 | tf_op jit(solution)/shard_map/ppermute | solution.py:539
  1437.5 25.0 %collective-permute-done.31 = bf16[384,2048]{1,0:T(8,128)(2,1)S(1)} collective-permute-done((bf16[384,2048]{1,0:T(8,128)(2,1)S(1)}, bf16[384,2048]{1,0:T(8,128)(2,1)S(1)}, u32[]{:S(2)}, u32[]{:S(2)}) %collective-permute-start.31) | collective-permute-done | bytes 1572896 | tf_op jit(solution)/shard_map/ppermute | solution.py:539
  1466.2 38.3 %psum.7 = f32[2,2048]{1,0:T(2,128)S(1)} all-reduce(f32[2,2048]{1,0:T(2,128)S(1)} %pad_maximum_fusion.6), channel_id=1, replica_groups=mesh['wide'=8,'narrow'=4] {'wide','narrow'}, use_global_device_ids=true, to_apply=%region_13.14 | all-reduce | flops 4096 | bytes 32768 | tf_op jit(solution)/shard_map/psum | solution.py:748
  1512.3 45.7 %update_units.1 = (f32[26,1,1024,128]{3,2,1,0:T(8,128)}, f32[26,1,1024,128]{3,2,1,0:T(8,128)}, bf16[26,1,1024,128]{3,2,1,0:T(8,128)(2,1)}, f32[26,1,1024,128]{3,2,1,0:T(8,128)}, f32[26,1,1024,128]{3,2,1,0:T(8,128)}) custom-call(s32[1]{0:T(128)} %dynamic_slice.55.count_ref, bf16[8,26,16,1024]{3,2,1,0:T(8,128)(2,1)} %all-to-all-done.3.grad_ref, ...), custom_call_target="tpu_custom_call" | custom-call | flops 40894464 | bytes 109051904 | tf_op jit(solution)/shard_map/update_units/pallas_call | solution.py:195
  (382 shorter events, 531.5 us)
Async XLA Ops:
  18.5 82.9 %all-to-all-start = ((bf16[1,26,8,16,1024]{4,3,1,0,2:T(8,128)(2,1)}), bf16[1,26,8,16,1024]{4,3,1,0,2:T(8,128)(2,1)}, u32[]{:S(2)}, u32[]{:S(2)}) async-start(bf16[1,26,8,16,1024]{4,3,1,0,2:T(8,128)(2,1)} %copy.39), calls=%async_computation | async-start | bytes 13631488 | tf_op jit(solution)/shard_map/all_to_all | solution.py:610
  23.8 224.6 %all-gather.9.cloned.1.call-start = ((), (), s32[]{:S(2)}) async-start(), calls=%async_computation.11 | async-start | bytes 1310720 | tf_op jit(solution)/shard_map/all_gather | solution.py:623
  220.1 212.7 %all-gather.7.cloned.1.call-start = ((), (), s32[]{:S(2)}) async-start(), calls=%async_computation.10 | async-start | bytes 3538944 | tf_op jit(solution)/shard_map/all_gather | solution.py:618
  221.9 301.2 %all-gather.11.cloned.1.call-start = ((), (), s32[]{:S(2)}) async-start(), calls=%async_computation.12 | async-start | bytes 9437184 | tf_op jit(solution)/shard_map/all_gather | solution.py:624
  251.3 71.5 %collective-permute-start.20 = (bf16[384,2048]{1,0:T(8,128)(2,1)}, bf16[384,2048]{1,0:T(8,128)(2,1)}, u32[]{:S(2)}, u32[]{:S(2)}) collective-permute-start(bf16[384,2048]{1,0:T(8,128)(2,1)} %refs_4_.1), channel_id=1, source_target_pairs={{0,1},{1,2},{2,3},{3,0},{4,5},{5,6},{6,7},{7,4},{8,9},{9,10},{10,1... | collective-permute-start | bytes 4718600 | tf_op jit(solution)/shard_map/ppermute | solution.py:531
  254.0 71.5 %collective-permute-start.3 = (bf16[384,2048]{1,0:T(8,128)(2,1)}, bf16[384,2048]{1,0:T(8,128)(2,1)}, u32[]{:S(2)}, u32[]{:S(2)}) collective-permute-start(bf16[384,2048]{1,0:T(8,128)(2,1)} %pad_maximum_fusion.1), channel_id=1, source_target_pairs={{0,8},{4,12},{8,24},{12,28},{24,16},{28,20},{16,0},{20,4},{1,9},{5... | collective-permute-start | bytes 4718600 | tf_op jit(solution)/shard_map/ppermute | solution.py:559
  288.9 67.5 %collective-permute-start.1 = (bf16[384,2048]{1,0:T(8,128)(2,1)S(1)}, bf16[384,2048]{1,0:T(8,128)(2,1)}, u32[]{:S(2)}, u32[]{:S(2)}) collective-permute-start(bf16[384,2048]{1,0:T(8,128)(2,1)S(1)} %collective-permute-done.rows_ref.refs_5_), channel_id=1, source_target_pairs={{0,1},{1,2},{2,3},{3,0},{4,5},{5,6},{6,7},{7,4},{8,9},{9,10},{10,1... | collective-permute-start | bytes 4718600 | tf_op jit(solution)/shard_map/ppermute | solution.py:531
  322.8 67.4 %collective-permute-start.21 = (bf16[384,2048]{1,0:T(8,128)(2,1)}, bf16[384,2048]{1,0:T(8,128)(2,1)}, u32[]{:S(2)}, u32[]{:S(2)}) collective-permute-start(bf16[384,2048]{1,0:T(8,128)(2,1)} %collective-permute-done.20.back_ref.refs_5_), channel_id=1, source_target_pairs={{0,1},{1,2},{2,3},{3,0},{4,5},{5,6},{6,7},{7,4},{8,9},{9,10},{10,1... | collective-permute-start | bytes 4718600 | tf_op jit(solution)/shard_map/ppermute | solution.py:531
  325.6 67.9 %collective-permute-start.5 = (bf16[384,2048]{1,0:T(8,128)(2,1)}, bf16[384,2048]{1,0:T(8,128)(2,1)}, u32[]{:S(2)}, u32[]{:S(2)}) collective-permute-start(bf16[384,2048]{1,0:T(8,128)(2,1)} %collective-permute-done.3), channel_id=1, source_target_pairs={{0,8},{4,12},{8,24},{12,28},{24,16},{28,20},{16,0},{20,4},{1,9},{5... | collective-permute-start | bytes 4718600 | tf_op jit(solution)/shard_map/ppermute | solution.py:559
  356.5 85.4 %collective-permute-start.2 = (bf16[384,2048]{1,0:T(8,128)(2,1)}, bf16[384,2048]{1,0:T(8,128)(2,1)}, u32[]{:S(2)}, u32[]{:S(2)}) collective-permute-start(bf16[384,2048]{1,0:T(8,128)(2,1)} %collective-permute-done.1.rows_ref.refs_6_), channel_id=1, source_target_pairs={{0,1},{1,2},{2,3},{3,0},{4,5},{5,6},{6,7},{7,4},{8,9},{9,10},{10,1... | collective-permute-start | bytes 4718600 | tf_op jit(solution)/shard_map/ppermute | solution.py:531
  390.2 261.2 %collective-permute-start.22 = (bf16[384,2048]{1,0:T(8,128)(2,1)}, bf16[384,2048]{1,0:T(8,128)(2,1)}, u32[]{:S(2)}, u32[]{:S(2)}) collective-permute-start(bf16[384,2048]{1,0:T(8,128)(2,1)} %collective-permute-done.21.back_ref.refs_6_), channel_id=1, source_target_pairs={{0,1},{1,2},{2,3},{3,0},{4,5},{5,6},{6,7},{7,4},{8,9},{9,10},{10,1... | collective-permute-start | bytes 4718600 | tf_op jit(solution)/shard_map/ppermute | solution.py:531
  393.4 94.7 %collective-permute-start.9 = (bf16[384,2048]{1,0:T(8,128)(2,1)}, bf16[384,2048]{1,0:T(8,128)(2,1)}, u32[]{:S(2)}, u32[]{:S(2)}) collective-permute-start(bf16[384,2048]{1,0:T(8,128)(2,1)} %pad_maximum_fusion.1), channel_id=1, source_target_pairs={{0,4},{4,0},{8,12},{12,8},{16,20},{20,16},{24,28},{28,24},{1,5},{5... | collective-permute-start | bytes 4718600 | tf_op jit(solution)/shard_map/ppermute | solution.py:562
  424.3 67.0 %collective-permute-start.10 = (bf16[384,2048]{1,0:T(8,128)(2,1)}, bf16[384,2048]{1,0:T(8,128)(2,1)}, u32[]{:S(2)}, u32[]{:S(2)}) collective-permute-start(bf16[384,2048]{1,0:T(8,128)(2,1)} %pad_maximum_fusion.2), channel_id=1, source_target_pairs={{0,4},{4,0},{8,12},{12,8},{16,20},{20,16},{24,28},{28,24},{1,5},{5... | collective-permute-start | bytes 4718600 | tf_op jit(solution)/shard_map/ppermute | solution.py:562
  485.1 619.3 %reduce-scatter.6.cloned.1.call-start = ((), (), s32[]{:S(2)}) async-start(), calls=%async_computation.8 | async-start | bytes 9437184 | tf_op jit(solution)/shard_map/reduce_scatter | solution.py:722
  862.7 151.0 %collective-permute-start.32 = (bf16[1024,2048]{1,0:T(8,128)(2,1)}, bf16[1024,2048]{1,0:T(8,128)(2,1)}, u32[]{:S(2)}, u32[]{:S(2)}) collective-permute-start(bf16[1024,2048]{1,0:T(8,128)(2,1)} %slice.407), channel_id=1, source_target_pairs={{0,4},{4,0},{8,12},{12,8},{16,20},{20,16},{24,28},{28,24},{1,5},{5... | collective-permute-start | bytes 12582920 | tf_op jit(solution)/shard_map/ppermute | solution.py:567
  874.3 254.4 %reduce-scatter.4.cloned.1.call-start = ((), (), s32[]{:S(2)}) async-start(), calls=%async_computation.7 | async-start | bytes 3538944 | tf_op jit(solution)/shard_map/reduce_scatter | solution.py:722
  902.2 119.1 %collective-permute-start.39 = (bf16[1024,2048]{1,0:T(8,128)(2,1)}, bf16[1024,2048]{1,0:T(8,128)(2,1)}, u32[]{:S(2)}, u32[]{:S(2)}) collective-permute-start(bf16[1024,2048]{1,0:T(8,128)(2,1)} %slice.417), channel_id=1, source_target_pairs={{0,4},{4,0},{8,12},{12,8},{16,20},{20,16},{24,28},{28,24},{1,5},{5... | collective-permute-start | bytes 12582920 | tf_op jit(solution)/shard_map/ppermute | solution.py:567
  930.7 96.8 %collective-permute-start.46 = (bf16[1024,2048]{1,0:T(8,128)(2,1)}, bf16[1024,2048]{1,0:T(8,128)(2,1)}, u32[]{:S(2)}, u32[]{:S(2)}) collective-permute-start(bf16[1024,2048]{1,0:T(8,128)(2,1)} %slice.427), channel_id=1, source_target_pairs={{0,4},{4,0},{8,12},{12,8},{16,20},{20,16},{24,28},{28,24},{1,5},{5... | collective-permute-start | bytes 12582920 | tf_op jit(solution)/shard_map/ppermute | solution.py:567
  996.3 108.1 %collective-permute-start.29 = (bf16[384,2048]{1,0:T(8,128)(2,1)}, bf16[384,2048]{1,0:T(8,128)(2,1)}, u32[]{:S(2)}, u32[]{:S(2)}) collective-permute-start(bf16[384,2048]{1,0:T(8,128)(2,1)} %convolution_convert_fusion.2), channel_id=1, source_target_pairs={{0,1},{1,2},{2,3},{3,0},{4,5},{5,6},{6,7},{7,4},{8,9},{9,10},{10,1... | collective-permute-start | bytes 4718600 | tf_op jit(solution)/shard_map/ppermute | solution.py:538
  1013.6 122.6 %reduce-scatter.8.cloned.1.call-start = ((), (), s32[]{:S(2)}) async-start(), calls=%async_computation.9 | async-start | bytes 1310720 | tf_op jit(solution)/shard_map/reduce_scatter | solution.py:725
  1081.8 300.7 %collective-permute-start.24 = (bf16[384,2048]{1,0:T(8,128)(2,1)}, bf16[384,2048]{1,0:T(8,128)(2,1)}, u32[]{:S(2)}, u32[]{:S(2)}) collective-permute-start(bf16[384,2048]{1,0:T(8,128)(2,1)} %add_convert_fusion.10), channel_id=1, source_target_pairs={{0,1},{1,2},{2,3},{3,0},{4,5},{5,6},{6,7},{7,4},{8,9},{9,10},{10,1... | collective-permute-start | bytes 4718600 | tf_op jit(solution)/shard_map/ppermute | solution.py:538
  1141.5 250.2 %collective-permute-start.30 = (bf16[384,2048]{1,0:T(8,128)(2,1)}, bf16[384,2048]{1,0:T(8,128)(2,1)}, u32[]{:S(2)}, u32[]{:S(2)}) collective-permute-start(bf16[384,2048]{1,0:T(8,128)(2,1)} %add_convert_fusion.4), channel_id=1, source_target_pairs={{0,1},{1,2},{2,3},{3,0},{4,5},{5,6},{6,7},{7,4},{8,9},{9,10},{10,1... | collective-permute-start | bytes 4718600 | tf_op jit(solution)/shard_map/ppermute | solution.py:538
  1377.7 134.7 %all-to-all-start.3 = ((bf16[8,26,16,1024]{3,2,1,0:T(8,128)(2,1)}), bf16[8,26,16,1024]{3,2,1,0:T(8,128)(2,1)}, u32[]{:S(2)}, u32[]{:S(2)}) async-start(bf16[8,26,16,1024]{3,2,1,0:T(8,128)(2,1)} %bitcast.98), calls=%async_computation.6 | async-start | bytes 13631488 | tf_op jit(solution)/shard_map/all_to_all | solution.py:735
  1393.8 68.6 %collective-permute-start.31 = (bf16[384,2048]{1,0:T(8,128)(2,1)S(1)}, bf16[384,2048]{1,0:T(8,128)(2,1)S(1)}, u32[]{:S(2)}, u32[]{:S(2)}) collective-permute-start(bf16[384,2048]{1,0:T(8,128)(2,1)S(1)} %add_convert_fusion.3), channel_id=1, source_target_pairs={{0,1},{1,2},{2,3},{3,0},{4,5},{5,6},{6,7},{7,4},{8,9},{9,10},{10,1... | collective-permute-start | bytes 4718600 | tf_op jit(solution)/shard_map/ppermute | solution.py:539
  (112 other events, 4669.2 us)
Sparse Core Ops, SparseCore 0:
  220.2 28.0 all-gather.8
  250.8 44.6 all-gather.6
  297.4 76.5 all-gather.10
  783.3 67.6 reduce-scatter.5
  1013.7 57.1 reduce-scatter.3
  1104.6 31.6 reduce-scatter.7

commit v2 on v1

--- a/solution.py
+++ b/solution.py
@@ -117,68 +117,67 @@
                 pl.BlockSpec(memory_space=pltpu.SMEM),
                 pl.BlockSpec(memory_space=pl.ANY),
             ],
-            out_specs=pl.BlockSpec(memory_space=pl.ANY),
+            out_specs=pl.BlockSpec(memory_space=pltpu.VMEM),
             out_shape=jax.ShapeDtypeStruct((col_blocks * piece, row_blocks * unit_rows), bf16),
             scratch_shapes=[pltpu.SemaphoreType.DMA],
-            cost_estimate=cost(0, unit_count * piece * unit_rows * 4),
+            compiler_params=params(24),
+            cost_estimate=cost(0, unit_count * piece * unit_rows * 12),
             name="pick_units",
         )(slot_place, got)
     units = jnp.take(got, slot_place, axis=0).reshape(row_blocks, col_blocks, piece, unit_rows)
     return jnp.transpose(units, (1, 2, 0, 3)).reshape(col_blocks * piece, row_blocks * unit_rows)
 
 
-def unpick_kernel(unit_ref, rows_ref, out_ref, sem, *, col_blocks, piece, unit_rows):
+def unpick_kernel(block_ref, half_ref, rows_ref, out_ref, sem, *, piece, unit_rows):
     def start(slot, carry):
-        unit = unit_ref[slot]
-        half = unit // col_blocks
-        block = unit - half * col_blocks
         pltpu.make_async_copy(
             rows_ref.at[
-                pl.ds(pl.multiple_of(block * piece, piece), piece),
-                pl.ds(pl.multiple_of(half * unit_rows, unit_rows), unit_rows),
+                pl.ds(pl.multiple_of(block_ref[slot] * piece, piece), piece),
+                pl.ds(pl.multiple_of(half_ref[slot] * unit_rows, unit_rows), unit_rows),
             ],
             out_ref.at[slot],
             sem,
         ).start()
         return carry
 
-    lax.fori_loop(0, unit_ref.shape[0], start, 0)
+    lax.fori_loop(0, block_ref.shape[0], start, 0)
     pltpu.make_async_copy(out_ref, out_ref, sem).wait()
 
 
-def unpick_units(rows, unit_of, unit_count, piece, unit_rows):
-    row_blocks = rows.shape[1] // unit_rows
-    col_blocks = unit_count // row_blocks
-    slots = unit_of.shape[0]
+def unpick_units(rows, block_of, half_of, piece, unit_rows):
+    slots = block_of.shape[0]
     if piece % 16 == 0:
         return pl.pallas_call(
-            functools.partial(
-                unpick_kernel, col_blocks=col_blocks, piece=piece, unit_rows=unit_rows
-            ),
+            functools.partial(unpick_kernel, piece=piece, unit_rows=unit_rows),
             in_specs=[
                 pl.BlockSpec(memory_space=pltpu.SMEM),
-                pl.BlockSpec(memory_space=pl.ANY),
+                pl.BlockSpec(memory_space=pltpu.SMEM),
+                pl.BlockSpec(memory_space=pltpu.VMEM),
             ],
             out_specs=pl.BlockSpec(memory_space=pl.ANY),
             out_shape=jax.ShapeDtypeStruct((slots, piece, unit_rows), bf16),
             scratch_shapes=[pltpu.SemaphoreType.DMA],
-            cost_estimate=cost(0, slots * piece * unit_rows * 4),
+            compiler_params=params(24),
+            cost_estimate=cost(0, slots * piece * unit_rows * 8),
             name="unpick_units",
-        )(unit_of, rows)
-    units = jnp.transpose(
-        rows.reshape(col_blocks, piece, row_blocks, unit_rows), (2, 0, 1, 3)
-    ).reshape(unit_count, piece, unit_rows)
-    return jnp.take(units, unit_of, axis=0)
+        )(block_of, half_of, rows)
+    row_blocks = rows.shape[1] // unit_rows
+    units = jnp.transpose(rows.reshape(-1, piece, row_blocks, unit_rows), (0, 2, 1, 3))
+    units = units.reshape(-1, piece, unit_rows)
+    return jnp.take(units, block_of * row_blocks + half_of, axis=0)
 
 
 def update_kernel(
-    count_ref, grad_ref, master_ref, one_ref, two_ref,
-    grad_out, master_out, copy_out, one_out, two_out,
+    block_ref, half_ref, count_ref, grad_ref, attn_ref, master_ref, one_ref, two_ref,
+    grad_out, master_out, copy_out, one_out, two_out, *, attn_blocks,
 ):
-    filled = pl.program_id(0) < count_ref[0]
+    slot = pl.program_id(0)
+    filled = slot < count_ref[0]
+    from_attn = block_ref[slot] < attn_blocks
     parts, _, piece, unit_rows = grad_ref.shape
-    turned = grad_ref[:, 0].astype(f32).reshape(parts * piece, unit_rows)
-    gradient = jnp.where(filled, jnp.transpose(turned, (1, 0)), 0.0)
+    mine = jnp.where(from_attn, attn_ref[:, 0].astype(f32), grad_ref[:, 0].astype(f32))
+    mine = mine.reshape(parts * piece, unit_rows)
+    gradient = jnp.where(filled, jnp.transpose(mine, (1, 0)), 0.0)
     weight, one, two = adamw(master_ref[0, 0], gradient, one_ref[0, 0], two_ref[0, 0], 0.02, 0.1)
     grad_out[0, 0] = gradient
     master_out[0, 0] = weight
@@ -187,27 +186,37 @@
     two_out[0, 0] = two
 
 
-def update_units(count, grads, master, moment_one, moment_two):
+def update_units(block_of, half_of, count, grads, attn, master, moment_one, moment_two):
     capacity, _, unit_rows, unit_cols = master.shape
     parts, _, piece, _ = grads.shape
-    unit = pl.BlockSpec((1, 1, unit_rows, unit_cols), lambda s: (s, 0, 0, 0))
+    attn_blocks = attn.shape[1]
+    unit = pl.BlockSpec((1, 1, unit_rows, unit_cols), lambda s, *refs: (s, 0, 0, 0))
     whole = jax.ShapeDtypeStruct(master.shape, f32)
+
+    def attn_place(s, block_ref, half_ref, count_ref):
+        block = block_ref[s]
+        inside = block < attn_blocks
+        return (0, jnp.where(inside, block, 0), 0, jnp.where(inside, half_ref[s], 0))
+
     return pl.pallas_call(
-        update_kernel,
-        grid=(capacity,),
-        in_specs=[
-            pl.BlockSpec(memory_space=pltpu.SMEM),
-            pl.BlockSpec((parts, 1, piece, unit_rows), lambda s: (0, s, 0, 0)),
-            unit,
-            unit,
-            unit,
-        ],
-        out_specs=[unit] * 5,
+        functools.partial(update_kernel, attn_blocks=attn_blocks),
+        grid_spec=pltpu.PrefetchScalarGridSpec(
+            num_scalar_prefetch=3,
+            grid=(capacity,),
+            in_specs=[
+                pl.BlockSpec((parts, 1, piece, unit_rows), lambda s, *refs: (0, s, 0, 0)),
+                pl.BlockSpec((parts, 1, piece, unit_rows), attn_place),
+                unit,
+                unit,
+                unit,
+            ],
+            out_specs=[unit] * 5,
+        ),
         out_shape=[whole, whole, jax.ShapeDtypeStruct(master.shape, bf16), whole, whole],
         compiler_params=params(40),
         cost_estimate=cost(master.size * 12, master.size * 32),
         name="update_units",
-    )(count, grads, master, moment_one, moment_two)
+    )(block_of, half_of, count, grads, attn, master, moment_one, moment_two)
 
 
 def lane_index(shape):
@@ -246,16 +255,24 @@
         out_ref[:, start : start + LANES] = tile
 
 
-def project(rows, w_qkv, cos_rows, sin_rows, query_width, kv_width):
+def project(rows, w_qkv, cos_all, sin_all, query_width, kv_width, step):
     count = rows.shape[0]
     width = w_qkv.shape[0]
     return pl.pallas_call(
         functools.partial(project_kernel, query_width=query_width, kv_width=kv_width),
+        grid=(count // step,),
+        in_specs=[
+            pl.BlockSpec((step, D), lambda i: (i, 0)),
+            pl.BlockSpec((width, D), lambda i: (0, 0)),
+            pl.BlockSpec((step, LANES), lambda i: (i, 0)),
+            pl.BlockSpec((step, LANES), lambda i: (i, 0)),
+        ],
+        out_specs=pl.BlockSpec((step, width), lambda i: (i, 0)),
         out_shape=jax.ShapeDtypeStruct((count, width), bf16),
         compiler_params=params(40),
         cost_estimate=cost(2 * count * width * D, 2 * (count + width) * D),
         name="project",
-    )(rows, w_qkv, cos_rows, sin_rows)
+    )(rows, w_qkv, cos_all, sin_all)
 
 
 def extend(tile_ref, offset, out_ref):
@@ -459,7 +476,67 @@
     )(length, qkv, qkv, qkv, back, out, logs, cos_all, sin_all)
 
 
-def hidden_kernel(rows_ref, back_ref, wg_ref, wu_ref, wd_ref, hid_ref, dgate_ref, dup_ref):
+def branch_kernel(attended_ref, w_ref, tokens_ref, gain_ref, residual_ref, normed_ref):
+    total = tokens_ref[...].astype(f32)
+    groups, _, width = attended_ref.shape
+    for n in range(groups):
+        total = total + dot(attended_ref[n], w_ref[n * width : (n + 1) * width, :], 1, 0)
+    residual_ref[...] = total
+    normed_ref[...] = rmsnorm(total, gain_ref[...]).astype(bf16)
+
+
+def branch(attended, w_out, tokens, gain):
+    groups, count, width = attended.shape
+    step = 128 if count % 128 == 0 else 64
+    return pl.pallas_call(
+        branch_kernel,
+        grid=(count // step,),
+        in_specs=[
+            pl.BlockSpec((groups, step, width), lambda i: (0, i, 0)),
+            pl.BlockSpec((D, D), lambda i: (0, 0)),
+            pl.BlockSpec((step, D), lambda i: (i, 0)),
+            pl.BlockSpec((1, D), lambda i: (0, 0)),
+        ],
+        out_specs=[pl.BlockSpec((step, D), lambda i: (i, 0))] * 2,
+        out_shape=[
+            jax.ShapeDtypeStruct((count, D), f32),
+            jax.ShapeDtypeStruct((count, D), bf16),
+        ],
+        compiler_params=params(56),
+        cost_estimate=cost(2 * count * D * D, 2 * D * D + 8 * count * D),
+        name="branch",
+    )(attended, w_out, tokens, gain)
+
+
+def spread_kernel(back_ref, w_ref, out_ref):
+    out_ref[0] = dot(back_ref[...], w_ref[...], 1, 1).astype(bf16)
+
+
+def spread(back, w_out, groups):
+    count = back.shape[0]
+    width = D // groups
+    return pl.pallas_call(
+        spread_kernel,
+        grid=(groups,),
+        in_specs=[
+            pl.BlockSpec((count, D), lambda i: (0, 0)),
+            pl.BlockSpec((width, D), lambda i: (i, 0)),
+        ],
+        out_specs=pl.BlockSpec((1, count, width), lambda i: (i, 0, 0)),
+        out_shape=jax.ShapeDtypeStruct((groups, count, width), bf16),
+        compiler_params=params(40),
+        cost_estimate=cost(2 * count * D * D, 2 * D * D + 4 * count * D),
+        name="spread",
+    )(back, w_out)
+
+
+def hidden_kernel(place_ref, rows_ref, back_ref, wg_ref, wu_ref, wd_ref, *refs):
+    hid_ref, dgate_ref, dup_ref, keep_ref = refs[-4:]
+
+    @pl.when(pl.program_id(0) == 0)
+    def _():
+        keep_ref[...] = rows_ref[...]
+
     gate = dot(rows_ref[...], wg_ref[...], 1, 1)
     up = dot(rows_ref[...], wu_ref[...], 1, 1)
     hidden_back = dot(back_ref[...], wd_ref[...], 1, 1)
@@ -470,55 +547,96 @@
     dup_ref[...] = (hidden_back * silu).astype(bf16)
 
 
-def hidden_pass(rows, back, wg, wu, wd):
+def hidden_pass(place, rows, back, wg, wu, wd, kept):
     count = rows.shape[0]
+    seq_len = back.shape[0]
     ff_width = wg.shape[0]
     step = 256
-    resident = pl.BlockSpec((count, D), lambda i: (0, 0))
-    weight = pl.BlockSpec((step, D), lambda i: (i, 0))
-    given = pl.BlockSpec((count, step), lambda i: (0, i))
-    shape = jax.ShapeDtypeStruct((count, ff_width), bf16)
+    weight = pl.BlockSpec((step, D), lambda i, p: (i, 0))
+    wide_rows = jax.ShapeDtypeStruct((seq_len, ff_width), bf16)
+    given = pl.BlockSpec((count, step), lambda i, p: (p[0], i))
     return pl.pallas_call(
         hidden_kernel,
-        grid=(ff_width // step,),
-        in_specs=[resident, resident, weight, weight, weight],
-        out_specs=[given] * 3,
-        out_shape=[shape] * 3,
+        grid_spec=pltpu.PrefetchScalarGridSpec(
+            num_scalar_prefetch=1,
+            grid=(ff_width // step,),
+            in_specs=[
+                pl.BlockSpec((count, D), lambda i, p: (0, 0)),
+                pl.BlockSpec((count, D), lambda i, p: (p[0], 0)),
+                weight,
+                weight,
+                weight,
+            ]
+            + [pl.BlockSpec(memory_space=pl.ANY)] * len(kept),
+            out_specs=[given] * 3 + [pl.BlockSpec((count, D), lambda i, p: (p[0], 0))],
+        ),
+        out_shape=[wide_rows] * 3 + [jax.ShapeDtypeStruct((seq_len, D), bf16)],
+        input_output_aliases={6 + k: k for k in range(len(kept))},
         compiler_params=params(48),
         cost_estimate=cost(6 * count * ff_width * D, 6 * ff_width * D, count * ff_width),
         name="hidden_pass",
-    )(rows, back, wg, wu, wd)
-
-
-def outer_kernel(*refs):
+    )(place, rows, back, wg, wu, wd, *kept)
+
+
+def norm_back_kernel(place_ref, dgate_ref, dup_ref, wg_ref, wu_ref, *refs):
     out_ref = refs[-1]
-    count = (len(refs) - 1) // 2
-    total = None
-    for k in range(count):
-        part = dot(refs[k][...], refs[count + k][...], 0, 0)
-        total = part if total is None else total + part
-    out_ref[...] = total.astype(bf16)
-
-
-def outer(firsts, seconds):
-    rows, height = firsts[0].shape
-    width = seconds[0].shape[1]
-    step = 512 if height % 512 == 0 else 256 if height % 256 == 0 else LANES
-    chunks = len(firsts)
+    total = dot(dgate_ref[...], wg_ref[...], 1, 0) + dot(dup_ref[...], wu_ref[...], 1, 0)
+    if len(refs) > 1:
+        total = total + refs[0][...].astype(f32)
+    out_ref[...] = total.astype(out_ref.dtype)
+
+
+def norm_back(place, dgate, dup, wg, wu, count, before, kind):
+    ff_width = wg.shape[0]
+    step = 512
+    taken = pl.BlockSpec((count, ff_width), lambda i, p: (p[0], 0))
+    weight = pl.BlockSpec((ff_width, step), lambda i, p: (0, i))
+    given = pl.BlockSpec((count, step), lambda i, p: (0, i))
+    extra = [] if before is None else [before]
+    return pl.pallas_call(
+        norm_back_kernel,
+        grid_spec=pltpu.PrefetchScalarGridSpec(
+            num_scalar_prefetch=1,
+            grid=(D // step,),
+            in_specs=[taken, taken, weight, weight] + [given] * len(extra),
+            out_specs=given,
+        ),
+        out_shape=jax.ShapeDtypeStruct((count, D), kind),
+        compiler_params=params(48),
+        cost_estimate=cost(4 * count * ff_width * D, 4 * ff_width * D),
+        name="norm_back",
+    )(place, dgate, dup, wg, wu, *extra)
+
+
+def outer_kernel(first_ref, second_ref, out_ref):
+    first = first_ref[...]
+    if len(first.shape) == 3:
+        first = first[0]
+    out_ref[...] = dot(first, second_ref[...], 0, 0).astype(bf16)
+
+
+def outer(first, second):
+    rows, width = second.shape
+    if len(first.shape) == 3:
+        groups, _, step = first.shape
+        height = groups * step
+        taken = pl.BlockSpec((1, rows, step), lambda i: (i, 0, 0))
+    else:
+        height = first.shape[1]
+        step = next(k for k in (512, 384, 256, 192, LANES) if height % k == 0)
+        taken = pl.BlockSpec((rows, step), lambda i: (0, i))
     return pl.pallas_call(
         outer_kernel,
         grid=(height // step,),
-        in_specs=[pl.BlockSpec((rows, step), lambda i: (0, i))] * chunks
-        + [pl.BlockSpec((rows, width), lambda i: (0, 0))] * chunks,
+        in_specs=[taken, pl.BlockSpec((rows, width), lambda i: (0, 0))],
         out_specs=pl.BlockSpec((step, width), lambda i: (i, 0)),
         out_shape=jax.ShapeDtypeStruct((height, width), bf16),
         compiler_params=params(56),
         cost_estimate=cost(
-            2 * chunks * rows * height * width,
-            2 * (chunks * rows * (height + width) + height * width),
+            2 * rows * height * width, 2 * (rows * (height + width) + height * width)
         ),
         name="outer",
-    )(*firsts, *seconds)
+    )(first, second)
 
 
 def cycle(count, step=1):
@@ -532,18 +650,23 @@
     return blocks
 
 
-def ring_reduce(parts, count):
-    total = parts[1]().astype(bf16)
-    for s in range(2, count):
-        total = (parts[s]() + lax.ppermute(total, "narrow", cycle(count)).astype(f32)).astype(bf16)
-    return parts[0]() + lax.ppermute(total, "narrow", cycle(count)).astype(f32)
+def butterfly(value):
+    for axis in ("wide", "narrow"):
+        count = lax.axis_size(axis)
+        step = 1
+        while step < count:
+            value = value + lax.ppermute(value, axis, [(i, i ^ step) for i in range(count)])
+            step *= 2
+    return value
+
+
+ORDER = (0, 1, 3, 2)
 
 
 def square_pairs(step):
-    order = (0, 1, 3, 2)
     pairs = []
-    for place, chip in enumerate(order):
-        target = order[(place + step) % 4]
+    for place, chip in enumerate(ORDER):
+        target = ORDER[(place + step) % 4]
         pairs += [(chip * 2 + core, target * 2 + core) for core in range(2)]
     return pairs
 
@@ -552,32 +675,107 @@
     return [(i, i ^ 1) for i in range(8)]
 
 
-def plane_gather(halves):
-    first, second = halves
-    blocks = [first, second]
+def plane_ring(first, second):
+    firsts, seconds = [first], [second]
     for _ in range(3):
-        first = lax.ppermute(first, "wide", square_pairs(1))
-        second = lax.ppermute(second, "wide", square_pairs(-1))
-        blocks += [first, second]
-    return blocks + [lax.ppermute(block, "wide", swap_pairs()) for block in blocks]
-
-
-def plane_reduce(grad):
-    half = grad.shape[0] // 2
-    own = grad[:half].astype(f32) + lax.ppermute(grad[half:], "wide", swap_pairs()).astype(f32)
-    own = own.astype(bf16)
-    size = half // 8
-    blocks = [own[k * size : (k + 1) * size] for k in range(8)]
+        firsts.append(lax.ppermute(firsts[-1], "wide", square_pairs(1)))
+        seconds.append(lax.ppermute(seconds[-1], "wide", square_pairs(-1)))
+    firsts += [lax.ppermute(part, "wide", swap_pairs()) for part in firsts]
+    seconds += [lax.ppermute(part, "wide", swap_pairs()) for part in seconds]
+    return firsts, seconds
+
+
+def plane_ring_back(firsts, seconds):
     ends = []
-    for side, step in ((0, 1), (1, -1)):
-        total = blocks[2 + side]
+    for parts, step in ((firsts, 1), (seconds, -1)):
+        total = parts[1]
         for s in (2, 3, 0):
             total = (
-                blocks[2 * s + side].astype(f32)
+                parts[s].astype(f32)
                 + lax.ppermute(total, "wide", square_pairs(step)).astype(f32)
             ).astype(bf16)
         ends.append(total)
     return ends
+
+
+def ring_orders():
+    wide_index = lax.axis_index("wide")
+    order = jnp.array(ORDER, jnp.int32)
+    core = wide_index % 2
+    place = order[wide_index // 2]
+    entry = jnp.arange(8, dtype=jnp.int32)
+    device = entry
+    entry_core = (core + entry // 4) % 2
+    apart = order[device // 2] - place
+    away = 4 * ((device % 2 + core) % 2)
+    return (
+        order[(place - entry) % 4] * 2 + entry_core,
+        order[(place + entry) % 4] * 2 + entry_core,
+        (-apart) % 4 + away,
+        apart % 4 + away,
+    )
+
+
+def plane_all(part):
+    count = lax.axis_size("wide")
+    if count != 8:
+        return lax.all_gather(part, "wide", axis=0)
+    half = part.shape[0] // 2
+    firsts, seconds = plane_ring(part[:half], part[half:])
+    _, _, at_first, at_second = ring_orders()
+    return jnp.concatenate(
+        [
+            jnp.take(jnp.stack(firsts), at_first, axis=0),
+            jnp.take(jnp.stack(seconds), at_second, axis=0),
+        ],
+        axis=1,
+    )
+
+
+def plane_sum(grad):
+    count = lax.axis_size("wide")
+    if count != 8:
+        return lax.psum_scatter(grad, "wide", scatter_dimension=0, tiled=False)
+    half = grad.shape[1] // 2
+    from_first, from_second, _, _ = ring_orders()
+    firsts = jnp.take(grad[:, :half], from_first, axis=0)
+    seconds = jnp.take(grad[:, half:], from_second, axis=0)
+    joined = jnp.stack([firsts, seconds])
+    own = (
+        joined[:, :4].astype(f32)
+        + lax.ppermute(joined[:, 4:], "wide", swap_pairs()).astype(f32)
+    ).astype(bf16)
+    return jnp.concatenate(
+        plane_ring_back([own[0, s] for s in range(4)], [own[1, s] for s in range(4)]), axis=0
+    )
+
+
+def ff_gather(parts):
+    if lax.axis_size("wide") != 8:
+        return [lax.all_gather(part, "wide", axis=0, tiled=True) for part in parts]
+    half = parts[0].shape[0] // 2
+    firsts, seconds = plane_ring(
+        jnp.concatenate([part[:half] for part in parts], axis=0),
+        jnp.concatenate([part[half:] for part in parts], axis=0),
+    )
+    blocks = [block for pair in zip(firsts, seconds) for block in pair]
+    return [
+        jnp.concatenate([block[k * half : (k + 1) * half] for block in blocks], axis=0)
+        for k in range(3)
+    ]
+
+
+def ff_sum(grad):
+    if lax.axis_size("wide") != 8:
+        return [lax.psum_scatter(grad, "wide", scatter_dimension=0, tiled=True)]
+    middle = grad.shape[0] // 2
+    own = (
+        grad[:middle].astype(f32)
+        + lax.ppermute(grad[middle:], "wide", swap_pairs()).astype(f32)
+    ).astype(bf16)
+    size = middle // 8
+    blocks = [own[k * size : (k + 1) * size] for k in range(8)]
+    return plane_ring_back(blocks[0::2], blocks[1::2])
 
 
 def local(
@@ -591,6 +789,7 @@
     row_count = tokens.shape[0]
     seq_len = row_count * narrow_count
     row_blocks = D // unit_rows
+    col_blocks = unit_count // row_blocks
     piece = unit_cols // wide_count
     query_width = H // narrow_count * HD
     kv_width = KV // narrow_count * HD
@@ -600,152 +799,128 @@
     narrow_index = lax.axis_index("narrow")
     length = lax.dynamic_slice(lengths, (wide_index,), (1,))
     block = min(256, seq_len)
+    qkv_blocks = qkv_width // unit_cols
+    out_blocks = query_width // unit_cols
+    attn_blocks = qkv_blocks + out_blocks
 
     inputs = tokens.astype(f32)
     normed = rmsnorm(inputs, norm_gains[0]).astype(bf16)
-    normed_blocks = ring_gather(normed, narrow_count)
+    normed_all = lax.all_gather(normed, "narrow", axis=0, tiled=True)
 
     slot_place, counts = positions(owners, wide_count, capacity)
     turned = turn_units(master).reshape(capacity, wide_count, piece, unit_rows)
     got = lax.all_to_all(turned, "wide", split_axis=1, concat_axis=0)
     got = got.reshape(wide_count * capacity, piece, unit_rows)
     rows = pick_units(got, slot_place, row_blocks)
-    qkv_end = qkv_width // wide_count
-    out_end = qkv_end + query_width // wide_count
+    qkv_end = qkv_blocks * piece
+    out_end = attn_blocks * piece
     ff_rows = ff_width // wide_count
 
-    def plane_all(part, width):
-        gathered = lax.all_gather(part, "wide", axis=0)
-        gathered = gathered.reshape(wide_count, width // unit_cols, piece, D)
-        return jnp.transpose(gathered, (1, 0, 2, 3)).reshape(width, D)
-
-    w_qkv = plane_all(rows[:qkv_end], qkv_width)
-    out_part = lax.all_gather(rows[qkv_end:out_end], "narrow", axis=0)
-    w_out = lax.all_gather(out_part, "wide", axis=0)
-    w_out = jnp.transpose(
-        w_out.reshape(wide_count, narrow_count, query_width // unit_cols, piece, D),
-        (1, 2, 0, 3, 4),
-    ).reshape(D, D)
+    w_qkv = plane_all(rows[:qkv_end]).reshape(wide_count, qkv_blocks, piece, D)
+    w_qkv = jnp.transpose(w_qkv, (1, 0, 2, 3)).reshape(qkv_width, D)
+    out_part = jnp.stack(ring_gather(rows[qkv_end:out_end], narrow_count))
+    by_place = (narrow_index - jnp.arange(narrow_count, dtype=jnp.int32)) % narrow_count
+    out_part = jnp.take(out_part, by_place, axis=0)
+    w_out = plane_all(out_part.reshape(narrow_count * out_blocks * piece, D))
+    w_out = w_out.reshape(wide_count, narrow_count * out_blocks, piece, D)
+    w_out = jnp.transpose(w_out, (1, 0, 2, 3)).reshape(D, D)
     ff_parts = [rows[out_end + k * ff_rows : out_end + (k + 1) * ff_rows] for k in range(3)]
-    if wide_count == 8:
-        half = ff_rows // 2
-        halves = [
-            jnp.concatenate([part[:half] for part in ff_parts], axis=0),
-            jnp.concatenate([part[half:] for part in ff_parts], axis=0),
-        ]
-        ff_blocks = plane_gather(halves)
-        w_gate, w_upper, w_down = [
-            jnp.concatenate([b[k * half : (k + 1) * half] for b in ff_blocks], axis=0)
-            for k in range(3)
-        ]
-    else:
-        w_gate, w_upper, w_down = [
-            lax.all_gather(part, "wide", axis=0, tiled=True) for part in ff_parts
-        ]
+    w_gate, w_upper, w_down = ff_gather(ff_parts)
 
     cos_table, sin_table = tables(seq_len, HD)
     cos_all = jnp.concatenate([cos_table] * (LANES // HD), axis=1)
     sin_all = jnp.concatenate([sin_table] * (LANES // HD), axis=1)
-    projected = []
-    for s in range(narrow_count):
-        first_row = (narrow_index - s) % narrow_count * row_count
-        projected.append(
-            project(
-                normed_blocks[s],
-                w_qkv,
-                lax.dynamic_slice(cos_all, (first_row, 0), (row_count, LANES)),
-                lax.dynamic_slice(sin_all, (first_row, 0), (row_count, LANES)),
-                query_width,
-                kv_width,
-            )
-        )
-    back_by = (narrow_index - jnp.arange(narrow_count, dtype=jnp.int32)) % narrow_count
-    qkv = jnp.take(jnp.stack(projected), back_by, axis=0).reshape(seq_len, qkv_width)
+    cotangent_later, normed_all = lax.optimization_barrier((cotangent, normed_all))
+    back_all = lax.all_gather(cotangent_later, "narrow", axis=0, tiled=True)
+    qkv = project(normed_all, w_qkv, cos_all, sin_all, query_width, kv_width, row_count)
     attended, logs = attend_forward(length, qkv, query_width, kv_width, block)
     attended_rows = lax.all_to_all(
         attended.reshape(narrow_count, row_count, query_width), "narrow", 0, 0
     )
-    attended_rows = jnp.transpose(attended_rows, (1, 0, 2)).reshape(row_count, D)
-    residual = inputs + dot(attended_rows, w_out, 1, 0)
-
-    normed_two = rmsnorm(residual, norm_gains[1]).astype(bf16)
+    residual, normed_two = branch(attended_rows, w_out, tokens, norm_gains[1:2])
+
     mlp_blocks = ring_gather(normed_two, narrow_count)
-    back_blocks = ring_gather(cotangent, narrow_count)
-    passes = [
-        hidden_pass(mlp_blocks[s], back_blocks[s], w_gate, w_upper, w_down)
-        for s in range(narrow_count)
-    ]
-
-    def norm_back_part(s):
-        return lambda: dot(passes[s][1], w_gate, 1, 0) + dot(passes[s][2], w_upper, 1, 0)
-
-    norm_two_back = ring_reduce([norm_back_part(s) for s in range(narrow_count)], narrow_count)
-    output = residual + ring_reduce(
-        [functools.partial(dot, passes[s][0], w_down, 1, 0) for s in range(narrow_count)],
-        narrow_count,
-    )
-    ff_grads = [
-        outer([p[1] for p in passes], mlp_blocks),
-        outer([p[2] for p in passes], mlp_blocks),
-        outer([p[0] for p in passes], back_blocks),
-    ]
-
-    def plane_sum(grad):
-        if wide_count == 8:
-            return plane_reduce(grad)
-        return [lax.psum_scatter(grad, "wide", scatter_dimension=0, tiled=True)]
-
-    ff_sums = [part for grad in ff_grads for part in plane_sum(grad)]
+    places = [((narrow_index - s) % narrow_count).reshape(1) for s in range(narrow_count)]
+    kept = ()
+    for s in range(narrow_count):
+        kept = hidden_pass(places[s], mlp_blocks[s], back_all, w_gate, w_upper, w_down, kept)
+    hidden, dgate, dup, mlp_all = kept
+    total = None
+    for s in range(1, narrow_count + 1):
+        last = s == narrow_count
+        total = norm_back(
+            places[s % narrow_count], dgate, dup, w_gate, w_upper, row_count, total,
+            f32 if last else bf16,
+        )
+        if not last:
+            total = lax.ppermute(total, "narrow", cycle(narrow_count))
+    norm_two_back = total
 
     _, norm_two_pull = jax.vjp(rmsnorm, residual, norm_gains[1])
     resid_part, gain_two = norm_two_pull(norm_two_back)
     resid_back = cotangent.astype(f32) + resid_part
     attn_back = resid_back.astype(bf16)
-    out_back = dot(attn_back, w_out, 1, 1).astype(bf16)
-    out_back = jnp.transpose(out_back.reshape(row_count, narrow_count, query_width), (1, 0, 2))
-    out_back = lax.all_to_all(out_back, "narrow", 0, 0).reshape(seq_len, query_width)
-    grad_out = outer([attended_rows], [attn_back])
-    qkv_back = attend_backward(
-        length, qkv, out_back, attended, logs, cos_all, sin_all, query_width, kv_width, block
-    )
-    qkv_blocks = [
-        lax.dynamic_slice(
-            qkv_back, ((narrow_index - s) % narrow_count * row_count, 0), (row_count, qkv_width)
-        )
-        for s in range(narrow_count)
-    ]
-    grad_qkv = outer(qkv_blocks, normed_blocks)
-
-    def plane_split(grad, width, lead):
-        shaped = grad.reshape(lead, width // unit_cols, wide_count, piece, D)
-        shaped = jnp.transpose(shaped, (2, 0, 1, 3, 4)).reshape(wide_count * lead * width // wide_count, D)
-        return lax.psum_scatter(shaped, "wide", scatter_dimension=0, tiled=True)
-
-    grad_out = plane_split(grad_out, query_width, narrow_count)
-    grad_out = lax.psum_scatter(grad_out, "narrow", scatter_dimension=0, tiled=True)
-    grad_qkv = plane_split(grad_qkv, qkv_width, 1)
-
-    grad_rows = jnp.concatenate([grad_qkv, grad_out] + ff_sums, axis=0)
+    out_back = lax.all_to_all(spread(attn_back, w_out, narrow_count), "narrow", 0, 0)
+    out_back = out_back.reshape(seq_len, query_width)
+
+    ff_term = dot(hidden, w_down, 1, 0).astype(bf16)
+    output = residual + lax.psum_scatter(
+        ff_term, "narrow", scatter_dimension=0, tiled=True
+    ).astype(f32)
+    ff_grads = [outer(hidden, back_all), outer(dgate, mlp_all), outer(dup, mlp_all)]
+    ff_sums = [ff_sum(grad) for grad in ff_grads]
+    ff_sums = ff_sums[1] + ff_sums[2] + ff_sums[0]
+
     slots = wide_count * capacity
     unit_of = jnp.zeros((slots,), jnp.int32).at[slot_place].set(
         jnp.arange(unit_count, dtype=jnp.int32)
     )
-    sent = unpick_units(grad_rows, unit_of, unit_count, piece, unit_rows)
+    half_of = unit_of // col_blocks
+    block_of = unit_of - half_of * col_blocks
+    sent = unpick_units(
+        jnp.concatenate(ff_sums, axis=0),
+        jnp.maximum(block_of - attn_blocks, 0),
+        half_of,
+        piece,
+        unit_rows,
+    )
     sent = sent.reshape(wide_count, capacity, piece, unit_rows)
     owned = lax.all_to_all(sent, "wide", split_axis=0, concat_axis=0)
-    count = lax.dynamic_slice(counts, (wide_index,), (1,))
+
+    grad_out = outer(attended_rows, attn_back)
+    grad_out = grad_out.reshape(narrow_count * out_blocks, wide_count, piece, D)
+    grad_out = jnp.transpose(grad_out, (1, 0, 2, 3))
+    grad_out = plane_sum(grad_out.reshape(wide_count, narrow_count * out_blocks * piece, D))
+    grad_out = lax.psum_scatter(grad_out, "narrow", scatter_dimension=0, tiled=True)
+    qkv_back = attend_backward(
+        length, qkv, out_back, attended, logs, cos_all, sin_all, query_width, kv_width, block
+    )
+    grad_qkv = outer(qkv_back, normed_all)
+    gain_one = jnp.sum(w_qkv.astype(f32) * grad_qkv.astype(f32), axis=0) / norm_gains[0]
+    gain_grads = butterfly(jnp.stack([gain_one, gain_two]))
+    grad_qkv = jnp.transpose(grad_qkv.reshape(qkv_blocks, wide_count, piece, D), (1, 0, 2, 3))
+    grad_qkv = plane_sum(grad_qkv.reshape(wide_count, qkv_blocks * piece, D))
+    attn_grads = plane_all(jnp.concatenate([grad_qkv, grad_out], axis=0))
+    attn_grads = attn_grads.reshape(wide_count, attn_blocks, piece, D)
+
+    first_slot = wide_index * capacity
     owned_grads, new_master, new_copy, new_first, new_second = update_units(
-        count, owned, master, moment_one, moment_two
-    )
-
-    norm_one_back = ring_reduce(
-        [functools.partial(dot, qkv_blocks[s], w_qkv, 1, 0) for s in range(narrow_count)],
-        narrow_count,
-    )
-    _, norm_one_pull = jax.vjp(rmsnorm, inputs, norm_gains[0])
-    input_part, gain_one = norm_one_pull(norm_one_back)
+        lax.dynamic_slice(block_of, (first_slot,), (capacity,)),
+        lax.dynamic_slice(half_of, (first_slot,), (capacity,)),
+        lax.dynamic_slice(counts, (wide_index,), (1,)),
+        owned,
+        attn_grads,
+        master,
+        moment_one,
+        moment_two,
+    )
+
+    norm_one_back = lax.psum_scatter(
+        dot(qkv_back, w_qkv, 1, 0).astype(bf16), "narrow", scatter_dimension=0, tiled=True
+    ).astype(f32)
+    _, norm_one_pull = jax.vjp(lambda values: rmsnorm(values, norm_gains[0]), inputs)
+    (input_part,) = norm_one_pull(norm_one_back)
     input_grad = (resid_back + input_part).astype(bf16)
-    gain_grads = lax.psum(jnp.stack([gain_one, gain_two]), ("wide", "narrow"))
     new_gains, _, gain_second_new = adamw(
         norm_gains, gain_grads, gain_first, gain_second, 0.5, 0.0
     )

time: 1580 us -> 1440 us (0.911)
  Pallas kernels: 625 us -> 359 us
  waiting for transfers between devices: 540 us -> 656 us
  matrix products: 115 us -> 27.7 us
  local copies, waits for them, and re-layouts: 109 us -> 181 us
  blocking collectives: 38.3 us -> 0 us
  starting transfers between devices: 49.3 us -> 84.2 us
  other arithmetic: 73.5 us -> 108 us
    ppermute x44 -> x99, waiting for transfers between devices: 224 us -> 467 us  [the longest x12 160 us: plane_ring(): firsts.append(lax.ppermute(firsts[-1], 'wide', square_pairs(1)))]
    pallas_call x11 -> x17, Pallas kernels: 410 us -> 260 us  [the longest x5 74.1 us: outer(): pl.pallas_call(outer_kernel, grid=(height // step,), in_specs=[taken, pl....]
    pallas_call x1, Pallas kernels: 117 us -> 3.3 us  [pick_units(): pl.pallas_call(functools.partial(pick_kernel, col_blocks=col_blocks, piec...]
    ppermute x9 -> x6, waiting for transfers between devices: 184 us -> 75.2 us  [ring_gather(): blocks.append(lax.ppermute(blocks[-1], 'narrow', cycle(count)))]
    dot_general x18 -> x2, matrix products: 115 us -> 27.7 us  [dot(): lax.dot_general(first_op, second_op, (((first_dim,), (second_dim,)), ((),...]
    psum x1 -> x0, blocking collectives: 38.3 us -> none  [local(): gain_grads = lax.psum(jnp.stack([gain_one, gain_two]), ('wide', 'narrow'))]
    gather x1 -> x14, local copies, waits for them, and re-layouts: 2.36 us -> 38.8 us  [the longest x3 11.3 us: plane_all(): jnp.take(jnp.stack(seconds), at_second, axis=0)]
    ppermute x44 -> x99, starting transfers between devices: 27.1 us -> 61.9 us  [the longest x30 27.6 us: plane_ring_back(): lax.ppermute(total, 'wide', square_pairs(step)).astype(f32)]
  transfers between devices with their start and end apart: 63 -> 114, of which waited for: 28 -> 51; matrix products, arithmetic and copies ran while one was open for 16% -> 17% of each run, Pallas kernels for 29% -> 20%
where the time goes in v2:
time: 1440 us; the launch traced here: 1430 us
  waiting for transfers between devices  656 us (46%)
  Pallas kernels  359 us (25%)
  local copies, waits for them, and re-layouts  181 us (13%)
  other arithmetic  108 us (8%)
  starting transfers between devices  84.2 us (6%)
  matrix products  27.7 us (2%)
  between operations  15.5 us (1%)
    ppermute x12, waiting for transfers between devices, plane_ring(): firsts.append(lax.ppermute(firsts[-1], 'wide', square_pairs(1)))  160 us
    ppermute x30, waiting for transfers between devices, plane_ring_back(): lax.ppermute(total, 'wide', square_pairs(step)).astype(f32)  129 us
    ppermute x3, waiting for transfers between devices, local(): total = lax.ppermute(total, 'narrow', cycle(narrow_count))  97.7 us
    unnamed x179, local copies, waits for them, and re-layouts  82 us
    ppermute x6, waiting for transfers between devices, ring_gather(): blocks.append(lax.ppermute(blocks[-1], 'narrow', cycle(count)))  75.2 us
    pallas_call x5, Pallas kernels, outer(): pl.pallas_call(outer_kernel, grid=(height // step,), in_specs=[taken, pl....  74.1 us
    pallas_call x4, Pallas kernels, hidden_pass(): pl.pallas_call(hidden_kernel, grid_spec=pltpu.PrefetchScalarGridSpec(num_...  71.6 us
    ppermute x12, waiting for transfers between devices, plane_ring(): seconds.append(lax.ppermute(seconds[-1], 'wide', square_pairs(-1)))  68.6 us
  transfers between devices with their start and end apart: 114, of which 51 were waited for; matrix products, arithmetic and copies ran while one was open for 17% of the time, Pallas kernels for 20%

profile of v2, /device:TPU:0, one launch (start us, length us, event | category | flops | bytes accessed | tf_op | source)
XLA Modules:
  0.0 1430.3 jit_solution(6302925558885081052)
XLA Ops:
  36.8 64.5 %all-to-all-done = bf16[1,26,8,16,1024]{4,3,1,0,2:T(8,128)(2,1)} async-done(((bf16[1,26,8,16,1024]{4,3,1,0,2:T(8,128)(2,1)}), bf16[1,26,8,16,1024]{4,3,1,0,2:T(8,128)(2,1)}, u32[]{:S(2)}, u32[]{:S(2)}) %all-to-all-start) | async-done | bytes 6815776 | tf_op jit(solution)/shard_map/all_to_all | solution.py:812
  113.1 33.9 %collective-permute-done = bf16[48,2048]{1,0:T(8,128)(2,1)S(1)} collective-permute-done((bf16[48,2048]{1,0:T(8,128)(2,1)S(1)}, bf16[48,2048]{1,0:T(8,128)(2,1)S(1)}, u32[]{:S(2)}, u32[]{:S(2)}) %collective-permute-start) | collective-permute-done | bytes 196640 | tf_op jit(solution)/shard_map/ppermute | solution.py:681
  172.4 34.2 %collective-permute-done.9 = bf16[48,2048]{1,0:T(8,128)(2,1)S(1)} collective-permute-done((bf16[48,2048]{1,0:T(8,128)(2,1)S(1)}, bf16[48,2048]{1,0:T(8,128)(2,1)S(1)}, u32[]{:S(2)}, u32[]{:S(2)}) %collective-permute-start.9) | collective-permute-done | bytes 196640 | tf_op jit(solution)/shard_map/ppermute | solution.py:682
  353.8 27.3 %attend_forward.1 = (bf16[1536,512]{1,0:T(8,128)(2,1)}, f32[4,8,1536]{2,1,0:T(8,128)}) custom-call(s32[1]{0:T(128)} %dynamic_slice.27.length_ref, bf16[1536,768]{1,0:T(8,128)(2,1)} %copy-done.13, bf16[1536,768]{1,0:T(8,128)(2,1)} %copy-done.13, bf16[1536,768]{1,0:T(8,128)(2,1)} %copy-done.13), custom_call_target="tpu_custom_call" | custom-call | flops 9663676416 | bytes 4718592 | tf_op jit(solution)/shard_map/attend_forward/pallas_call | solution.py:340
  413.2 43.7 %all-to-all-done.1.attended_ref.first_ref = bf16[4,384,512]{2,1,0:T(8,128)(2,1)} async-done(((bf16[4,384,512]{2,1,0:T(8,128)(2,1)}), bf16[4,384,512]{2,1,0:T(8,128)(2,1)}, u32[]{:S(2)}, u32[]{:S(2)}) %all-to-all-start.1) | async-done | bytes 1572896 | tf_op jit(solution)/shard_map/all_to_all | solution.py:837
  477.0 26.3 %collective-permute-done.31.rows_ref = bf16[384,2048]{1,0:T(8,128)(2,1)S(1)} collective-permute-done((bf16[384,2048]{1,0:T(8,128)(2,1)}, bf16[384,2048]{1,0:T(8,128)(2,1)S(1)}, u32[]{:S(2)}, u32[]{:S(2)}) %collective-permute-start.31) | collective-permute-done | bytes 1572896 | tf_op jit(solution)/shard_map/ppermute | solution.py:649
  510.0 29.4 %collective-permute-done.32.rows_ref = bf16[384,2048]{1,0:T(8,128)(2,1)} collective-permute-done((bf16[384,2048]{1,0:T(8,128)(2,1)S(1)}, bf16[384,2048]{1,0:T(8,128)(2,1)}, u32[]{:S(2)}, u32[]{:S(2)}) %collective-permute-start.32) | collective-permute-done | bytes 1572896 | tf_op jit(solution)/shard_map/ppermute | solution.py:649
  541.0 17.8 %hidden_pass.4 = (bf16[1536,2048]{1,0:T(8,128)(2,1)}, bf16[1536,2048]{1,0:T(8,128)(2,1)}, bf16[1536,2048]{1,0:T(8,128)(2,1)}, bf16[1536,2048]{1,0:T(8,128)(2,1)}) custom-call(s32[1]{0:T(128)} %bitcast.56.place_ref, bf16[384,2048]{1,0:T(8,128)(2,1)S(1)} %copy-done.12, bf16[1536,2048]{1,0:T(8,128)(2,1)} %all-gather.5.cloned.1.call-done.back_ref.second_ref, ...), custom_call_target="tpu_custom_call" | custom-call | flops 9663676416 | bytes 25165824 | tf_op jit(solution)/shard_map/hidden_pass/pallas_call | solution.py:558
  558.8 17.8 %hidden_pass.5 = (bf16[1536,2048]{1,0:T(8,128)(2,1)}, bf16[1536,2048]{1,0:T(8,128)(2,1)}, bf16[1536,2048]{1,0:T(8,128)(2,1)}, bf16[1536,2048]{1,0:T(8,128)(2,1)}) custom-call(s32[1]{0:T(128)} %bitcast.55.place_ref, bf16[384,2048]{1,0:T(8,128)(2,1)S(1)} %copy-done.8, ...), custom_call_target="tpu_custom_call", output_to_operand_aliasing={{0}: (6, {}), {1}: (7, {}), {2}: (8, {}), {3}: (9, {})} | custom-call | flops 9663676416 | bytes 25165824 | tf_op jit(solution)/shard_map/hidden_pass/pallas_call | solution.py:558
  576.6 18.0 %hidden_pass.6 = (bf16[1536,2048]{1,0:T(8,128)(2,1)}, bf16[1536,2048]{1,0:T(8,128)(2,1)}, bf16[1536,2048]{1,0:T(8,128)(2,1)}, bf16[1536,2048]{1,0:T(8,128)(2,1)}) custom-call(s32[1]{0:T(128)} %bitcast.54.place_ref, bf16[384,2048]{1,0:T(8,128)(2,1)} %collective-permute-done.32.rows_ref, ...), custom_call_target="tpu_custom_call", output_to_operand_aliasing={{0}: (6, {}), {1}: (7, {}), {2}: (8, {}), {3}: (9, {})} | custom-call | flops 9663676416 | bytes 25165824 | tf_op jit(solution)/shard_map/hidden_pass/pallas_call | solution.py:558
  594.6 18.0 %hidden_pass.7 = (bf16[1536,2048]{1,0:T(8,128)(2,1)}, bf16[1536,2048]{1,0:T(8,128)(2,1)}, bf16[1536,2048]{1,0:T(8,128)(2,1)}, bf16[1536,2048]{1,0:T(8,128)(2,1)}) custom-call(s32[1]{0:T(128)} %bitcast.53.place_ref, bf16[384,2048]{1,0:T(8,128)(2,1)} %collective-permute-done.33.rows_ref, ...), custom_call_target="tpu_custom_call", output_to_operand_aliasing={{0}: (6, {}), {1}: (7, {}), {2}: (8, {}), {3}: (9, {})} | custom-call | flops 9663676416 | bytes 25165824 | tf_op jit(solution)/shard_map/hidden_pass/pallas_call | solution.py:558
  623.6 35.0 %collective-permute-done.48.refs_0_ = bf16[384,2048]{1,0:T(8,128)(2,1)S(1)} collective-permute-done((bf16[384,2048]{1,0:T(8,128)(2,1)S(1)}, bf16[384,2048]{1,0:T(8,128)(2,1)S(1)}, u32[]{:S(2)}, u32[]{:S(2)}) %collective-permute-start.48) | collective-permute-done | bytes 1572896 | tf_op jit(solution)/shard_map/ppermute | solution.py:856
  669.8 34.1 %collective-permute-done.49.refs_0_ = bf16[384,2048]{1,0:T(8,128)(2,1)S(1)} collective-permute-done((bf16[384,2048]{1,0:T(8,128)(2,1)S(1)}, bf16[384,2048]{1,0:T(8,128)(2,1)S(1)}, u32[]{:S(2)}, u32[]{:S(2)}) %collective-permute-start.49) | collective-permute-done | bytes 1572896 | tf_op jit(solution)/shard_map/ppermute | solution.py:856
  703.9 11.9 norm_back.6
  720.9 28.6 %collective-permute-done.50.refs_0_ = bf16[384,2048]{1,0:T(8,128)(2,1)} collective-permute-done((bf16[384,2048]{1,0:T(8,128)(2,1)}, bf16[384,2048]{1,0:T(8,128)(2,1)}, u32[]{:S(2)}, u32[]{:S(2)}) %collective-permute-start.50) | collective-permute-done | bytes 1572896 | tf_op jit(solution)/shard_map/ppermute | solution.py:856
  749.5 11.8 norm_back.7
  817.7 13.4 collective-permute-done.87
  891.2 58.9 %attend_backward.1.first_ref = bf16[1536,768]{1,0:T(8,128)(2,1)} custom-call(s32[1]{0:T(128)} %dynamic_slice.27.length_ref, bf16[1536,768]{1,0:T(8,128)(2,1)} %copy-done.13, bf16[1536,768]{1,0:T(8,128)(2,1)} %copy-done.13, bf16[1536,768]{1,0:T(8,128)(2,1)} %copy-done.13, bf16[1536,512]{1,0:T(8,128)(2,1)} %bitcast.58.back_ref, ...), custom_call_target="tpu_custom_call" | custom-call | flops 24159191040 | bytes 7077888 | tf_op jit(solution)/shard_map/attend_backward/pallas_call | solution.py:449
  960.7 19.2 %outer.7 = bf16[2048,2048]{1,0:T(8,128)(2,1)} custom-call(bf16[1536,2048]{1,0:T(8,128)(2,1)} %get-tuple-element.57.first_ref, bf16[1536,2048]{1,0:T(8,128)(2,1)} %all-gather.5.cloned.1.call-done.back_ref.second_ref), custom_call_target="tpu_custom_call" | custom-call | flops 12884901888 | bytes 20971520 | tf_op jit(solution)/shard_map/outer/pallas_call | solution.py:628
  984.7 18.4 %outer.5 = bf16[2048,2048]{1,0:T(8,128)(2,1)} custom-call(bf16[1536,2048]{1,0:T(8,128)(2,1)} %get-tuple-element.58.dgate_ref.first_ref, bf16[1536,2048]{1,0:T(8,128)(2,1)} %get-tuple-element.61.second_ref), custom_call_target="tpu_custom_call" | custom-call | flops 12884901888 | bytes 20971520 | tf_op jit(solution)/shard_map/outer/pallas_call | solution.py:628
  1008.3 18.4 %outer.6 = bf16[2048,2048]{1,0:T(8,128)(2,1)} custom-call(bf16[1536,2048]{1,0:T(8,128)(2,1)} %get-tuple-element.59.dup_ref.first_ref, bf16[1536,2048]{1,0:T(8,128)(2,1)} %get-tuple-element.61.second_ref), custom_call_target="tpu_custom_call" | custom-call | flops 12884901888 | bytes 20971520 | tf_op jit(solution)/shard_map/outer/pallas_call | solution.py:628
  1031.6 19.1 %convolution_convert_fusion.1 = bf16[1536,2048]{1,0:T(8,128)(2,1)} fusion(bf16[1536,2048]{1,0:T(8,128)(2,1)} %get-tuple-element.57.first_ref, bf16[2048,2048]{1,0:T(8,128)(2,1)} %get-tuple-element.132.wd_ref), kind=kOutput, calls=%fused_computation.23 | convolution fusion | flops 12888047616 | bytes 20971520 | tf_op jit(solution)/shard_map/dot_general | solution.py:24
  1241.5 77.2 %collective-permute-done.79 = bf16[80,2048]{1,0:T(8,128)(2,1)S(1)} collective-permute-done((bf16[80,2048]{1,0:T(8,128)(2,1)S(1)}, bf16[80,2048]{1,0:T(8,128)(2,1)S(1)}, u32[]{:S(2)}, u32[]{:S(2)}) %collective-permute-start.79) | collective-permute-done | bytes 327712 | tf_op jit(solution)/shard_map/ppermute | solution.py:681
  1368.3 46.6 %update_units.1 = (f32[26,1,1024,128]{3,2,1,0:T(8,128)}, f32[26,1,1024,128]{3,2,1,0:T(8,128)}, bf16[26,1,1024,128]{3,2,1,0:T(8,128)(2,1)}, f32[26,1,1024,128]{3,2,1,0:T(8,128)}, f32[26,1,1024,128]{3,2,1,0:T(8,128)}) custom-call(s32[26]{0:T(128)S(1)} %dynamic_slice.30.block_ref, s32[26]{0:T(128)S(1)} %dynamic_slice.31.half_ref, s32[1]{0:T(128)} %dynamic_slice.32.count_ref, ...), custom_call_target="tpu_custom_call" | custom-call | flops 40894464 | bytes 109051904 | tf_op jit(solution)/shard_map/update_units/pallas_call | solution.py:201
  (553 shorter events, 691.4 us)
Async XLA Ops:
  18.5 82.8 %all-to-all-start = ((bf16[1,26,8,16,1024]{4,3,1,0,2:T(8,128)(2,1)}), bf16[1,26,8,16,1024]{4,3,1,0,2:T(8,128)(2,1)}, u32[]{:S(2)}, u32[]{:S(2)}) async-start(bf16[1,26,8,16,1024]{4,3,1,0,2:T(8,128)(2,1)} %copy.44), calls=%async_computation | async-start | bytes 13631488 | tf_op jit(solution)/shard_map/all_to_all | solution.py:812
  23.8 287.7 %all-gather.3.cloned.1.call-start = ((), (), s32[]{:S(2)}) async-start(), calls=%async_computation.7 | async-start | bytes 7864320 | tf_op jit(solution)/shard_map/all_gather | solution.py:808
  27.1 512.5 %all-gather.5.cloned.1.call-start = ((), (), s32[]{:S(2)}) async-start(), calls=%async_computation.8 | async-start | bytes 7864320 | tf_op jit(solution)/shard_map/all_gather | solution.py:834
  108.2 145.8 %collective-permute-start.34 = (bf16[384,2048]{1,0:T(8,128)(2,1)}, bf16[384,2048]{1,0:T(8,128)(2,1)}, u32[]{:S(2)}, u32[]{:S(2)}) collective-permute-start(bf16[384,2048]{1,0:T(8,128)(2,1)} %pad_maximum_fusion.5), channel_id=1, source_target_pairs={{0,8},{4,12},{8,24},{12,28},{24,16},{28,20},{16,0},{20,4},{1,9},{5... | collective-permute-start | bytes 4718600 | tf_op jit(solution)/shard_map/ppermute | solution.py:681
  108.8 357.3 %collective-permute-start.40 = (bf16[384,2048]{1,0:T(8,128)(2,1)}, bf16[384,2048]{1,0:T(8,128)(2,1)}, u32[]{:S(2)}, u32[]{:S(2)}) collective-permute-start(bf16[384,2048]{1,0:T(8,128)(2,1)} %pad_maximum_fusion.5), channel_id=1, source_target_pairs={{0,4},{4,0},{8,12},{12,8},{16,20},{20,16},{24,28},{28,24},{1,5},{5... | collective-permute-start | bytes 4718600 | tf_op jit(solution)/shard_map/ppermute | solution.py:683
  167.6 89.9 %collective-permute-start.35 = (bf16[384,2048]{1,0:T(8,128)(2,1)}, bf16[384,2048]{1,0:T(8,128)(2,1)}, u32[]{:S(2)}, u32[]{:S(2)}) collective-permute-start(bf16[384,2048]{1,0:T(8,128)(2,1)} %pad_maximum_fusion.6), channel_id=1, source_target_pairs={{0,16},{4,20},{8,0},{12,4},{24,8},{28,12},{16,24},{20,28},{1,17},{... | collective-permute-start | bytes 4718600 | tf_op jit(solution)/shard_map/ppermute | solution.py:682
  249.3 219.4 %collective-permute-start.41 = (bf16[384,2048]{1,0:T(8,128)(2,1)}, bf16[384,2048]{1,0:T(8,128)(2,1)}, u32[]{:S(2)}, u32[]{:S(2)}) collective-permute-start(bf16[384,2048]{1,0:T(8,128)(2,1)} %pad_maximum_fusion.6), channel_id=1, source_target_pairs={{0,4},{4,0},{8,12},{12,8},{16,20},{20,16},{24,28},{28,24},{1,5},{5... | collective-permute-start | bytes 4718600 | tf_op jit(solution)/shard_map/ppermute | solution.py:684
  311.6 159.8 %collective-permute-start.42 = (bf16[384,2048]{1,0:T(8,128)(2,1)}, bf16[384,2048]{1,0:T(8,128)(2,1)}, u32[]{:S(2)}, u32[]{:S(2)}) collective-permute-start(bf16[384,2048]{1,0:T(8,128)(2,1)} %collective-permute-done.34), channel_id=1, source_target_pairs={{0,4},{4,0},{8,12},{12,8},{16,20},{20,16},{24,28},{28,24},{1,5},{5... | collective-permute-start | bytes 4718600 | tf_op jit(solution)/shard_map/ppermute | solution.py:683
  334.2 73.4 %collective-permute-start.38 = (bf16[384,2048]{1,0:T(8,128)(2,1)}, bf16[384,2048]{1,0:T(8,128)(2,1)}, u32[]{:S(2)}, u32[]{:S(2)}) collective-permute-start(bf16[384,2048]{1,0:T(8,128)(2,1)} %collective-permute-done.36), channel_id=1, source_target_pairs={{0,8},{4,12},{8,24},{12,28},{24,16},{28,20},{16,0},{20,4},{1,9},{5... | collective-permute-start | bytes 4718600 | tf_op jit(solution)/shard_map/ppermute | solution.py:681
  341.1 69.1 %collective-permute-start.39 = (bf16[384,2048]{1,0:T(8,128)(2,1)}, bf16[384,2048]{1,0:T(8,128)(2,1)}, u32[]{:S(2)}, u32[]{:S(2)}) collective-permute-start(bf16[384,2048]{1,0:T(8,128)(2,1)} %collective-permute-done.37), channel_id=1, source_target_pairs={{0,16},{4,20},{8,0},{12,4},{24,8},{28,12},{16,24},{20,28},{1,17},{... | collective-permute-start | bytes 4718600 | tf_op jit(solution)/shard_map/ppermute | solution.py:682
  381.1 75.8 %all-to-all-start.1 = ((bf16[4,384,512]{2,1,0:T(8,128)(2,1)}), bf16[4,384,512]{2,1,0:T(8,128)(2,1)}, u32[]{:S(2)}, u32[]{:S(2)}) async-start(bf16[4,384,512]{2,1,0:T(8,128)(2,1)} %bitcast.244), calls=%async_computation.1 | async-start | bytes 3145728 | tf_op jit(solution)/shard_map/all_to_all | solution.py:837
  407.6 66.8 %collective-permute-start.43 = (bf16[384,2048]{1,0:T(8,128)(2,1)}, bf16[384,2048]{1,0:T(8,128)(2,1)}, u32[]{:S(2)}, u32[]{:S(2)}) collective-permute-start(bf16[384,2048]{1,0:T(8,128)(2,1)} %collective-permute-done.35), channel_id=1, source_target_pairs={{0,4},{4,0},{8,12},{12,8},{16,20},{20,16},{24,28},{28,24},{1,5},{5... | collective-permute-start | bytes 4718600 | tf_op jit(solution)/shard_map/ppermute | solution.py:684
  410.2 93.1 %collective-permute-start.44 = (bf16[384,2048]{1,0:T(8,128)(2,1)}, bf16[384,2048]{1,0:T(8,128)(2,1)}, u32[]{:S(2)}, u32[]{:S(2)}) collective-permute-start(bf16[384,2048]{1,0:T(8,128)(2,1)} %collective-permute-done.36), channel_id=1, source_target_pairs={{0,4},{4,0},{8,12},{12,8},{16,20},{20,16},{24,28},{28,24},{1,5},{5... | collective-permute-start | bytes 4718600 | tf_op jit(solution)/shard_map/ppermute | solution.py:683
  855.5 380.3 %reduce-scatter.8.cloned.1.call-start = ((), (), s32[]{:S(2)}) async-start(), calls=%async_computation.11 | async-start | bytes 1310720 | tf_op jit(solution)/shard_map/reduce_scatter | solution.py:894
  885.4 529.5 %reduce-scatter.6.cloned.1.call-start = ((), (), s32[]{:S(2)}) async-start(), calls=%async_computation.10 | async-start | bytes 7864320 | tf_op jit(solution)/shard_map/reduce_scatter | solution.py:918
  958.7 458.8 %reduce-scatter.4.cloned.1.call-start = ((), (), s32[]{:S(2)}) async-start(), calls=%async_computation.9 | async-start | bytes 7864320 | tf_op jit(solution)/shard_map/reduce_scatter | solution.py:867
  984.7 66.0 %collective-permute-start.65 = (bf16[1024,2048]{1,0:T(8,128)(2,1)}, bf16[1024,2048]{1,0:T(8,128)(2,1)}, u32[]{:S(2)}, u32[]{:S(2)}) collective-permute-start(bf16[1024,2048]{1,0:T(8,128)(2,1)} %slice.585), channel_id=1, source_target_pairs={{0,4},{4,0},{8,12},{12,8},{16,20},{20,16},{24,28},{28,24},{1,5},{5... | collective-permute-start | bytes 12582920 | tf_op jit(solution)/shard_map/ppermute | solution.py:774
  1131.0 86.2 %collective-permute-start.71 = (bf16[128,2048]{1,0:T(8,128)(2,1)}, bf16[128,2048]{1,0:T(8,128)(2,1)}, u32[]{:S(2)}, u32[]{:S(2)}) collective-permute-start(bf16[128,2048]{1,0:T(8,128)(2,1)} %get-tuple-element.97), channel_id=1, source_target_pairs={{0,16},{4,20},{8,0},{12,4},{24,8},{28,12},{16,24},{20,28},{1,17},{... | collective-permute-start | bytes 1572872 | tf_op jit(solution)/shard_map/ppermute | solution.py:695
  1142.8 67.4 %collective-permute-start.68 = (bf16[128,2048]{1,0:T(8,128)(2,1)}, bf16[128,2048]{1,0:T(8,128)(2,1)}, u32[]{:S(2)}, u32[]{:S(2)}) collective-permute-start(bf16[128,2048]{1,0:T(8,128)(2,1)} %add_convert_fusion.10), channel_id=1, source_target_pairs={{0,8},{4,12},{8,24},{12,28},{24,16},{28,20},{16,0},{20,4},{1,9},{5... | collective-permute-start | bytes 1572872 | tf_op jit(solution)/shard_map/ppermute | solution.py:695
  1230.6 135.1 %all-to-all-start.3 = ((bf16[8,26,16,1024]{3,2,1,0:T(8,128)(2,1)}), bf16[8,26,16,1024]{3,2,1,0:T(8,128)(2,1)}, u32[]{:S(2)}, u32[]{:S(2)}) async-start(bf16[8,26,16,1024]{3,2,1,0:T(8,128)(2,1)} %bitcast.230), calls=%async_computation.5 | async-start | bytes 13631488 | tf_op jit(solution)/shard_map/all_to_all | solution.py:888
  1237.6 81.1 %collective-permute-start.79 = (bf16[80,2048]{1,0:T(8,128)(2,1)S(1)}, bf16[80,2048]{1,0:T(8,128)(2,1)S(1)}, u32[]{:S(2)}, u32[]{:S(2)}) collective-permute-start(bf16[80,2048]{1,0:T(8,128)(2,1)S(1)} %get-tuple-element.75), channel_id=1, source_target_pairs={{0,8},{4,12},{8,24},{12,28},{24,16},{28,20},{16,0},{20,4},{1,9},{5... | collective-permute-start | bytes 983048 | tf_op jit(solution)/shard_map/ppermute | solution.py:681
  1239.5 79.7 %collective-permute-start.93 = (bf16[80,2048]{1,0:T(8,128)(2,1)S(1)}, bf16[80,2048]{1,0:T(8,128)(2,1)S(1)}, u32[]{:S(2)}, u32[]{:S(2)}) collective-permute-start(bf16[80,2048]{1,0:T(8,128)(2,1)S(1)} %get-tuple-element.179), channel_id=1, source_target_pairs={{0,16},{4,20},{8,0},{12,4},{24,8},{28,12},{16,24},{20,28},{1,17},{... | collective-permute-start | bytes 983048 | tf_op jit(solution)/shard_map/ppermute | solution.py:682
  1241.0 98.6 %collective-permute-start.82 = (bf16[80,2048]{1,0:T(8,128)(2,1)S(1)}, bf16[80,2048]{1,0:T(8,128)(2,1)S(1)}, u32[]{:S(2)}, u32[]{:S(2)}) collective-permute-start(bf16[80,2048]{1,0:T(8,128)(2,1)S(1)} %get-tuple-element.75), channel_id=1, source_target_pairs={{0,4},{4,0},{8,12},{12,8},{16,20},{20,16},{24,28},{28,24},{1,5},{5... | collective-permute-start | bytes 983048 | tf_op jit(solution)/shard_map/ppermute | solution.py:683
  1241.0 110.1 %collective-permute-start.96 = (bf16[80,2048]{1,0:T(8,128)(2,1)S(1)}, bf16[80,2048]{1,0:T(8,128)(2,1)S(1)}, u32[]{:S(2)}, u32[]{:S(2)}) collective-permute-start(bf16[80,2048]{1,0:T(8,128)(2,1)S(1)} %get-tuple-element.179), channel_id=1, source_target_pairs={{0,4},{4,0},{8,12},{12,8},{16,20},{20,16},{24,28},{28,24},{1,5},{5... | collective-permute-start | bytes 983048 | tf_op jit(solution)/shard_map/ppermute | solution.py:684
  (153 other events, 4213.4 us)
Sparse Core Ops, SparseCore 0:
  27.2 118.0 all-gather.2
  311.7 146.4 all-gather.4
  885.5 25.9 reduce-scatter.7
  958.9 109.0 reduce-scatter.5
  1070.2 111.2 reduce-scatter.3

commit v3 on v0

--- a/solution.py
+++ b/solution.py
@@ -1,6 +1,10 @@
+import functools
+
 import jax
 import jax.numpy as jnp
 from jax import lax
+from jax.experimental import pallas as pl
+from jax.experimental.pallas import tpu as pltpu
 from jax.sharding import PartitionSpec as P
 
 D = 2048
@@ -9,24 +13,177 @@
 HD = 64
 FF = 8192
 STEP = 5
-
-
-def rotate(values, cos_table, sin_table):
-    middle = values.shape[-1] // 2
-    turned = jnp.concatenate([-values[..., middle:], values[..., :middle]], axis=-1)
-    return values * cos_table + turned * sin_table
-
-
-def unrotate(gradient, cos_table, sin_table):
-    middle = gradient.shape[-1] // 2
-    weighted = gradient * sin_table
-    turned = jnp.concatenate([weighted[..., middle:], -weighted[..., :middle]], axis=-1)
-    return gradient * cos_table + turned
+LANES = 128
+MIB = 1 << 20
+ANY = pl.BlockSpec(memory_space=pl.ANY)
+VMEM = pl.BlockSpec(memory_space=pltpu.VMEM)
+SMEM = pl.BlockSpec(memory_space=pltpu.SMEM)
+
+f32 = jnp.float32
+bf16 = jnp.bfloat16
+
+
+def dot(first_op, second_op, first_dim, second_dim):
+    return lax.dot_general(
+        first_op,
+        second_op,
+        (((first_dim,), (second_dim,)), ((), ())),
+        preferred_element_type=f32,
+    )
+
+
+def shaped(shape, kind=bf16):
+    return jax.ShapeDtypeStruct(shape, kind)
+
+
+def blocks(shape, place):
+    return pl.BlockSpec(shape, place)
+
+
+class Send:
+    def __init__(self, source, land, axis, step, source_at=None, land_at=None, landed=False, needs=()):
+        self.source, self.land, self.axis, self.step = source, land, axis, step
+        self.source_at, self.land_at = source_at, land_at
+        self.landed, self.needs = landed, needs
+
+
+COLLECTIVE = [0]
+
+
+def run_sends(sends, sources, lands, send_sem, recv_sem):
+    count = lax.axis_size("narrow")
+    wide, narrow = lax.axis_index("wide"), lax.axis_index("narrow")
+
+    def target(axis, step):
+        if axis == "wide":
+            return {"wide": jnp.bitwise_xor(wide, step)}
+        return {"narrow": lax.rem(narrow + step, count)}
+
+    copies = []
+    for k, send in enumerate(sends):
+        ref = (lands if send.landed else sources)[send.source]
+        if send.source_at is not None:
+            ref = ref.at[send.source_at(wide, narrow)]
+        land = lands[send.land]
+        if send.land_at is not None:
+            land = land.at[send.land_at(wide, narrow)]
+        copies.append(
+            pltpu.make_async_remote_copy(
+                src_ref=ref,
+                dst_ref=land,
+                send_sem=send_sem.at[k],
+                recv_sem=recv_sem.at[k],
+                device_id=target(send.axis, send.step),
+                device_id_type=pl.DeviceIdType.MESH,
+            )
+        )
+
+    def start():
+        partners = set()
+        for send in sends:
+            if send.axis == "wide":
+                partners.add(("wide", send.step))
+            else:
+                partners.add(("narrow", send.step % count))
+                partners.add(("narrow", -send.step % count))
+        barrier = pltpu.get_barrier_semaphore()
+        for axis, step in sorted(partners):
+            pl.semaphore_signal(
+                barrier, inc=1, device_id=target(axis, step), device_id_type=pl.DeviceIdType.MESH
+            )
+        pl.semaphore_wait(barrier, len(partners))
+        for send, copy in zip(sends, copies):
+            if not send.needs:
+                copy.start()
+
+    def finish():
+        arrived = set()
+        for send, copy in zip(sends, copies):
+            for k in send.needs:
+                if k not in arrived:
+                    copies[k].wait_recv()
+                    arrived.add(k)
+            if send.needs:
+                copy.start()
+        for k, copy in enumerate(copies):
+            copy.wait_send()
+            if k not in arrived:
+                copy.wait_recv()
+
+    return start, finish
+
+
+def call(
+    body, ins, in_specs, out_shape, out_specs, *, name, grid=(), prefetch=(), scratch=(), deps=(),
+    aliases=None, mib=56, flops=0, moved=0, sends=(), sources=(), lands=(), closing=None,
+):
+    first = len(prefetch) + len(ins)
+    single = not isinstance(out_shape, (list, tuple))
+    out_shapes = [out_shape] if single else list(out_shape)
+    specs = [out_specs] if single else list(out_specs)
+    out_count = len(out_shapes)
+    land_count = len(lands)
+
+    def wrapped(*refs):
+        given = refs[:first]
+        refs = refs[first:]
+        source_refs = refs[: len(sources)]
+        refs = refs[len(sources) + len(deps) :]
+        outs, refs = refs[:out_count], refs[out_count:]
+        land_refs, refs = refs[:land_count], refs[land_count:]
+        if not sends:
+            body(*given, *outs, *refs)
+            return
+        own, (send_sem, recv_sem) = refs[:-2], refs[-2:]
+        start, finish = run_sends(sends, source_refs, land_refs, send_sem, recv_sem)
+
+        def last():
+            finish()
+            if closing is not None:
+                closing(land_refs, (*given, *outs, *own))
+
+        if grid:
+            steps = [pl.program_id(k) for k in range(len(grid))]
+            begins = functools.reduce(jnp.logical_and, [step == 0 for step in steps])
+            ends = functools.reduce(
+                jnp.logical_and, [step == size - 1 for step, size in zip(steps, grid)]
+            )
+            pl.when(begins)(start)
+            body(*given, *outs, *own)
+            pl.when(ends)(last)
+        else:
+            start()
+            body(*given, *outs, *own)
+            last()
+
+    extra = {}
+    if sends:
+        COLLECTIVE[0] += 1
+        extra = {"collective_id": COLLECTIVE[0], "has_side_effects": True}
+        scratch = [*scratch] + [pltpu.SemaphoreType.DMA((len(sends),))] * 2
+    results = pl.pallas_call(
+        wrapped,
+        grid_spec=pltpu.PrefetchScalarGridSpec(
+            num_scalar_prefetch=len(prefetch),
+            grid=grid,
+            in_specs=list(in_specs) + [ANY] * (len(sources) + len(deps)),
+            out_specs=specs + [ANY] * land_count,
+            scratch_shapes=list(scratch),
+        ),
+        out_shape=out_shapes + [shaped(*land) if isinstance(land[0], tuple) else shaped(land) for land in lands],
+        input_output_aliases=aliases or {},
+        compiler_params=pltpu.CompilerParams(vmem_limit_bytes=mib * MIB, **extra),
+        cost_estimate=pl.CostEstimate(
+            flops=int(flops), bytes_accessed=int(moved), transcendentals=0
+        ),
+        name=name,
+    )(*prefetch, *ins, *sources, *deps)
+    return results[0] if single and not sends else list(results)
 
 
 def tables(length_all, head_size):
-    inverse = 500000.0 ** (-jnp.arange(0, head_size, 2, dtype=jnp.float32) / head_size)
-    angles = jnp.arange(length_all, dtype=jnp.float32)[:, None] * inverse[None, :]
+    inverse = 500000.0 ** (-jnp.arange(0, head_size, 2, dtype=f32) / head_size)
+    angles = jnp.arange(length_all, dtype=f32)[:, None] * inverse[None, :]
     angles = jnp.concatenate([angles, angles], axis=1)
     return (jnp.cos(angles), jnp.sin(angles))
 
@@ -40,19 +197,7 @@
 def positions(owners, wide_count, capacity):
     onehot = (owners[:, None] == jnp.arange(wide_count, dtype=jnp.int32)[None, :]).astype(jnp.int32)
     before = jnp.cumsum(onehot, axis=0) - onehot
-    return owners * capacity + jnp.sum(before * onehot, axis=1)
-
-
-def matmul_rows(first_op, second_op):
-    return lax.dot_general(
-        first_op, second_op, (((0,), (0,)), ((), ())), preferred_element_type=jnp.float32
-    )
-
-
-def matmul_cols(first_op, second_op):
-    return lax.dot_general(
-        first_op, second_op, (((1,), (1,)), ((), ())), preferred_element_type=jnp.float32
-    )
+    return (owners * capacity + jnp.sum(before * onehot, axis=1), jnp.sum(onehot, axis=0))
 
 
 def adamw(weight, gradient, moment_one, moment_two, rate, decay):
@@ -63,7 +208,1536 @@
     return (weight - rate * (update + decay * weight), moment_one, moment_two)
 
 
-def project(normed_all, w_qkv, cos_heads, sin_heads, heads_here, kv_here):
+def turn_kernel(unit_ref, out_ref):
+    parts, step, piece, unit_rows = out_ref.shape
+    for k in range(step):
+        out_ref[:, k] = (
+            jnp.transpose(unit_ref[k, 0], (1, 0)).reshape(parts, piece, unit_rows).astype(bf16)
+        )
+
+
+def turn_units(master, parts, deps):
+    capacity, _, unit_rows, unit_cols = master.shape
+    piece = unit_cols // parts
+    step = 2 if capacity % 2 == 0 else 1
+    return call(
+        turn_kernel,
+        [master],
+        [blocks((step, 1, unit_rows, unit_cols), lambda s: (s, 0, 0, 0))],
+        shaped((parts, capacity, piece, unit_rows)),
+        blocks((parts, step, piece, unit_rows), lambda s: (0, s, 0, 0)),
+        grid=(capacity // step,),
+        deps=deps,
+        mib=20,
+        moved=master.size * 6,
+        name="turn_units",
+    )
+
+
+def pick_kernel(turn_ref, place_ref, own_ref, got_ref, out_ref, sem, *, col_blocks):
+    _, capacity, piece, unit_rows = got_ref.shape
+
+    def start(unit, carry):
+        half = unit // col_blocks
+        block = unit - half * col_blocks
+        owner = place_ref[unit] // capacity
+        slot = place_ref[unit] - owner * capacity
+        target = out_ref.at[
+            pl.ds(pl.multiple_of(block * piece, piece), piece),
+            pl.ds(pl.multiple_of(half * unit_rows, unit_rows), unit_rows),
+        ]
+
+        @pl.when(owner == turn_ref[0])
+        def _():
+            pltpu.make_async_copy(own_ref.at[owner, slot], target, sem).start()
+
+        @pl.when(owner != turn_ref[0])
+        def _():
+            pltpu.make_async_copy(got_ref.at[owner, slot], target, sem).start()
+
+        return carry
+
+    lax.fori_loop(0, place_ref.shape[0], start, 0)
+    pltpu.make_async_copy(out_ref, out_ref, sem).wait()
+
+
+def pick_units(turn, slot_place, own, got, row_blocks):
+    _, _, piece, unit_rows = got.shape
+    unit_count = slot_place.shape[0]
+    col_blocks = unit_count // row_blocks
+    return call(
+        functools.partial(pick_kernel, col_blocks=col_blocks),
+        [turn, slot_place, own, got],
+        [SMEM, SMEM, ANY, ANY],
+        shaped((col_blocks * piece, row_blocks * unit_rows)),
+        VMEM,
+        scratch=[pltpu.SemaphoreType.DMA],
+        moved=unit_count * piece * unit_rows * 12,
+        name="pick_units",
+    )
+
+
+def unpick_kernel(block_ref, half_ref, rows_ref, low_ref, high_ref, sems, *, piece, unit_rows):
+    owners, part, _, _ = low_ref.shape
+
+    def start(owner, carry):
+        for slot in range(2 * part):
+            out_ref = high_ref if slot >= part else low_ref
+            place = owner * 2 * part + slot
+            pltpu.make_async_copy(
+                rows_ref.at[
+                    pl.ds(pl.multiple_of(block_ref[place] * piece, piece), piece),
+                    pl.ds(pl.multiple_of(half_ref[place] * unit_rows, unit_rows), unit_rows),
+                ],
+                out_ref.at[owner, slot % part],
+                sems.at[slot // part],
+            ).start()
+        return carry
+
+    lax.fori_loop(0, owners, start, 0)
+    pltpu.make_async_copy(low_ref, low_ref, sems.at[0]).wait()
+    pltpu.make_async_copy(high_ref, high_ref, sems.at[1]).wait()
+
+
+def unpick_units(rows, block_of, half_of, owners, piece, unit_rows):
+    slots = block_of.shape[0]
+    shape = shaped((owners, slots // owners // 2, piece, unit_rows))
+    return call(
+        functools.partial(unpick_kernel, piece=piece, unit_rows=unit_rows),
+        [block_of, half_of, rows],
+        [SMEM, SMEM, VMEM],
+        [shape, shape],
+        [ANY, ANY],
+        scratch=[pltpu.SemaphoreType.DMA((2,))],
+        moved=slots * piece * unit_rows * 8,
+        name="unpick_units",
+    )
+
+
+def apply_update(gradient, master_ref, one_ref, two_ref, outs):
+    grad_out, master_out, copy_out, one_out, two_out = outs
+    weight, one, two = adamw(master_ref[0, 0], gradient, one_ref[0, 0], two_ref[0, 0], 0.02, 0.1)
+    grad_out[0, 0] = gradient
+    master_out[0, 0] = weight
+    copy_out[0, 0] = weight.astype(bf16)
+    one_out[0, 0] = one
+    two_out[0, 0] = two
+
+
+def unit_gradient(parts, piece, unit_rows):
+    return jnp.transpose(parts.astype(f32).reshape(-1, unit_rows), (1, 0))
+
+
+def update_kernel(count_ref, grad_ref, master_ref, one_ref, two_ref, *refs, first):
+    filled = pl.program_id(0) + first < count_ref[0]
+    piece, unit_rows = grad_ref.shape[2:]
+    gradient = jnp.where(filled, unit_gradient(grad_ref[:, 0], piece, unit_rows), 0.0)
+    apply_update(gradient, master_ref, one_ref, two_ref, refs[-5:])
+
+
+def update_outs(master):
+    whole = shaped(master.shape, f32)
+    return [whole, whole, shaped(master.shape), whole, whole]
+
+
+def update_units(count, grads, first, master, moment_one, moment_two, done):
+    _, _, unit_rows, unit_cols = master.shape
+    parts, slots, piece, _ = grads.shape
+    unit = blocks((1, 1, unit_rows, unit_cols), lambda s, *refs: (s + first, 0, 0, 0))
+    return call(
+        functools.partial(update_kernel, first=first),
+        [grads, master, moment_one, moment_two, *done],
+        [blocks((parts, 1, piece, unit_rows), lambda s, *refs: (0, s, 0, 0)), unit, unit, unit]
+        + [ANY] * len(done),
+        update_outs(master),
+        [unit] * 5,
+        grid=(slots,),
+        prefetch=[count],
+        aliases={5 + k: k for k in range(len(done))},
+        moved=master.size * 16,
+        name="update_units",
+    )
+
+
+def update_attn_kernel(
+    slot_ref, block_ref, half_ref, count_ref, qkv_ref, out_ref, grad_ref, master_ref, one_ref,
+    two_ref, *refs, qkv_blocks,
+):
+    entry = pl.program_id(0)
+    parts, _, piece, unit_rows = grad_ref.shape
+
+    @pl.when((entry == 0) | (entry < count_ref[0]))
+    def _():
+        from_qkv = block_ref[entry] < qkv_blocks
+        turn = count_ref[2]
+        taken = []
+        for j in range(parts):
+            place = jnp.bitwise_xor(turn, j)
+            taken.append(
+                jnp.where(
+                    from_qkv,
+                    qkv_ref[pl.ds(place, 1), 0].astype(f32),
+                    out_ref[pl.ds(place, 1), 0].astype(f32),
+                )
+            )
+        attn = jnp.concatenate(taken, axis=0)
+        gradient = jnp.where(count_ref[0] > 0, attn, grad_ref[:, 0].astype(f32))
+        gradient = unit_gradient(gradient, piece, unit_rows)
+        gradient = jnp.where(slot_ref[entry] < count_ref[1], gradient, 0.0)
+        apply_update(gradient, master_ref, one_ref, two_ref, refs[-5:])
+
+
+def update_attn(
+    slots, places, halves, count, qkv, out, grads, master, moment_one, moment_two, done
+):
+    _, _, unit_rows, unit_cols = master.shape
+    parts, _, piece, _ = grads.shape
+    qkv_blocks, out_blocks = qkv.shape[1], out.shape[1]
+    unit = blocks((1, 1, unit_rows, unit_cols), lambda k, slot, *refs: (slot[k], 0, 0, 0))
+    piece_of = (parts, 1, piece, unit_rows)
+    return call(
+        functools.partial(update_attn_kernel, qkv_blocks=qkv_blocks),
+        [qkv, out, grads, master, moment_one, moment_two, *done],
+        [
+            blocks(
+                piece_of,
+                lambda k, slot, block, half, count: (
+                    0, jnp.minimum(block[k], qkv_blocks - 1), 0, half[k]
+                ),
+            ),
+            blocks(
+                piece_of,
+                lambda k, slot, block, half, count: (
+                    0, jnp.clip(block[k] - qkv_blocks, 0, out_blocks - 1), 0, half[k]
+                ),
+            ),
+            blocks(
+                piece_of, lambda k, slot, *refs: (0, jnp.minimum(slot[k], grads.shape[1] - 1), 0, 0)
+            ),
+            unit,
+            unit,
+            unit,
+        ]
+        + [ANY] * 5,
+        update_outs(master),
+        [unit] * 5,
+        grid=(slots.shape[0],),
+        prefetch=[slots, places, halves, count],
+        aliases={10 + k: k for k in range(5)},
+        moved=master.size * 6,
+        name="update_attn",
+    )
+
+
+def lane_index(shape):
+    return lax.broadcasted_iota(jnp.int32, shape, 1)
+
+
+def rope(tile, cos_tile, sin_tile):
+    lower = lane_index(tile.shape) % HD < HD // 2
+    ahead = pltpu.roll(tile, LANES - HD // 2, 1)
+    behind = pltpu.roll(tile, HD // 2, 1)
+    return tile * cos_tile + jnp.where(lower, -ahead, behind) * sin_tile
+
+
+def unrope(tile, cos_tile, sin_tile):
+    lower = lane_index(tile.shape) % HD < HD // 2
+    weighted = tile * sin_tile
+    ahead = pltpu.roll(weighted, LANES - HD // 2, 1)
+    behind = pltpu.roll(weighted, HD // 2, 1)
+    return tile * cos_tile + jnp.where(lower, ahead, -behind)
+
+
+def project_kernel(rows_ref, w_ref, cos_ref, sin_ref, out_ref, *, group_width):
+    product = dot(rows_ref[...], w_ref[...], 1, 1)
+    for start in range(0, out_ref.shape[1], LANES):
+        tile = product[:, start : start + LANES]
+        turned = rope(tile, cos_ref[...], sin_ref[...])
+        if (start + LANES) % group_width == 0:
+            tile = jnp.where(lane_index(tile.shape) < HD, turned, tile).astype(bf16)
+        else:
+            tile = turned.astype(bf16) * HD ** (-0.5)
+        out_ref[:, start : start + LANES] = tile
+
+
+def project(rows, w_qkv, cos_all, sin_all, group_width, step, deps):
+    count = rows.shape[0]
+    width = w_qkv.shape[0]
+    return call(
+        functools.partial(project_kernel, group_width=group_width),
+        [rows, w_qkv, cos_all, sin_all],
+        [
+            blocks((step, D), lambda i: (i, 0)),
+            blocks((width, D), lambda i: (0, 0)),
+            blocks((step, LANES), lambda i: (i, 0)),
+            blocks((step, LANES), lambda i: (i, 0)),
+        ],
+        shaped((count, width)),
+        blocks((step, width), lambda i: (i, 0)),
+        grid=(count // step,),
+        deps=deps,
+        flops=2 * count * width * D,
+        name="project",
+    )
+
+
+def extend(tile, kx, vx):
+    tile = tile.astype(f32)
+    other = pltpu.roll(tile, HD, 1)
+    low = lane_index(tile.shape) < HD
+    kx[0] = jnp.where(low, tile, 0.0).astype(bf16)
+    kx[1] = jnp.where(low, 0.0, other).astype(bf16)
+    vx[0] = jnp.where(low, other, 0.0).astype(bf16)
+    vx[1] = jnp.where(low, 0.0, tile).astype(bf16)
+
+
+def forward_kernel(length_ref, qkv_ref, out_ref, log_ref, kx, vx, *, block):
+    length = length_ref[0]
+    seq_len, group_width = qkv_ref.shape
+    pairs = group_width // LANES - 1
+    extend(qkv_ref[:, pairs * LANES :], kx, vx)
+    row = lax.broadcasted_iota(jnp.int32, (block, block), 0)
+    col = lax.broadcasted_iota(jnp.int32, (block, block), 1)
+    causal = col <= row
+    key_row = lax.broadcasted_iota(jnp.int32, (1, seq_len), 1)
+    bias = jnp.where(key_row < length, 0.0, -1e30).astype(f32)
+    low = lane_index((block, LANES)) < HD
+    for pair in range(pairs):
+        lanes = slice(pair * LANES, (pair + 1) * LANES)
+        for start in range(0, seq_len, block):
+            query = qkv_ref[start : start + block, lanes]
+            total = None
+            logs = []
+            for half in range(2):
+                diagonal = dot(query, kx[half, start : start + block, :], 1, 1)
+                diagonal = jnp.where(causal, diagonal + bias[:, start : start + block], -1e30)
+                peak = jnp.max(diagonal, axis=1, keepdims=True)
+                if start:
+                    before = dot(query, kx[half, :start, :], 1, 1) + bias[:, :start]
+                    peak = jnp.maximum(peak, jnp.max(before, axis=1, keepdims=True))
+                    before = jnp.exp(before - peak)
+                diagonal = jnp.exp(diagonal - peak)
+                row_sum = jnp.sum(diagonal, axis=1, keepdims=True)
+                part = dot(diagonal.astype(bf16), vx[half, start : start + block, :], 1, 0)
+                if start:
+                    row_sum = row_sum + jnp.sum(before, axis=1, keepdims=True)
+                    part = part + dot(before.astype(bf16), vx[half, :start, :], 1, 0)
+                part = part / row_sum
+                total = part if total is None else total + part
+                logs.append(peak + jnp.log(row_sum))
+            out_ref[start : start + block, lanes] = total.astype(bf16)
+            tile = jnp.transpose(jnp.where(low, logs[0], logs[1]), (1, 0))
+            log_ref[0, 2 * pair : 2 * pair + 1, start : start + block] = tile[0:1]
+            log_ref[0, 2 * pair + 1 : 2 * pair + 2, start : start + block] = tile[HD : HD + 1]
+
+
+def attend_forward(length, qkv, groups, block, deps=(), **beside):
+    seq_len, width = qkv.shape
+    group_width = width // groups
+    query_width = group_width - LANES
+    return call(
+        functools.partial(forward_kernel, block=block),
+        [length, qkv],
+        [SMEM, blocks((seq_len, group_width), lambda g: (0, g))],
+        [shaped((seq_len, groups * query_width)), shaped((groups, 8, seq_len), f32)],
+        [
+            blocks((seq_len, query_width), lambda g: (0, g)),
+            blocks((1, 8, seq_len), lambda g: (g, 0, 0)),
+        ],
+        grid=(groups,),
+        scratch=[pltpu.VMEM((2, seq_len, LANES), bf16), pltpu.VMEM((2, seq_len, LANES), bf16)],
+        deps=deps,
+        mib=48,
+        flops=groups * seq_len * seq_len * 2048,
+        **beside,
+        name="attend_forward",
+    )
+
+
+def backward_kernel(
+    length_ref, qkv_ref, back_ref, out_ref, log_ref, cos_ref, sin_ref, *refs, block
+):
+    grad_ref, kx, vx, dk, dv = refs
+    length = length_ref[0]
+    seq_len, group_width = qkv_ref.shape
+    pairs = group_width // LANES - 1
+    extend(qkv_ref[:, pairs * LANES :], kx, vx)
+    dk[...] = jnp.zeros(dk.shape, f32)
+    dv[...] = jnp.zeros(dv.shape, f32)
+    key = lax.broadcasted_iota(jnp.int32, (block, block), 0)
+    row = lax.broadcasted_iota(jnp.int32, (block, block), 1)
+    causal = key <= row
+    for pair in range(pairs):
+        lanes = slice(pair * LANES, (pair + 1) * LANES)
+        for start in range(0, seq_len, block):
+            here = slice(start, start + block)
+            query = qkv_ref[here, lanes]
+            back = back_ref[here, lanes]
+            turned = jnp.transpose(back.astype(f32) * out_ref[here, lanes].astype(f32), (1, 0))
+            query_grad = None
+            for half in range(2):
+                log_row = log_ref[0, 2 * pair + half : 2 * pair + half + 1, here]
+                shift = jnp.sum(turned[half * HD : half * HD + HD], axis=0, keepdims=True)
+                for first in range(0, start + block, block):
+                    keys = slice(first, first + block)
+                    scores = dot(kx[half, keys, :], query, 1, 1)
+                    probs = jnp.exp(scores - log_row)
+                    if first + block > seq_len // 2:
+                        probs = jnp.where(key + first < length, probs, 0.0)
+                    if first == start:
+                        probs = jnp.where(causal, probs, 0.0)
+                    probs_back = dot(vx[half, keys, :], back, 1, 1)
+                    scores_back = (probs * (probs_back - shift)).astype(bf16)
+                    dv[half, keys, :] += dot(probs.astype(bf16), back, 1, 0)
+                    dk[half, keys, :] += dot(scores_back, query, 1, 0)
+                    part = dot(scores_back, kx[half, keys, :], 0, 0)
+                    query_grad = part if query_grad is None else query_grad + part
+            query_grad = unrope(query_grad * HD ** (-0.5), cos_ref[here, :], sin_ref[here, :])
+            grad_ref[here, lanes] = query_grad.astype(bf16)
+
+    low = lane_index((seq_len, LANES)) < HD
+    key_grad = jnp.where(low, dk[0] + pltpu.roll(dk[1], HD, 1), 0.0)
+    key_grad = unrope(key_grad, cos_ref[...], sin_ref[...])
+    value_grad = pltpu.roll(dv[0], HD, 1) + dv[1]
+    grad_ref[:, pairs * LANES :] = jnp.where(low, key_grad, value_grad).astype(bf16)
+
+
+def attend_backward(group, groups, length, qkv, back, out, logs, cos_all, sin_all, block, deps=(), **beside):
+    seq_len, width = qkv.shape
+    group_width = width // groups
+    query_width = group_width - LANES
+    given = blocks((seq_len, query_width), lambda i: (0, group))
+    table = blocks((seq_len, LANES), lambda i: (0, 0))
+    return call(
+        functools.partial(backward_kernel, block=block),
+        [length, qkv, back, out, logs, cos_all, sin_all],
+        [
+            SMEM,
+            blocks((seq_len, group_width), lambda i: (0, group)),
+            given,
+            given,
+            blocks((1, 8, seq_len), lambda i: (group, 0, 0)),
+            table,
+            table,
+        ],
+        shaped((seq_len, group_width)),
+        blocks((seq_len, group_width), lambda i: (0, 0)),
+        grid=(1,),
+        scratch=[
+            pltpu.VMEM((2, seq_len, LANES), bf16),
+            pltpu.VMEM((2, seq_len, LANES), bf16),
+            pltpu.VMEM((2, seq_len, LANES), f32),
+            pltpu.VMEM((2, seq_len, LANES), f32),
+        ],
+        deps=deps,
+        mib=48,
+        flops=seq_len * seq_len * 5120,
+        **beside,
+        name="attend_backward",
+    )
+
+
+def branch_kernel(
+    attended_ref, others_ref, w_ref, tokens_ref, gain_ref, residual_ref, normed_ref
+):
+    parts = others_ref.shape[0] + 1
+    step, width = others_ref.shape[1:]
+    here = lax.axis_index("narrow")
+    first = here * (attended_ref.shape[0] // parts) + pl.program_id(0) * step
+    total = tokens_ref[...].astype(f32)
+    for k in range(parts):
+        part = (
+            others_ref[k - 1]
+            if k
+            else attended_ref[pl.ds(pl.multiple_of(first, step), step), :]
+        )
+        place = lax.rem(here - k + parts, parts) * width
+        total = total + dot(part, w_ref[pl.ds(pl.multiple_of(place, width), width), :], 1, 0)
+    residual_ref[...] = total
+    normed_ref[...] = rmsnorm(total, gain_ref[...]).astype(bf16)
+
+
+def branch(attended, others, w_out, tokens, gain, **beside):
+    groups, count, width = others.shape
+    step = 128
+    rows = blocks((step, D), lambda i: (i, 0))
+    return call(
+        branch_kernel,
+        [attended, others, w_out, tokens, gain],
+        [
+            blocks(attended.shape, lambda i: (0, 0)),
+            blocks((groups, step, width), lambda i: (0, i, 0)),
+            blocks((D, D), lambda i: (0, 0)),
+            rows,
+            blocks((1, D), lambda i: (0, 0)),
+        ],
+        [shaped((count, D), f32), shaped((count, D))],
+        [rows, rows],
+        grid=(count // step,),
+        flops=2 * count * D * D,
+        name="branch",
+        **beside,
+    )
+
+
+def spread_kernel(turn_ref, back_ref, w_ref, out_ref):
+    out_ref[0] = dot(back_ref[...], w_ref[...], 1, 1).astype(bf16)
+
+
+def spread(turn, back, w_out, groups, deps=()):
+    count = back.shape[0]
+    width = D // groups
+    return call(
+        spread_kernel,
+        [back, w_out],
+        [
+            blocks((count, D), lambda i, t: (0, 0)),
+            blocks((width, D), lambda i, t: (lax.rem(t[1] + i, groups), 0)),
+        ],
+        shaped((groups, count, width)),
+        blocks((1, count, width), lambda i, t: (i, 0, 0)),
+        grid=(groups,),
+        prefetch=[turn],
+        deps=deps,
+        flops=2 * count * D * D,
+        name="spread",
+    )
+
+
+def first_back_kernel(*refs):
+    groups = (len(refs) - 1) // 2
+    total = sum(dot(refs[g][...], refs[groups + g][...], 1, 0) for g in range(groups))
+    refs[-1][...] = total.astype(bf16)
+
+
+def first_back(qkv_back, w_qkv, step, deps=()):
+    groups = len(qkv_back)
+    seq_len, width = qkv_back[0].shape
+    return call(
+        first_back_kernel,
+        [*qkv_back, *([w_qkv] * groups)],
+        [blocks((step, width), lambda i: (i, 0))] * groups
+        + [blocks((width, D), lambda i, g=g: (g, 0)) for g in range(groups)],
+        shaped((seq_len, D)),
+        blocks((step, D), lambda i: (i, 0)),
+        grid=(seq_len // step,),
+        deps=deps,
+        flops=2 * seq_len * width * groups * D,
+        name="first_back",
+    )
+
+
+def stream(entry_refs, layout, low, high, buffer, sems, use):
+    def copies(i):
+        found = []
+        for part, (ref, start, end, offset) in enumerate(layout[i]):
+            first, last = max(start, low), min(end, high)
+            if first < last:
+                found.append(
+                    pltpu.make_async_copy(
+                        entry_refs[ref].at[pl.ds(first - start + offset, last - first)],
+                        buffer.at[i % 2, pl.ds(first - low, last - first)],
+                        sems.at[i % 2, part],
+                    )
+                )
+        return found
+
+    for copy in copies(0):
+        copy.start()
+    for i in range(len(layout)):
+        if i + 1 < len(layout):
+            for copy in copies(i + 1):
+                copy.start()
+        for copy in copies(i):
+            copy.wait()
+        use(i, buffer.at[i % 2])
+
+
+def stream_scratch(rows):
+    return [pltpu.VMEM((2, rows, D), bf16), pltpu.SemaphoreType.DMA((2, 3))]
+
+
+def entry_layout(entries):
+    arrays, layout = [], []
+    for entry in entries:
+        start, parts = 0, []
+        for array, offset, count in entry:
+            known = [k for k, other in enumerate(arrays) if other is array]
+            if not known:
+                known = [len(arrays)]
+                arrays.append(array)
+            parts.append((known[0], start, start + count, offset))
+            start += count
+        layout.append(parts)
+    return arrays, layout, start // 3
+
+
+def ff_kernel(rows_ref, back_all_ref, *refs, layout, size, s, parts):
+    hid_ref, dgate_ref, dup_ref, keep_ref, keep_back_ref, _, total, buffer, sems = refs[-12:-3]
+    back_ref, sem = refs[-3], refs[-1]
+    count = rows_ref.shape[0]
+    place = lax.rem(lax.axis_index("narrow") - s + parts, parts) * count
+    copy = pltpu.make_async_copy(
+        back_all_ref.at[pl.ds(pl.multiple_of(place, count), count)], back_ref, sem
+    )
+    copy.start()
+    keep_ref[...] = rows_ref[...]
+    copy.wait()
+    keep_back_ref[...] = back_ref[...]
+
+    def use(i, weights):
+        gate = dot(rows_ref[...], weights[:size], 1, 1)
+        up = dot(rows_ref[...], weights[size : 2 * size], 1, 1)
+        hidden_back = dot(back_ref[...], weights[2 * size :], 1, 1)
+        sig = 1.0 / (1.0 + jnp.exp(-gate))
+        silu = gate * sig
+        here = slice(i * size, (i + 1) * size)
+        hid_ref[:, here] = (silu * up).astype(bf16)
+        dgate = (hidden_back * up * (sig * (1.0 + gate * (1.0 - sig)))).astype(bf16)
+        dup = (hidden_back * silu).astype(bf16)
+        dgate_ref[:, here] = dgate
+        dup_ref[:, here] = dup
+        part = dot(dgate, weights[:size], 1, 0) + dot(dup, weights[size : 2 * size], 1, 0)
+        if i:
+            part = part + total[...]
+        total[...] = part
+
+    stream(refs, layout, 0, 3 * size, buffer, sems, use)
+
+
+def ff_close(lands, refs, *, added):
+    out_ref, total, _, _, _, arrived, sem = refs[-7:]
+    value = total[...]
+    if added:
+        copy = pltpu.make_async_copy(lands[0], arrived, sem)
+        copy.start()
+        copy.wait()
+        value = value + arrived[...].astype(f32)
+    out_ref[...] = value.astype(out_ref.dtype)
+
+
+def ff_step(s, rows, back_all, entries, kept, moving, before=None, last=False):
+    count = rows.shape[0]
+    seq_len = back_all.shape[0]
+    arrays, layout, size = entry_layout(entries)
+    ff_width = size * len(entries)
+    wide_rows = shaped((seq_len, ff_width))
+    given = blocks((count, ff_width), lambda i: (s, 0))
+    here = blocks((count, D), lambda i: (s, 0))
+    whole = blocks((count, D), lambda i: (0, 0))
+    order = sorted(range(1, seq_len // count)) + [0]
+    first = order[0] == s
+    return call(
+        functools.partial(
+            ff_kernel, layout=layout, size=size, s=s, parts=seq_len // count
+        ),
+        [rows, back_all, *arrays, *kept],
+        [whole, ANY] + [ANY] * (len(arrays) + len(kept)),
+        [wide_rows] * 3
+        + [shaped((seq_len, D))] * 2
+        + [shaped((count, D), f32 if last else bf16)],
+        [given] * 3 + [here, here, whole],
+        grid=(1,),
+        scratch=[pltpu.VMEM((count, D), f32)]
+        + stream_scratch(3 * size)
+        + [pltpu.VMEM((count, D), bf16)] * 2
+        + [pltpu.SemaphoreType.DMA],
+        aliases={2 + len(arrays) + k: k for k in range(len(kept))},
+        mib=56,
+        flops=10 * count * ff_width * D,
+        name="ff_step",
+        sends=[Send(0, 0, "narrow", 1)],
+        sources=[moving],
+        lands=[moving.shape],
+        closing=functools.partial(ff_close, added=not first),
+    )
+
+
+def down_kernel(hid_ref, *refs, layout, size):
+    out_ref, weights, sems = refs[-3:]
+
+    @pl.when(pl.program_id(0) == 0)
+    def _():
+        copies = []
+        for i, parts in enumerate(layout):
+            for ref, start, end, offset in parts:
+                begin = max(start, 2 * size)
+                if begin < end:
+                    copies.append(
+                        pltpu.make_async_copy(
+                            refs[ref].at[pl.ds(begin - start + offset, end - begin)],
+                            weights.at[pl.ds(i * size + begin - 2 * size, end - begin)],
+                            sems.at[len(copies)],
+                        )
+                    )
+        for copy in copies:
+            copy.start()
+        for copy in copies:
+            copy.wait()
+
+    out_ref[...] = dot(hid_ref[...], weights[...], 1, 0).astype(bf16)
+
+
+def down_pass(hidden, entries, count, deps=(), **beside):
+    arrays, layout, size = entry_layout(entries)
+    seq_len, ff_width = hidden.shape
+    parts = seq_len // count
+    return call(
+        functools.partial(down_kernel, layout=layout, size=size),
+        [hidden, *arrays],
+        [blocks((count, ff_width), lambda i: (i, 0))] + [ANY] * len(arrays),
+        shaped((seq_len, D)),
+        blocks(
+            (count, D), lambda i: (lax.rem(lax.axis_index("narrow") - i + parts, parts), 0)
+        ),
+        grid=(parts,),
+        scratch=[
+            pltpu.VMEM((ff_width, D), bf16),
+            pltpu.SemaphoreType.DMA((2 * len(entries),)),
+        ],
+        deps=deps,
+        flops=2 * seq_len * ff_width * D,
+        name="down_pass",
+        **beside,
+    )
+
+
+def add_kernel(*refs):
+    refs[-1][...] = sum(ref[...].astype(f32) for ref in refs[:-1]).astype(refs[-1].dtype)
+
+
+def add(terms, kind=bf16, deps=()):
+    count, width = terms[0].shape
+    step = 128 if count % 128 == 0 else 64 if count % 64 == 0 else count
+    given = blocks((step, width), lambda i: (i, 0))
+    return call(
+        add_kernel,
+        terms,
+        [given] * len(terms),
+        shaped((count, width), kind),
+        given,
+        grid=(count // step,),
+        deps=deps,
+        moved=count * width * 8,
+        name="add",
+    )
+
+
+def outer_kernel(first_ref, second_ref, *outs):
+    first = first_ref[...]
+    if len(first.shape) == 3:
+        first = first[0]
+    product = dot(first, second_ref[...], 0, 0).astype(bf16)
+    each = pl.num_programs(0) // len(outs)
+    for k, out_ref in enumerate(outs):
+
+        @pl.when(pl.program_id(0) // each == k)
+        def _(out_ref=out_ref):
+            out_ref[...] = product
+
+
+def outer(first, second, split=1, deps=(), **beside):
+    rows, width = second.shape
+    if len(first.shape) == 3:
+        groups, _, step = first.shape
+        height = groups * step
+        taken = blocks((1, rows, step), lambda i: (i, 0, 0))
+    else:
+        height = first.shape[1]
+        step = next(k for k in (512, 384, 256, 192, LANES) if height % (k * split) == 0)
+        taken = blocks((rows, step), lambda i: (0, i))
+    each = height // step // split
+    return call(
+        outer_kernel,
+        [first, second],
+        [taken, blocks((rows, width), lambda i: (0, 0))],
+        [shaped((height // split, width))] * split,
+        [
+            blocks((step, width), lambda i, k=k: (jnp.clip(i - k * each, 0, each - 1), 0))
+            for k in range(split)
+        ],
+        grid=(height // step,),
+        deps=deps,
+        mib=56,
+        flops=2 * rows * height * width,
+        **beside,
+        name="outer",
+    )
+
+
+def pass_kernel(*refs):
+    pass
+
+
+def after(value, *deps):
+    return call(
+        pass_kernel, [value], [ANY], shaped(value.shape, value.dtype), ANY, deps=deps,
+        aliases={0: 0}, name="after",
+    )
+
+
+def shift(count, step=1):
+    return [(i, (i + step) % count) for i in range(count)]
+
+
+def butterfly(value):
+    for axis in ("wide", "narrow"):
+        count = lax.axis_size(axis)
+        step = 1
+        while step < count:
+            value = value + lax.ppermute(value, axis, [(i, i ^ step) for i in range(count)])
+            step *= 2
+    return value
+
+
+def nothing(*refs):
+    pass
+
+
+def sum_places_kernel(place_ref, own_ref, others_ref, out_ref):
+    total = jnp.zeros(own_ref.shape, f32)
+    for k in range(others_ref.shape[0]):
+        total = total + jnp.where(place_ref[0] == k, own_ref[...], others_ref[k])
+    out_ref[...] = total
+
+
+def sum_places(place, own, others):
+    return call(
+        sum_places_kernel,
+        [place, own, others],
+        [SMEM, VMEM, VMEM],
+        shaped(own.shape, f32),
+        VMEM,
+        name="sum_places",
+    )
+
+
+def move(sends, sources, lands, deps=()):
+    return call(
+        nothing, [], [], [], [], sends=sends, sources=sources, lands=lands, deps=deps, name="move"
+    )
+
+
+def rows_at(first, count):
+    return lambda wide, narrow: pl.ds(first, count)
+
+
+def exchange_units(turned):
+    return move(
+        [
+            Send(
+                0, 0, "wide", e,
+                lambda wide, narrow, e=e: jnp.bitwise_xor(wide, e),
+                lambda wide, narrow: wide,
+            )
+            for e in range(1, turned.shape[0])
+        ],
+        [turned],
+        [turned.shape],
+    )[0]
+
+
+def near_and_across(source, land, at=None, needs=()):
+    return [
+        Send(source, land, "wide", 2, at, needs=needs),
+        Send(source, land + 1, "wide", 4, at, needs=needs),
+    ]
+
+
+def sum_entries_kernel(first_ref, second_ref, *outs):
+    total = (first_ref[0].astype(f32) + second_ref[0].astype(f32)).astype(bf16)
+    for r, out_ref in enumerate(outs):
+
+        @pl.when(pl.program_id(0) == r)
+        def _(out_ref=out_ref):
+            out_ref[...] = total
+
+
+def sum_entries(first, second):
+    count, rows, width = first.shape
+    given = blocks((1, rows, width), lambda i: (i, 0, 0))
+    return call(
+        sum_entries_kernel,
+        [first, second],
+        [given, given],
+        [shaped((rows, width))] * count,
+        [blocks((rows, width), lambda i: (0, 0))] * count,
+        grid=(count,),
+        moved=first.size * 6,
+        name="sum_entries",
+    )
+
+
+def ff_meet_kernel(own_ref, other_ref, *outs):
+    total = (own_ref[...].astype(f32) + other_ref[...].astype(f32)).astype(bf16)
+    half = total.shape[0] // 2
+    for r in range(3):
+
+        @pl.when(pl.program_id(0) == r)
+        def _(r=r):
+            outs[r][...] = total
+
+    @pl.when(pl.program_id(0) == 3)
+    def _():
+        outs[3][...] = total[:half]
+        outs[4][...] = total[half:]
+
+
+def ff_meet(own, other, deps=()):
+    height, width = own.shape
+    rows = height // 4
+    given = blocks((rows, width), lambda i: (i, 0))
+    sizes = [rows, rows, rows, rows // 2, rows // 2]
+    return call(
+        ff_meet_kernel,
+        [own, other],
+        [given, given],
+        [shaped((size, width)) for size in sizes],
+        [blocks((size, width), lambda i: (0, 0)) for size in sizes],
+        grid=(4,),
+        deps=deps,
+        moved=own.size * 6,
+        name="ff_meet",
+    )
+
+
+def ff_join_kernel(x_ref, first_ref, y_ref, second_ref, x_out, y_out):
+    half = first_ref.shape[0]
+    x_out[:half] = (x_ref[:half].astype(f32) + first_ref[...].astype(f32)).astype(bf16)
+    x_out[half:] = x_ref[half:]
+    y_out[:half] = y_ref[:half]
+    y_out[half:] = (y_ref[half:].astype(f32) + second_ref[...].astype(f32)).astype(bf16)
+
+
+def ff_join(met, first, second, deps=()):
+    shape = shaped(met[1].shape)
+    return call(
+        ff_join_kernel,
+        [met[1], first, met[2], second],
+        [VMEM] * 4,
+        [shape, shape],
+        [VMEM] * 2,
+        deps=deps,
+        moved=met[1].size * 8,
+        name="ff_join",
+    )
+
+
+def across_sends(source, land):
+    return [Send(source, land, "wide", 4), Send(source + 1, land + 1, "wide", 2)]
+
+
+def near_sends(source, land):
+    return [Send(source, land, "wide", 2), Send(source + 1, land + 1, "wide", 4)]
+
+
+def unit_row(col, query_width, kv_width, by_head, group_width):
+    start, offset = col
+    if start < query_width:
+        return start // by_head * group_width + start % by_head + offset
+    start -= query_width
+    last = start >= kv_width
+    if last:
+        start -= kv_width
+    head = (start + offset) // HD
+    return head * group_width + by_head + last * HD + (start + offset) % HD
+
+
+def assemble_qkv_kernel(
+    turn_ref, own_ref, near_ref, other_ref, out_ref, *, piece, unit_cols, sizes
+):
+    height = near_ref.shape[1]
+    for e in range(8):
+        j = jnp.bitwise_xor(turn_ref[0], e)
+        for c in range(height // piece):
+            here = slice(c * piece, (c + 1) * piece)
+            row = unit_row((c * unit_cols, j * piece), *sizes)
+            if e % 2:
+                value = other_ref[e // 2, here, :]
+            elif e:
+                value = near_ref[e // 2 - 1, here, :]
+            else:
+                value = own_ref[here, :]
+            out_ref[pl.ds(pl.multiple_of(row, piece), piece), :] = value
+
+
+def assemble_qkv(turn, rows, near, other, piece, unit_cols, sizes):
+    _, height, _ = near.shape
+    return call(
+        functools.partial(
+            assemble_qkv_kernel, piece=piece, unit_cols=unit_cols, sizes=sizes
+        ),
+        [turn, rows, near, other],
+        [SMEM, blocks((height, D), lambda i: (0, 0)), whole_block(near), whole_block(other)],
+        shaped((height * 8, D)),
+        blocks((height * 8, D), lambda i: (0, 0)),
+        grid=(1,),
+        mib=32,
+        moved=height * 8 * D * 4,
+        name="assemble_qkv",
+    )
+
+
+def whole_block(array):
+    return blocks(array.shape, lambda i: (0,) * len(array.shape))
+
+
+def arrange_qkv_kernel(turn_ref, *refs, piece, unit_cols, sizes):
+    own_ref, other_ref = refs[-2:]
+    group_width = sizes[3]
+    for j in range(unit_cols // piece):
+        e = jnp.bitwise_xor(turn_ref[0], j)
+        for core, out_ref in enumerate((own_ref, other_ref)):
+
+            @pl.when(e % 2 == core)
+            def _(j=j, e=e, out_ref=out_ref):
+                for c in range(out_ref.shape[1] // piece):
+                    row = unit_row((c * unit_cols, j * piece), *sizes)
+                    grad_ref = refs[row // group_width]
+                    first = row % group_width
+                    out_ref[e // 2, c * piece : (c + 1) * piece, :] = grad_ref[
+                        first : first + piece, :
+                    ]
+
+
+def arrange_qkv(turn, grads, piece, unit_cols, sizes):
+    count = unit_cols // piece
+    rows = sizes[3] * len(grads) // count
+    shape = shaped((count // 2, rows, D))
+    return call(
+        functools.partial(arrange_qkv_kernel, piece=piece, unit_cols=unit_cols, sizes=sizes),
+        [turn, *grads],
+        [SMEM] + [VMEM] * len(grads),
+        [shape, shape],
+        [VMEM] * 2,
+        moved=rows * count * D * 4,
+        name="arrange_qkv",
+    )
+
+
+def out_row(turn_ref, k, c, j, parts, piece, unit_cols, sign):
+    n = lax.rem(turn_ref[1] + sign * k + parts, parts)
+    return n * (D // parts) + c * unit_cols + j * piece
+
+
+def assemble_out_kernel(
+    turn_ref, rows_ref, z_ref, x_ref, y_ref, across_ref, other_ref, out_ref, *, first, piece,
+    unit_cols, parts,
+):
+    height = z_ref.shape[1]
+    for e in range(8):
+        j = jnp.bitwise_xor(turn_ref[0], e)
+        for k in range(parts):
+            for c in range(height // piece):
+                here = slice(c * piece, (c + 1) * piece)
+                row = out_row(turn_ref, k, c, j, parts, piece, unit_cols, -1)
+                if e % 2:
+                    value = other_ref[e // 2, k, here, :]
+                elif e:
+                    value = (x_ref, y_ref, across_ref)[e // 2 - 1][k, here, :]
+                elif k:
+                    value = z_ref[k - 1, here, :]
+                else:
+                    value = rows_ref[first + c * piece : first + (c + 1) * piece, :]
+                out_ref[pl.ds(pl.multiple_of(row, piece), piece), :] = value
+
+
+def assemble_out(turn, rows, first, given, piece, unit_cols, parts, deps=()):
+    height = given[0].shape[1]
+    return call(
+        functools.partial(
+            assemble_out_kernel, first=first, piece=piece, unit_cols=unit_cols, parts=parts
+        ),
+        [turn, rows, *given],
+        [SMEM, blocks((first + height, D), lambda i: (0, 0))] + [whole_block(a) for a in given],
+        shaped((D, D)),
+        blocks((D, D), lambda i: (0, 0)),
+        grid=(1,),
+        mib=52,
+        deps=deps,
+        moved=D * D * 4,
+        name="assemble_out",
+    )
+
+
+def arrange_out_kernel(grad_ref, own_ref, other_ref, *, piece, unit_cols, parts):
+    per = own_ref.shape[1] // piece // parts
+    for j in range(unit_cols // piece):
+        e = jnp.bitwise_xor(lax.axis_index("wide"), j)
+        for core, out_ref in enumerate((own_ref, other_ref)):
+
+            @pl.when(e % 2 == core)
+            def _(j=j, e=e, out_ref=out_ref):
+                for k in range(parts):
+                    for c in range(per):
+                        row = (parts - k) % parts * (grad_ref.shape[0] // parts) + c * unit_cols + j * piece
+                        first = (k * per + c) * piece
+                        out_ref[e // 2, first : first + piece, :] = grad_ref[
+                            row : row + piece, :
+                        ]
+
+
+def arrange_out(grad, piece, unit_cols, parts, **beside):
+    count = unit_cols // piece
+    shape = shaped((count // 2, D // count, D))
+    return call(
+        functools.partial(arrange_out_kernel, piece=piece, unit_cols=unit_cols, parts=parts),
+        [grad],
+        [VMEM],
+        [shape, shape],
+        [VMEM] * 2,
+        moved=D * D * 4,
+        name="arrange_out",
+        **beside,
+    )
+
+
+def local(
+    tokens, cotangent, lengths, owners, master, moment_one, moment_two, norm_gains, gain_first,
+    gain_second,
+):
+    wide_count = lax.axis_size("wide")
+    narrow_count = lax.axis_size("narrow")
+    capacity, _, unit_rows, unit_cols = master.shape
+    unit_count = owners.shape[0]
+    row_count = tokens.shape[0]
+    seq_len = row_count * narrow_count
+    row_blocks = D // unit_rows
+    col_blocks = unit_count // row_blocks
+    piece = unit_cols // wide_count
+    query_width = H // narrow_count * HD
+    kv_width = KV // narrow_count * HD
+    ff_width = FF // narrow_count
+    qkv_width = query_width + 2 * kv_width
+    groups = KV // narrow_count
+    group_width = qkv_width // groups
+    by_head = group_width - 2 * HD
+    wide_index = lax.axis_index("wide")
+    narrow_index = lax.axis_index("narrow")
+    turn = jnp.stack([wide_index, narrow_index]).astype(jnp.int32)
+    length = lax.dynamic_slice(lengths, (wide_index,), (1,))
+    block = min(256, seq_len)
+    qkv_blocks = qkv_width // unit_cols
+    out_blocks = query_width // unit_cols
+    attn_blocks = qkv_blocks + out_blocks
+    sizes = (query_width, kv_width, by_head, group_width)
+    back_by = (narrow_index - jnp.arange(narrow_count, dtype=jnp.int32)) % narrow_count
+
+    inputs = tokens.astype(f32)
+    normed = rmsnorm(inputs, norm_gains[0]).astype(bf16)
+    normed_all = lax.all_gather(normed, "narrow", axis=0, tiled=True)
+
+    slot_place, counts = positions(owners, wide_count, capacity)
+    turned = turn_units(master, wide_count, (normed,))
+    got = exchange_units(turned)
+    rows = pick_units(turn, slot_place, turned, got, row_blocks)
+    qkv_rows = qkv_blocks * piece
+    out_rows = out_blocks * piece
+    ff_first = qkv_rows + out_rows
+    ff_rows = 3 * ff_width // wide_count
+
+    qkv_at, out_at = rows_at(0, qkv_rows), rows_at(qkv_rows, out_rows)
+
+    def entry(k):
+        return lambda wide, narrow: k
+
+    near_qkv, other_qkv, narrow_out = move(
+        [Send(0, 0, "wide", 2 * r, qkv_at, entry(r - 1)) for r in (1, 2, 3)]
+        + [Send(0, 1, "wide", 1, qkv_at, entry(0))]
+        + [Send(0, 2, "narrow", k, out_at, entry(k - 1)) for k in range(1, narrow_count)]
+        + [
+            Send(0, 1, "wide", 1, entry(r - 1), entry(r), landed=True, needs=(r - 1,))
+            for r in (1, 2, 3)
+        ],
+        [rows],
+        [
+            (3, qkv_rows, D),
+            (4, qkv_rows, D),
+            (narrow_count - 1, out_rows, D),
+        ],
+    )
+    w_qkv = assemble_qkv(turn, rows, near_qkv, other_qkv, piece, unit_cols, sizes)
+
+    cos_table, sin_table = tables(seq_len, HD)
+    cos_all = jnp.concatenate([cos_table] * (LANES // HD), axis=1)
+    sin_all = jnp.concatenate([sin_table] * (LANES // HD), axis=1)
+    cotangent_then = after(cotangent, normed_all, w_qkv)
+    back_all = lax.all_gather(cotangent_then, "narrow", axis=0, tiled=True)
+    qkv = project(
+        normed_all, w_qkv, cos_all, sin_all, group_width, row_count, (cotangent_then,)
+    )
+    out_shape = (narrow_count, out_rows, D)
+
+    def first_entry(wide, narrow):
+        return 0
+
+    def later_entries(wide, narrow):
+        return pl.ds(1, narrow_count - 1)
+
+    attended, logs, out_x, out_y = attend_forward(
+        length, qkv, groups, block,
+        sends=[
+            Send(0, 0, "wide", 2, out_at, first_entry),
+            Send(0, 1, "wide", 4, out_at, first_entry),
+            Send(1, 0, "wide", 2, None, later_entries),
+            Send(1, 1, "wide", 4, None, later_entries),
+        ],
+        sources=[rows, narrow_out],
+        lands=[out_shape, out_shape],
+    )
+    out_x, out_y = out_x, out_y
+
+    half = narrow_count // 2
+    third = ff_rows // 3
+
+    def heads_of(k):
+        return lambda wide, narrow: pl.ds(
+            pl.multiple_of(lax.rem(narrow + k, narrow_count) * row_count, row_count), row_count
+        )
+
+    def part_of(k, at):
+        return lambda wide, narrow: (k, at)
+
+    low_part, high_part = pl.ds(0, half), pl.ds(half, narrow_count - half)
+    attended_others, out_across, out_other, x_first, y_first = move(
+        [Send(0, 0, "narrow", k, heads_of(k), entry(k - 1)) for k in range(1, narrow_count)]
+        + [
+            Send(2, 1, "wide", 4, lambda w, n: low_part, lambda w, n: low_part),
+            Send(3, 1, "wide", 2, lambda w, n: high_part, lambda w, n: high_part),
+            Send(1, 2, "wide", 1, out_at, lambda w, n: (0, 0)),
+            Send(4, 2, "wide", 1, None, lambda w, n: (0, pl.ds(1, narrow_count - 1))),
+            Send(2, 2, "wide", 1, None, entry(1)),
+            Send(3, 2, "wide", 1, None, entry(2)),
+            Send(1, 3, "wide", 2, rows_at(ff_first, third)),
+            Send(1, 4, "wide", 4, rows_at(ff_first, third)),
+            Send(
+                1, 2, "wide", 1, None, entry(3), landed=True,
+                needs=(narrow_count - 1, narrow_count),
+            ),
+        ],
+        [attended, rows, out_x, out_y, narrow_out],
+        [
+            (narrow_count - 1, row_count, query_width),
+            out_shape,
+            (4, *out_shape),
+            (third, D),
+            (third, D),
+        ],
+    )
+    w_out = assemble_out(
+        turn, rows, qkv_rows, [narrow_out, out_x, out_y, out_across, out_other], piece,
+        unit_cols, narrow_count,
+    )
+    sixth = third // 2
+    residual, normed_two, x_second, y_second = branch(
+        attended, attended_others, w_out, tokens, norm_gains[1:2],
+        sends=near_and_across(0, 0, rows_at(ff_first + third, sixth)),
+        sources=[rows],
+        lands=[(sixth, D), (sixth, D)],
+    )
+
+    rest = ff_rows - third - sixth
+    block_one, x_third, y_third, *swapped = move(
+        [Send(0, 0, "narrow", 1)]
+        + near_and_across(1, 1, rows_at(ff_first + third + sixth, rest))
+        + [Send(1, 3, "wide", 1, rows_at(ff_first, ff_rows))]
+        + [Send(2 + k, 4 + k, "wide", 1) for k in range(4)],
+        [normed_two, rows, x_first, x_second, y_first, y_second],
+        [normed_two.shape, (rest, D), (rest, D), (ff_rows, D)]
+        + [(third, D), (sixth, D), (third, D), (sixth, D)],
+    )
+    own_swap, x_first_swap, x_second_swap, y_first_swap, y_second_swap = swapped
+    block_two, across_first, across_second, across_third, *swapped = move(
+        [
+            Send(0, 0, "narrow", 1),
+            Send(1, 1, "wide", 4),
+            Send(2, 2, "wide", 4),
+            Send(4, 3, "wide", 2),
+            Send(3, 4, "wide", 1),
+            Send(4, 5, "wide", 1),
+            Send(1, 6, "wide", 1, landed=True, needs=(1,)),
+            Send(2, 7, "wide", 1, landed=True, needs=(2,)),
+            Send(3, 8, "wide", 1, landed=True, needs=(3,)),
+        ],
+        [block_one, x_first, x_second, x_third, y_third],
+        [block_one.shape, (third, D), (sixth, D), (rest, D), (rest, D), (rest, D)]
+        + [(third, D), (sixth, D), (rest, D)],
+    )
+    x_third_swap, y_third_swap, *across_swap = swapped
+
+    def pieces(first, second, last):
+        return [(first, 0, third), (second, 0, sixth), (last, 0, rest)]
+
+    entries = [
+        [(rows, ff_first, ff_rows)],
+        pieces(x_first, x_second, x_third),
+        pieces(y_first, y_second, y_third),
+        pieces(across_first, across_second, across_third),
+        [(own_swap, 0, ff_rows)],
+        pieces(x_first_swap, x_second_swap, x_third_swap),
+        pieces(y_first_swap, y_second_swap, y_third_swap),
+        pieces(*across_swap),
+    ]
+
+    *kept, total, block_three = ff_step(1, block_one, back_all, entries, (), block_two)
+    *kept, total, _ = ff_step(2, block_two, back_all, entries, kept, total, True)
+    *kept, total, _ = ff_step(3, block_three, back_all, entries, kept, total, True)
+    *kept, norm_two_back, _ = ff_step(0, normed_two, back_all, entries, kept, total, True, True)
+    hidden, dgate, dup, mlp_all, back_kept = kept
+
+    _, norm_two_pull = jax.vjp(rmsnorm, residual, norm_gains[1])
+    resid_part, gain_two = norm_two_pull(norm_two_back)
+    resid_back = cotangent.astype(f32) + resid_part
+    attn_back = resid_back.astype(bf16)
+    by_heads = spread(turn, attn_back, w_out, narrow_count)
+
+    def heads_send(k, land):
+        return Send(0, land, "narrow", k, entry(k))
+
+    heads_shape = (row_count, query_width)
+    attended_rows = jnp.concatenate(
+        [
+            lax.dynamic_slice(attended, (narrow_index * row_count, 0), (row_count, query_width))[
+                None
+            ],
+            attended_others,
+        ],
+        axis=0,
+    )
+    grad_out, heads_one = outer(
+        attended_rows, attn_back, 1,
+        sends=[heads_send(1, 0)], sources=[by_heads], lands=[heads_shape],
+    )
+    own_out, other_out, heads_three = arrange_out(
+        grad_out, piece, unit_cols, narrow_count,
+        sends=[heads_send(3, 0)], sources=[by_heads], lands=[heads_shape],
+    )
+    *grad_down, heads_two, out_swap = outer(
+        hidden, back_kept, 2, (own_out,),
+        sends=[heads_send(2, 0), Send(1, 1, "wide", 1)],
+        sources=[by_heads, other_out],
+        lands=[heads_shape, other_out.shape],
+    )
+    out_back = jnp.stack([by_heads[0], heads_one, heads_two, heads_three])
+    out_back = jnp.take(out_back, back_by, axis=0).reshape(seq_len, query_width)
+    met_out = sum_entries(own_out, out_swap)
+    met_shape = met_out[0].shape
+    ff_term, out_x, out_y, down_swap = down_pass(
+        hidden, entries, row_count,
+        sends=[Send(0, 0, "wide", 2), Send(1, 1, "wide", 4), Send(2, 2, "wide", 1)],
+        sources=[met_out[1], met_out[2], grad_down[1]],
+        lands=[met_shape, met_shape, grad_down[1].shape],
+    )
+    output = residual + lax.psum_scatter(
+        ff_term, "narrow", scatter_dimension=0, tiled=True
+    ).astype(f32)
+    met_down = ff_meet(grad_down[0], down_swap)
+    half_shape, near_shape = met_down[3].shape, met_down[1].shape
+    *grad_gate, down_a, down_b = outer(
+        dgate, mlp_all, 2,
+        sends=across_sends(0, 0), sources=met_down[3:], lands=[half_shape] * 2,
+    )
+    joined_down = ff_join(met_down, down_a, down_b)
+    *grad_upper, gate_swap, down_x, down_y = outer(
+        dup, mlp_all, 2, (joined_down[0],),
+        sends=[Send(0, 0, "wide", 1)] + near_sends(1, 1),
+        sources=[grad_gate[1], *joined_down],
+        lands=[grad_gate[1].shape, near_shape, near_shape],
+    )
+    met_gate = ff_meet(grad_gate[0], gate_swap)
+
+    qkv_back = [None, None]
+    qkv_back[0], upper_swap, gate_a, gate_b, out_across = attend_backward(
+        0, groups, length, qkv, out_back, attended, logs, cos_all, sin_all, block,
+        sends=[Send(0, 0, "wide", 1)] + across_sends(1, 1) + [Send(3, 3, "wide", 6)],
+        sources=[grad_upper[1], *met_gate[3:], met_out[3]],
+        lands=[grad_upper[1].shape, half_shape, half_shape, met_shape],
+    )
+    joined_gate = ff_join(met_gate, gate_a, gate_b)
+    met_upper = ff_meet(grad_upper[0], upper_swap)
+    out_sum = add([met_out[0], out_x, out_y, out_across])
+    qkv_back[1], upper_a, upper_b, gate_x, gate_y = attend_backward(
+        1, groups, length, qkv, out_back, attended, logs, cos_all, sin_all, block,
+        sends=across_sends(0, 0) + near_sends(2, 2),
+        sources=[*met_upper[3:], *joined_gate],
+        lands=[half_shape] * 2 + [near_shape] * 2,
+        deps=(out_sum,),
+    )
+    joined_upper = ff_join(met_upper, upper_a, upper_b)
+    norm_one_term = first_back(qkv_back, w_qkv, row_count, (joined_upper[0],))
+    first_qkv, upper_x, upper_y = outer(
+        qkv_back[0], normed_all, 1, (norm_one_term,),
+        sends=near_sends(0, 0), sources=list(joined_upper), lands=[near_shape] * 2,
+    )
+    ff_sums = [
+        add([met_gate[0], gate_x, gate_y]),
+        add([met_upper[0], upper_x, upper_y]),
+        add([met_down[0], down_x, down_y]),
+    ]
+
+    slots = wide_count * capacity
+    unit_of = jnp.zeros((slots,), jnp.int32).at[slot_place].set(
+        jnp.arange(unit_count, dtype=jnp.int32)
+    )
+    half_of = unit_of // col_blocks
+    block_of = unit_of - half_of * col_blocks
+    sent = unpick_units(
+        jnp.concatenate(ff_sums, axis=0),
+        jnp.maximum(block_of - attn_blocks, 0),
+        half_of,
+        wide_count,
+        piece,
+        unit_rows,
+    )
+    owned = [lax.all_to_all(part, "wide", split_axis=0, concat_axis=0) for part in sent]
+    count = lax.dynamic_slice(counts, (wide_index,), (1,))
+
+    (second_qkv,) = outer(qkv_back[1], normed_all, 1, tuple(sent))
+    grad_qkv = [first_qkv, second_qkv]
+    gain_one = sum(
+        jnp.sum(
+            w_qkv[g * group_width : (g + 1) * group_width].astype(f32) * grad_qkv[g].astype(f32),
+            axis=0,
+        )
+        for g in range(groups)
+    )
+    gain_terms = jnp.stack([gain_one / norm_gains[0], gain_two])
+    own_qkv, other_qkv = arrange_qkv(turn, grad_qkv, piece, unit_cols, sizes)
+
+    def by_wide(wide, narrow):
+        return wide
+
+    def by_narrow(wide, narrow):
+        return narrow
+
+    qkv_swap, gain_others, *out_parts = move(
+        [Send(0, 0, "wide", 1)]
+        + [Send(1, 1, "wide", e, None, by_wide) for e in range(1, wide_count)]
+        + [
+            Send(2, k + 1, "narrow", k, rows_at(k * out_rows, out_rows))
+            for k in range(1, narrow_count)
+        ],
+        [other_qkv, gain_terms, out_sum],
+        [other_qkv.shape, ((wide_count, *gain_terms.shape), f32)]
+        + [(out_rows, D)] * (narrow_count - 1),
+    )
+    met_qkv = sum_entries(own_qkv, qkv_swap)
+    gain_plane = sum_places(wide_index.reshape(1), gain_terms, gain_others)
+    out_sum = add([out_sum[:out_rows]] + list(out_parts))
+    *arrived, gain_others = move(
+        [Send(r - 1, r - 1, "wide", 2 * r) for r in (1, 2, 3)]
+        + [Send(3, 3, "narrow", k, None, by_narrow) for k in range(1, narrow_count)],
+        [*met_qkv[1:], gain_plane],
+        [met_qkv[0].shape] * 3 + [((narrow_count, *gain_terms.shape), f32)],
+    )
+    gain_grads = sum_places(narrow_index.reshape(1), gain_plane, gain_others)
+    qkv_sum = add([met_qkv[0]] + list(arrived))
+    near_qkv, near_out, other_qkv, other_out = move(
+        [Send(0, 0, "wide", 2 * r, None, entry(r)) for r in (1, 2, 3)]
+        + [Send(1, 1, "wide", 2 * r, None, entry(r)) for r in (1, 2, 3)]
+        + [
+            Send(0, 2, "wide", 1, None, entry(0)),
+            Send(1, 3, "wide", 1, None, entry(0)),
+        ]
+        + [
+            Send(0, 2, "wide", 1, entry(r), entry(r), landed=True, needs=(r - 1,))
+            for r in (1, 2, 3)
+        ]
+        + [
+            Send(1, 3, "wide", 1, entry(r), entry(r), landed=True, needs=(r + 2,))
+            for r in (1, 2, 3)
+        ],
+        [qkv_sum, out_sum],
+        [(4, qkv_rows, D), (4, out_rows, D)] * 2,
+    )
+
+    def by_device(own, near, other):
+        return jnp.stack(
+            [
+                other[e // 2] if e % 2 else near[e // 2] if e else own
+                for e in range(wide_count)
+            ]
+        )
+
+    qkv_grads = by_device(qkv_sum, near_qkv, other_qkv)
+    out_grads = by_device(out_sum, near_out, other_out)
+    qkv_grads = qkv_grads.reshape(wide_count, qkv_blocks, piece, D)
+    out_grads = out_grads.reshape(wide_count, out_blocks, piece, D)
+
+    updated = ()
+    for k in range(2):
+        updated = update_units(
+            count, owned[k], k * (capacity // 2), master, moment_one, moment_two, updated
+        )
+    first_slot = wide_index * capacity
+    own_block = lax.dynamic_slice(block_of, (first_slot,), (capacity,))
+    own_half = lax.dynamic_slice(half_of, (first_slot,), (capacity,))
+    slot = jnp.arange(capacity, dtype=jnp.int32)
+    is_attn = (own_block < attn_blocks) & (slot < count[0])
+    attn_count = jnp.sum(is_attn.astype(jnp.int32))
+    rank = jnp.cumsum(is_attn.astype(jnp.int32)) - 1
+    listed = min(capacity, attn_blocks * row_blocks)
+    wanted = jnp.minimum(jnp.arange(listed, dtype=jnp.int32), jnp.maximum(attn_count - 1, 0))
+    chosen = is_attn[None, :] & (rank[None, :] == wanted[:, None])
+
+    def entries_of(values):
+        return jnp.sum(jnp.where(chosen, values[None, :], 0), axis=1)
+
+    owned_grads, new_master, new_copy, new_first, new_second = update_attn(
+        entries_of(slot), entries_of(own_block), entries_of(own_half),
+        jnp.stack([attn_count, count[0], wide_index]).astype(jnp.int32),
+        qkv_grads, out_grads, owned[0], master, moment_one, moment_two, updated,
+    )
+
+    norm_one_back = lax.psum_scatter(
+        norm_one_term, "narrow", scatter_dimension=0, tiled=True
+    ).astype(f32)
+    _, norm_one_pull = jax.vjp(lambda values: rmsnorm(values, norm_gains[0]), inputs)
+    (input_part,) = norm_one_pull(norm_one_back)
+    input_grad = (resid_back + input_part).astype(bf16)
+    new_gains, _, gain_second_new = adamw(
+        norm_gains, gain_grads, gain_first, gain_second, 0.5, 0.0
+    )
+    return (
+        output.astype(bf16),
+        input_grad,
+        owned_grads,
+        new_master,
+        new_copy,
+        new_first,
+        new_second,
+        gain_grads,
+        gain_second_new,
+        new_gains,
+    )
+
+
+def rotate(values, cos_table, sin_table):
+    middle = values.shape[-1] // 2
+    turned = jnp.concatenate([-values[..., middle:], values[..., :middle]], axis=-1)
+    return values * cos_table + turned * sin_table
+
+
+def unrotate(gradient, cos_table, sin_table):
+    middle = gradient.shape[-1] // 2
+    weighted = gradient * sin_table
+    turned = jnp.concatenate([weighted[..., middle:], -weighted[..., :middle]], axis=-1)
+    return gradient * cos_table + turned
+
+
+def matmul_rows(first_op, second_op):
+    return lax.dot_general(
+        first_op, second_op, (((0,), (0,)), ((), ())), preferred_element_type=jnp.float32
+    )
+
+
+def matmul_cols(first_op, second_op):
+    return lax.dot_general(
+        first_op, second_op, (((1,), (1,)), ((), ())), preferred_element_type=jnp.float32
+    )
+
+
+def project_any(normed_all, w_qkv, cos_heads, sin_heads, heads_here, kv_here):
     seq_len = normed_all.shape[0]
     projected = jnp.dot(normed_all, w_qkv, preferred_element_type=jnp.float32)
     query_width = heads_here * HD
@@ -98,7 +1772,7 @@
     return jnp.where(allowed, scores, -1e30)
 
 
-def attend_forward(query_heads, key_heads, value_heads, length, block_rows):
+def attend_forward_any(query_heads, key_heads, value_heads, length, block_rows):
     seq_len = query_heads.shape[2]
     outputs = []
     log_sums = []
@@ -118,7 +1792,7 @@
     return (jnp.concatenate(outputs, axis=2), jnp.concatenate(log_sums, axis=2))
 
 
-def attend_backward(query_heads, key_heads, value_heads, out_back, log_sums, length, block_rows):
+def attend_backward_any(query_heads, key_heads, value_heads, out_back, log_sums, length, block_rows):
     seq_len = query_heads.shape[2]
     query_grads = []
     key_grad = jnp.zeros(key_heads.shape, jnp.float32)
@@ -148,7 +1822,7 @@
     return (jnp.concatenate(query_grads, axis=2), key_grad, value_grad)
 
 
-def local(
+def local_any(
     tokens,
     cotangent,
     lengths,
@@ -168,7 +1842,7 @@
     unit_count = owners.shape[0]
     row_count = tokens.shape[0]
     seq_len = row_count * narrow_count
-    slot_place = positions(owners, wide_count, capacity)
+    slot_place, _ = positions(owners, wide_count, capacity)
     own_slots = master[:, 0].astype(jnp.bfloat16)
     all_slots = lax.all_gather(own_slots, "wide", axis=0, tiled=True)
     unit_data = jnp.take(all_slots, slot_place, axis=0)
@@ -199,10 +1873,10 @@
     inputs = tokens.astype(jnp.float32)
     normed = rmsnorm(inputs, norm_gains[0]).astype(jnp.bfloat16)
     normed_all = lax.all_gather(normed, "narrow", axis=0, tiled=True)
-    query_heads, key_heads, value_heads = project(
+    query_heads, key_heads, value_heads = project_any(
         normed_all, w_qkv, cos_heads, sin_heads, heads_here, kv_here
     )
-    attended, log_sums = attend_forward(query_heads, key_heads, value_heads, length, block_rows)
+    attended, log_sums = attend_forward_any(query_heads, key_heads, value_heads, length, block_rows)
     attended = (
         jnp.transpose(attended.reshape(heads_here, seq_len, HD), (1, 0, 2))
         .reshape(seq_len, query_width)
@@ -245,7 +1919,7 @@
     resid_back = cotangent.astype(jnp.float32) + resid_part
     attn_back = lax.all_gather(resid_back.astype(jnp.bfloat16), "narrow", axis=0, tiled=True)
     normed_again = lax.all_gather(normed, "narrow", axis=0, tiled=True)
-    query_heads, key_heads, value_heads = project(
+    query_heads, key_heads, value_heads = project_any(
         normed_again, w_qkv, cos_heads, sin_heads, heads_here, kv_here
     )
     out_back = jnp.dot(attn_back, w_out_t, preferred_element_type=jnp.float32).astype(jnp.bfloat16)
@@ -253,7 +1927,7 @@
     out_back = jnp.transpose(out_back.reshape(seq_len, heads_here, HD), (1, 0, 2)).reshape(
         kv_here, group_size, seq_len, HD
     )
-    query_grad, key_grad, value_grad = attend_backward(
+    query_grad, key_grad, value_grad = attend_backward_any(
         query_heads, key_heads, value_heads, out_back, log_sums, length, block_rows
     )
     query_grad = jnp.transpose(query_grad.reshape(heads_here, seq_len, HD), (1, 0, 2))
@@ -304,33 +1978,13 @@
 
 
 def solution(mesh):
-    placed = (
-        P(("wide", "narrow"), None),
-        P(("wide", "narrow"), None),
-        P(),
-        P(),
-        P("wide", "narrow", None, None),
-        P("wide", "narrow", None, None),
-        P("wide", "narrow", None, None),
-        P(),
-        P(),
-        P(),
-    )
+    COLLECTIVE[0] = 0
+    rows = P(("wide", "narrow"), None)
+    units = P("wide", "narrow", None, None)
     return jax.shard_map(
-        local,
+        local if mesh.shape["wide"] == 8 and mesh.shape["narrow"] == 4 else local_any,
         mesh=mesh,
-        in_specs=placed,
-        out_specs=(
-            P(("wide", "narrow"), None),
-            P(("wide", "narrow"), None),
-            P("wide", "narrow", None, None),
-            P("wide", "narrow", None, None),
-            P("wide", "narrow", None, None),
-            P("wide", "narrow", None, None),
-            P("wide", "narrow", None, None),
-            P(),
-            P(),
-            P(),
-        ),
+        in_specs=(rows, rows, P(), P(), units, units, units, P(), P(), P()),
+        out_specs=(rows, rows, units, units, units, units, units, P(), P(), P()),
         check_vma=False,
     )

time: 2420 us -> 1160 us (0.48)
  waiting for transfers between devices: 1130 us -> 12 us
  Pallas kernels: 0 us -> 1030 us
  local copies, waits for them, and re-layouts: 497 us -> 46.1 us
  matrix products: 416 us -> 0 us
  other arithmetic: 301 us -> 41.1 us
  blocking collectives: 37.8 us -> 0 us
    pallas_call x0 -> x53, Pallas kernels: none -> 1030 us  [call(): pl.pallas_call(wrapped, grid_spec=pltpu.PrefetchScalarGridSpec(num_scalar...]
    all_gather x4 -> x1, waiting for transfers between devices: 555 us -> 0.02 us  [local(): back_all = lax.all_gather(cotangent_then, 'narrow', axis=0, tiled=True)]
    dot_general x30 -> x0, matrix products: 416 us -> none  [the longest x4 71.1 us: matmul_cols(): lax.dot_general(first_op, second_op, (((1,), (1,)), ((), ())), preferred_...]
    reduce_scatter x4 -> x2, waiting for transfers between devices: 321 us -> 0.04 us  [the longest x1 0.02 us: local(): lax.psum_scatter(norm_one_term, 'narrow', scatter_dimension=0, tiled=True)]
    unnamed x11 -> x4, waiting for transfers between devices: 256 us -> 0.56 us
    reshape x2 -> x0, local copies, waits for them, and re-layouts: 138 us -> none  [local(): grad_packed.reshape(row_blocks, unit_rows, col_blocks, unit_cols)]
    convert_element_type x10 -> x3, other arithmetic: 137 us -> 11.1 us  [the longest x1 5.86 us: local(): input_grad = (resid_back + input_part).astype(bf16)]
    scatter x1, local copies, waits for them, and re-layouts: 108 us -> 1.06 us  [local(): jnp.zeros((slots,), jnp.int32).at[slot_place]]
  transfers between devices with their start and end apart: 10 -> 6, of which waited for: 7 -> 1; matrix products, arithmetic and copies ran while one was open for 31% -> 3% of each run, Pallas kernels for 0% -> 50%
where the time goes in v3:
time: 1160 us
  Pallas kernels  1030 us (89%)
  local copies, waits for them, and re-layouts  46.1 us (4%)
  other arithmetic  41.1 us (4%)
  between operations  15.8 us (1%)
  waiting for transfers between devices  12 us (1%)
    pallas_call x53, Pallas kernels, call(): pl.pallas_call(wrapped, grid_spec=pltpu.PrefetchScalarGridSpec(num_scalar...  1030 us
    unnamed x151, local copies, waits for them, and re-layouts  33.5 us
  transfers between devices with their start and end apart: 6, of which 1 were waited for; matrix products, arithmetic and copies ran while one was open for 3% of the time, Pallas kernels for 50%

profile of v3, /device:TPU:0, one launch (start us, length us, event | category | flops | bytes accessed | tf_op | source)
XLA Modules:
  0.0 1155.2 jit_solution(16044498401660763020)
XLA Ops:
  27.6 78.3 %move.8.refs_3_ = bf16[8,26,16,1024]{3,2,1,0:T(8,128)(2,1)} custom-call(bf16[8,26,16,1024]{3,2,1,0:T(8,128)(2,1)} %copy-done.2), custom_call_target="tpu_custom_call" | custom-call | tf_op jit(solution)/shard_map/move/pallas_call | solution.py:164
  114.3 33.8 %move.9 = (bf16[3,96,2048]{2,1,0:T(8,128)(2,1)}, bf16[4,96,2048]{2,1,0:T(8,128)(2,1)}, bf16[3,64,2048]{2,1,0:T(8,128)(2,1)}) custom-call(bf16[928,2048]{1,0:T(8,128)(2,1)} %pick_units.1.refs_0_.refs_1_.refs_2_.refs_5_), custom_call_target="tpu_custom_call" | custom-call | tf_op jit(solution)/shard_map/move/pallas_call | solution.py:164
  171.1 27.8 %attend_forward.1 = (bf16[1536,512]{1,0:T(8,128)(2,1)S(1)}, f32[2,8,1536]{2,1,0:T(8,128)S(1)}, bf16[4,64,2048]{2,1,0:T(8,128)(2,1)S(1)}, bf16[4,64,2048]{2,1,0:T(8,128)(2,1)S(1)}) custom-call(s32[1]{0:T(128)} %dynamic_slice.15.refs_0_, bf16[1536,768]{1,0:T(8,128)(2,1)} %project.1.refs_1_, bf16[928,2048]{1,0:T(8,128)(2,1)} %pick_units.1.refs_0_.refs_1_.refs_2_.refs_5_, ...), custom_call_target="tpu_custom_call" | custom-call | flops 9663676416 | tf_op jit(solution)/shard_map/attend_forward/pallas_call | solution.py:164
  202.0 60.7 %move.10 = (bf16[3,384,512]{2,1,0:T(8,128)(2,1)}, bf16[4,64,2048]{2,1,0:T(8,128)(2,1)}, bf16[4,4,64,2048]{3,2,1,0:T(8,128)(2,1)}, bf16[256,2048]{1,0:T(8,128)(2,1)}, bf16[256,2048]{1,0:T(8,128)(2,1)}) custom-call(bf16[1536,512]{1,0:T(8,128)(2,1)} %copy-done.6, bf16[928,2048]{1,0:T(8,128)(2,1)} %pick_units.1.refs_0_.refs_1_.refs_2_.refs_5_, ...), custom_call_target="tpu_custom_call" | custom-call | tf_op jit(solution)/shard_map/move/pallas_call | solution.py:164
  269.8 18.4 %branch.1 = (f32[384,2048]{1,0:T(8,128)}, bf16[384,2048]{1,0:T(8,128)(2,1)}, bf16[128,2048]{1,0:T(8,128)(2,1)}, bf16[128,2048]{1,0:T(8,128)(2,1)}) custom-call(bf16[1536,512]{1,0:T(8,128)(2,1)} %copy-done.6, bf16[3,384,512]{2,1,0:T(8,128)(2,1)} %get-tuple-element.170.refs_1_, bf16[2048,2048]{1,0:T(8,128)(2,1)} %assemble_out.1.refs_2_, ...), custom_call_target="tpu_custom_call" | custom-call | flops 3221225472 | tf_op jit(solution)/shard_map/branch/pallas_call | solution.py:164
  288.2 65.6 %move.11 = (bf16[384,2048]{1,0:T(8,128)(2,1)}, bf16[384,2048]{1,0:T(8,128)(2,1)}, bf16[384,2048]{1,0:T(8,128)(2,1)}, bf16[768,2048]{1,0:T(8,128)(2,1)}, bf16[256...) custom-call(bf16[384,2048]{1,0:T(8,128)(2,1)} %get-tuple-element.174.refs_, ...), custom_call_target="tpu_custom_call" | custom-call | tf_op jit(solution)/shard_map/move/pallas_call | solution.py:164
  353.8 40.7 %move.12 = (bf16[384,2048]{1,0:T(8,128)(2,1)}, bf16[256,2048]{1,0:T(8,128)(2,1)}, bf16[128,2048]{1,0:T(8,128)(2,1)}, bf16[384,2048]{1,0:T(8,128)(2,1)}, bf16[384...) custom-call(bf16[384,2048]{1,0:T(8,128)(2,1)} %get-tuple-element.181, ...), custom_call_target="tpu_custom_call" | custom-call | tf_op jit(solution)/shard_map/move/pallas_call | solution.py:164
  397.3 43.9 %ff_step.4 = (bf16[1536,2048]{1,0:T(8,128)(2,1)}, bf16[1536,2048]{1,0:T(8,128)(2,1)}, bf16[1536,2048]{1,0:T(8,128)(2,1)}, bf16[1536,2048]{1,0:T(8,128)(2,1)}, bf...) custom-call(bf16[384,2048]{1,0:T(8,128)(2,1)} %get-tuple-element.181.refs_0_, ...), custom_call_target="tpu_custom_call" | custom-call | flops 16106127360 | tf_op jit(solution)/shard_map/ff_step/pallas_call | solution.py:164
  441.3 44.5 %ff_step.5 = (bf16[1536,2048]{1,0:T(8,128)(2,1)}, bf16[1536,2048]{1,0:T(8,128)(2,1)}, bf16[1536,2048]{1,0:T(8,128)(2,1)}, bf16[1536,2048]{1,0:T(8,128)(2,1)}, bf...) custom-call(bf16[384,2048]{1,0:T(8,128)(2,1)} %get-tuple-element.195, ...), custom_call_target="tpu_custom_call", output_to_operand_aliasing={{0}: (22, {}), {1}: (23, {}), {2}: (24, {}), {3}: (25, {}),... | custom-call | flops 16106127360 | tf_op jit(solution)/shard_map/ff_step/pallas_call | solution.py:164
  485.8 43.6 %ff_step.6 = (bf16[1536,2048]{1,0:T(8,128)(2,1)}, bf16[1536,2048]{1,0:T(8,128)(2,1)}, bf16[1536,2048]{1,0:T(8,128)(2,1)}, bf16[1536,2048]{1,0:T(8,128)(2,1)}, bf...) custom-call(bf16[384,2048]{1,0:T(8,128)(2,1)} %get-tuple-element.196, ...), custom_call_target="tpu_custom_call", output_to_operand_aliasing={{0}: (22, {}), {1}: (23, {}), {2}: (24, {}), {3}: (25, {}),... | custom-call | flops 16106127360 | tf_op jit(solution)/shard_map/ff_step/pallas_call | solution.py:164
  529.4 43.4 %ff_step.7 = (bf16[1536,2048]{1,0:T(8,128)(2,1)}, bf16[1536,2048]{1,0:T(8,128)(2,1)}, bf16[1536,2048]{1,0:T(8,128)(2,1)}, bf16[1536,2048]{1,0:T(8,128)(2,1)}, bf...) custom-call(bf16[384,2048]{1,0:T(8,128)(2,1)} %get-tuple-element.174, ...), custom_call_target="tpu_custom_call", output_to_operand_aliasing={{0}: (22, {}), {1}: (23, {}), {2}: (24, {}), {3}: (25, {}),... | custom-call | flops 16106127360 | tf_op jit(solution)/shard_map/ff_step/pallas_call | solution.py:164
  599.6 14.8 %arrange_out.1 = (bf16[4,256,2048]{2,1,0:T(8,128)(2,1)}, bf16[4,256,2048]{2,1,0:T(8,128)(2,1)}, bf16[384,512]{1,0:T(8,128)(2,1)}) custom-call(bf16[2048,2048]{1,0:T(8,128)(2,1)} %get-tuple-element.217.refs_0_, bf16[4,384,512]{2,1,0:T(8,128)(2,1)} %spread.1.refs_2_.refs_1_), custom_call_target="tpu_custom_call" | custom-call | bytes 16777216 | tf_op jit(solution)/shard_map/arrange_out/pallas_call | solution.py:164
  614.4 26.2 %outer.7 = (bf16[1024,2048]{1,0:T(8,128)(2,1)}, bf16[1024,2048]{1,0:T(8,128)(2,1)}, bf16[384,512]{1,0:T(8,128)(2,1)}, bf16[4,256,2048]{2,1,0:T(8,128)(2,1)}) custom-call(bf16[1536,2048]{1,0:T(8,128)(2,1)} %get-tuple-element.215.refs_0_, bf16[1536,2048]{1,0:T(8,128)(2,1)} %get-tuple-element.219.refs_1_, bf16[4,384,512]{2,1,0:T(8,128)(2,1)} %spread.1.refs_2_.refs_1_, ...), custom_call_target="tpu_custom_call" | custom-call | flops 12884901888 | tf_op jit(solution)/shard_map/outer/pallas_call | solution.py:164
  647.6 28.2 %down_pass.1 = (bf16[1536,2048]{1,0:T(8,128)(2,1)}, bf16[256,2048]{1,0:T(8,128)(2,1)}, bf16[256,2048]{1,0:T(8,128)(2,1)}, bf16[1024,2048]{1,0:T(8,128)(2,1)}) custom-call(bf16[1536,2048]{1,0:T(8,128)(2,1)} %get-tuple-element.215.refs_0_, bf16[928,2048]{1,0:T(8,128)(2,1)} %pick_units.1.refs_0_.refs_1_.refs_2_.refs_5_, ...), custom_call_target="tpu_custom_call" | custom-call | flops 12884901888 | tf_op jit(solution)/shard_map/down_pass/pallas_call | solution.py:164
  685.4 21.1 %outer.8 = (bf16[1024,2048]{1,0:T(8,128)(2,1)}, bf16[1024,2048]{1,0:T(8,128)(2,1)}, bf16[128,2048]{1,0:T(8,128)(2,1)}, bf16[128,2048]{1,0:T(8,128)(2,1)}) custom-call(bf16[1536,2048]{1,0:T(8,128)(2,1)} %get-tuple-element.232.refs_0_, bf16[1536,2048]{1,0:T(8,128)(2,1)} %get-tuple-element.231.refs_1_, bf16[128,2048]{1,0:T(8,128)(2,1)} %get-tuple-element.235.refs_2_, ...), custom_call_target="tpu_custom_call" | custom-call | flops 12884901888 | tf_op jit(solution)/shard_map/outer/pallas_call | solution.py:164
  709.9 30.4 %outer.9 = (bf16[1024,2048]{1,0:T(8,128)(2,1)}, bf16[1024,2048]{1,0:T(8,128)(2,1)}, bf16[1024,2048]{1,0:T(8,128)(2,1)}, bf16[256,2048]{1,0:T(8,128)(2,1)}, bf16[256,2048]{1,0:T(8,128)(2,1)}) custom-call(bf16[1536,2048]{1,0:T(8,128)(2,1)} %get-tuple-element.230.refs_0_, bf16[1536,2048]{1,0:T(8,128)(2,1)} %get-tuple-element.231.refs_1_, ...), custom_call_target="tpu_custom_call" | custom-call | flops 12884901888 | tf_op jit(solution)/shard_map/outer/pallas_call | solution.py:164
  749.8 40.0 %attend_backward.2 = (bf16[1536,384]{1,0:T(8,128)(2,1)}, bf16[1024,2048]{1,0:T(8,128)(2,1)}, bf16[128,2048]{1,0:T(8,128)(2,1)S(1)}, bf16[128,2048]{1,0:T(8,128)(2,1)S(1)}, bf16[256,2048]{1,0:T(8,128)(2,1)S(1)}) custom-call(s32[1]{0:T(128)} %dynamic_slice.15.refs_0_, bf16[1536,768]{1,0:T(8,128)(2,1)} %project.1.refs_1_, ...), custom_call_target="tpu_custom_call" | custom-call | flops 12079595520 | tf_op jit(solution)/shard_map/attend_backward/pallas_call | solution.py:164
  806.6 38.2 %attend_backward.3 = (bf16[1536,384]{1,0:T(8,128)(2,1)}, bf16[128,2048]{1,0:T(8,128)(2,1)S(1)}, bf16[128,2048]{1,0:T(8,128)(2,1)S(1)}, bf16[256,2048]{1,0:T(8,128)(2,1)S(1)}, bf16[256,2048]{1,0:T(8,128)(2,1)S(1)}) custom-call(s32[1]{0:T(128)} %dynamic_slice.15.refs_0_, bf16[1536,768]{1,0:T(8,128)(2,1)} %project.1.refs_1_, ...), custom_call_target="tpu_custom_call" | custom-call | flops 12079595520 | tf_op jit(solution)/shard_map/attend_backward/pallas_call | solution.py:164
  878.0 27.4 %outer.10 = (bf16[384,2048]{1,0:T(8,128)(2,1)}, bf16[256,2048]{1,0:T(8,128)(2,1)}, bf16[256,2048]{1,0:T(8,128)(2,1)}) custom-call(bf16[1536,384]{1,0:T(8,128)(2,1)} %get-tuple-element.250.refs_0_, bf16[1536,2048]{1,0:T(8,128)(2,1)} %all-gather.3.cloned.1.call-done.refs_1_.refs_0_, bf16[256,2048]{1,0:T(8,128)(2,1)} %get-tuple-element.270.refs_4_.refs_2_, ...), custom_call_target="tpu_custom_call" | custom-call | flops 2415919104 | tf_op jit(solution)/shard_map/outer/pallas_call | solution.py:164
  933.9 38.0 %move.13 = (bf16[4,96,2048]{2,1,0:T(8,128)(2,1)}, f32[8,2,2048]{2,1,0:T(2,128)}, bf16[64,2048]{1,0:T(8,128)(2,1)}, bf16[64,2048]{1,0:T(8,128)(2,1)}, bf16[64,2048]{1,0:T(8,128)(2,1)}) custom-call(bf16[4,96,2048]{2,1,0:T(8,128)(2,1)} %get-tuple-element.285.refs_0_, f32[2,2048]{1,0:T(2,128)} %pad_maximum_fusion.6.refs_1_, bf16[256,2048]{1,0:T(8,128)(2,1)} %add.217.refs_11_.refs_2_), custom_call_target="tpu_custom_call" | custom-call | tf_op jit(solution)/shard_map/move/pallas_call | solution.py:164
  977.5 38.9 %move.14 = (bf16[96,2048]{1,0:T(8,128)(2,1)}, bf16[96,2048]{1,0:T(8,128)(2,1)}, bf16[96,2048]{1,0:T(8,128)(2,1)}, f32[4,2,2048]{2,1,0:T(2,128)}) custom-call(bf16[96,2048]{1,0:T(8,128)(2,1)} %get-tuple-element.288.refs_0_, bf16[96,2048]{1,0:T(8,128)(2,1)} %get-tuple-element.289.refs_1_, bf16[96,2048]{1,0:T(8,128)(2,1)} %get-tuple-element.290.refs_2_, ...), custom_call_target="tpu_custom_call" | custom-call | tf_op jit(solution)/shard_map/move/pallas_call | solution.py:164
  1022.3 32.2 %move.15 = (bf16[4,96,2048]{2,1,0:T(8,128)(2,1)}, bf16[4,64,2048]{2,1,0:T(8,128)(2,1)}, bf16[4,96,2048]{2,1,0:T(8,128)(2,1)}, bf16[4,64,2048]{2,1,0:T(8,128)(2,1)}) custom-call(bf16[96,2048]{1,0:T(8,128)(2,1)} %add.221.refs_0_, bf16[64,2048]{1,0:T(8,128)(2,1)} %add.222.refs_1_), custom_call_target="tpu_custom_call" | custom-call | tf_op jit(solution)/shard_map/move/pallas_call | solution.py:164
  1070.6 24.5 %update_units.2 = (f32[26,1,1024,128]{3,2,1,0:T(8,128)}, f32[26,1,1024,128]{3,2,1,0:T(8,128)}, bf16[26,1,1024,128]{3,2,1,0:T(8,128)(2,1)}, f32[26,1,1024,128]{3,2,1,0:T(8,128)}, f32[26,1,1024,128]{3,2,1,0:T(8,128)}) custom-call(s32[1]{0:T(128)} %dynamic_slice.18.refs_0_, bf16[8,13,16,1024]{3,2,1,0:T(8,128)(2,1)} %copy-done.31, f32[26,1,1024,128]{3,2,1,0:T(8,128)} %refs_7_.1, ...), custom_call_target="tpu_custom_call" | custom-call | bytes 54525952 | tf_op jit(solution)/shard_map/update_units/pallas_call | solution.py:164
  1106.5 24.5 %update_units.3 = (f32[26,1,1024,128]{3,2,1,0:T(8,128)}, f32[26,1,1024,128]{3,2,1,0:T(8,128)}, bf16[26,1,1024,128]{3,2,1,0:T(8,128)(2,1)}, f32[26,1,1024,128]{3,2,1,0:T(8,128)}, f32[26,1,1024,128]{3,2,1,0:T(8,128)}) custom-call(s32[1]{0:T(128)} %dynamic_slice.18.refs_0_, ...), custom_call_target="tpu_custom_call", output_to_operand_aliasing={{0}: (5, {}), {1}: (6, {}), {2}: (7, {}), {3}: (8, {}), {4}... | custom-call | bytes 54525952 | tf_op jit(solution)/shard_map/update_units/pallas_call | solution.py:164
  (256 shorter events, 254.3 us)
Async XLA Ops:
  7.2 7.6 copy-start.33
  7.2 146.0 %all-gather.3.cloned.1.call-start = ((), (), s32[]{:S(2)}) async-start(), calls=%async_computation.4 | async-start | bytes 7864320 | tf_op jit(solution)/shard_map/all_gather | solution.py:1328
  14.7 382.6 %all-gather.5.cloned.1.call-start = ((), (), s32[]{:S(2)}) async-start(), calls=%async_computation.5 | async-start | bytes 7864320 | tf_op jit(solution)/shard_map/all_gather | solution.py:1365
  27.6 78.3 %copy-start.64 = (s32[116]{0:T(128)S(1)}, s32[116]{0:T(128)}, u32[]{:S(2)}) copy-start(s32[116]{0:T(128)} %param.13) | copy-start | bytes 1396
  114.3 33.8 %copy-start = (bf16[928,2048]{1,0:T(8,128)(2,1)S(1)}, bf16[928,2048]{1,0:T(8,128)(2,1)}, u32[]{:S(2)}) copy-start(bf16[928,2048]{1,0:T(8,128)(2,1)} %pick_units.1.refs_0_.refs_1_.refs_2_.refs_5_) | copy-start | bytes 11403268
  114.3 33.8 %copy-start.23 = (s32[2]{0:T(128)S(1)}, s32[2]{0:T(128)}, u32[]{:S(2)}) copy-start(s32[2]{0:T(128)} %pad_add_fusion.refs_0_) | copy-start | bytes 28
  153.2 986.5 %reduce-scatter.5.cloned.1.call-start = ((), (), s32[]{:S(2)}) async-start(), calls=%async_computation.7 | async-start | bytes 7864320 | tf_op jit(solution)/shard_map/reduce_scatter | solution.py:1692
  160.2 10.8 copy-start.10
  201.9 60.7 %copy-start.8 = (bf16[4,64,2048]{2,1,0:T(8,128)(2,1)S(1)}, bf16[4,64,2048]{2,1,0:T(8,128)(2,1)}, u32[]{:S(2)}) copy-start(bf16[4,64,2048]{2,1,0:T(8,128)(2,1)} %copy-done.7) | copy-start | bytes 3145732
  201.9 60.7 %copy-start.11 = (bf16[3,64,2048]{2,1,0:T(8,128)(2,1)S(1)}, bf16[3,64,2048]{2,1,0:T(8,128)(2,1)}, u32[]{:S(2)}) copy-start(bf16[3,64,2048]{2,1,0:T(8,128)(2,1)} %get-tuple-element.166.refs_3_.refs_4_.refs_2_) | copy-start | bytes 2359300
  353.8 41.9 %copy-start.36 = (bf16[3,384,512]{2,1,0:T(8,128)(2,1)S(1)}, bf16[3,384,512]{2,1,0:T(8,128)(2,1)}, u32[]{:S(2)}) copy-start(bf16[3,384,512]{2,1,0:T(8,128)(2,1)} %get-tuple-element.170.refs_1_) | copy-start | bytes 3538948
  397.3 178.3 %copy-start.53 = (f32[384]{0:T(512)}, f32[384]{0:T(512)S(1)}, u32[]{:S(2)}) copy-start(f32[384]{0:T(512)S(1)} %fusion.15) | copy-start | bytes 4612
  529.4 43.4 %copy-start.47 = (f32[1,2048]{1,0:T(1,128)S(1)}, f32[1,2048]{1,0:T(1,128)}, u32[]{:S(2)}) copy-start(f32[1,2048]{1,0:T(1,128)} %get-tuple-element.355.refs_4_) | copy-start | bytes 24580
  740.3 7.4 copy-start.17
  740.4 7.4 copy-start.18
  740.4 7.4 copy-start.24
  862.5 279.9 %reduce-scatter.3.cloned.1.call-start = ((), (), s32[]{:S(2)}) async-start(), calls=%async_computation.6 | async-start | bytes 7864320 | tf_op jit(solution)/shard_map/reduce_scatter | solution.py:1531
  865.5 12.4 %copy-start.65 = (s32[208]{0:T(256)}, s32[208]{0:T(256)S(1)}, u32[]{:S(2)}) copy-start(s32[208]{0:T(256)S(1)} %get-tuple-element.331.refs_1_) | copy-start | bytes 2500
  915.8 143.4 %all-to-all-start = ((bf16[8,13,16,1024]{3,2,1,0:T(8,128)(2,1)}), bf16[8,13,16,1024]{3,2,1,0:T(8,128)(2,1)S(1)}, u32[]{:S(2)}, u32[]{:S(2)}) async-start(bf16[8,13,16,1024]{3,2,1,0:T(8,128)(2,1)} %get-tuple-element.282.refs_2_), calls=%async_computation.2 | async-start | bytes 6815744 | tf_op jit(solution)/shard_map/all_to_all | solution.py:1592
  919.5 11.1 copy-start.35
  1061.0 45.4 %all-to-all-start.1 = ((bf16[8,13,16,1024]{3,2,1,0:T(8,128)(2,1)}), bf16[8,13,16,1024]{3,2,1,0:T(8,128)(2,1)}, u32[]{:S(2)}, u32[]{:S(2)}) async-start(bf16[8,13,16,1024]{3,2,1,0:T(8,128)(2,1)} %get-tuple-element.283.refs_3_), calls=%async_computation.3 | async-start | bytes 6815744 | tf_op jit(solution)/shard_map/all_to_all | solution.py:1592
  1069.8 25.3 %copy-start.40 = (bf16[8,6,16,2048]{3,2,1,0:T(8,128)(2,1)}, bf16[8,6,16,2048]{3,2,1,0:T(8,128)(2,1)S(1)}, u32[]{:S(2)}) copy-start(bf16[8,6,16,2048]{3,2,1,0:T(8,128)(2,1)S(1)} %constant_dynamic-update-slice_fusion.refs_4_) | copy-start | bytes 9437188
  1131.0 8.8 copy-start.50
  1131.0 11.4 copy-start.58
  (51 other events, 125.6 us)
Sparse Core Ops, SparseCore 0:
  14.8 136.8 all-gather.2
  153.8 153.6 all-gather.4
  862.6 124.8 reduce-scatter.4
  989.7 115.4 reduce-scatter.2

commit v4 on v3

--- a/solution.py
+++ b/solution.py
@@ -93,7 +93,7 @@
             )
         pl.semaphore_wait(barrier, len(partners))
         for send, copy in zip(sends, copies):
-            if not send.needs:
+            if not send.needs and not send.landed:
                 copy.start()
 
     def finish():
@@ -103,7 +103,7 @@
                 if k not in arrived:
                     copies[k].wait_recv()
                     arrived.add(k)
-            if send.needs:
+            if send.needs or send.landed:
                 copy.start()
         for k, copy in enumerate(copies):
             copy.wait_send()
@@ -115,7 +115,7 @@
 
 def call(
     body, ins, in_specs, out_shape, out_specs, *, name, grid=(), prefetch=(), scratch=(), deps=(),
-    aliases=None, mib=56, flops=0, moved=0, sends=(), sources=(), lands=(), closing=None,
+    aliases=None, mib=56, flops=0, moved=0, sends=(), sources=(), lands=(), inner=(), closing=None,
 ):
     first = len(prefetch) + len(ins)
     single = not isinstance(out_shape, (list, tuple))
@@ -135,7 +135,9 @@
             body(*given, *outs, *refs)
             return
         own, (send_sem, recv_sem) = refs[:-2], refs[-2:]
-        start, finish = run_sends(sends, source_refs, land_refs, send_sem, recv_sem)
+        start, finish = run_sends(
+            sends, source_refs, [*land_refs, *[own[k] for k in inner]], send_sem, recv_sem
+        )
 
         def last():
             finish()
@@ -328,10 +330,18 @@
     return jnp.transpose(parts.astype(f32).reshape(-1, unit_rows), (1, 0))
 
 
-def update_kernel(count_ref, grad_ref, master_ref, one_ref, two_ref, *refs, first):
-    filled = pl.program_id(0) + first < count_ref[0]
+def all_pieces(grad_ref, own_ref, turn):
+    place = lax.broadcasted_iota(jnp.int32, (grad_ref.shape[0], 1, 1), 0)
+    return jnp.where(place == turn, own_ref[0].astype(f32), grad_ref[:, 0].astype(f32))
+
+
+def update_kernel(filled_ref, grad_ref, own_ref, master_ref, one_ref, two_ref, *refs, first):
     piece, unit_rows = grad_ref.shape[2:]
-    gradient = jnp.where(filled, unit_gradient(grad_ref[:, 0], piece, unit_rows), 0.0)
+    pieces = all_pieces(grad_ref, own_ref, lax.axis_index("wide"))
+    empty = lax.broadcasted_iota(jnp.int32, (unit_rows, 128), 0) * 0 + pl.program_id(0) + first
+    gradient = jnp.where(
+        empty < filled_ref[0], unit_gradient(pieces, piece, unit_rows), 0.0
+    )
     apply_update(gradient, master_ref, one_ref, two_ref, refs[-5:])
 
 
@@ -340,79 +350,87 @@
     return [whole, whole, shaped(master.shape), whole, whole]
 
 
-def update_units(count, grads, first, master, moment_one, moment_two, done):
+def update_units(filled, grads, own, first, master, moment_one, moment_two, done, deps=()):
     _, _, unit_rows, unit_cols = master.shape
     parts, slots, piece, _ = grads.shape
     unit = blocks((1, 1, unit_rows, unit_cols), lambda s, *refs: (s + first, 0, 0, 0))
     return call(
         functools.partial(update_kernel, first=first),
-        [grads, master, moment_one, moment_two, *done],
-        [blocks((parts, 1, piece, unit_rows), lambda s, *refs: (0, s, 0, 0)), unit, unit, unit]
+        [filled, grads, own, master, moment_one, moment_two, *done],
+        [
+            SMEM,
+            blocks((parts, 1, piece, unit_rows), lambda s: (0, s, 0, 0)),
+            blocks((1, 1, piece, unit_rows), lambda s: (lax.axis_index("wide"), s, 0, 0)),
+            unit,
+            unit,
+            unit,
+        ]
         + [ANY] * len(done),
         update_outs(master),
         [unit] * 5,
         grid=(slots,),
-        prefetch=[count],
-        aliases={5 + k: k for k in range(len(done))},
+        aliases={6 + k: k for k in range(len(done))},
         moved=master.size * 16,
+        mib=40,
+        deps=deps,
         name="update_units",
     )
 
 
 def update_attn_kernel(
-    slot_ref, block_ref, half_ref, count_ref, qkv_ref, out_ref, grad_ref, master_ref, one_ref,
-    two_ref, *refs, qkv_blocks,
+    slot_ref, block_ref, half_ref, count_ref, mine_ref, near_ref, other_ref, grad_ref, own_ref,
+    master_ref, one_ref, two_ref, *refs,
 ):
     entry = pl.program_id(0)
     parts, _, piece, unit_rows = grad_ref.shape
 
     @pl.when((entry == 0) | (entry < count_ref[0]))
     def _():
-        from_qkv = block_ref[entry] < qkv_blocks
         turn = count_ref[2]
         taken = []
         for j in range(parts):
-            place = jnp.bitwise_xor(turn, j)
-            taken.append(
-                jnp.where(
-                    from_qkv,
-                    qkv_ref[pl.ds(place, 1), 0].astype(f32),
-                    out_ref[pl.ds(place, 1), 0].astype(f32),
-                )
+            e = jnp.bitwise_xor(turn, j)
+            near = jnp.where(
+                e == 0, mine_ref[...].astype(f32), near_ref[pl.ds(e // 2, 1), 0].astype(f32)
             )
+            other = other_ref[pl.ds(e // 2, 1), 0].astype(f32)
+            taken.append(jnp.where(e % 2 == 0, near, other))
         attn = jnp.concatenate(taken, axis=0)
-        gradient = jnp.where(count_ref[0] > 0, attn, grad_ref[:, 0].astype(f32))
+        gradient = jnp.where(count_ref[0] > 0, attn, all_pieces(grad_ref, own_ref, turn))
         gradient = unit_gradient(gradient, piece, unit_rows)
         gradient = jnp.where(slot_ref[entry] < count_ref[1], gradient, 0.0)
         apply_update(gradient, master_ref, one_ref, two_ref, refs[-5:])
 
 
 def update_attn(
-    slots, places, halves, count, qkv, out, grads, master, moment_one, moment_two, done
+    slots, places, halves, count, attn, grads, own, master, moment_one, moment_two, done
 ):
     _, _, unit_rows, unit_cols = master.shape
-    parts, _, piece, _ = grads.shape
-    qkv_blocks, out_blocks = qkv.shape[1], out.shape[1]
+    parts, low, piece, _ = grads.shape
     unit = blocks((1, 1, unit_rows, unit_cols), lambda k, slot, *refs: (slot[k], 0, 0, 0))
-    piece_of = (parts, 1, piece, unit_rows)
-    return call(
-        functools.partial(update_attn_kernel, qkv_blocks=qkv_blocks),
-        [qkv, out, grads, master, moment_one, moment_two, *done],
+    given = blocks(
+        (parts // 2, 1, piece, unit_rows),
+        lambda k, slot, block, half, count: (0, block[k], 0, half[k]),
+    )
+    return call(
+        update_attn_kernel,
+        [*attn, grads, own, master, moment_one, moment_two, *done],
         [
             blocks(
-                piece_of,
-                lambda k, slot, block, half, count: (
-                    0, jnp.minimum(block[k], qkv_blocks - 1), 0, half[k]
-                ),
+                (1, piece, unit_rows),
+                lambda k, slot, block, half, count: (block[k], 0, half[k]),
+            ),
+            given,
+            given,
+            blocks(
+                (parts, 1, piece, unit_rows),
+                lambda k, slot, *refs: (0, jnp.minimum(slot[k], low - 1), 0, 0),
             ),
             blocks(
-                piece_of,
+                (1, 1, piece, unit_rows),
                 lambda k, slot, block, half, count: (
-                    0, jnp.clip(block[k] - qkv_blocks, 0, out_blocks - 1), 0, half[k]
+                    count[2], jnp.minimum(slot[k], low - 1), 0, 0
                 ),
-            ),
-            blocks(
-                piece_of, lambda k, slot, *refs: (0, jnp.minimum(slot[k], grads.shape[1] - 1), 0, 0)
             ),
             unit,
             unit,
@@ -423,8 +441,9 @@
         [unit] * 5,
         grid=(slots.shape[0],),
         prefetch=[slots, places, halves, count],
-        aliases={10 + k: k for k in range(5)},
+        aliases={12 + k: k for k in range(5)},
         moved=master.size * 6,
+        mib=40,
         name="update_attn",
     )
 
@@ -700,6 +719,7 @@
         prefetch=[turn],
         deps=deps,
         flops=2 * count * D * D,
+        mib=32,
         name="spread",
     )
 
@@ -710,7 +730,7 @@
     refs[-1][...] = total.astype(bf16)
 
 
-def first_back(qkv_back, w_qkv, step, deps=()):
+def first_back(qkv_back, w_qkv, step, deps=(), **beside):
     groups = len(qkv_back)
     seq_len, width = qkv_back[0].shape
     return call(
@@ -724,6 +744,8 @@
         deps=deps,
         flops=2 * seq_len * width * groups * D,
         name="first_back",
+        mib=60,
+        **beside,
     )
 
 
@@ -772,133 +794,108 @@
     return arrays, layout, start // 3
 
 
-def ff_kernel(rows_ref, back_all_ref, *refs, layout, size, s, parts):
-    hid_ref, dgate_ref, dup_ref, keep_ref, keep_back_ref, _, total, buffer, sems = refs[-12:-3]
-    back_ref, sem = refs[-3], refs[-1]
+def ff_kernel(rows_all_ref, low_ref, high_ref, *refs, layout, size, s, parts):
+    hid_all, dgate_all, dup_all, rows_kept, back_kept, term_all, _ = refs[-18:-11]
+    total, down, rows_ref, back_ref, hid_ref, dgate_ref, dup_ref, _, buffer, sems, own = refs[-11:]
     count = rows_ref.shape[0]
-    place = lax.rem(lax.axis_index("narrow") - s + parts, parts) * count
-    copy = pltpu.make_async_copy(
-        back_all_ref.at[pl.ds(pl.multiple_of(place, count), count)], back_ref, sem
-    )
-    copy.start()
-    keep_ref[...] = rows_ref[...]
-    copy.wait()
-    keep_back_ref[...] = back_ref[...]
+    half = count // 2
+    place = lax.rem(lax.axis_index("narrow") - s + parts, parts)
+    low_place = pl.ds(pl.multiple_of(place * half, half), half)
+    place = pl.ds(pl.multiple_of(place * count, count), count)
+    here = pl.ds(s * count, count)
+    copies = [
+        pltpu.make_async_copy(rows_all_ref, rows_ref, own.at[0]),
+        pltpu.make_async_copy(low_ref.at[low_place], back_ref.at[:half], own.at[1]),
+        pltpu.make_async_copy(high_ref.at[low_place], back_ref.at[half:], own.at[4]),
+    ]
+    for copy in copies:
+        copy.start()
+    kept = [
+        pltpu.make_async_copy(rows_ref, rows_kept.at[here], own.at[2]),
+        pltpu.make_async_copy(back_ref, back_kept.at[here], own.at[3]),
+    ]
 
     def use(i, weights):
+        if i == 0:
+            for copy in copies:
+                copy.wait()
+            for copy in kept:
+                copy.start()
         gate = dot(rows_ref[...], weights[:size], 1, 1)
         up = dot(rows_ref[...], weights[size : 2 * size], 1, 1)
         hidden_back = dot(back_ref[...], weights[2 * size :], 1, 1)
         sig = 1.0 / (1.0 + jnp.exp(-gate))
         silu = gate * sig
-        here = slice(i * size, (i + 1) * size)
-        hid_ref[:, here] = (silu * up).astype(bf16)
+        cols = slice(i * size, (i + 1) * size)
+        hid = (silu * up).astype(bf16)
         dgate = (hidden_back * up * (sig * (1.0 + gate * (1.0 - sig)))).astype(bf16)
         dup = (hidden_back * silu).astype(bf16)
-        dgate_ref[:, here] = dgate
-        dup_ref[:, here] = dup
+        hid_ref[:, cols] = hid
+        dgate_ref[:, cols] = dgate
+        dup_ref[:, cols] = dup
         part = dot(dgate, weights[:size], 1, 0) + dot(dup, weights[size : 2 * size], 1, 0)
+        term = dot(hid, weights[2 * size :], 1, 0)
         if i:
             part = part + total[...]
+            term = term + down[...]
         total[...] = part
+        down[...] = term
 
     stream(refs, layout, 0, 3 * size, buffer, sems, use)
+    for copy in kept:
+        copy.wait()
+    rows_ref[...] = down[...].astype(bf16)
+    copies = [
+        pltpu.make_async_copy(hid_ref, hid_all.at[here], own.at[0]),
+        pltpu.make_async_copy(dgate_ref, dgate_all.at[here], own.at[1]),
+        pltpu.make_async_copy(dup_ref, dup_all.at[here], own.at[2]),
+        pltpu.make_async_copy(rows_ref, term_all.at[place], own.at[3]),
+    ]
+    for copy in copies:
+        copy.start()
+    for copy in copies:
+        copy.wait()
 
 
 def ff_close(lands, refs, *, added):
-    out_ref, total, _, _, _, arrived, sem = refs[-7:]
+    out_ref, total = refs[-12:-10]
+    arrived = refs[-4]
     value = total[...]
     if added:
-        copy = pltpu.make_async_copy(lands[0], arrived, sem)
-        copy.start()
-        copy.wait()
         value = value + arrived[...].astype(f32)
     out_ref[...] = value.astype(out_ref.dtype)
 
 
-def ff_step(s, rows, back_all, entries, kept, moving, before=None, last=False):
+def ff_step(s, rows, back_low, back_high, entries, kept, moving, added=False, last=False):
     count = rows.shape[0]
-    seq_len = back_all.shape[0]
+    seq_len = back_low.shape[0] + back_high.shape[0]
     arrays, layout, size = entry_layout(entries)
     ff_width = size * len(entries)
-    wide_rows = shaped((seq_len, ff_width))
-    given = blocks((count, ff_width), lambda i: (s, 0))
-    here = blocks((count, D), lambda i: (s, 0))
-    whole = blocks((count, D), lambda i: (0, 0))
-    order = sorted(range(1, seq_len // count)) + [0]
-    first = order[0] == s
     return call(
         functools.partial(
             ff_kernel, layout=layout, size=size, s=s, parts=seq_len // count
         ),
-        [rows, back_all, *arrays, *kept],
-        [whole, ANY] + [ANY] * (len(arrays) + len(kept)),
-        [wide_rows] * 3
-        + [shaped((seq_len, D))] * 2
+        [rows, back_low, back_high, *arrays, *kept],
+        [ANY] * (3 + len(arrays) + len(kept)),
+        [shaped((seq_len, ff_width))] * 3
+        + [shaped((seq_len, D))] * 3
         + [shaped((count, D), f32 if last else bf16)],
-        [given] * 3 + [here, here, whole],
-        grid=(1,),
-        scratch=[pltpu.VMEM((count, D), f32)]
+        [ANY] * 6 + [VMEM],
+        scratch=[pltpu.VMEM((count, D), f32)] * 2
+        + [pltpu.VMEM((count, D), bf16)] * 2
+        + [pltpu.VMEM((count, ff_width), bf16)] * 3
+        + [pltpu.VMEM((count, D), bf16)]
         + stream_scratch(3 * size)
-        + [pltpu.VMEM((count, D), bf16)] * 2
-        + [pltpu.SemaphoreType.DMA],
-        aliases={2 + len(arrays) + k: k for k in range(len(kept))},
-        mib=56,
+        + [pltpu.SemaphoreType.DMA((5,))],
+        aliases={3 + len(arrays) + k: k for k in range(len(kept))},
+        mib=60,
         flops=10 * count * ff_width * D,
         name="ff_step",
         sends=[Send(0, 0, "narrow", 1)],
         sources=[moving],
-        lands=[moving.shape],
-        closing=functools.partial(ff_close, added=not first),
-    )
-
-
-def down_kernel(hid_ref, *refs, layout, size):
-    out_ref, weights, sems = refs[-3:]
-
-    @pl.when(pl.program_id(0) == 0)
-    def _():
-        copies = []
-        for i, parts in enumerate(layout):
-            for ref, start, end, offset in parts:
-                begin = max(start, 2 * size)
-                if begin < end:
-                    copies.append(
-                        pltpu.make_async_copy(
-                            refs[ref].at[pl.ds(begin - start + offset, end - begin)],
-                            weights.at[pl.ds(i * size + begin - 2 * size, end - begin)],
-                            sems.at[len(copies)],
-                        )
-                    )
-        for copy in copies:
-            copy.start()
-        for copy in copies:
-            copy.wait()
-
-    out_ref[...] = dot(hid_ref[...], weights[...], 1, 0).astype(bf16)
-
-
-def down_pass(hidden, entries, count, deps=(), **beside):
-    arrays, layout, size = entry_layout(entries)
-    seq_len, ff_width = hidden.shape
-    parts = seq_len // count
-    return call(
-        functools.partial(down_kernel, layout=layout, size=size),
-        [hidden, *arrays],
-        [blocks((count, ff_width), lambda i: (i, 0))] + [ANY] * len(arrays),
-        shaped((seq_len, D)),
-        blocks(
-            (count, D), lambda i: (lax.rem(lax.axis_index("narrow") - i + parts, parts), 0)
-        ),
-        grid=(parts,),
-        scratch=[
-            pltpu.VMEM((ff_width, D), bf16),
-            pltpu.SemaphoreType.DMA((2 * len(entries),)),
-        ],
-        deps=deps,
-        flops=2 * seq_len * ff_width * D,
-        name="down_pass",
-        **beside,
+        lands=[] if added else [moving.shape],
+        inner=(7,) if added else (),
+        closing=functools.partial(ff_close, added=added),
     )
 
 
@@ -906,7 +903,7 @@
     refs[-1][...] = sum(ref[...].astype(f32) for ref in refs[:-1]).astype(refs[-1].dtype)
 
 
-def add(terms, kind=bf16, deps=()):
+def add(terms, kind=bf16, deps=(), **beside):
     count, width = terms[0].shape
     step = 128 if count % 128 == 0 else 64 if count % 64 == 0 else count
     given = blocks((step, width), lambda i: (i, 0))
@@ -920,6 +917,7 @@
         deps=deps,
         moved=count * width * 8,
         name="add",
+        **beside,
     )
 
 
@@ -965,6 +963,33 @@
     )
 
 
+def outer_pair_kernel(first_ref, second_ref, rows_ref, *outs):
+    for part, (taken_ref, out_ref) in enumerate(zip((first_ref, second_ref), outs)):
+
+        @pl.when(pl.program_id(0) == part)
+        def _(taken_ref=taken_ref, out_ref=out_ref):
+            out_ref[...] = dot(taken_ref[...], rows_ref[...], 0, 0).astype(bf16)
+
+
+def outer_pair(firsts, second, deps=(), **beside):
+    rows, height = firsts[0].shape
+    width = second.shape[1]
+    taken = blocks((rows, height), lambda i: (0, 0))
+    return call(
+        outer_pair_kernel,
+        [*firsts, second],
+        [taken, taken, blocks((rows, width), lambda i: (0, 0))],
+        [shaped((height, width))] * 2,
+        [blocks((height, width), lambda i: (0, 0))] * 2,
+        grid=(2,),
+        deps=deps,
+        flops=4 * rows * height * width,
+        name="outer_pair",
+        mib=60,
+        **beside,
+    )
+
+
 def pass_kernel(*refs):
     pass
 
@@ -980,14 +1005,8 @@
     return [(i, (i + step) % count) for i in range(count)]
 
 
-def butterfly(value):
-    for axis in ("wide", "narrow"):
-        count = lax.axis_size(axis)
-        step = 1
-        while step < count:
-            value = value + lax.ppermute(value, axis, [(i, i ^ step) for i in range(count)])
-            step *= 2
-    return value
+def flip(value, bits):
+    return lax.ppermute(value, "wide", [(i, i ^ bits) for i in range(8)])
 
 
 def nothing(*refs):
@@ -1121,6 +1140,10 @@
         moved=met[1].size * 8,
         name="ff_join",
     )
+
+
+def shaped_rows(array, parts):
+    return (array.shape[0] // parts, array.shape[1])
 
 
 def across_sends(source, land):
@@ -1182,9 +1205,10 @@
     return blocks(array.shape, lambda i: (0,) * len(array.shape))
 
 
-def arrange_qkv_kernel(turn_ref, *refs, piece, unit_cols, sizes):
-    own_ref, other_ref = refs[-2:]
-    group_width = sizes[3]
+def arrange_attn_kernel(turn_ref, *refs, piece, unit_cols, sizes):
+    *grads, own_ref, other_ref = refs
+    query_width, kv_width, _, group_width = sizes
+    out_first = query_width + 2 * kv_width
     for j in range(unit_cols // piece):
         e = jnp.bitwise_xor(turn_ref[0], j)
         for core, out_ref in enumerate((own_ref, other_ref)):
@@ -1192,26 +1216,31 @@
             @pl.when(e % 2 == core)
             def _(j=j, e=e, out_ref=out_ref):
                 for c in range(out_ref.shape[1] // piece):
-                    row = unit_row((c * unit_cols, j * piece), *sizes)
-                    grad_ref = refs[row // group_width]
-                    first = row % group_width
+                    if c * unit_cols < out_first:
+                        row = unit_row((c * unit_cols, j * piece), *sizes)
+                        grad_ref = grads[row // group_width]
+                        row = row % group_width
+                    else:
+                        row = c * unit_cols - out_first + j * piece
+                        grad_ref = grads[-1]
                     out_ref[e // 2, c * piece : (c + 1) * piece, :] = grad_ref[
-                        first : first + piece, :
+                        row : row + piece, :
                     ]
 
 
-def arrange_qkv(turn, grads, piece, unit_cols, sizes):
+def arrange_attn(turn, grads, piece, unit_cols, sizes):
     count = unit_cols // piece
-    rows = sizes[3] * len(grads) // count
+    rows = sum(grad.shape[0] for grad in grads) // count
     shape = shaped((count // 2, rows, D))
     return call(
-        functools.partial(arrange_qkv_kernel, piece=piece, unit_cols=unit_cols, sizes=sizes),
+        functools.partial(arrange_attn_kernel, piece=piece, unit_cols=unit_cols, sizes=sizes),
         [turn, *grads],
         [SMEM] + [VMEM] * len(grads),
         [shape, shape],
         [VMEM] * 2,
+        mib=32,
         moved=rows * count * D * 4,
-        name="arrange_qkv",
+        name="arrange_attn",
     )
 
 
@@ -1257,38 +1286,6 @@
         deps=deps,
         moved=D * D * 4,
         name="assemble_out",
-    )
-
-
-def arrange_out_kernel(grad_ref, own_ref, other_ref, *, piece, unit_cols, parts):
-    per = own_ref.shape[1] // piece // parts
-    for j in range(unit_cols // piece):
-        e = jnp.bitwise_xor(lax.axis_index("wide"), j)
-        for core, out_ref in enumerate((own_ref, other_ref)):
-
-            @pl.when(e % 2 == core)
-            def _(j=j, e=e, out_ref=out_ref):
-                for k in range(parts):
-                    for c in range(per):
-                        row = (parts - k) % parts * (grad_ref.shape[0] // parts) + c * unit_cols + j * piece
-                        first = (k * per + c) * piece
-                        out_ref[e // 2, first : first + piece, :] = grad_ref[
-                            row : row + piece, :
-                        ]
-
-
-def arrange_out(grad, piece, unit_cols, parts, **beside):
-    count = unit_cols // piece
-    shape = shaped((count // 2, D // count, D))
-    return call(
-        functools.partial(arrange_out_kernel, piece=piece, unit_cols=unit_cols, parts=parts),
-        [grad],
-        [VMEM],
-        [shape, shape],
-        [VMEM] * 2,
-        moved=D * D * 4,
-        name="arrange_out",
-        **beside,
     )
 
 
@@ -1328,7 +1325,7 @@
     normed_all = lax.all_gather(normed, "narrow", axis=0, tiled=True)
 
     slot_place, counts = positions(owners, wide_count, capacity)
-    turned = turn_units(master, wide_count, (normed,))
+    turned = turn_units(master, wide_count, ())
     got = exchange_units(turned)
     rows = pick_units(turn, slot_place, turned, got, row_blocks)
     qkv_rows = qkv_blocks * piece
@@ -1341,28 +1338,24 @@
     def entry(k):
         return lambda wide, narrow: k
 
-    near_qkv, other_qkv, narrow_out = move(
+    near_qkv, other_qkv = move(
         [Send(0, 0, "wide", 2 * r, qkv_at, entry(r - 1)) for r in (1, 2, 3)]
         + [Send(0, 1, "wide", 1, qkv_at, entry(0))]
-        + [Send(0, 2, "narrow", k, out_at, entry(k - 1)) for k in range(1, narrow_count)]
         + [
             Send(0, 1, "wide", 1, entry(r - 1), entry(r), landed=True, needs=(r - 1,))
             for r in (1, 2, 3)
         ],
         [rows],
-        [
-            (3, qkv_rows, D),
-            (4, qkv_rows, D),
-            (narrow_count - 1, out_rows, D),
-        ],
+        [(3, qkv_rows, D), (4, qkv_rows, D)],
     )
     w_qkv = assemble_qkv(turn, rows, near_qkv, other_qkv, piece, unit_cols, sizes)
 
     cos_table, sin_table = tables(seq_len, HD)
     cos_all = jnp.concatenate([cos_table] * (LANES // HD), axis=1)
     sin_all = jnp.concatenate([sin_table] * (LANES // HD), axis=1)
-    cotangent_then = after(cotangent, normed_all, w_qkv)
-    back_all = lax.all_gather(cotangent_then, "narrow", axis=0, tiled=True)
+    low_rows = row_count // 2
+    cotangent_then = after(cotangent[:low_rows], normed_all, w_qkv)
+    back_low = lax.all_gather(cotangent_then, "narrow", axis=0, tiled=True)
     qkv = project(
         normed_all, w_qkv, cos_all, sin_all, group_width, row_count, (cotangent_then,)
     )
@@ -1374,21 +1367,18 @@
     def later_entries(wide, narrow):
         return pl.ds(1, narrow_count - 1)
 
-    attended, logs, out_x, out_y = attend_forward(
+    third = ff_rows // 3
+    attended, logs, narrow_out, x_first, y_first = attend_forward(
         length, qkv, groups, block,
         sends=[
-            Send(0, 0, "wide", 2, out_at, first_entry),
-            Send(0, 1, "wide", 4, out_at, first_entry),
-            Send(1, 0, "wide", 2, None, later_entries),
-            Send(1, 1, "wide", 4, None, later_entries),
-        ],
-        sources=[rows, narrow_out],
-        lands=[out_shape, out_shape],
-    )
-    out_x, out_y = out_x, out_y
+            Send(0, 0, "narrow", k, out_at, entry(k - 1)) for k in range(1, narrow_count)
+        ]
+        + near_and_across(0, 1, rows_at(ff_first, third)),
+        sources=[rows],
+        lands=[(narrow_count - 1, out_rows, D), (third, D), (third, D)],
+    )
 
     half = narrow_count // 2
-    third = ff_rows // 3
 
     def heads_of(k):
         return lambda wide, narrow: pl.ds(
@@ -1399,30 +1389,38 @@
         return lambda wide, narrow: (k, at)
 
     low_part, high_part = pl.ds(0, half), pl.ds(half, narrow_count - half)
-    attended_others, out_across, out_other, x_first, y_first = move(
+    first_sends = narrow_count - 1
+    attended_others, out_x, out_y, out_across, out_other = move(
         [Send(0, 0, "narrow", k, heads_of(k), entry(k - 1)) for k in range(1, narrow_count)]
         + [
-            Send(2, 1, "wide", 4, lambda w, n: low_part, lambda w, n: low_part),
-            Send(3, 1, "wide", 2, lambda w, n: high_part, lambda w, n: high_part),
-            Send(1, 2, "wide", 1, out_at, lambda w, n: (0, 0)),
-            Send(4, 2, "wide", 1, None, lambda w, n: (0, pl.ds(1, narrow_count - 1))),
-            Send(2, 2, "wide", 1, None, entry(1)),
-            Send(3, 2, "wide", 1, None, entry(2)),
-            Send(1, 3, "wide", 2, rows_at(ff_first, third)),
-            Send(1, 4, "wide", 4, rows_at(ff_first, third)),
+            Send(1, 1, "wide", 2, out_at, first_entry),
+            Send(2, 1, "wide", 2, None, later_entries),
+            Send(1, 2, "wide", 4, out_at, first_entry),
+            Send(2, 2, "wide", 4, None, later_entries),
+            Send(1, 4, "wide", 1, out_at, lambda w, n: (0, 0)),
+            Send(2, 4, "wide", 1, None, lambda w, n: (0, later_entries(w, n))),
             Send(
-                1, 2, "wide", 1, None, entry(3), landed=True,
-                needs=(narrow_count - 1, narrow_count),
+                1, 3, "wide", 4, lambda w, n: low_part, lambda w, n: low_part, landed=True,
+                needs=(first_sends, first_sends + 1),
+            ),
+            Send(
+                2, 3, "wide", 2, lambda w, n: high_part, lambda w, n: high_part, landed=True,
+                needs=(first_sends + 2, first_sends + 3),
+            ),
+            Send(1, 4, "wide", 1, None, entry(1), landed=True),
+            Send(2, 4, "wide", 1, None, entry(2), landed=True),
+            Send(
+                3, 4, "wide", 1, None, entry(3), landed=True,
+                needs=(first_sends + 6, first_sends + 7),
             ),
         ],
-        [attended, rows, out_x, out_y, narrow_out],
-        [
-            (narrow_count - 1, row_count, query_width),
-            out_shape,
-            (4, *out_shape),
-            (third, D),
-            (third, D),
-        ],
+        [attended, rows, narrow_out],
+        [(narrow_count - 1, row_count, query_width)]
+        + [out_shape] * 3
+        + [(4, *out_shape)],
+    )
+    back_high = lax.all_gather(
+        after(cotangent[low_rows:], attended_others, back_low), "narrow", axis=0, tiled=True
     )
     w_out = assemble_out(
         turn, rows, qkv_rows, [narrow_out, out_x, out_y, out_across, out_other], piece,
@@ -1441,29 +1439,32 @@
         [Send(0, 0, "narrow", 1)]
         + near_and_across(1, 1, rows_at(ff_first + third + sixth, rest))
         + [Send(1, 3, "wide", 1, rows_at(ff_first, ff_rows))]
-        + [Send(2 + k, 4 + k, "wide", 1) for k in range(4)],
+        + [Send(2 + k, 4 + k, "wide", 1) for k in range(4)]
+        + [
+            Send(1, 8, "wide", 1, landed=True, needs=(1,)),
+            Send(2, 9, "wide", 1, landed=True, needs=(2,)),
+        ],
         [normed_two, rows, x_first, x_second, y_first, y_second],
         [normed_two.shape, (rest, D), (rest, D), (ff_rows, D)]
-        + [(third, D), (sixth, D), (third, D), (sixth, D)],
-    )
-    own_swap, x_first_swap, x_second_swap, y_first_swap, y_second_swap = swapped
+        + [(third, D), (sixth, D)] * 2
+        + [(rest, D)] * 2,
+    )
+    own_swap, x_first_swap, x_second_swap, y_first_swap, y_second_swap = swapped[:5]
+    x_third_swap, y_third_swap = swapped[5:]
     block_two, across_first, across_second, across_third, *swapped = move(
         [
             Send(0, 0, "narrow", 1),
             Send(1, 1, "wide", 4),
             Send(2, 2, "wide", 4),
-            Send(4, 3, "wide", 2),
-            Send(3, 4, "wide", 1),
-            Send(4, 5, "wide", 1),
-            Send(1, 6, "wide", 1, landed=True, needs=(1,)),
-            Send(2, 7, "wide", 1, landed=True, needs=(2,)),
-            Send(3, 8, "wide", 1, landed=True, needs=(3,)),
+            Send(3, 3, "wide", 2),
+            Send(1, 4, "wide", 1, landed=True, needs=(1,)),
+            Send(2, 5, "wide", 1, landed=True, needs=(2,)),
+            Send(3, 6, "wide", 1, landed=True, needs=(3,)),
         ],
-        [block_one, x_first, x_second, x_third, y_third],
-        [block_one.shape, (third, D), (sixth, D), (rest, D), (rest, D), (rest, D)]
-        + [(third, D), (sixth, D), (rest, D)],
-    )
-    x_third_swap, y_third_swap, *across_swap = swapped
+        [block_one, x_first, x_second, y_third],
+        [block_one.shape] + [(third, D), (sixth, D), (rest, D)] * 2,
+    )
+    across_swap = swapped
 
     def pieces(first, second, last):
         return [(first, 0, third), (second, 0, sixth), (last, 0, rest)]
@@ -1479,11 +1480,11 @@
         pieces(*across_swap),
     ]
 
-    *kept, total, block_three = ff_step(1, block_one, back_all, entries, (), block_two)
-    *kept, total, _ = ff_step(2, block_two, back_all, entries, kept, total, True)
-    *kept, total, _ = ff_step(3, block_three, back_all, entries, kept, total, True)
-    *kept, norm_two_back, _ = ff_step(0, normed_two, back_all, entries, kept, total, True, True)
-    hidden, dgate, dup, mlp_all, back_kept = kept
+    *kept, total, block_three = ff_step(1, block_one, back_low, back_high, entries, (), block_two)
+    *kept, total = ff_step(2, block_two, back_low, back_high, entries, kept, total, True)
+    *kept, total = ff_step(3, block_three, back_low, back_high, entries, kept, total, True)
+    *kept, norm_two_back = ff_step(0, normed_two, back_low, back_high, entries, kept, total, True, True)
+    hidden, dgate, dup, mlp_all, back_kept, ff_term = kept
 
     _, norm_two_pull = jax.vjp(rmsnorm, residual, norm_gains[1])
     resid_part, gain_two = norm_two_pull(norm_two_back)
@@ -1495,84 +1496,72 @@
         return Send(0, land, "narrow", k, entry(k))
 
     heads_shape = (row_count, query_width)
-    attended_rows = jnp.concatenate(
-        [
-            lax.dynamic_slice(attended, (narrow_index * row_count, 0), (row_count, query_width))[
-                None
-            ],
-            attended_others,
-        ],
-        axis=0,
-    )
-    grad_out, heads_one = outer(
-        attended_rows, attn_back, 1,
-        sends=[heads_send(1, 0)], sources=[by_heads], lands=[heads_shape],
-    )
-    own_out, other_out, heads_three = arrange_out(
-        grad_out, piece, unit_cols, narrow_count,
-        sends=[heads_send(3, 0)], sources=[by_heads], lands=[heads_shape],
-    )
-    *grad_down, heads_two, out_swap = outer(
-        hidden, back_kept, 2, (own_out,),
+    *grad_down, heads_one, heads_three = outer(
+        hidden, back_kept, 2,
+        sends=[heads_send(1, 0), heads_send(3, 1)],
+        sources=[by_heads],
+        lands=[heads_shape, heads_shape],
+    )
+    half_shape, near_shape = shaped_rows(grad_down[0], 8), shaped_rows(grad_down[0], 4)
+    *grad_gate, heads_two, down_swap = outer(
+        dgate, mlp_all, 2,
         sends=[heads_send(2, 0), Send(1, 1, "wide", 1)],
-        sources=[by_heads, other_out],
-        lands=[heads_shape, other_out.shape],
+        sources=[by_heads, grad_down[1]],
+        lands=[heads_shape, grad_down[1].shape],
     )
     out_back = jnp.stack([by_heads[0], heads_one, heads_two, heads_three])
     out_back = jnp.take(out_back, back_by, axis=0).reshape(seq_len, query_width)
-    met_out = sum_entries(own_out, out_swap)
-    met_shape = met_out[0].shape
-    ff_term, out_x, out_y, down_swap = down_pass(
-        hidden, entries, row_count,
-        sends=[Send(0, 0, "wide", 2), Send(1, 1, "wide", 4), Send(2, 2, "wide", 1)],
-        sources=[met_out[1], met_out[2], grad_down[1]],
-        lands=[met_shape, met_shape, grad_down[1].shape],
-    )
+    attn_back_all = lax.all_gather(after(attn_back, heads_two), "narrow", axis=0, tiled=True)
     output = residual + lax.psum_scatter(
-        ff_term, "narrow", scatter_dimension=0, tiled=True
+        after(ff_term, attn_back_all), "narrow", scatter_dimension=0, tiled=True
     ).astype(f32)
     met_down = ff_meet(grad_down[0], down_swap)
-    half_shape, near_shape = met_down[3].shape, met_down[1].shape
-    *grad_gate, down_a, down_b = outer(
-        dgate, mlp_all, 2,
-        sends=across_sends(0, 0), sources=met_down[3:], lands=[half_shape] * 2,
+    *grad_upper, gate_swap, down_a, down_b = outer(
+        dup, mlp_all, 2,
+        sends=[Send(0, 0, "wide", 1)] + across_sends(1, 1),
+        sources=[grad_gate[1], *met_down[3:]],
+        lands=[grad_gate[1].shape, half_shape, half_shape],
     )
     joined_down = ff_join(met_down, down_a, down_b)
-    *grad_upper, gate_swap, down_x, down_y = outer(
-        dup, mlp_all, 2, (joined_down[0],),
-        sends=[Send(0, 0, "wide", 1)] + near_sends(1, 1),
-        sources=[grad_gate[1], *joined_down],
-        lands=[grad_gate[1].shape, near_shape, near_shape],
-    )
     met_gate = ff_meet(grad_gate[0], gate_swap)
 
     qkv_back = [None, None]
-    qkv_back[0], upper_swap, gate_a, gate_b, out_across = attend_backward(
+    qkv_back[0], upper_swap, gate_a, gate_b, down_x, down_y = attend_backward(
         0, groups, length, qkv, out_back, attended, logs, cos_all, sin_all, block,
-        sends=[Send(0, 0, "wide", 1)] + across_sends(1, 1) + [Send(3, 3, "wide", 6)],
-        sources=[grad_upper[1], *met_gate[3:], met_out[3]],
-        lands=[grad_upper[1].shape, half_shape, half_shape, met_shape],
+        sends=[Send(0, 0, "wide", 1)] + across_sends(1, 1) + near_sends(3, 3),
+        sources=[grad_upper[1], *met_gate[3:], *joined_down],
+        lands=[grad_upper[1].shape, half_shape, half_shape, near_shape, near_shape],
     )
     joined_gate = ff_join(met_gate, gate_a, gate_b)
     met_upper = ff_meet(grad_upper[0], upper_swap)
-    out_sum = add([met_out[0], out_x, out_y, out_across])
     qkv_back[1], upper_a, upper_b, gate_x, gate_y = attend_backward(
         1, groups, length, qkv, out_back, attended, logs, cos_all, sin_all, block,
         sends=across_sends(0, 0) + near_sends(2, 2),
         sources=[*met_upper[3:], *joined_gate],
         lands=[half_shape] * 2 + [near_shape] * 2,
-        deps=(out_sum,),
     )
     joined_upper = ff_join(met_upper, upper_a, upper_b)
-    norm_one_term = first_back(qkv_back, w_qkv, row_count, (joined_upper[0],))
-    first_qkv, upper_x, upper_y = outer(
-        qkv_back[0], normed_all, 1, (norm_one_term,),
-        sends=near_sends(0, 0), sources=list(joined_upper), lands=[near_shape] * 2,
+    half_rows = near_shape[0] // 2
+    halves = [
+        [
+            Send(0, 0, "wide", 2, rows_at(k * half_rows, half_rows)),
+            Send(1, 1, "wide", 4, rows_at(k * half_rows, half_rows)),
+        ]
+        for k in range(2)
+    ]
+    norm_one_term, upper_xa, upper_ya = first_back(
+        qkv_back, w_qkv, row_count,
+        sends=halves[0], sources=list(joined_upper), lands=[half_shape] * 2,
+    )
+    *grad_qkv, upper_xb, upper_yb = outer_pair(
+        qkv_back, normed_all, (norm_one_term,),
+        sends=halves[1], sources=list(joined_upper), lands=[half_shape] * 2,
     )
     ff_sums = [
-        add([met_gate[0], gate_x, gate_y]),
-        add([met_upper[0], upper_x, upper_y]),
-        add([met_down[0], down_x, down_y]),
+        add([met_gate[0], gate_x, gate_y], deps=(norm_one_term,)),
+        add([met_upper[0][:half_rows], upper_xa, upper_ya], deps=(grad_qkv[0],)),
+        add([met_upper[0][half_rows:], upper_xb, upper_yb]),
+        add([met_down[0], down_x, down_y], deps=(norm_one_term,)),
     ]
 
     slots = wide_count * capacity
@@ -1581,7 +1570,7 @@
     )
     half_of = unit_of // col_blocks
     block_of = unit_of - half_of * col_blocks
-    sent = unpick_units(
+    low, high = unpick_units(
         jnp.concatenate(ff_sums, axis=0),
         jnp.maximum(block_of - attn_blocks, 0),
         half_of,
@@ -1589,11 +1578,17 @@
         piece,
         unit_rows,
     )
-    owned = [lax.all_to_all(part, "wide", split_axis=0, concat_axis=0) for part in sent]
-    count = lax.dynamic_slice(counts, (wide_index,), (1,))
-
-    (second_qkv,) = outer(qkv_back[1], normed_all, 1, tuple(sent))
-    grad_qkv = [first_qkv, second_qkv]
+
+    def by_wide(wide, narrow):
+        return wide
+
+    def by_narrow(wide, narrow):
+        return narrow
+
+    (grad_out,) = outer(attended, attn_back_all, 1, (grad_qkv[0],))
+    own_attn, other_attn = arrange_attn(
+        turn, [*grad_qkv, grad_out], piece, unit_cols, sizes
+    )
     gain_one = sum(
         jnp.sum(
             w_qkv[g * group_width : (g + 1) * group_width].astype(f32) * grad_qkv[g].astype(f32),
@@ -1602,78 +1597,58 @@
         for g in range(groups)
     )
     gain_terms = jnp.stack([gain_one / norm_gains[0], gain_two])
-    own_qkv, other_qkv = arrange_qkv(turn, grad_qkv, piece, unit_cols, sizes)
-
-    def by_wide(wide, narrow):
-        return wide
-
-    def by_narrow(wide, narrow):
-        return narrow
-
-    qkv_swap, gain_others, *out_parts = move(
-        [Send(0, 0, "wide", 1)]
-        + [Send(1, 1, "wide", e, None, by_wide) for e in range(1, wide_count)]
+    owned_high = lax.all_to_all(high, "wide", split_axis=0, concat_axis=0)
+    owned_low, attn_swap, gain_others = move(
+        [
+            Send(
+                0, 0, "wide", e,
+                lambda wide, narrow, e=e: jnp.bitwise_xor(wide, e),
+                by_wide,
+            )
+            for e in range(1, wide_count)
+        ]
+        + [Send(1, 1, "wide", 1)]
+        + [Send(2, 2, "wide", e, None, by_wide) for e in range(1, wide_count)],
+        [low, other_attn, gain_terms],
+        [low.shape, other_attn.shape, ((wide_count, *gain_terms.shape), f32)],
+    )
+    met_attn = sum_entries(own_attn, attn_swap)
+    gain_plane = sum_places(wide_index.reshape(1), gain_terms, gain_others)
+    filled = jnp.concatenate(
+        [lax.dynamic_slice(counts, (wide_index,), (1,)), wide_index.reshape(1)]
+    ).astype(jnp.int32)
+    arrived = [flip(met_attn[r], 2 * r) for r in (1, 2, 3)]
+    updated = update_units(
+        filled, owned_low, low, 0, master, moment_one, moment_two, (), (met_attn[0],)
+    )
+    gain_others = jnp.stack(
+        [gain_plane]
         + [
-            Send(2, k + 1, "narrow", k, rows_at(k * out_rows, out_rows))
+            after(lax.ppermute(gain_plane, "narrow", shift(narrow_count, k)), updated[0])
             for k in range(1, narrow_count)
-        ],
-        [other_qkv, gain_terms, out_sum],
-        [other_qkv.shape, ((wide_count, *gain_terms.shape), f32)]
-        + [(out_rows, D)] * (narrow_count - 1),
-    )
-    met_qkv = sum_entries(own_qkv, qkv_swap)
-    gain_plane = sum_places(wide_index.reshape(1), gain_terms, gain_others)
-    out_sum = add([out_sum[:out_rows]] + list(out_parts))
-    *arrived, gain_others = move(
-        [Send(r - 1, r - 1, "wide", 2 * r) for r in (1, 2, 3)]
-        + [Send(3, 3, "narrow", k, None, by_narrow) for k in range(1, narrow_count)],
-        [*met_qkv[1:], gain_plane],
-        [met_qkv[0].shape] * 3 + [((narrow_count, *gain_terms.shape), f32)],
-    )
-    gain_grads = sum_places(narrow_index.reshape(1), gain_plane, gain_others)
-    qkv_sum = add([met_qkv[0]] + list(arrived))
-    near_qkv, near_out, other_qkv, other_out = move(
-        [Send(0, 0, "wide", 2 * r, None, entry(r)) for r in (1, 2, 3)]
-        + [Send(1, 1, "wide", 2 * r, None, entry(r)) for r in (1, 2, 3)]
-        + [
-            Send(0, 2, "wide", 1, None, entry(0)),
-            Send(1, 3, "wide", 1, None, entry(0)),
         ]
-        + [
-            Send(0, 2, "wide", 1, entry(r), entry(r), landed=True, needs=(r - 1,))
-            for r in (1, 2, 3)
-        ]
-        + [
-            Send(1, 3, "wide", 1, entry(r), entry(r), landed=True, needs=(r + 2,))
-            for r in (1, 2, 3)
-        ],
-        [qkv_sum, out_sum],
-        [(4, qkv_rows, D), (4, out_rows, D)] * 2,
-    )
-
-    def by_device(own, near, other):
-        return jnp.stack(
-            [
-                other[e // 2] if e % 2 else near[e // 2] if e else own
-                for e in range(wide_count)
-            ]
-        )
-
-    qkv_grads = by_device(qkv_sum, near_qkv, other_qkv)
-    out_grads = by_device(out_sum, near_out, other_out)
-    qkv_grads = qkv_grads.reshape(wide_count, qkv_blocks, piece, D)
-    out_grads = out_grads.reshape(wide_count, out_blocks, piece, D)
-
-    updated = ()
-    for k in range(2):
-        updated = update_units(
-            count, owned[k], k * (capacity // 2), master, moment_one, moment_two, updated
-        )
+    )
+    gain_grads = sum_places(
+        narrow_index.reshape(1), gain_plane, jnp.take(gain_others, back_by, axis=0)
+    )
+    attn_sum = add([met_attn[0]] + arrived, deps=(updated[0],))
+    updated = update_units(
+        filled, owned_high, owned_high, capacity // 2, master, moment_one, moment_two, updated
+    )
+    near = [attn_sum] + [
+        after(flip(attn_sum, 2 * r), updated[0]) for r in (1, 2, 3)
+    ]
+    other = [flip(part, 1) for part in near]
+    attn_grads = [attn_sum.reshape(attn_blocks, piece, D)] + [
+        jnp.stack(part).reshape(wide_count // 2, attn_blocks, piece, D)
+        for part in (near, other)
+    ]
+
     first_slot = wide_index * capacity
     own_block = lax.dynamic_slice(block_of, (first_slot,), (capacity,))
     own_half = lax.dynamic_slice(half_of, (first_slot,), (capacity,))
     slot = jnp.arange(capacity, dtype=jnp.int32)
-    is_attn = (own_block < attn_blocks) & (slot < count[0])
+    is_attn = (own_block < attn_blocks) & (slot < filled[0])
     attn_count = jnp.sum(is_attn.astype(jnp.int32))
     rank = jnp.cumsum(is_attn.astype(jnp.int32)) - 1
     listed = min(capacity, attn_blocks * row_blocks)
@@ -1685,8 +1660,8 @@
 
     owned_grads, new_master, new_copy, new_first, new_second = update_attn(
         entries_of(slot), entries_of(own_block), entries_of(own_half),
-        jnp.stack([attn_count, count[0], wide_index]).astype(jnp.int32),
-        qkv_grads, out_grads, owned[0], master, moment_one, moment_two, updated,
+        jnp.stack([attn_count, filled[0], wide_index]).astype(jnp.int32),
+        attn_grads, owned_low, low, master, moment_one, moment_two, updated,
     )
 
     norm_one_back = lax.psum_scatter(

time: 1160 us -> 1030 us (0.89)
  Pallas kernels: 1030 us -> 887 us
    pallas_call x53 -> x55, Pallas kernels: 1030 us -> 887 us  [call(): pl.pallas_call(wrapped, grid_spec=pltpu.PrefetchScalarGridSpec(num_scalar...]
    unnamed x151 -> x160, local copies, waits for them, and re-layouts: 33.5 us -> 37.5 us
  transfers between devices with their start and end apart: 6 -> 20, of which waited for: 1 -> 3; matrix products, arithmetic and copies ran while one was open for 3% -> 4% of each run, Pallas kernels for 50% -> 66%
where the time goes in v4:
time: 1030 us; the launch traced here: 1020 us
  Pallas kernels  887 us (86%)
  other arithmetic  47.9 us (5%)
  local copies, waits for them, and re-layouts  47.8 us (5%)
  between operations  16 us (2%)
  starting transfers between devices  13.1 us (1%)
    pallas_call x55, Pallas kernels, call(): pl.pallas_call(wrapped, grid_spec=pltpu.PrefetchScalarGridSpec(num_scalar...  887 us
    unnamed x160, local copies, waits for them, and re-layouts  37.5 us
  transfers between devices with their start and end apart: 20, of which 3 were waited for; matrix products, arithmetic and copies ran while one was open for 4% of the time, Pallas kernels for 66%

profile of v4, /device:TPU:0, one launch (start us, length us, event | category | flops | bytes accessed | tf_op | source)
XLA Modules:
  0.0 1020.7 jit_solution(4539743802904378448)
XLA Ops:
  25.7 78.4 %move.6.refs_3_ = bf16[8,26,16,1024]{3,2,1,0:T(8,128)(2,1)} custom-call(bf16[8,26,16,1024]{3,2,1,0:T(8,128)(2,1)} %copy-done.2), custom_call_target="tpu_custom_call" | custom-call | tf_op jit(solution)/shard_map/move/pallas_call | solution.py:166
  112.4 23.2 %move.7 = (bf16[3,96,2048]{2,1,0:T(8,128)(2,1)}, bf16[4,96,2048]{2,1,0:T(8,128)(2,1)}) custom-call(bf16[928,2048]{1,0:T(8,128)(2,1)} %pick_units.1.refs_0_.refs_1_.refs_2_.refs_5_.refs_3_), custom_call_target="tpu_custom_call" | custom-call | tf_op jit(solution)/shard_map/move/pallas_call | solution.py:166
  148.3 11.0 %project.1.refs_1_ = bf16[1536,768]{1,0:T(8,128)(2,1)} custom-call(bf16[1536,2048]{1,0:T(8,128)(2,1)} %all-gather.5.cloned.1.call-done.refs_1_.refs_0_.refs_2_, bf16[768,2048]{1,0:T(8,128)(2,1)} %copy-done.4, f32[1536,128]{1,0:T(8,128)} %get-tuple-element.319.refs_2_.refs_5_, f32[1536,128]{1,0:T(8,128)} %get-tuple-element.320.refs_3_.refs_6_, ...), custom_call_target="tpu_custom_call" | custom-call | flops 4831838208 | tf_op jit(solution)/shard_map/project/pallas_call | solution.py:166
  159.3 40.7 %attend_forward.1 = (bf16[1536,512]{1,0:T(8,128)(2,1)S(1)}, f32[2,8,1536]{2,1,0:T(8,128)S(1)}, bf16[3,64,2048]{2,1,0:T(8,128)(2,1)S(1)}, bf16[256,2048]{1,0:T(8,128)(2,1)S(1)}, bf16[256,2048]{1,0:T(8,128)(2,1)S(1)}) custom-call(s32[1]{0:T(128)} %dynamic_slice.12.refs_0_, bf16[1536,768]{1,0:T(8,128)(2,1)} %project.1.refs_1_, ...), custom_call_target="tpu_custom_call" | custom-call | flops 9663676416 | tf_op jit(solution)/shard_map/attend_forward/pallas_call | solution.py:166
  204.0 60.4 %move.8 = (bf16[3,384,512]{2,1,0:T(8,128)(2,1)}, bf16[4,64,2048]{2,1,0:T(8,128)(2,1)}, bf16[4,64,2048]{2,1,0:T(8,128)(2,1)}, bf16[4,64,2048]{2,1,0:T(8,128)(2,1)}, bf16[4,4,64,2048]{3,2,1,0:T(8,128)(2,1)}) custom-call(bf16[1536,512]{1,0:T(8,128)(2,1)} %copy-done.12, bf16[928,2048]{1,0:T(8,128)(2,1)} %pick_units.1.refs_0_.refs_1_.refs_2_.refs_5_.refs_3_, ...), custom_call_target="tpu_custom_call" | custom-call | tf_op jit(solution)/shard_map/move/pallas_call | solution.py:166
  272.9 20.5 %branch.1 = (f32[384,2048]{1,0:T(8,128)}, bf16[384,2048]{1,0:T(8,128)(2,1)}, bf16[128,2048]{1,0:T(8,128)(2,1)}, bf16[128,2048]{1,0:T(8,128)(2,1)}) custom-call(bf16[1536,512]{1,0:T(8,128)(2,1)} %copy-done.12, bf16[3,384,512]{2,1,0:T(8,128)(2,1)} %get-tuple-element.154.refs_1_, bf16[2048,2048]{1,0:T(8,128)(2,1)} %assemble_out.1.refs_2_, ...), custom_call_target="tpu_custom_call" | custom-call | flops 3221225472 | tf_op jit(solution)/shard_map/branch/pallas_call | solution.py:166
  293.4 66.8 %move.9 = (bf16[384,2048]{1,0:T(8,128)(2,1)}, bf16[384,2048]{1,0:T(8,128)(2,1)}, bf16[384,2048]{1,0:T(8,128)(2,1)}, bf16[768,2048]{1,0:T(8,128)(2,1)}, bf16[256,...) custom-call(bf16[384,2048]{1,0:T(8,128)(2,1)} %get-tuple-element.160, ...), custom_call_target="tpu_custom_call" | custom-call | tf_op jit(solution)/shard_map/move/pallas_call | solution.py:166
  360.2 41.4 %move.10 = (bf16[384,2048]{1,0:T(8,128)(2,1)}, bf16[256,2048]{1,0:T(8,128)(2,1)}, bf16[128,2048]{1,0:T(8,128)(2,1)}, bf16[384,2048]{1,0:T(8,128)(2,1)}, bf16[256...) custom-call(bf16[384,2048]{1,0:T(8,128)(2,1)} %get-tuple-element.167.refs_0_, ...), custom_call_target="tpu_custom_call" | custom-call | tf_op jit(solution)/shard_map/move/pallas_call | solution.py:166
  402.0 40.3 %ff_step.4 = (bf16[1536,2048]{1,0:T(8,128)(2,1)}, bf16[1536,2048]{1,0:T(8,128)(2,1)}, bf16[1536,2048]{1,0:T(8,128)(2,1)}, bf16[1536,2048]{1,0:T(8,128)(2,1)}, bf...) custom-call(bf16[384,2048]{1,0:T(8,128)(2,1)} %get-tuple-element.167, ...), custom_call_target="tpu_custom_call" | custom-call | flops 16106127360 | tf_op jit(solution)/shard_map/ff_step/pallas_call | solution.py:166
  442.3 39.5 %ff_step.5 = (bf16[1536,2048]{1,0:T(8,128)(2,1)}, bf16[1536,2048]{1,0:T(8,128)(2,1)}, bf16[1536,2048]{1,0:T(8,128)(2,1)}, bf16[1536,2048]{1,0:T(8,128)(2,1)}, bf...) custom-call(bf16[384,2048]{1,0:T(8,128)(2,1)} %get-tuple-element.181, ...), custom_call_target="tpu_custom_call", output_to_operand_aliasing={{0}: (23, {}), {1}: (24, {}), {2}: (25, {}), {3}: (26, {}),... | custom-call | flops 16106127360 | tf_op jit(solution)/shard_map/ff_step/pallas_call | solution.py:166
  481.8 38.6 %ff_step.6 = (bf16[1536,2048]{1,0:T(8,128)(2,1)}, bf16[1536,2048]{1,0:T(8,128)(2,1)}, bf16[1536,2048]{1,0:T(8,128)(2,1)}, bf16[1536,2048]{1,0:T(8,128)(2,1)}, bf...) custom-call(bf16[384,2048]{1,0:T(8,128)(2,1)} %get-tuple-element.182, ...), custom_call_target="tpu_custom_call", output_to_operand_aliasing={{0}: (23, {}), {1}: (24, {}), {2}: (25, {}), {3}: (26, {}),... | custom-call | flops 16106127360 | tf_op jit(solution)/shard_map/ff_step/pallas_call | solution.py:166
  520.4 39.6 %ff_step.7 = (bf16[1536,2048]{1,0:T(8,128)(2,1)}, bf16[1536,2048]{1,0:T(8,128)(2,1)}, bf16[1536,2048]{1,0:T(8,128)(2,1)}, bf16[1536,2048]{1,0:T(8,128)(2,1)}, bf...) custom-call(bf16[384,2048]{1,0:T(8,128)(2,1)} %get-tuple-element.160, ...), custom_call_target="tpu_custom_call", output_to_operand_aliasing={{0}: (23, {}), {1}: (24, {}), {2}: (25, {}), {3}: (26, {}),... | custom-call | flops 16106127360 | tf_op jit(solution)/shard_map/ff_step/pallas_call | solution.py:166
  573.9 23.1 %outer.4 = (bf16[1024,2048]{1,0:T(8,128)(2,1)}, bf16[1024,2048]{1,0:T(8,128)(2,1)}, bf16[384,512]{1,0:T(8,128)(2,1)}, bf16[384,512]{1,0:T(8,128)(2,1)}) custom-call(bf16[1536,2048]{1,0:T(8,128)(2,1)} %get-tuple-element.208.refs_0_, bf16[1536,2048]{1,0:T(8,128)(2,1)} %get-tuple-element.209.refs_1_, bf16[4,384,512]{2,1,0:T(8,128)(2,1)} %copy-done.34), custom_call_target="tpu_custom_call" | custom-call | flops 12884901888 | tf_op jit(solution)/shard_map/outer/pallas_call | solution.py:166
  597.0 26.5 %outer.5 = (bf16[1024,2048]{1,0:T(8,128)(2,1)}, bf16[1024,2048]{1,0:T(8,128)(2,1)}, bf16[384,512]{1,0:T(8,128)(2,1)}, bf16[1024,2048]{1,0:T(8,128)(2,1)}) custom-call(bf16[1536,2048]{1,0:T(8,128)(2,1)} %get-tuple-element.206.refs_0_, bf16[1536,2048]{1,0:T(8,128)(2,1)} %get-tuple-element.207.refs_1_, bf16[4,384,512]{2,1,0:T(8,128)(2,1)} %copy-done.34, ...), custom_call_target="tpu_custom_call" | custom-call | flops 12884901888 | tf_op jit(solution)/shard_map/outer/pallas_call | solution.py:166
  636.0 21.2 %outer.6 = (bf16[1024,2048]{1,0:T(8,128)(2,1)}, bf16[1024,2048]{1,0:T(8,128)(2,1)}, bf16[1024,2048]{1,0:T(8,128)(2,1)}, bf16[128,2048]{1,0:T(8,128)(2,1)}, bf16[128,2048]{1,0:T(8,128)(2,1)}) custom-call(bf16[1536,2048]{1,0:T(8,128)(2,1)} %get-tuple-element.215.refs_0_, bf16[1536,2048]{1,0:T(8,128)(2,1)} %get-tuple-element.207.refs_1_, ...), custom_call_target="tpu_custom_call" | custom-call | flops 12884901888 | tf_op jit(solution)/shard_map/outer/pallas_call | solution.py:166
  669.4 39.6 %attend_backward.2 = (bf16[1536,384]{1,0:T(8,128)(2,1)}, bf16[1024,2048]{1,0:T(8,128)(2,1)}, bf16[128,2048]{1,0:T(8,128)(2,1)S(1)}, bf16[128,2048]{1,0:T(8,128)(...) custom-call(s32[1]{0:T(128)} %dynamic_slice.12.refs_0_, bf16[1536,768]{1,0:T(8,128)(2,1)} %project.1.refs_1_, ...), custom_call_target="tpu_custom_call" | custom-call | flops 12079595520 | tf_op jit(solution)/shard_map/attend_backward/pallas_call | solution.py:166
  723.2 38.8 %attend_backward.3 = (bf16[1536,384]{1,0:T(8,128)(2,1)}, bf16[128,2048]{1,0:T(8,128)(2,1)S(1)}, bf16[128,2048]{1,0:T(8,128)(2,1)S(1)}, bf16[256,2048]{1,0:T(8,128)(2,1)S(1)}, bf16[256,2048]{1,0:T(8,128)(2,1)S(1)}) custom-call(s32[1]{0:T(128)} %dynamic_slice.12.refs_0_, bf16[1536,768]{1,0:T(8,128)(2,1)} %project.1.refs_1_, ...), custom_call_target="tpu_custom_call" | custom-call | flops 12079595520 | tf_op jit(solution)/shard_map/attend_backward/pallas_call | solution.py:166
  768.9 15.8 %first_back.1 = (bf16[1536,2048]{1,0:T(8,128)(2,1)}, bf16[128,2048]{1,0:T(8,128)(2,1)}, bf16[128,2048]{1,0:T(8,128)(2,1)}) custom-call(bf16[1536,384]{1,0:T(8,128)(2,1)} %get-tuple-element.232.refs_0_, bf16[1536,384]{1,0:T(8,128)(2,1)} %get-tuple-element.243.refs_1_, bf16[768,2048]{1,0:T(8,128)(2,1)} %copy-done.4, bf16[768,2048]{1,0:T(8,128)(2,1)} %copy-done.4, ...), custom_call_target="tpu_custom_call" | custom-call | flops 4831838208 | tf_op jit(solution)/shard_map/first_back/pallas_call | solution.py:166
  790.4 17.2 %outer_pair.1 = (bf16[384,2048]{1,0:T(8,128)(2,1)}, bf16[384,2048]{1,0:T(8,128)(2,1)}, bf16[128,2048]{1,0:T(8,128)(2,1)}, bf16[128,2048]{1,0:T(8,128)(2,1)}) custom-call(bf16[1536,384]{1,0:T(8,128)(2,1)} %get-tuple-element.232.refs_0_, bf16[1536,384]{1,0:T(8,128)(2,1)} %get-tuple-element.243.refs_1_, ...), custom_call_target="tpu_custom_call" | custom-call | flops 4831838208 | tf_op jit(solution)/shard_map/outer_pair/pallas_call | solution.py:166
  834.4 8.2 outer.7.refs_3_
  848.2 59.1 %move.11 = (bf16[8,13,16,1024]{3,2,1,0:T(8,128)(2,1)}, bf16[4,160,2048]{2,1,0:T(8,128)(2,1)}, f32[8,2,2048]{2,1,0:T(2,128)}) custom-call(bf16[8,13,16,1024]{3,2,1,0:T(8,128)(2,1)} %get-tuple-element.265.refs_0_.refs_2_.refs_8_, bf16[4,160,2048]{2,1,0:T(8,128)(2,1)} %copy-done.18, f32[2,2048]{1,0:T(2,128)} %pad_maximum_fusion.8.refs_2_.refs_1_), custom_call_target="tpu_custom_call" | custom-call | tf_op jit(solution)/shard_map/move/pallas_call | solution.py:166
  930.9 22.5 %update_units.2 = (f32[26,1,1024,128]{3,2,1,0:T(8,128)}, f32[26,1,1024,128]{3,2,1,0:T(8,128)}, bf16[26,1,1024,128]{3,2,1,0:T(8,128)(2,1)}, f32[26,1,1024,128]{3,2,1,0:T(8,128)}, f32[26,1,1024,128]{3,2,1,0:T(8,128)}) custom-call(s32[2]{0:T(128)S(1)} %pad_add_fusion.2.refs_0_, bf16[8,13,16,1024]{3,2,1,0:T(8,128)(2,1)S(1)} %copy-done.10, ...), custom_call_target="tpu_custom_call" | custom-call | bytes 54525952 | tf_op jit(solution)/shard_map/update_units/pallas_call | solution.py:166
  965.4 24.2 %update_units.3 = (f32[26,1,1024,128]{3,2,1,0:T(8,128)}, f32[26,1,1024,128]{3,2,1,0:T(8,128)}, bf16[26,1,1024,128]{3,2,1,0:T(8,128)(2,1)}, f32[26,1,1024,128]{3,2,1,0:T(8,128)}, f32[26,1,1024,128]{3,2,1,0:T(8,128)}) custom-call(s32[2]{0:T(128)S(1)} %pad_add_fusion.2.refs_0_, ...), custom_call_target="tpu_custom_call", output_to_operand_aliasing={{0}: (6, {}), {1}: (7, {}), {2}: (8, {}), {3}: (9, {}), {4}... | custom-call | bytes 54525952 | tf_op jit(solution)/shard_map/update_units/pallas_call | solution.py:166
  995.7 8.3 update_attn.1
  (297 shorter events, 199.8 us)
Async XLA Ops:
  7.2 134.9 %all-gather.5.cloned.1.call-start = ((), (), s32[]{:S(2)}) async-start(), calls=%async_computation.3 | async-start | bytes 7864320 | tf_op jit(solution)/shard_map/all_gather | solution.py:1325
  14.6 249.9 %all-gather.7.cloned.1.call-start = ((), (), s32[]{:S(2)}) async-start(), calls=%async_computation.4 | async-start | bytes 3932160 | tf_op jit(solution)/shard_map/all_gather | solution.py:1358
  25.7 78.4 %copy-start.74 = (s32[116]{0:T(128)S(1)}, s32[116]{0:T(128)}, u32[]{:S(2)}) copy-start(s32[116]{0:T(128)} %param.13) | copy-start | bytes 1396
  142.1 259.9 %all-gather.9.cloned.1.call-start = ((), (), s32[]{:S(2)}) async-start(), calls=%async_computation.5 | async-start | bytes 3932160 | tf_op jit(solution)/shard_map/all_gather | solution.py:1422
  264.5 520.3 %all-gather.11.cloned.1.call-start = ((), (), s32[]{:S(2)}) async-start(), calls=%async_computation.6 | async-start | bytes 7864320 | tf_op jit(solution)/shard_map/all_gather | solution.py:1514
  360.2 41.5 %copy-start.40 = (f32[384,2048]{1,0:T(8,128)S(1)}, f32[384,2048]{1,0:T(8,128)}, u32[]{:S(2)}) copy-start(f32[384,2048]{1,0:T(8,128)} %get-tuple-element.159) | copy-start | bytes 9437188
  401.9 161.9 %copy-start.64 = (f32[384]{0:T(512)}, f32[384]{0:T(512)S(1)}, u32[]{:S(2)}) copy-start(f32[384]{0:T(512)S(1)} %fusion.15) | copy-start | bytes 4612
  520.4 39.6 %copy-start.51 = (f32[1,2048]{1,0:T(1,128)S(1)}, f32[1,2048]{1,0:T(1,128)}, u32[]{:S(2)}) copy-start(f32[1,2048]{1,0:T(1,128)} %get-tuple-element.317.refs_4_) | copy-start | bytes 24580
  623.6 380.5 %reduce-scatter.5.cloned.1.call-start = ((), (), s32[]{:S(2)}) async-start(), calls=%async_computation.8 | async-start | bytes 7864320 | tf_op jit(solution)/shard_map/reduce_scatter | solution.py:1667
  784.8 223.0 %reduce-scatter.3.cloned.1.call-start = ((), (), s32[]{:S(2)}) async-start(), calls=%async_computation.7 | async-start | bytes 7864320 | tf_op jit(solution)/shard_map/reduce_scatter | solution.py:1515
  823.8 141.6 %all-to-all-start = ((bf16[8,13,16,1024]{3,2,1,0:T(8,128)(2,1)}), bf16[8,13,16,1024]{3,2,1,0:T(8,128)(2,1)}, u32[]{:S(2)}, u32[]{:S(2)}) async-start(bf16[8,13,16,1024]{3,2,1,0:T(8,128)(2,1)} %get-tuple-element.274), calls=%async_computation.2 | async-start | bytes 6815744 | tf_op jit(solution)/shard_map/all_to_all | solution.py:1600
  913.0 41.7 %collective-permute-start = (bf16[160,2048]{1,0:T(8,128)(2,1)}, bf16[160,2048]{1,0:T(8,128)(2,1)}, u32[]{:S(2)}, u32[]{:S(2)}) collective-permute-start(bf16[160,2048]{1,0:T(8,128)(2,1)} %get-tuple-element.269), channel_id=1, source_target_pairs={{0,8},{4,12},{8,0},{12,4},{16,24},{20,28},{24,16},{28,20},{1,9},{5... | collective-permute-start | bytes 1966088 | tf_op jit(solution)/shard_map/ppermute | solution.py:1009
  913.6 41.1 %collective-permute-start.1 = (bf16[160,2048]{1,0:T(8,128)(2,1)}, bf16[160,2048]{1,0:T(8,128)(2,1)}, u32[]{:S(2)}, u32[]{:S(2)}) collective-permute-start(bf16[160,2048]{1,0:T(8,128)(2,1)} %get-tuple-element.270), channel_id=1, source_target_pairs={{0,16},{4,20},{8,24},{12,28},{16,0},{20,4},{24,8},{28,12},{1,17},{... | collective-permute-start | bytes 1966088 | tf_op jit(solution)/shard_map/ppermute | solution.py:1009
  913.9 40.7 %collective-permute-start.2 = (bf16[160,2048]{1,0:T(8,128)(2,1)}, bf16[160,2048]{1,0:T(8,128)(2,1)}, u32[]{:S(2)}, u32[]{:S(2)}) collective-permute-start(bf16[160,2048]{1,0:T(8,128)(2,1)} %get-tuple-element.271), channel_id=1, source_target_pairs={{0,24},{4,28},{8,16},{12,20},{16,8},{20,12},{24,0},{28,4},{1,25},{... | collective-permute-start | bytes 1966088 | tf_op jit(solution)/shard_map/ppermute | solution.py:1009
  919.2 7.3 collective-permute-start.12
  919.9 33.5 %collective-permute-start.11 = (f32[2,2048]{1,0:T(2,128)}, f32[2,2048]{1,0:T(2,128)S(1)}, u32[]{:S(2)}, u32[]{:S(2)}) collective-permute-start(f32[2,2048]{1,0:T(2,128)} %sum_places.2.refs_1_), channel_id=1, source_target_pairs={{0,2},{1,3},{2,0},{3,1},{4,6},{5,7},{6,4},{7,5},{8,10},{9,11},{10,... | collective-permute-start | bytes 49160 | tf_op jit(solution)/shard_map/ppermute | solution.py:1627
  926.5 27.5 %collective-permute-start.10 = (f32[2,2048]{1,0:T(2,128)}, f32[2,2048]{1,0:T(2,128)S(1)}, u32[]{:S(2)}, u32[]{:S(2)}) collective-permute-start(f32[2,2048]{1,0:T(2,128)} %sum_places.2.refs_1_), channel_id=1, source_target_pairs={{0,1},{1,2},{2,3},{3,0},{4,5},{5,6},{6,7},{7,4},{8,9},{9,10},{10,1... | collective-permute-start | bytes 49160 | tf_op jit(solution)/shard_map/ppermute | solution.py:1627
  957.5 32.1 %collective-permute-start.5 = (bf16[160,2048]{1,0:T(8,128)(2,1)}, bf16[160,2048]{1,0:T(8,128)(2,1)}, u32[]{:S(2)}, u32[]{:S(2)}) collective-permute-start(bf16[160,2048]{1,0:T(8,128)(2,1)} %add.220), channel_id=1, source_target_pairs={{0,24},{4,28},{8,16},{12,20},{16,8},{20,12},{24,0},{28,4},{1,25},{... | collective-permute-start | bytes 1966088 | tf_op jit(solution)/shard_map/ppermute | solution.py:1009
  957.5 32.6 %collective-permute-start.4 = (bf16[160,2048]{1,0:T(8,128)(2,1)}, bf16[160,2048]{1,0:T(8,128)(2,1)}, u32[]{:S(2)}, u32[]{:S(2)}) collective-permute-start(bf16[160,2048]{1,0:T(8,128)(2,1)} %add.220), channel_id=1, source_target_pairs={{0,16},{4,20},{8,24},{12,28},{16,0},{20,4},{24,8},{28,12},{1,17},{... | collective-permute-start | bytes 1966088 | tf_op jit(solution)/shard_map/ppermute | solution.py:1009
  957.5 32.8 %collective-permute-start.3 = (bf16[160,2048]{1,0:T(8,128)(2,1)}, bf16[160,2048]{1,0:T(8,128)(2,1)}, u32[]{:S(2)}, u32[]{:S(2)}) collective-permute-start(bf16[160,2048]{1,0:T(8,128)(2,1)} %add.220), channel_id=1, source_target_pairs={{0,8},{4,12},{8,0},{12,4},{16,24},{20,28},{24,16},{28,20},{1,9},{5... | collective-permute-start | bytes 1966088 | tf_op jit(solution)/shard_map/ppermute | solution.py:1009
  965.3 28.0 %collective-permute-start.6 = (bf16[160,2048]{1,0:T(8,128)(2,1)}, bf16[160,2048]{1,0:T(8,128)(2,1)}, u32[]{:S(2)}, u32[]{:S(2)}) collective-permute-start(bf16[160,2048]{1,0:T(8,128)(2,1)} %add.220), channel_id=1, source_target_pairs={{0,4},{4,0},{8,12},{12,8},{16,20},{20,16},{24,28},{28,24},{1,5},{5... | collective-permute-start | bytes 1966088 | tf_op jit(solution)/shard_map/ppermute | solution.py:1009
  989.6 3.8 collective-permute-start.9
  990.2 3.2 collective-permute-start.8
  990.3 3.6 collective-permute-start.7
  (77 other events, 327.4 us)
Sparse Core Ops, SparseCore 0:
  14.7 118.0 all-gather.4
  142.2 106.8 all-gather.6
  264.6 88.8 all-gather.8
  623.7 112.9 all-gather.10
  784.9 108.3 reduce-scatter.4
  895.4 112.2 reduce-scatter.2

commit v5 on v4

--- a/solution.py
+++ b/solution.py
@@ -2,6 +2,7 @@
 
 import jax
 import jax.numpy as jnp
+import numpy as np
 from jax import lax
 from jax.experimental import pallas as pl
 from jax.experimental.pallas import tpu as pltpu
@@ -190,6 +191,13 @@
     return (jnp.cos(angles), jnp.sin(angles))
 
 
+def turn_tables(length_all):
+    inverse = np.float32(500000.0) ** (-np.arange(0, HD, 2, dtype=np.float32) / np.float32(HD))
+    angles = np.arange(length_all, dtype=np.float32)[:, None] * inverse[None, :]
+    angles = np.concatenate([angles] * (2 * LANES // HD), axis=1).astype(np.float32)
+    return jnp.asarray(np.cos(angles)), jnp.asarray(np.sin(angles))
+
+
 def rmsnorm(values, weight_gain):
     return (
         values * lax.rsqrt(jnp.mean(values * values, axis=-1, keepdims=True) + 1e-05) * weight_gain
@@ -281,18 +289,19 @@
 
 def unpick_kernel(block_ref, half_ref, rows_ref, low_ref, high_ref, sems, *, piece, unit_rows):
     owners, part, _, _ = low_ref.shape
+    capacity = part + high_ref.shape[1]
 
     def start(owner, carry):
-        for slot in range(2 * part):
+        for slot in range(capacity):
             out_ref = high_ref if slot >= part else low_ref
-            place = owner * 2 * part + slot
+            place = owner * capacity + slot
             pltpu.make_async_copy(
                 rows_ref.at[
                     pl.ds(pl.multiple_of(block_ref[place] * piece, piece), piece),
                     pl.ds(pl.multiple_of(half_ref[place] * unit_rows, unit_rows), unit_rows),
                 ],
-                out_ref.at[owner, slot % part],
-                sems.at[slot // part],
+                out_ref.at[owner, slot - part if slot >= part else slot],
+                sems.at[int(slot >= part)],
             ).start()
         return carry
 
@@ -303,12 +312,14 @@
 
 def unpick_units(rows, block_of, half_of, owners, piece, unit_rows):
     slots = block_of.shape[0]
-    shape = shaped((owners, slots // owners // 2, piece, unit_rows))
+    capacity = slots // owners
+    low = capacity // 4 * 2
+    sizes = (low, capacity - low)
     return call(
         functools.partial(unpick_kernel, piece=piece, unit_rows=unit_rows),
         [block_of, half_of, rows],
         [SMEM, SMEM, VMEM],
-        [shape, shape],
+        [shaped((owners, size, piece, unit_rows)) for size in sizes],
         [ANY, ANY],
         scratch=[pltpu.SemaphoreType.DMA((2,))],
         moved=slots * piece * unit_rows * 8,
@@ -316,33 +327,35 @@
     )
 
 
-def apply_update(gradient, master_ref, one_ref, two_ref, outs):
+def apply_update(gradient, master_ref, one_ref, two_ref, outs, k=0):
     grad_out, master_out, copy_out, one_out, two_out = outs
-    weight, one, two = adamw(master_ref[0, 0], gradient, one_ref[0, 0], two_ref[0, 0], 0.02, 0.1)
-    grad_out[0, 0] = gradient
-    master_out[0, 0] = weight
-    copy_out[0, 0] = weight.astype(bf16)
-    one_out[0, 0] = one
-    two_out[0, 0] = two
+    weight, one, two = adamw(master_ref[k, 0], gradient, one_ref[k, 0], two_ref[k, 0], 0.02, 0.1)
+    grad_out[k, 0] = gradient
+    master_out[k, 0] = weight
+    copy_out[k, 0] = weight.astype(bf16)
+    one_out[k, 0] = one
+    two_out[k, 0] = two
 
 
 def unit_gradient(parts, piece, unit_rows):
     return jnp.transpose(parts.astype(f32).reshape(-1, unit_rows), (1, 0))
 
 
-def all_pieces(grad_ref, own_ref, turn):
+def all_pieces(grad_ref, own_ref, turn, k=0):
     place = lax.broadcasted_iota(jnp.int32, (grad_ref.shape[0], 1, 1), 0)
-    return jnp.where(place == turn, own_ref[0].astype(f32), grad_ref[:, 0].astype(f32))
+    own = own_ref[0, k : k + 1].astype(f32)
+    return jnp.where(place == turn, own, grad_ref[:, k].astype(f32))
 
 
 def update_kernel(filled_ref, grad_ref, own_ref, master_ref, one_ref, two_ref, *refs, first):
-    piece, unit_rows = grad_ref.shape[2:]
-    pieces = all_pieces(grad_ref, own_ref, lax.axis_index("wide"))
-    empty = lax.broadcasted_iota(jnp.int32, (unit_rows, 128), 0) * 0 + pl.program_id(0) + first
-    gradient = jnp.where(
-        empty < filled_ref[0], unit_gradient(pieces, piece, unit_rows), 0.0
-    )
-    apply_update(gradient, master_ref, one_ref, two_ref, refs[-5:])
+    _, step, piece, unit_rows = grad_ref.shape
+    for k in range(step):
+        pieces = all_pieces(grad_ref, own_ref, lax.axis_index("wide"), k)
+        slot = jnp.zeros((unit_rows, 1), jnp.int32) + (pl.program_id(0) * step + k + first)
+        gradient = jnp.where(
+            slot < filled_ref[0], unit_gradient(pieces, piece, unit_rows), 0.0
+        )
+        apply_update(gradient, master_ref, one_ref, two_ref, refs[-5:], k)
 
 
 def update_outs(master):
@@ -353,14 +366,15 @@
 def update_units(filled, grads, own, first, master, moment_one, moment_two, done, deps=()):
     _, _, unit_rows, unit_cols = master.shape
     parts, slots, piece, _ = grads.shape
-    unit = blocks((1, 1, unit_rows, unit_cols), lambda s, *refs: (s + first, 0, 0, 0))
+    step = 2 if slots % 2 == 0 and first % 2 == 0 else 1
+    unit = blocks((step, 1, unit_rows, unit_cols), lambda s: (s + first // step, 0, 0, 0))
     return call(
         functools.partial(update_kernel, first=first),
         [filled, grads, own, master, moment_one, moment_two, *done],
         [
             SMEM,
-            blocks((parts, 1, piece, unit_rows), lambda s: (0, s, 0, 0)),
-            blocks((1, 1, piece, unit_rows), lambda s: (lax.axis_index("wide"), s, 0, 0)),
+            blocks((parts, step, piece, unit_rows), lambda s: (0, s, 0, 0)),
+            blocks((1, step, piece, unit_rows), lambda s: (lax.axis_index("wide"), s, 0, 0)),
             unit,
             unit,
             unit,
@@ -368,7 +382,7 @@
         + [ANY] * len(done),
         update_outs(master),
         [unit] * 5,
-        grid=(slots,),
+        grid=(slots // step,),
         aliases={6 + k: k for k in range(len(done))},
         moved=master.size * 16,
         mib=40,
@@ -1072,7 +1086,7 @@
             out_ref[...] = total
 
 
-def sum_entries(first, second):
+def sum_entries(first, second, **beside):
     count, rows, width = first.shape
     given = blocks((1, rows, width), lambda i: (i, 0, 0))
     return call(
@@ -1084,61 +1098,84 @@
         grid=(count,),
         moved=first.size * 6,
         name="sum_entries",
-    )
-
-
-def ff_meet_kernel(own_ref, other_ref, *outs):
+        **beside,
+    )
+
+
+def ff_meet_kernel(own_ref, other_ref, first_out, second_out):
     total = (own_ref[...].astype(f32) + other_ref[...].astype(f32)).astype(bf16)
-    half = total.shape[0] // 2
-    for r in range(3):
-
-        @pl.when(pl.program_id(0) == r)
-        def _(r=r):
-            outs[r][...] = total
-
-    @pl.when(pl.program_id(0) == 3)
-    def _():
-        outs[3][...] = total[:half]
-        outs[4][...] = total[half:]
+    half = first_out.shape[0]
+    first_out[...] = total[:half]
+    second_out[...] = total[half:]
 
 
 def ff_meet(own, other, deps=()):
-    height, width = own.shape
-    rows = height // 4
-    given = blocks((rows, width), lambda i: (i, 0))
-    sizes = [rows, rows, rows, rows // 2, rows // 2]
+    rows, width = own.shape[0] // 4, own.shape[1]
+    last = blocks((rows, width), lambda i: (3, 0))
+    half = blocks((rows // 2, width), lambda i: (0, 0))
     return call(
         ff_meet_kernel,
         [own, other],
-        [given, given],
-        [shaped((size, width)) for size in sizes],
-        [blocks((size, width), lambda i: (0, 0)) for size in sizes],
-        grid=(4,),
+        [last, last],
+        [shaped((rows // 2, width))] * 2,
+        [half, half],
+        grid=(1,),
         deps=deps,
-        moved=own.size * 6,
+        moved=own.size * 2,
         name="ff_meet",
     )
 
 
-def ff_join_kernel(x_ref, first_ref, y_ref, second_ref, x_out, y_out):
+def ff_join_kernel(
+    own_x, other_x, first_ref, own_y, other_y, second_ref, x_out, y_out
+):
     half = first_ref.shape[0]
-    x_out[:half] = (x_ref[:half].astype(f32) + first_ref[...].astype(f32)).astype(bf16)
-    x_out[half:] = x_ref[half:]
-    y_out[:half] = y_ref[:half]
-    y_out[half:] = (y_ref[half:].astype(f32) + second_ref[...].astype(f32)).astype(bf16)
-
-
-def ff_join(met, first, second, deps=()):
-    shape = shaped(met[1].shape)
+    x = own_x[...].astype(f32) + other_x[...].astype(f32)
+    y = own_y[...].astype(f32) + other_y[...].astype(f32)
+    x_out[:half] = (x[:half] + first_ref[...].astype(f32)).astype(bf16)
+    x_out[half:] = x[half:].astype(bf16)
+    y_out[:half] = y[:half].astype(bf16)
+    y_out[half:] = (y[half:] + second_ref[...].astype(f32)).astype(bf16)
+
+
+def ff_join(own, other, first, second, deps=()):
+    rows, width = own.shape[0] // 4, own.shape[1]
+
+    def quarter(k):
+        return blocks((rows, width), lambda i: (k, 0))
+
+    half = blocks((rows // 2, width), lambda i: (0, 0))
+    shape = shaped((rows, width))
     return call(
         ff_join_kernel,
-        [met[1], first, met[2], second],
-        [VMEM] * 4,
+        [own, other, first, own, other, second],
+        [quarter(1), quarter(1), half, quarter(2), quarter(2), half],
         [shape, shape],
-        [VMEM] * 2,
+        [quarter(0), quarter(0)],
+        grid=(1,),
         deps=deps,
-        moved=met[1].size * 8,
+        moved=own.size * 4,
         name="ff_join",
+    )
+
+
+def ff_end_kernel(*refs):
+    refs[-1][...] = sum(ref[...].astype(f32) for ref in refs[:-1]).astype(bf16)
+
+
+def ff_end(own, other, near, deps=()):
+    rows, width = own.shape[0] // 4, own.shape[1]
+    first = blocks((rows, width), lambda i: (0, 0))
+    return call(
+        ff_end_kernel,
+        [own, other, *near],
+        [first] * (2 + len(near)),
+        shaped((rows, width)),
+        first,
+        grid=(1,),
+        deps=deps,
+        moved=own.size * 2,
+        name="ff_end",
     )
 
 
@@ -1350,9 +1387,7 @@
     )
     w_qkv = assemble_qkv(turn, rows, near_qkv, other_qkv, piece, unit_cols, sizes)
 
-    cos_table, sin_table = tables(seq_len, HD)
-    cos_all = jnp.concatenate([cos_table] * (LANES // HD), axis=1)
-    sin_all = jnp.concatenate([sin_table] * (LANES // HD), axis=1)
+    cos_all, sin_all = turn_tables(seq_len)
     low_rows = row_count // 2
     cotangent_then = after(cotangent[:low_rows], normed_all, w_qkv)
     back_low = lax.all_gather(cotangent_then, "narrow", axis=0, tiled=True)
@@ -1426,58 +1461,52 @@
         turn, rows, qkv_rows, [narrow_out, out_x, out_y, out_across, out_other], piece,
         unit_cols, narrow_count,
     )
-    sixth = third // 2
-    residual, normed_two, x_second, y_second = branch(
-        attended, attended_others, w_out, tokens, norm_gains[1:2],
-        sends=near_and_across(0, 0, rows_at(ff_first + third, sixth)),
-        sources=[rows],
-        lands=[(sixth, D), (sixth, D)],
-    )
-
-    rest = ff_rows - third - sixth
-    block_one, x_third, y_third, *swapped = move(
+    residual, normed_two = branch(
+        attended, attended_others, w_out, tokens, norm_gains[1:2]
+    )
+
+    rest = ff_rows - third
+    half_rest = ff_rows // 2 - third
+    block_one, x_last, y_last, own_swap, x_first_swap, y_first_swap, x_last_swap, y_last_swap = move(
         [Send(0, 0, "narrow", 1)]
-        + near_and_across(1, 1, rows_at(ff_first + third + sixth, rest))
+        + near_and_across(1, 1, rows_at(ff_first + third, rest))
         + [Send(1, 3, "wide", 1, rows_at(ff_first, ff_rows))]
-        + [Send(2 + k, 4 + k, "wide", 1) for k in range(4)]
+        + [Send(2, 4, "wide", 1), Send(3, 5, "wide", 1)]
         + [
-            Send(1, 8, "wide", 1, landed=True, needs=(1,)),
-            Send(2, 9, "wide", 1, landed=True, needs=(2,)),
+            Send(1, 6, "wide", 1, landed=True, needs=(1,)),
+            Send(2, 7, "wide", 1, landed=True, needs=(2,)),
         ],
-        [normed_two, rows, x_first, x_second, y_first, y_second],
+        [normed_two, rows, x_first, y_first],
         [normed_two.shape, (rest, D), (rest, D), (ff_rows, D)]
-        + [(third, D), (sixth, D)] * 2
+        + [(third, D)] * 2
         + [(rest, D)] * 2,
     )
-    own_swap, x_first_swap, x_second_swap, y_first_swap, y_second_swap = swapped[:5]
-    x_third_swap, y_third_swap = swapped[5:]
-    block_two, across_first, across_second, across_third, *swapped = move(
+    block_two, *across = move(
         [
             Send(0, 0, "narrow", 1),
             Send(1, 1, "wide", 4),
-            Send(2, 2, "wide", 4),
-            Send(3, 3, "wide", 2),
+            Send(2, 2, "wide", 4, rows_at(0, half_rest)),
+            Send(3, 3, "wide", 2, rows_at(half_rest, ff_rows // 2)),
             Send(1, 4, "wide", 1, landed=True, needs=(1,)),
             Send(2, 5, "wide", 1, landed=True, needs=(2,)),
             Send(3, 6, "wide", 1, landed=True, needs=(3,)),
         ],
-        [block_one, x_first, x_second, y_third],
-        [block_one.shape] + [(third, D), (sixth, D), (rest, D)] * 2,
-    )
-    across_swap = swapped
-
-    def pieces(first, second, last):
-        return [(first, 0, third), (second, 0, sixth), (last, 0, rest)]
+        [block_one, x_first, x_last, y_last],
+        [block_one.shape] + [(third, D), (half_rest, D), (ff_rows // 2, D)] * 2,
+    )
+
+    def pieces(*arrays):
+        return [(array, 0, array.shape[0]) for array in arrays]
 
     entries = [
         [(rows, ff_first, ff_rows)],
-        pieces(x_first, x_second, x_third),
-        pieces(y_first, y_second, y_third),
-        pieces(across_first, across_second, across_third),
+        pieces(x_first, x_last),
+        pieces(y_first, y_last),
+        pieces(*across[:3]),
         [(own_swap, 0, ff_rows)],
-        pieces(x_first_swap, x_second_swap, x_third_swap),
-        pieces(y_first_swap, y_second_swap, y_third_swap),
-        pieces(*across_swap),
+        pieces(x_first_swap, x_last_swap),
+        pieces(y_first_swap, y_last_swap),
+        pieces(*across[3:]),
     ]
 
     *kept, total, block_three = ff_step(1, block_one, back_low, back_high, entries, (), block_two)
@@ -1511,36 +1540,39 @@
     )
     out_back = jnp.stack([by_heads[0], heads_one, heads_two, heads_three])
     out_back = jnp.take(out_back, back_by, axis=0).reshape(seq_len, query_width)
-    attn_back_all = lax.all_gather(after(attn_back, heads_two), "narrow", axis=0, tiled=True)
-    output = residual + lax.psum_scatter(
-        after(ff_term, attn_back_all), "narrow", scatter_dimension=0, tiled=True
-    ).astype(f32)
-    met_down = ff_meet(grad_down[0], down_swap)
+    ff_sum = lax.psum_scatter(
+        after(ff_term, heads_two), "narrow", scatter_dimension=0, tiled=True
+    )
+    output = residual + ff_sum.astype(f32)
+    down_across = ff_meet(grad_down[0], down_swap)
     *grad_upper, gate_swap, down_a, down_b = outer(
         dup, mlp_all, 2,
         sends=[Send(0, 0, "wide", 1)] + across_sends(1, 1),
-        sources=[grad_gate[1], *met_down[3:]],
+        sources=[grad_gate[1], *down_across],
         lands=[grad_gate[1].shape, half_shape, half_shape],
     )
-    joined_down = ff_join(met_down, down_a, down_b)
-    met_gate = ff_meet(grad_gate[0], gate_swap)
+    joined_down = ff_join(grad_down[0], down_swap, down_a, down_b)
+    gate_across = ff_meet(grad_gate[0], gate_swap)
 
     qkv_back = [None, None]
     qkv_back[0], upper_swap, gate_a, gate_b, down_x, down_y = attend_backward(
         0, groups, length, qkv, out_back, attended, logs, cos_all, sin_all, block,
         sends=[Send(0, 0, "wide", 1)] + across_sends(1, 1) + near_sends(3, 3),
-        sources=[grad_upper[1], *met_gate[3:], *joined_down],
+        sources=[grad_upper[1], *gate_across, *joined_down],
         lands=[grad_upper[1].shape, half_shape, half_shape, near_shape, near_shape],
     )
-    joined_gate = ff_join(met_gate, gate_a, gate_b)
-    met_upper = ff_meet(grad_upper[0], upper_swap)
+    upper_across = ff_meet(grad_upper[0], upper_swap)
+    joined_gate = ff_join(grad_gate[0], gate_swap, gate_a, gate_b)
     qkv_back[1], upper_a, upper_b, gate_x, gate_y = attend_backward(
         1, groups, length, qkv, out_back, attended, logs, cos_all, sin_all, block,
         sends=across_sends(0, 0) + near_sends(2, 2),
-        sources=[*met_upper[3:], *joined_gate],
+        sources=[*upper_across, *joined_gate],
         lands=[half_shape] * 2 + [near_shape] * 2,
     )
-    joined_upper = ff_join(met_upper, upper_a, upper_b)
+    attn_back_all = lax.all_gather(
+        after(attn_back, ff_sum, qkv_back[1]), "narrow", axis=0, tiled=True
+    )
+    joined_upper = ff_join(grad_upper[0], upper_swap, upper_a, upper_b)
     half_rows = near_shape[0] // 2
     halves = [
         [
@@ -1553,16 +1585,20 @@
         qkv_back, w_qkv, row_count,
         sends=halves[0], sources=list(joined_upper), lands=[half_shape] * 2,
     )
+    down_sum = ff_end(grad_down[0], down_swap, [down_x, down_y], (norm_one_term,))
+    gate_sum = ff_end(grad_gate[0], gate_swap, [gate_x, gate_y], (norm_one_term,))
     *grad_qkv, upper_xb, upper_yb = outer_pair(
         qkv_back, normed_all, (norm_one_term,),
         sends=halves[1], sources=list(joined_upper), lands=[half_shape] * 2,
     )
-    ff_sums = [
-        add([met_gate[0], gate_x, gate_y], deps=(norm_one_term,)),
-        add([met_upper[0][:half_rows], upper_xa, upper_ya], deps=(grad_qkv[0],)),
-        add([met_upper[0][half_rows:], upper_xb, upper_yb]),
-        add([met_down[0], down_x, down_y], deps=(norm_one_term,)),
-    ]
+    upper_sum = ff_end(
+        grad_upper[0], upper_swap,
+        [
+            jnp.concatenate([upper_xa, upper_xb], axis=0),
+            jnp.concatenate([upper_ya, upper_yb], axis=0),
+        ],
+    )
+    ff_sums = [gate_sum, upper_sum, down_sum]
 
     slots = wide_count * capacity
     unit_of = jnp.zeros((slots,), jnp.int32).at[slot_place].set(
@@ -1585,10 +1621,6 @@
     def by_narrow(wide, narrow):
         return narrow
 
-    (grad_out,) = outer(attended, attn_back_all, 1, (grad_qkv[0],))
-    own_attn, other_attn = arrange_attn(
-        turn, [*grad_qkv, grad_out], piece, unit_cols, sizes
-    )
     gain_one = sum(
         jnp.sum(
             w_qkv[g * group_width : (g + 1) * group_width].astype(f32) * grad_qkv[g].astype(f32),
@@ -1597,8 +1629,7 @@
         for g in range(groups)
     )
     gain_terms = jnp.stack([gain_one / norm_gains[0], gain_two])
-    owned_high = lax.all_to_all(high, "wide", split_axis=0, concat_axis=0)
-    owned_low, attn_swap, gain_others = move(
+    owned_low, gain_others = move(
         [
             Send(
                 0, 0, "wide", e,
@@ -1607,13 +1638,24 @@
             )
             for e in range(1, wide_count)
         ]
-        + [Send(1, 1, "wide", 1)]
-        + [Send(2, 2, "wide", e, None, by_wide) for e in range(1, wide_count)],
-        [low, other_attn, gain_terms],
-        [low.shape, other_attn.shape, ((wide_count, *gain_terms.shape), f32)],
+        + [Send(1, 1, "wide", e, None, by_wide) for e in range(1, wide_count)],
+        [low, gain_terms],
+        [low.shape, ((wide_count, *gain_terms.shape), f32)],
+    )
+    owned_high = lax.all_to_all(after(high, owned_low), "wide", split_axis=0, concat_axis=0)
+    gain_plane = sum_places(wide_index.reshape(1), gain_terms, gain_others)
+    (grad_out,) = outer(attended, attn_back_all, 1, (owned_low,))
+    own_attn, other_attn = arrange_attn(
+        turn, [*grad_qkv, grad_out], piece, unit_cols, sizes
+    )
+    attn_swap, gain_others = move(
+        [Send(0, 0, "wide", 1)]
+        + [Send(1, 1, "narrow", k, None, by_narrow) for k in range(1, narrow_count)],
+        [other_attn, gain_plane],
+        [other_attn.shape, ((narrow_count, *gain_terms.shape), f32)],
     )
     met_attn = sum_entries(own_attn, attn_swap)
-    gain_plane = sum_places(wide_index.reshape(1), gain_terms, gain_others)
+    gain_grads = sum_places(narrow_index.reshape(1), gain_plane, gain_others)
     filled = jnp.concatenate(
         [lax.dynamic_slice(counts, (wide_index,), (1,)), wide_index.reshape(1)]
     ).astype(jnp.int32)
@@ -1621,23 +1663,13 @@
     updated = update_units(
         filled, owned_low, low, 0, master, moment_one, moment_two, (), (met_attn[0],)
     )
-    gain_others = jnp.stack(
-        [gain_plane]
-        + [
-            after(lax.ppermute(gain_plane, "narrow", shift(narrow_count, k)), updated[0])
-            for k in range(1, narrow_count)
-        ]
-    )
-    gain_grads = sum_places(
-        narrow_index.reshape(1), gain_plane, jnp.take(gain_others, back_by, axis=0)
-    )
-    attn_sum = add([met_attn[0]] + arrived, deps=(updated[0],))
+    attn_sum = add([met_attn[0]] + [after(part, updated[0]) for part in arrived])
+    near = [flip(attn_sum, 2 * r) for r in (1, 2, 3)]
     updated = update_units(
-        filled, owned_high, owned_high, capacity // 2, master, moment_one, moment_two, updated
-    )
-    near = [attn_sum] + [
-        after(flip(attn_sum, 2 * r), updated[0]) for r in (1, 2, 3)
-    ]
+        filled, owned_high, owned_high, low.shape[1], master, moment_one, moment_two, updated,
+        (attn_sum,),
+    )
+    near = [attn_sum] + [after(part, updated[0]) for part in near]
     other = [flip(part, 1) for part in near]
     attn_grads = [attn_sum.reshape(attn_blocks, piece, D)] + [
         jnp.stack(part).reshape(wide_count // 2, attn_blocks, piece, D)
@@ -1666,7 +1698,8 @@
 
     norm_one_back = lax.psum_scatter(
         norm_one_term, "narrow", scatter_dimension=0, tiled=True
-    ).astype(f32)
+    )
+    norm_one_back = after(norm_one_back, owned_grads).astype(f32)
     _, norm_one_pull = jax.vjp(lambda values: rmsnorm(values, norm_gains[0]), inputs)
     (input_part,) = norm_one_pull(norm_one_back)
     input_grad = (resid_back + input_part).astype(bf16)

time: 1030 us -> 1010 us (0.981)
  Pallas kernels: 887 us -> 861 us
    pallas_call x55 -> x57, Pallas kernels: 887 us -> 861 us  [call(): pl.pallas_call(wrapped, grid_spec=pltpu.PrefetchScalarGridSpec(num_scalar...]
  transfers between devices with their start and end apart: 20 -> 17, of which waited for: 3 -> 3; matrix products, arithmetic and copies ran while one was open for 4% -> 3% of each run, Pallas kernels for 66% -> 65%
where the time goes in v5:
time: 1010 us; the launch traced here: 998 us
  Pallas kernels  861 us (85%)
  local copies, waits for them, and re-layouts  51.1 us (5%)
  other arithmetic  41.7 us (4%)
  between operations  16.6 us (2%)
  waiting for transfers between devices  14.1 us (1%)
  starting transfers between devices  13.2 us (1%)
    pallas_call x57, Pallas kernels, call(): pl.pallas_call(wrapped, grid_spec=pltpu.PrefetchScalarGridSpec(num_scalar...  861 us
    unnamed x160, local copies, waits for them, and re-layouts  42.7 us
  transfers between devices with their start and end apart: 17, of which 3 were waited for; matrix products, arithmetic and copies ran while one was open for 3% of the time, Pallas kernels for 65%

profile of v5, /device:TPU:0, one launch (start us, length us, event | category | flops | bytes accessed | tf_op | source)
XLA Modules:
  0.0 998.1 jit_solution(1347238632701543517)
XLA Ops:
  25.7 78.4 %move.7.refs_3_ = bf16[8,26,16,1024]{3,2,1,0:T(8,128)(2,1)} custom-call(bf16[8,26,16,1024]{3,2,1,0:T(8,128)(2,1)} %copy-done.2), custom_call_target="tpu_custom_call" | custom-call | tf_op jit(solution)/shard_map/move/pallas_call | solution.py:167
  112.4 23.2 %move.8 = (bf16[3,96,2048]{2,1,0:T(8,128)(2,1)}, bf16[4,96,2048]{2,1,0:T(8,128)(2,1)}) custom-call(bf16[928,2048]{1,0:T(8,128)(2,1)} %pick_units.1.refs_0_.refs_1_.refs_2_.refs_3_), custom_call_target="tpu_custom_call" | custom-call | tf_op jit(solution)/shard_map/move/pallas_call | solution.py:167
  143.3 10.7 %project.1.refs_1_ = bf16[1536,768]{1,0:T(8,128)(2,1)} custom-call(bf16[1536,2048]{1,0:T(8,128)(2,1)} %all-gather.5.cloned.1.call-done.refs_1_.refs_0_.refs_2_, bf16[768,2048]{1,0:T(8,128)(2,1)} %copy-done.6, f32[1536,128]{1,0:T(8,128)} %constant.102.clone.refs_2_.refs_5_, f32[1536,128]{1,0:T(8,128)} %constant.103.clone.refs_3_.refs_6_, ...), custom_call_target="tpu_custom_call" | custom-call | flops 4831838208 | tf_op jit(solution)/shard_map/project/pallas_call | solution.py:167
  154.0 40.8 %attend_forward.1 = (bf16[1536,512]{1,0:T(8,128)(2,1)S(1)}, f32[2,8,1536]{2,1,0:T(8,128)S(1)}, bf16[3,64,2048]{2,1,0:T(8,128)(2,1)S(1)}, bf16[256,2048]{1,0:T(8,128)(2,1)S(1)}, bf16[256,2048]{1,0:T(8,128)(2,1)S(1)}) custom-call(s32[1]{0:T(128)} %dynamic_slice.12.refs_0_, bf16[1536,768]{1,0:T(8,128)(2,1)} %project.1.refs_1_, ...), custom_call_target="tpu_custom_call" | custom-call | flops 9663676416 | tf_op jit(solution)/shard_map/attend_forward/pallas_call | solution.py:167
  198.7 60.3 %move.9 = (bf16[3,384,512]{2,1,0:T(8,128)(2,1)}, bf16[4,64,2048]{2,1,0:T(8,128)(2,1)}, bf16[4,64,2048]{2,1,0:T(8,128)(2,1)}, bf16[4,64,2048]{2,1,0:T(8,128)(2,1)}, bf16[4,4,64,2048]{3,2,1,0:T(8,128)(2,1)}) custom-call(bf16[1536,512]{1,0:T(8,128)(2,1)} %copy-done.11, bf16[928,2048]{1,0:T(8,128)(2,1)} %pick_units.1.refs_0_.refs_1_.refs_2_.refs_3_, ...), custom_call_target="tpu_custom_call" | custom-call | tf_op jit(solution)/shard_map/move/pallas_call | solution.py:167
  267.5 10.7 %branch.1 = (f32[384,2048]{1,0:T(8,128)}, bf16[384,2048]{1,0:T(8,128)(2,1)}) custom-call(bf16[1536,512]{1,0:T(8,128)(2,1)} %copy-done.11, bf16[3,384,512]{2,1,0:T(8,128)(2,1)} %get-tuple-element.142.refs_1_, bf16[2048,2048]{1,0:T(8,128)(2,1)} %assemble_out.1.refs_2_, bf16[384,2048]{1,0:T(8,128)(2,1)} %refs_3_.4, f32[1,2048]{1,0:T(1,128)} %get-tuple-element.289.refs_4_), custom_call_target="tpu_custom_call" | custom-call | flops 3221225472 | tf_op jit(solution)/shard_map/branch/pallas_call | solution.py:167
  278.2 75.2 %move.10 = (bf16[384,2048]{1,0:T(8,128)(2,1)}, bf16[512,2048]{1,0:T(8,128)(2,1)}, bf16[512,2048]{1,0:T(8,128)(2,1)}, bf16[768,2048]{1,0:T(8,128)(2,1)}, bf16[256...) custom-call(bf16[384,2048]{1,0:T(8,128)(2,1)} %get-tuple-element.148.refs_, ...), custom_call_target="tpu_custom_call" | custom-call | tf_op jit(solution)/shard_map/move/pallas_call | solution.py:167
  353.4 46.3 %move.11 = (bf16[384,2048]{1,0:T(8,128)(2,1)}, bf16[256,2048]{1,0:T(8,128)(2,1)}, bf16[128,2048]{1,0:T(8,128)(2,1)}, bf16[384,2048]{1,0:T(8,128)(2,1)}, bf16[256...) custom-call(bf16[384,2048]{1,0:T(8,128)(2,1)} %get-tuple-element.153.refs_0_, ...), custom_call_target="tpu_custom_call" | custom-call | tf_op jit(solution)/shard_map/move/pallas_call | solution.py:167
  400.0 40.3 %ff_step.4 = (bf16[1536,2048]{1,0:T(8,128)(2,1)}, bf16[1536,2048]{1,0:T(8,128)(2,1)}, bf16[1536,2048]{1,0:T(8,128)(2,1)}, bf16[1536,2048]{1,0:T(8,128)(2,1)}, bf...) custom-call(bf16[384,2048]{1,0:T(8,128)(2,1)} %get-tuple-element.153, ...), custom_call_target="tpu_custom_call" | custom-call | flops 16106127360 | tf_op jit(solution)/shard_map/ff_step/pallas_call | solution.py:167
  440.3 39.5 %ff_step.5 = (bf16[1536,2048]{1,0:T(8,128)(2,1)}, bf16[1536,2048]{1,0:T(8,128)(2,1)}, bf16[1536,2048]{1,0:T(8,128)(2,1)}, bf16[1536,2048]{1,0:T(8,128)(2,1)}, bf...) custom-call(bf16[384,2048]{1,0:T(8,128)(2,1)} %get-tuple-element.165, ...), custom_call_target="tpu_custom_call", output_to_operand_aliasing={{0}: (19, {}), {1}: (20, {}), {2}: (21, {}), {3}: (22, {}),... | custom-call | flops 16106127360 | tf_op jit(solution)/shard_map/ff_step/pallas_call | solution.py:167
  479.8 38.6 %ff_step.6 = (bf16[1536,2048]{1,0:T(8,128)(2,1)}, bf16[1536,2048]{1,0:T(8,128)(2,1)}, bf16[1536,2048]{1,0:T(8,128)(2,1)}, bf16[1536,2048]{1,0:T(8,128)(2,1)}, bf...) custom-call(bf16[384,2048]{1,0:T(8,128)(2,1)} %get-tuple-element.166, ...), custom_call_target="tpu_custom_call", output_to_operand_aliasing={{0}: (19, {}), {1}: (20, {}), {2}: (21, {}), {3}: (22, {}),... | custom-call | flops 16106127360 | tf_op jit(solution)/shard_map/ff_step/pallas_call | solution.py:167
  518.4 39.3 %ff_step.7 = (bf16[1536,2048]{1,0:T(8,128)(2,1)}, bf16[1536,2048]{1,0:T(8,128)(2,1)}, bf16[1536,2048]{1,0:T(8,128)(2,1)}, bf16[1536,2048]{1,0:T(8,128)(2,1)}, bf...) custom-call(bf16[384,2048]{1,0:T(8,128)(2,1)} %get-tuple-element.148, ...), custom_call_target="tpu_custom_call", output_to_operand_aliasing={{0}: (19, {}), {1}: (20, {}), {2}: (21, {}), {3}: (22, {}),... | custom-call | flops 16106127360 | tf_op jit(solution)/shard_map/ff_step/pallas_call | solution.py:167
  572.0 23.1 %outer.4 = (bf16[1024,2048]{1,0:T(8,128)(2,1)}, bf16[1024,2048]{1,0:T(8,128)(2,1)}, bf16[384,512]{1,0:T(8,128)(2,1)}, bf16[384,512]{1,0:T(8,128)(2,1)}) custom-call(bf16[1536,2048]{1,0:T(8,128)(2,1)} %get-tuple-element.192.refs_0_, bf16[1536,2048]{1,0:T(8,128)(2,1)} %get-tuple-element.193.refs_1_, bf16[4,384,512]{2,1,0:T(8,128)(2,1)} %copy-done.33), custom_call_target="tpu_custom_call" | custom-call | flops 12884901888 | tf_op jit(solution)/shard_map/outer/pallas_call | solution.py:167
  595.1 26.5 %outer.5 = (bf16[1024,2048]{1,0:T(8,128)(2,1)}, bf16[1024,2048]{1,0:T(8,128)(2,1)}, bf16[384,512]{1,0:T(8,128)(2,1)}, bf16[1024,2048]{1,0:T(8,128)(2,1)}) custom-call(bf16[1536,2048]{1,0:T(8,128)(2,1)} %get-tuple-element.189.refs_0_, bf16[1536,2048]{1,0:T(8,128)(2,1)} %get-tuple-element.190.refs_1_, bf16[4,384,512]{2,1,0:T(8,128)(2,1)} %copy-done.33, ...), custom_call_target="tpu_custom_call" | custom-call | flops 12884901888 | tf_op jit(solution)/shard_map/outer/pallas_call | solution.py:167
  629.4 21.5 %outer.6 = (bf16[1024,2048]{1,0:T(8,128)(2,1)}, bf16[1024,2048]{1,0:T(8,128)(2,1)}, bf16[1024,2048]{1,0:T(8,128)(2,1)}, bf16[128,2048]{1,0:T(8,128)(2,1)}, bf16[128,2048]{1,0:T(8,128)(2,1)}) custom-call(bf16[1536,2048]{1,0:T(8,128)(2,1)} %get-tuple-element.199.refs_0_, bf16[1536,2048]{1,0:T(8,128)(2,1)} %get-tuple-element.190.refs_1_, ...), custom_call_target="tpu_custom_call" | custom-call | flops 12884901888 | tf_op jit(solution)/shard_map/outer/pallas_call | solution.py:167
  660.1 39.5 %attend_backward.2 = (bf16[1536,384]{1,0:T(8,128)(2,1)}, bf16[1024,2048]{1,0:T(8,128)(2,1)}, bf16[128,2048]{1,0:T(8,128)(2,1)S(1)}, bf16[128,2048]{1,0:T(8,128)(...) custom-call(s32[1]{0:T(128)} %dynamic_slice.12.refs_0_, bf16[1536,768]{1,0:T(8,128)(2,1)} %project.1.refs_1_, ...), custom_call_target="tpu_custom_call" | custom-call | flops 12079595520 | tf_op jit(solution)/shard_map/attend_backward/pallas_call | solution.py:167
  712.6 38.7 %attend_backward.3 = (bf16[1536,384]{1,0:T(8,128)(2,1)}, bf16[128,2048]{1,0:T(8,128)(2,1)S(1)}, bf16[128,2048]{1,0:T(8,128)(2,1)S(1)}, bf16[256,2048]{1,0:T(8,128)(2,1)S(1)}, bf16[256,2048]{1,0:T(8,128)(2,1)S(1)}) custom-call(s32[1]{0:T(128)} %dynamic_slice.12.refs_0_, bf16[1536,768]{1,0:T(8,128)(2,1)} %project.1.refs_1_, ...), custom_call_target="tpu_custom_call" | custom-call | flops 12079595520 | tf_op jit(solution)/shard_map/attend_backward/pallas_call | solution.py:167
  759.2 15.7 %first_back.1 = (bf16[1536,2048]{1,0:T(8,128)(2,1)}, bf16[128,2048]{1,0:T(8,128)(2,1)}, bf16[128,2048]{1,0:T(8,128)(2,1)}) custom-call(bf16[1536,384]{1,0:T(8,128)(2,1)} %get-tuple-element.214.refs_0_, bf16[1536,384]{1,0:T(8,128)(2,1)} %get-tuple-element.223.refs_1_.refs_2_, bf16[768,2048]{1,0:T(8,128)(2,1)} %copy-done.6, bf16[768,2048]{1,0:T(8,128)(2,1)} %copy-done.6, ...), custom_call_target="tpu_custom_call" | custom-call | flops 4831838208 | tf_op jit(solution)/shard_map/first_back/pallas_call | solution.py:167
  783.9 16.5 %outer_pair.1 = (bf16[384,2048]{1,0:T(8,128)(2,1)}, bf16[384,2048]{1,0:T(8,128)(2,1)}, bf16[128,2048]{1,0:T(8,128)(2,1)}, bf16[128,2048]{1,0:T(8,128)(2,1)}) custom-call(bf16[1536,384]{1,0:T(8,128)(2,1)} %get-tuple-element.214.refs_0_, bf16[1536,384]{1,0:T(8,128)(2,1)} %get-tuple-element.223.refs_1_.refs_2_, ...), custom_call_target="tpu_custom_call" | custom-call | flops 4831838208 | tf_op jit(solution)/shard_map/outer_pair/pallas_call | solution.py:167
  817.3 39.8 %move.12 = (bf16[8,12,16,1024]{3,2,1,0:T(8,128)(2,1)}, f32[8,2,2048]{2,1,0:T(2,128)}) custom-call(bf16[8,12,16,1024]{3,2,1,0:T(8,128)(2,1)} %get-tuple-element.239.refs_0_.refs_2_.refs_8_, f32[2,2048]{1,0:T(2,128)} %pad_maximum_fusion.6.refs_1_), custom_call_target="tpu_custom_call" | custom-call | tf_op jit(solution)/shard_map/move/pallas_call | solution.py:167
  881.8 10.2 %move.13 = (bf16[4,160,2048]{2,1,0:T(8,128)(2,1)}, f32[4,2,2048]{2,1,0:T(2,128)}) custom-call(bf16[4,160,2048]{2,1,0:T(8,128)(2,1)} %copy-done.20, f32[2,2048]{1,0:T(2,128)} %sum_places.2.refs_1_), custom_call_target="tpu_custom_call" | custom-call | tf_op jit(solution)/shard_map/move/pallas_call | solution.py:167
  907.3 17.2 %update_units.2 = (f32[26,1,1024,128]{3,2,1,0:T(8,128)}, f32[26,1,1024,128]{3,2,1,0:T(8,128)}, bf16[26,1,1024,128]{3,2,1,0:T(8,128)(2,1)}, f32[26,1,1024,128]{3,2,1,0:T(8,128)}, f32[26,1,1024,128]{3,2,1,0:T(8,128)}) custom-call(s32[2]{0:T(128)S(1)} %pad_add_fusion.2.refs_0_, bf16[8,12,16,1024]{3,2,1,0:T(8,128)(2,1)S(1)} %copy-done.3, ...), custom_call_target="tpu_custom_call" | custom-call | bytes 54525952 | tf_op jit(solution)/shard_map/update_units/pallas_call | solution.py:167
  924.5 8.7 collective-permute-done.1.refs_0_
  944.0 22.7 %update_units.3 = (f32[26,1,1024,128]{3,2,1,0:T(8,128)}, f32[26,1,1024,128]{3,2,1,0:T(8,128)}, bf16[26,1,1024,128]{3,2,1,0:T(8,128)(2,1)}, f32[26,1,1024,128]{3,2,1,0:T(8,128)}, f32[26,1,1024,128]{3,2,1,0:T(8,128)}) custom-call(s32[2]{0:T(128)S(1)} %pad_add_fusion.2.refs_0_, ...), custom_call_target="tpu_custom_call", output_to_operand_aliasing={{0}: (6, {}), {1}: (7, {}), {2}: (8, {}), {3}: (9, {}), {4}... | custom-call | bytes 54525952 | tf_op jit(solution)/shard_map/update_units/pallas_call | solution.py:167
  (286 shorter events, 198.4 us)
Async XLA Ops:
  7.2 134.8 %all-gather.5.cloned.1.call-start = ((), (), s32[]{:S(2)}) async-start(), calls=%async_computation.3 | async-start | bytes 7864320 | tf_op jit(solution)/shard_map/all_gather | solution.py:1362
  14.6 244.5 %all-gather.7.cloned.1.call-start = ((), (), s32[]{:S(2)}) async-start(), calls=%async_computation.4 | async-start | bytes 3932160 | tf_op jit(solution)/shard_map/all_gather | solution.py:1393
  25.7 78.4 %copy-start.74 = (s32[116]{0:T(128)S(1)}, s32[116]{0:T(128)}, u32[]{:S(2)}) copy-start(s32[116]{0:T(128)} %param.15) | copy-start | bytes 1396
  112.4 23.2 %copy-start = (bf16[928,2048]{1,0:T(8,128)(2,1)S(1)}, bf16[928,2048]{1,0:T(8,128)(2,1)}, u32[]{:S(2)}) copy-start(bf16[928,2048]{1,0:T(8,128)(2,1)} %pick_units.1.refs_0_.refs_1_.refs_2_.refs_3_) | copy-start | bytes 11403268
  112.4 23.2 %copy-start.34 = (s32[2]{0:T(128)S(1)}, s32[2]{0:T(128)}, u32[]{:S(2)}) copy-start(s32[2]{0:T(128)} %pad_add_fusion.refs_0_) | copy-start | bytes 28
  142.1 258.0 %all-gather.9.cloned.1.call-start = ((), (), s32[]{:S(2)}) async-start(), calls=%async_computation.5 | async-start | bytes 3932160 | tf_op jit(solution)/shard_map/all_gather | solution.py:1457
  259.1 495.7 %reduce-scatter.3.cloned.1.call-start = ((), (), s32[]{:S(2)}) async-start(), calls=%async_computation.6 | async-start | bytes 7864320 | tf_op jit(solution)/shard_map/reduce_scatter | solution.py:1543
  353.4 46.3 %copy-start.41 = (f32[384,2048]{1,0:T(8,128)S(1)}, f32[384,2048]{1,0:T(8,128)}, u32[]{:S(2)}) copy-start(f32[384,2048]{1,0:T(8,128)} %get-tuple-element.147) | copy-start | bytes 9437188
  400.0 161.5 %copy-start.64 = (f32[384]{0:T(512)}, f32[384]{0:T(512)S(1)}, u32[]{:S(2)}) copy-start(f32[384]{0:T(512)S(1)} %fusion.13) | copy-start | bytes 4612
  518.4 39.3 %copy-start.58 = (f32[1,2048]{1,0:T(1,128)S(1)}, f32[1,2048]{1,0:T(1,128)}, u32[]{:S(2)}) copy-start(f32[1,2048]{1,0:T(1,128)} %get-tuple-element.289.refs_4_) | copy-start | bytes 24580
  621.6 246.2 %all-gather.11.cloned.1.call-start = ((), (), s32[]{:S(2)}) async-start(), calls=%async_computation.8 | async-start | bytes 7864320 | tf_op jit(solution)/shard_map/all_gather | solution.py:1572
  754.9 226.4 %reduce-scatter.5.cloned.1.call-start = ((), (), s32[]{:S(2)}) async-start(), calls=%async_computation.7 | async-start | bytes 7864320 | tf_op jit(solution)/shard_map/reduce_scatter | solution.py:1699
  783.9 16.5 %copy-start.7 = (bf16[768,2048]{1,0:T(8,128)(2,1)S(1)}, bf16[768,2048]{1,0:T(8,128)(2,1)}, u32[]{:S(2)}) copy-start(bf16[768,2048]{1,0:T(8,128)(2,1)} %copy-done.6) | copy-start | bytes 9437188
  857.1 85.8 %all-to-all-start = ((bf16[8,14,16,1024]{3,2,1,0:T(8,128)(2,1)}), bf16[8,14,16,1024]{3,2,1,0:T(8,128)(2,1)}, u32[]{:S(2)}, u32[]{:S(2)}) async-start(bf16[8,14,16,1024]{3,2,1,0:T(8,128)(2,1)} %after.19), calls=%async_computation.2 | async-start | bytes 7340032 | tf_op jit(solution)/shard_map/all_to_all | solution.py:1645
  897.4 27.1 %collective-permute-start.2 = (bf16[160,2048]{1,0:T(8,128)(2,1)}, bf16[160,2048]{1,0:T(8,128)(2,1)}, u32[]{:S(2)}, u32[]{:S(2)}) collective-permute-start(bf16[160,2048]{1,0:T(8,128)(2,1)} %get-tuple-element.249), channel_id=1, source_target_pairs={{0,24},{4,28},{8,16},{12,20},{16,8},{20,12},{24,0},{28,4},{1,25},{... | collective-permute-start | bytes 1966088 | tf_op jit(solution)/shard_map/ppermute | solution.py:1023
  899.8 33.4 %collective-permute-start.1 = (bf16[160,2048]{1,0:T(8,128)(2,1)}, bf16[160,2048]{1,0:T(8,128)(2,1)}, u32[]{:S(2)}, u32[]{:S(2)}) collective-permute-start(bf16[160,2048]{1,0:T(8,128)(2,1)} %get-tuple-element.248), channel_id=1, source_target_pairs={{0,16},{4,20},{8,24},{12,28},{16,0},{20,4},{24,8},{28,12},{1,17},{... | collective-permute-start | bytes 1966088 | tf_op jit(solution)/shard_map/ppermute | solution.py:1023
  900.4 32.8 %collective-permute-start = (bf16[160,2048]{1,0:T(8,128)(2,1)}, bf16[160,2048]{1,0:T(8,128)(2,1)}, u32[]{:S(2)}, u32[]{:S(2)}) collective-permute-start(bf16[160,2048]{1,0:T(8,128)(2,1)} %get-tuple-element.246), channel_id=1, source_target_pairs={{0,8},{4,12},{8,0},{12,4},{16,24},{20,28},{24,16},{28,20},{1,9},{5... | collective-permute-start | bytes 1966088 | tf_op jit(solution)/shard_map/ppermute | solution.py:1023
  936.0 30.7 %collective-permute-start.5 = (bf16[160,2048]{1,0:T(8,128)(2,1)}, bf16[160,2048]{1,0:T(8,128)(2,1)}, u32[]{:S(2)}, u32[]{:S(2)}) collective-permute-start(bf16[160,2048]{1,0:T(8,128)(2,1)} %add.210.refs_11_), channel_id=1, source_target_pairs={{0,24},{4,28},{8,16},{12,20},{16,8},{20,12},{24,0},{28,4},{1,25},{... | collective-permute-start | bytes 1966088 | tf_op jit(solution)/shard_map/ppermute | solution.py:1023
  936.7 30.7 %collective-permute-start.4 = (bf16[160,2048]{1,0:T(8,128)(2,1)}, bf16[160,2048]{1,0:T(8,128)(2,1)}, u32[]{:S(2)}, u32[]{:S(2)}) collective-permute-start(bf16[160,2048]{1,0:T(8,128)(2,1)} %add.210.refs_11_), channel_id=1, source_target_pairs={{0,16},{4,20},{8,24},{12,28},{16,0},{20,4},{24,8},{28,12},{1,17},{... | collective-permute-start | bytes 1966088 | tf_op jit(solution)/shard_map/ppermute | solution.py:1023
  938.0 29.5 %collective-permute-start.3 = (bf16[160,2048]{1,0:T(8,128)(2,1)}, bf16[160,2048]{1,0:T(8,128)(2,1)}, u32[]{:S(2)}, u32[]{:S(2)}) collective-permute-start(bf16[160,2048]{1,0:T(8,128)(2,1)} %add.210.refs_11_), channel_id=1, source_target_pairs={{0,8},{4,12},{8,0},{12,4},{16,24},{20,28},{24,16},{28,20},{1,9},{5... | collective-permute-start | bytes 1966088 | tf_op jit(solution)/shard_map/ppermute | solution.py:1023
  942.9 27.7 %collective-permute-start.6 = (bf16[160,2048]{1,0:T(8,128)(2,1)}, bf16[160,2048]{1,0:T(8,128)(2,1)}, u32[]{:S(2)}, u32[]{:S(2)}) collective-permute-start(bf16[160,2048]{1,0:T(8,128)(2,1)} %add.210.refs_11_), channel_id=1, source_target_pairs={{0,4},{4,0},{8,12},{12,8},{16,20},{20,16},{24,28},{28,24},{1,5},{5... | collective-permute-start | bytes 1966088 | tf_op jit(solution)/shard_map/ppermute | solution.py:1023
  966.7 3.9 collective-permute-start.9
  967.4 3.2 collective-permute-start.8
  967.5 3.7 collective-permute-start.7
  (74 other events, 202.0 us)
Sparse Core Ops, SparseCore 0:
  14.7 118.0 all-gather.4
  142.2 110.6 all-gather.6
  259.2 99.1 all-gather.8
  621.8 108.2 reduce-scatter.2
  755.0 112.8 all-gather.10
  870.0 110.0 reduce-scatter.4

commit v6 on v5

--- a/solution.py
+++ b/solution.py
@@ -229,7 +229,7 @@
 def turn_units(master, parts, deps):
     capacity, _, unit_rows, unit_cols = master.shape
     piece = unit_cols // parts
-    step = 2 if capacity % 2 == 0 else 1
+    step = capacity // 2 if capacity % 2 == 0 else 1
     return call(
         turn_kernel,
         [master],
@@ -238,7 +238,7 @@
         blocks((parts, step, piece, unit_rows), lambda s: (0, s, 0, 0)),
         grid=(capacity // step,),
         deps=deps,
-        mib=20,
+        mib=60,
         moved=master.size * 6,
         name="turn_units",
     )
@@ -388,77 +388,6 @@
         mib=40,
         deps=deps,
         name="update_units",
-    )
-
-
-def update_attn_kernel(
-    slot_ref, block_ref, half_ref, count_ref, mine_ref, near_ref, other_ref, grad_ref, own_ref,
-    master_ref, one_ref, two_ref, *refs,
-):
-    entry = pl.program_id(0)
-    parts, _, piece, unit_rows = grad_ref.shape
-
-    @pl.when((entry == 0) | (entry < count_ref[0]))
-    def _():
-        turn = count_ref[2]
-        taken = []
-        for j in range(parts):
-            e = jnp.bitwise_xor(turn, j)
-            near = jnp.where(
-                e == 0, mine_ref[...].astype(f32), near_ref[pl.ds(e // 2, 1), 0].astype(f32)
-            )
-            other = other_ref[pl.ds(e // 2, 1), 0].astype(f32)
-            taken.append(jnp.where(e % 2 == 0, near, other))
-        attn = jnp.concatenate(taken, axis=0)
-        gradient = jnp.where(count_ref[0] > 0, attn, all_pieces(grad_ref, own_ref, turn))
-        gradient = unit_gradient(gradient, piece, unit_rows)
-        gradient = jnp.where(slot_ref[entry] < count_ref[1], gradient, 0.0)
-        apply_update(gradient, master_ref, one_ref, two_ref, refs[-5:])
-
-
-def update_attn(
-    slots, places, halves, count, attn, grads, own, master, moment_one, moment_two, done
-):
-    _, _, unit_rows, unit_cols = master.shape
-    parts, low, piece, _ = grads.shape
-    unit = blocks((1, 1, unit_rows, unit_cols), lambda k, slot, *refs: (slot[k], 0, 0, 0))
-    given = blocks(
-        (parts // 2, 1, piece, unit_rows),
-        lambda k, slot, block, half, count: (0, block[k], 0, half[k]),
-    )
-    return call(
-        update_attn_kernel,
-        [*attn, grads, own, master, moment_one, moment_two, *done],
-        [
-            blocks(
-                (1, piece, unit_rows),
-                lambda k, slot, block, half, count: (block[k], 0, half[k]),
-            ),
-            given,
-            given,
-            blocks(
-                (parts, 1, piece, unit_rows),
-                lambda k, slot, *refs: (0, jnp.minimum(slot[k], low - 1), 0, 0),
-            ),
-            blocks(
-                (1, 1, piece, unit_rows),
-                lambda k, slot, block, half, count: (
-                    count[2], jnp.minimum(slot[k], low - 1), 0, 0
-                ),
-            ),
-            unit,
-            unit,
-            unit,
-        ]
-        + [ANY] * 5,
-        update_outs(master),
-        [unit] * 5,
-        grid=(slots.shape[0],),
-        prefetch=[slots, places, halves, count],
-        aliases={12 + k: k for k in range(5)},
-        moved=master.size * 6,
-        mib=40,
-        name="update_attn",
     )
 
 
@@ -812,15 +741,16 @@
     hid_all, dgate_all, dup_all, rows_kept, back_kept, term_all, _ = refs[-18:-11]
     total, down, rows_ref, back_ref, hid_ref, dgate_ref, dup_ref, _, buffer, sems, own = refs[-11:]
     count = rows_ref.shape[0]
-    half = count // 2
+    low = low_ref.shape[0] // parts
     place = lax.rem(lax.axis_index("narrow") - s + parts, parts)
-    low_place = pl.ds(pl.multiple_of(place * half, half), half)
+    low_place = pl.ds(pl.multiple_of(place * low, low), low)
+    high_place = pl.ds(pl.multiple_of(place * (count - low), count - low), count - low)
     place = pl.ds(pl.multiple_of(place * count, count), count)
     here = pl.ds(s * count, count)
     copies = [
         pltpu.make_async_copy(rows_all_ref, rows_ref, own.at[0]),
-        pltpu.make_async_copy(low_ref.at[low_place], back_ref.at[:half], own.at[1]),
-        pltpu.make_async_copy(high_ref.at[low_place], back_ref.at[half:], own.at[4]),
+        pltpu.make_async_copy(low_ref.at[low_place], back_ref.at[:low], own.at[1]),
+        pltpu.make_async_copy(high_ref.at[high_place], back_ref.at[low:], own.at[4]),
     ]
     for copy in copies:
         copy.start()
@@ -1019,10 +949,6 @@
     return [(i, (i + step) % count) for i in range(count)]
 
 
-def flip(value, bits):
-    return lax.ppermute(value, "wide", [(i, i ^ bits) for i in range(8)])
-
-
 def nothing(*refs):
     pass
 
@@ -1163,7 +1089,7 @@
     refs[-1][...] = sum(ref[...].astype(f32) for ref in refs[:-1]).astype(bf16)
 
 
-def ff_end(own, other, near, deps=()):
+def ff_end(own, other, near, deps=(), **beside):
     rows, width = own.shape[0] // 4, own.shape[1]
     first = blocks((rows, width), lambda i: (0, 0))
     return call(
@@ -1176,6 +1102,7 @@
         deps=deps,
         moved=own.size * 2,
         name="ff_end",
+        **beside,
     )
 
 
@@ -1375,15 +1302,20 @@
     def entry(k):
         return lambda wide, narrow: k
 
-    near_qkv, other_qkv = move(
+    near_qkv, other_qkv, narrow_out = move(
         [Send(0, 0, "wide", 2 * r, qkv_at, entry(r - 1)) for r in (1, 2, 3)]
         + [Send(0, 1, "wide", 1, qkv_at, entry(0))]
+        + [Send(0, 2, "narrow", k, out_at, entry(k - 1)) for k in range(1, narrow_count)]
         + [
             Send(0, 1, "wide", 1, entry(r - 1), entry(r), landed=True, needs=(r - 1,))
             for r in (1, 2, 3)
         ],
         [rows],
-        [(3, qkv_rows, D), (4, qkv_rows, D)],
+        [
+            (3, qkv_rows, D),
+            (4, qkv_rows, D),
+            (narrow_count - 1, out_rows, D),
+        ],
     )
     w_qkv = assemble_qkv(turn, rows, near_qkv, other_qkv, piece, unit_cols, sizes)
 
@@ -1402,18 +1334,20 @@
     def later_entries(wide, narrow):
         return pl.ds(1, narrow_count - 1)
 
-    third = ff_rows // 3
-    attended, logs, narrow_out, x_first, y_first = attend_forward(
+    attended, logs, out_x, out_y = attend_forward(
         length, qkv, groups, block,
         sends=[
-            Send(0, 0, "narrow", k, out_at, entry(k - 1)) for k in range(1, narrow_count)
-        ]
-        + near_and_across(0, 1, rows_at(ff_first, third)),
-        sources=[rows],
-        lands=[(narrow_count - 1, out_rows, D), (third, D), (third, D)],
+            Send(0, 0, "wide", 2, out_at, first_entry),
+            Send(0, 1, "wide", 4, out_at, first_entry),
+            Send(1, 0, "wide", 2, None, later_entries),
+            Send(1, 1, "wide", 4, None, later_entries),
+        ],
+        sources=[rows, narrow_out],
+        lands=[out_shape, out_shape],
     )
 
     half = narrow_count // 2
+    third = ff_rows // 3
 
     def heads_of(k):
         return lambda wide, narrow: pl.ds(
@@ -1424,35 +1358,30 @@
         return lambda wide, narrow: (k, at)
 
     low_part, high_part = pl.ds(0, half), pl.ds(half, narrow_count - half)
-    first_sends = narrow_count - 1
-    attended_others, out_x, out_y, out_across, out_other = move(
+    attended_others, out_across, out_other, x_first, y_first = move(
         [Send(0, 0, "narrow", k, heads_of(k), entry(k - 1)) for k in range(1, narrow_count)]
         + [
-            Send(1, 1, "wide", 2, out_at, first_entry),
-            Send(2, 1, "wide", 2, None, later_entries),
-            Send(1, 2, "wide", 4, out_at, first_entry),
-            Send(2, 2, "wide", 4, None, later_entries),
-            Send(1, 4, "wide", 1, out_at, lambda w, n: (0, 0)),
-            Send(2, 4, "wide", 1, None, lambda w, n: (0, later_entries(w, n))),
+            Send(2, 1, "wide", 4, lambda w, n: low_part, lambda w, n: low_part),
+            Send(3, 1, "wide", 2, lambda w, n: high_part, lambda w, n: high_part),
+            Send(1, 2, "wide", 1, out_at, lambda w, n: (0, 0)),
+            Send(4, 2, "wide", 1, None, lambda w, n: (0, pl.ds(1, narrow_count - 1))),
+            Send(2, 2, "wide", 1, None, entry(1)),
+            Send(3, 2, "wide", 1, None, entry(2)),
+            Send(1, 3, "wide", 2, rows_at(ff_first, third)),
+            Send(1, 4, "wide", 4, rows_at(ff_first, third)),
             Send(
-                1, 3, "wide", 4, lambda w, n: low_part, lambda w, n: low_part, landed=True,
-                needs=(first_sends, first_sends + 1),
-            ),
-            Send(
-                2, 3, "wide", 2, lambda w, n: high_part, lambda w, n: high_part, landed=True,
-                needs=(first_sends + 2, first_sends + 3),
-            ),
-            Send(1, 4, "wide", 1, None, entry(1), landed=True),
-            Send(2, 4, "wide", 1, None, entry(2), landed=True),
-            Send(
-                3, 4, "wide", 1, None, entry(3), landed=True,
-                needs=(first_sends + 6, first_sends + 7),
+                1, 2, "wide", 1, None, entry(3), landed=True,
+                needs=(narrow_count - 1, narrow_count),
             ),
         ],
-        [attended, rows, narrow_out],
-        [(narrow_count - 1, row_count, query_width)]
-        + [out_shape] * 3
-        + [(4, *out_shape)],
+        [attended, rows, out_x, out_y, narrow_out],
+        [
+            (narrow_count - 1, row_count, query_width),
+            out_shape,
+            (4, *out_shape),
+            (third, D),
+            (third, D),
+        ],
     )
     back_high = lax.all_gather(
         after(cotangent[low_rows:], attended_others, back_low), "narrow", axis=0, tiled=True
@@ -1467,7 +1396,10 @@
 
     rest = ff_rows - third
     half_rest = ff_rows // 2 - third
-    block_one, x_last, y_last, own_swap, x_first_swap, y_first_swap, x_last_swap, y_last_swap = move(
+    (
+        block_one, x_last, y_last, own_swap, x_first_swap, y_first_swap, x_last_swap, y_last_swap,
+        across_first,
+    ) = move(
         [Send(0, 0, "narrow", 1)]
         + near_and_across(1, 1, rows_at(ff_first + third, rest))
         + [Send(1, 3, "wide", 1, rows_at(ff_first, ff_rows))]
@@ -1475,25 +1407,28 @@
         + [
             Send(1, 6, "wide", 1, landed=True, needs=(1,)),
             Send(2, 7, "wide", 1, landed=True, needs=(2,)),
+            Send(2, 8, "wide", 4),
         ],
         [normed_two, rows, x_first, y_first],
         [normed_two.shape, (rest, D), (rest, D), (ff_rows, D)]
         + [(third, D)] * 2
-        + [(rest, D)] * 2,
+        + [(rest, D)] * 2
+        + [(third, D)],
     )
     block_two, *across = move(
         [
             Send(0, 0, "narrow", 1),
-            Send(1, 1, "wide", 4),
-            Send(2, 2, "wide", 4, rows_at(0, half_rest)),
-            Send(3, 3, "wide", 2, rows_at(half_rest, ff_rows // 2)),
+            Send(2, 1, "wide", 4, rows_at(0, half_rest)),
+            Send(3, 2, "wide", 2, rows_at(half_rest, ff_rows // 2)),
+            Send(1, 3, "wide", 1),
             Send(1, 4, "wide", 1, landed=True, needs=(1,)),
             Send(2, 5, "wide", 1, landed=True, needs=(2,)),
-            Send(3, 6, "wide", 1, landed=True, needs=(3,)),
         ],
-        [block_one, x_first, x_last, y_last],
-        [block_one.shape] + [(third, D), (half_rest, D), (ff_rows // 2, D)] * 2,
-    )
+        [block_one, across_first, x_last, y_last],
+        [block_one.shape, (half_rest, D), (ff_rows // 2, D)]
+        + [(third, D), (half_rest, D), (ff_rows // 2, D)],
+    )
+    across = [across_first, *across]
 
     def pieces(*arrays):
         return [(array, 0, array.shape[0]) for array in arrays]
@@ -1540,6 +1475,7 @@
     )
     out_back = jnp.stack([by_heads[0], heads_one, heads_two, heads_three])
     out_back = jnp.take(out_back, back_by, axis=0).reshape(seq_len, query_width)
+    attn_back_all = lax.all_gather(after(attn_back, heads_two), "narrow", axis=0, tiled=True)
     ff_sum = lax.psum_scatter(
         after(ff_term, heads_two), "narrow", scatter_dimension=0, tiled=True
     )
@@ -1569,58 +1505,43 @@
         sources=[*upper_across, *joined_gate],
         lands=[half_shape] * 2 + [near_shape] * 2,
     )
-    attn_back_all = lax.all_gather(
-        after(attn_back, ff_sum, qkv_back[1]), "narrow", axis=0, tiled=True
-    )
     joined_upper = ff_join(grad_upper[0], upper_swap, upper_a, upper_b)
-    half_rows = near_shape[0] // 2
-    halves = [
-        [
-            Send(0, 0, "wide", 2, rows_at(k * half_rows, half_rows)),
-            Send(1, 1, "wide", 4, rows_at(k * half_rows, half_rows)),
-        ]
-        for k in range(2)
-    ]
-    norm_one_term, upper_xa, upper_ya = first_back(
-        qkv_back, w_qkv, row_count,
-        sends=halves[0], sources=list(joined_upper), lands=[half_shape] * 2,
-    )
-    down_sum = ff_end(grad_down[0], down_swap, [down_x, down_y], (norm_one_term,))
-    gate_sum = ff_end(grad_gate[0], gate_swap, [gate_x, gate_y], (norm_one_term,))
-    *grad_qkv, upper_xb, upper_yb = outer_pair(
-        qkv_back, normed_all, (norm_one_term,),
-        sends=halves[1], sources=list(joined_upper), lands=[half_shape] * 2,
-    )
-    upper_sum = ff_end(
-        grad_upper[0], upper_swap,
-        [
-            jnp.concatenate([upper_xa, upper_xb], axis=0),
-            jnp.concatenate([upper_ya, upper_yb], axis=0),
-        ],
-    )
-    ff_sums = [gate_sum, upper_sum, down_sum]
+    *grad_qkv, upper_x, upper_y = outer_pair(
+        qkv_back, normed_all, (joined_upper[0],),
+        sends=near_sends(0, 0), sources=list(joined_upper), lands=[near_shape] * 2,
+    )
+    (grad_out,) = outer(attended, attn_back_all, 1, (grad_qkv[0],))
+    own_attn, other_attn = arrange_attn(
+        turn, [*grad_qkv, grad_out], piece, unit_cols, sizes
+    )
+    gate_sum, attn_swap = ff_end(
+        grad_gate[0], gate_swap, [gate_x, gate_y],
+        sends=[Send(0, 0, "wide", 1)], sources=[other_attn], lands=[other_attn.shape],
+    )
+    down_sum = ff_end(grad_down[0], down_swap, [down_x, down_y], (grad_qkv[0],))
+    upper_sum = ff_end(grad_upper[0], upper_swap, [upper_x, upper_y])
+    met_attn = sum_entries(own_attn, attn_swap)
+    norm_one_term, *arrived = first_back(
+        qkv_back, w_qkv, row_count, (down_sum, upper_sum),
+        sends=[Send(r - 1, r - 1, "wide", 2 * r) for r in (1, 2, 3)],
+        sources=met_attn[1:],
+        lands=[met_attn[0].shape] * 3,
+    )
+    attn_sum = add([met_attn[0]] + arrived)
 
     slots = wide_count * capacity
     unit_of = jnp.zeros((slots,), jnp.int32).at[slot_place].set(
         jnp.arange(unit_count, dtype=jnp.int32)
     )
     half_of = unit_of // col_blocks
-    block_of = unit_of - half_of * col_blocks
     low, high = unpick_units(
-        jnp.concatenate(ff_sums, axis=0),
-        jnp.maximum(block_of - attn_blocks, 0),
+        jnp.concatenate([attn_sum, gate_sum, upper_sum, down_sum], axis=0),
+        unit_of - half_of * col_blocks,
         half_of,
         wide_count,
         piece,
         unit_rows,
     )
-
-    def by_wide(wide, narrow):
-        return wide
-
-    def by_narrow(wide, narrow):
-        return narrow
-
     gain_one = sum(
         jnp.sum(
             w_qkv[g * group_width : (g + 1) * group_width].astype(f32) * grad_qkv[g].astype(f32),
@@ -1634,70 +1555,40 @@
             Send(
                 0, 0, "wide", e,
                 lambda wide, narrow, e=e: jnp.bitwise_xor(wide, e),
-                by_wide,
+                lambda wide, narrow: wide,
             )
             for e in range(1, wide_count)
         ]
-        + [Send(1, 1, "wide", e, None, by_wide) for e in range(1, wide_count)],
+        + [
+            Send(1, 1, "wide", e, None, lambda wide, narrow: wide) for e in range(1, wide_count)
+        ],
         [low, gain_terms],
         [low.shape, ((wide_count, *gain_terms.shape), f32)],
     )
     owned_high = lax.all_to_all(after(high, owned_low), "wide", split_axis=0, concat_axis=0)
     gain_plane = sum_places(wide_index.reshape(1), gain_terms, gain_others)
-    (grad_out,) = outer(attended, attn_back_all, 1, (owned_low,))
-    own_attn, other_attn = arrange_attn(
-        turn, [*grad_qkv, grad_out], piece, unit_cols, sizes
-    )
-    attn_swap, gain_others = move(
-        [Send(0, 0, "wide", 1)]
-        + [Send(1, 1, "narrow", k, None, by_narrow) for k in range(1, narrow_count)],
-        [other_attn, gain_plane],
-        [other_attn.shape, ((narrow_count, *gain_terms.shape), f32)],
-    )
-    met_attn = sum_entries(own_attn, attn_swap)
-    gain_grads = sum_places(narrow_index.reshape(1), gain_plane, gain_others)
     filled = jnp.concatenate(
         [lax.dynamic_slice(counts, (wide_index,), (1,)), wide_index.reshape(1)]
     ).astype(jnp.int32)
-    arrived = [flip(met_attn[r], 2 * r) for r in (1, 2, 3)]
     updated = update_units(
-        filled, owned_low, low, 0, master, moment_one, moment_two, (), (met_attn[0],)
-    )
-    attn_sum = add([met_attn[0]] + [after(part, updated[0]) for part in arrived])
-    near = [flip(attn_sum, 2 * r) for r in (1, 2, 3)]
-    updated = update_units(
-        filled, owned_high, owned_high, low.shape[1], master, moment_one, moment_two, updated,
-        (attn_sum,),
-    )
-    near = [attn_sum] + [after(part, updated[0]) for part in near]
-    other = [flip(part, 1) for part in near]
-    attn_grads = [attn_sum.reshape(attn_blocks, piece, D)] + [
-        jnp.stack(part).reshape(wide_count // 2, attn_blocks, piece, D)
-        for part in (near, other)
-    ]
-
-    first_slot = wide_index * capacity
-    own_block = lax.dynamic_slice(block_of, (first_slot,), (capacity,))
-    own_half = lax.dynamic_slice(half_of, (first_slot,), (capacity,))
-    slot = jnp.arange(capacity, dtype=jnp.int32)
-    is_attn = (own_block < attn_blocks) & (slot < filled[0])
-    attn_count = jnp.sum(is_attn.astype(jnp.int32))
-    rank = jnp.cumsum(is_attn.astype(jnp.int32)) - 1
-    listed = min(capacity, attn_blocks * row_blocks)
-    wanted = jnp.minimum(jnp.arange(listed, dtype=jnp.int32), jnp.maximum(attn_count - 1, 0))
-    chosen = is_attn[None, :] & (rank[None, :] == wanted[:, None])
-
-    def entries_of(values):
-        return jnp.sum(jnp.where(chosen, values[None, :], 0), axis=1)
-
-    owned_grads, new_master, new_copy, new_first, new_second = update_attn(
-        entries_of(slot), entries_of(own_block), entries_of(own_half),
-        jnp.stack([attn_count, filled[0], wide_index]).astype(jnp.int32),
-        attn_grads, owned_low, low, master, moment_one, moment_two, updated,
+        filled, owned_low, low, 0, master, moment_one, moment_two, ()
+    )
+    owned_grads, new_master, new_copy, new_first, new_second = update_units(
+        filled, owned_high, owned_high, low.shape[1], master, moment_one, moment_two, updated
+    )
+    gain_others = jnp.stack(
+        [gain_plane]
+        + [
+            after(lax.ppermute(gain_plane, "narrow", shift(narrow_count, k)), owned_grads)
+            for k in range(1, narrow_count)
+        ]
+    )
+    gain_grads = sum_places(
+        narrow_index.reshape(1), gain_plane, jnp.take(gain_others, back_by, axis=0)
     )
 
     norm_one_back = lax.psum_scatter(
-        norm_one_term, "narrow", scatter_dimension=0, tiled=True
+        after(norm_one_term, ff_sum, attn_sum), "narrow", scatter_dimension=0, tiled=True
     )
     norm_one_back = after(norm_one_back, owned_grads).astype(f32)
     _, norm_one_pull = jax.vjp(lambda values: rmsnorm(values, norm_gains[0]), inputs)

time: 1010 us -> 1010 us (level)
  Pallas kernels: 861 us -> 883 us
  local copies, waits for them, and re-layouts: 51.1 us -> 39.5 us
    pallas_call x57 -> x53, Pallas kernels: 861 us -> 883 us  [call(): pl.pallas_call(wrapped, grid_spec=pltpu.PrefetchScalarGridSpec(num_scalar...]
    all_to_all x1, waiting for transfers between devices: 0.01 us -> 19.5 us  [local(): lax.all_to_all(after(high, owned_low), 'wide', split_axis=0, concat_axis=0)]
    unnamed x160 -> x158, local copies, waits for them, and re-layouts: 42.7 us -> 31.1 us
  transfers between devices with their start and end apart: 17 -> 10, of which waited for: 3 -> 1; matrix products, arithmetic and copies ran while one was open for 3% -> 2% of each run, Pallas kernels for 65% -> 67%
where the time goes in v6:
time: 1010 us; the launch traced here: 1000 us
  Pallas kernels  883 us (87%)
  local copies, waits for them, and re-layouts  39.5 us (4%)
  other arithmetic  35.6 us (4%)
  waiting for transfers between devices  20.1 us (2%)
  between operations  15.7 us (2%)
    pallas_call x53, Pallas kernels, call(): pl.pallas_call(wrapped, grid_spec=pltpu.PrefetchScalarGridSpec(num_scalar...  883 us
    unnamed x158, local copies, waits for them, and re-layouts  31.1 us
  transfers between devices with their start and end apart: 10, of which 1 were waited for; matrix products, arithmetic and copies ran while one was open for 2% of the time, Pallas kernels for 67%

profile of v6, /device:TPU:0, one launch (start us, length us, event | category | flops | bytes accessed | tf_op | source)
XLA Modules:
  0.0 1000.8 jit_solution(18349827739445686337)
XLA Ops:
  22.3 78.4 %move.6.refs_3_ = bf16[8,26,16,1024]{3,2,1,0:T(8,128)(2,1)} custom-call(bf16[8,26,16,1024]{3,2,1,0:T(8,128)(2,1)} %turn_units.1.refs_0_.refs_2_), custom_call_target="tpu_custom_call" | custom-call | tf_op jit(solution)/shard_map/move/pallas_call | solution.py:167
  109.0 37.8 %move.7 = (bf16[3,96,2048]{2,1,0:T(8,128)(2,1)}, bf16[4,96,2048]{2,1,0:T(8,128)(2,1)}, bf16[3,64,2048]{2,1,0:T(8,128)(2,1)}) custom-call(bf16[928,2048]{1,0:T(8,128)(2,1)} %pick_units.1.refs_0_.refs_1_.refs_2_.refs_3_), custom_call_target="tpu_custom_call" | custom-call | tf_op jit(solution)/shard_map/move/pallas_call | solution.py:167
  154.4 10.8 %project.1.refs_1_ = bf16[1536,768]{1,0:T(8,128)(2,1)} custom-call(bf16[1536,2048]{1,0:T(8,128)(2,1)} %all-gather.5.cloned.1.call-done.refs_1_.refs_0_.refs_2_, bf16[768,2048]{1,0:T(8,128)(2,1)} %copy-done.1, f32[1536,128]{1,0:T(8,128)} %constant.101.clone.refs_2_.refs_5_, f32[1536,128]{1,0:T(8,128)} %constant.102.clone.refs_3_.refs_6_, ...), custom_call_target="tpu_custom_call" | custom-call | flops 4831838208 | tf_op jit(solution)/shard_map/project/pallas_call | solution.py:167
  165.2 28.9 %attend_forward.1 = (bf16[1536,512]{1,0:T(8,128)(2,1)S(1)}, f32[2,8,1536]{2,1,0:T(8,128)S(1)}, bf16[4,64,2048]{2,1,0:T(8,128)(2,1)S(1)}, bf16[4,64,2048]{2,1,0:T(8,128)(2,1)S(1)}) custom-call(s32[1]{0:T(128)} %dynamic_slice.6.refs_0_, bf16[1536,768]{1,0:T(8,128)(2,1)} %project.1.refs_1_, bf16[928,2048]{1,0:T(8,128)(2,1)} %pick_units.1.refs_0_.refs_1_.refs_2_.refs_3_, ...), custom_call_target="tpu_custom_call" | custom-call | flops 9663676416 | tf_op jit(solution)/shard_map/attend_forward/pallas_call | solution.py:167
  197.1 51.5 %move.8 = (bf16[3,384,512]{2,1,0:T(8,128)(2,1)}, bf16[4,64,2048]{2,1,0:T(8,128)(2,1)}, bf16[4,4,64,2048]{3,2,1,0:T(8,128)(2,1)}, bf16[256,2048]{1,0:T(8,128)(2,1)}, bf16[256,2048]{1,0:T(8,128)(2,1)}) custom-call(bf16[1536,512]{1,0:T(8,128)(2,1)} %copy-done.8, bf16[928,2048]{1,0:T(8,128)(2,1)} %pick_units.1.refs_0_.refs_1_.refs_2_.refs_3_, ...), custom_call_target="tpu_custom_call" | custom-call | tf_op jit(solution)/shard_map/move/pallas_call | solution.py:167
  257.1 10.2 %branch.1 = (f32[384,2048]{1,0:T(8,128)}, bf16[384,2048]{1,0:T(8,128)(2,1)}) custom-call(bf16[1536,512]{1,0:T(8,128)(2,1)} %copy-done.8, bf16[3,384,512]{2,1,0:T(8,128)(2,1)} %get-tuple-element.140.refs_1_, bf16[2048,2048]{1,0:T(8,128)(2,1)} %assemble_out.1.refs_2_, bf16[384,2048]{1,0:T(8,128)(2,1)} %refs_3_.4, f32[1,2048]{1,0:T(1,128)} %get-tuple-element.274.refs_4_), custom_call_target="tpu_custom_call" | custom-call | flops 3221225472 | tf_op jit(solution)/shard_map/branch/pallas_call | solution.py:167
  267.3 80.2 %move.9 = (bf16[384,2048]{1,0:T(8,128)(2,1)}, bf16[512,2048]{1,0:T(8,128)(2,1)}, bf16[512,2048]{1,0:T(8,128)(2,1)}, bf16[768,2048]{1,0:T(8,128)(2,1)}, bf16[256,...) custom-call(bf16[384,2048]{1,0:T(8,128)(2,1)} %get-tuple-element.144, ...), custom_call_target="tpu_custom_call" | custom-call | tf_op jit(solution)/shard_map/move/pallas_call | solution.py:167
  347.5 45.6 %move.10 = (bf16[384,2048]{1,0:T(8,128)(2,1)}, bf16[128,2048]{1,0:T(8,128)(2,1)}, bf16[384,2048]{1,0:T(8,128)(2,1)}, bf16[256,2048]{1,0:T(8,128)(2,1)}, bf16[128...) custom-call(bf16[384,2048]{1,0:T(8,128)(2,1)} %get-tuple-element.150.refs_0_, ...), custom_call_target="tpu_custom_call" | custom-call | tf_op jit(solution)/shard_map/move/pallas_call | solution.py:167
  393.5 40.3 %ff_step.4 = (bf16[1536,2048]{1,0:T(8,128)(2,1)}, bf16[1536,2048]{1,0:T(8,128)(2,1)}, bf16[1536,2048]{1,0:T(8,128)(2,1)}, bf16[1536,2048]{1,0:T(8,128)(2,1)}, bf...) custom-call(bf16[384,2048]{1,0:T(8,128)(2,1)} %get-tuple-element.150, ...), custom_call_target="tpu_custom_call" | custom-call | flops 16106127360 | tf_op jit(solution)/shard_map/ff_step/pallas_call | solution.py:167
  433.8 39.5 %ff_step.5 = (bf16[1536,2048]{1,0:T(8,128)(2,1)}, bf16[1536,2048]{1,0:T(8,128)(2,1)}, bf16[1536,2048]{1,0:T(8,128)(2,1)}, bf16[1536,2048]{1,0:T(8,128)(2,1)}, bf...) custom-call(bf16[384,2048]{1,0:T(8,128)(2,1)} %get-tuple-element.161, ...), custom_call_target="tpu_custom_call", output_to_operand_aliasing={{0}: (19, {}), {1}: (20, {}), {2}: (21, {}), {3}: (22, {}),... | custom-call | flops 16106127360 | tf_op jit(solution)/shard_map/ff_step/pallas_call | solution.py:167
  473.3 38.6 %ff_step.6 = (bf16[1536,2048]{1,0:T(8,128)(2,1)}, bf16[1536,2048]{1,0:T(8,128)(2,1)}, bf16[1536,2048]{1,0:T(8,128)(2,1)}, bf16[1536,2048]{1,0:T(8,128)(2,1)}, bf...) custom-call(bf16[384,2048]{1,0:T(8,128)(2,1)} %get-tuple-element.162, ...), custom_call_target="tpu_custom_call", output_to_operand_aliasing={{0}: (19, {}), {1}: (20, {}), {2}: (21, {}), {3}: (22, {}),... | custom-call | flops 16106127360 | tf_op jit(solution)/shard_map/ff_step/pallas_call | solution.py:167
  511.9 39.5 %ff_step.7 = (bf16[1536,2048]{1,0:T(8,128)(2,1)}, bf16[1536,2048]{1,0:T(8,128)(2,1)}, bf16[1536,2048]{1,0:T(8,128)(2,1)}, bf16[1536,2048]{1,0:T(8,128)(2,1)}, bf...) custom-call(bf16[384,2048]{1,0:T(8,128)(2,1)} %get-tuple-element.144, ...), custom_call_target="tpu_custom_call", output_to_operand_aliasing={{0}: (19, {}), {1}: (20, {}), {2}: (21, {}), {3}: (22, {}),... | custom-call | flops 16106127360 | tf_op jit(solution)/shard_map/ff_step/pallas_call | solution.py:167
  565.2 23.1 %outer.4 = (bf16[1024,2048]{1,0:T(8,128)(2,1)}, bf16[1024,2048]{1,0:T(8,128)(2,1)}, bf16[384,512]{1,0:T(8,128)(2,1)}, bf16[384,512]{1,0:T(8,128)(2,1)}) custom-call(bf16[1536,2048]{1,0:T(8,128)(2,1)} %get-tuple-element.188.refs_0_, bf16[1536,2048]{1,0:T(8,128)(2,1)} %get-tuple-element.189.refs_1_, bf16[4,384,512]{2,1,0:T(8,128)(2,1)} %copy-done.27), custom_call_target="tpu_custom_call" | custom-call | flops 12884901888 | tf_op jit(solution)/shard_map/outer/pallas_call | solution.py:167
  588.3 26.3 %outer.5 = (bf16[1024,2048]{1,0:T(8,128)(2,1)}, bf16[1024,2048]{1,0:T(8,128)(2,1)}, bf16[384,512]{1,0:T(8,128)(2,1)}, bf16[1024,2048]{1,0:T(8,128)(2,1)}) custom-call(bf16[1536,2048]{1,0:T(8,128)(2,1)} %get-tuple-element.185.refs_0_, bf16[1536,2048]{1,0:T(8,128)(2,1)} %get-tuple-element.186.refs_1_, bf16[4,384,512]{2,1,0:T(8,128)(2,1)} %copy-done.27, ...), custom_call_target="tpu_custom_call" | custom-call | flops 12884901888 | tf_op jit(solution)/shard_map/outer/pallas_call | solution.py:167
  622.6 21.9 %outer.6 = (bf16[1024,2048]{1,0:T(8,128)(2,1)}, bf16[1024,2048]{1,0:T(8,128)(2,1)}, bf16[1024,2048]{1,0:T(8,128)(2,1)}, bf16[128,2048]{1,0:T(8,128)(2,1)}, bf16[128,2048]{1,0:T(8,128)(2,1)}) custom-call(bf16[1536,2048]{1,0:T(8,128)(2,1)} %get-tuple-element.195.refs_0_, bf16[1536,2048]{1,0:T(8,128)(2,1)} %get-tuple-element.186.refs_1_, ...), custom_call_target="tpu_custom_call" | custom-call | flops 12884901888 | tf_op jit(solution)/shard_map/outer/pallas_call | solution.py:167
  653.6 39.3 %attend_backward.2 = (bf16[1536,384]{1,0:T(8,128)(2,1)}, bf16[1024,2048]{1,0:T(8,128)(2,1)}, bf16[128,2048]{1,0:T(8,128)(2,1)S(1)}, bf16[128,2048]{1,0:T(8,128)(...) custom-call(s32[1]{0:T(128)} %dynamic_slice.6.refs_0_, bf16[1536,768]{1,0:T(8,128)(2,1)} %project.1.refs_1_, ...), custom_call_target="tpu_custom_call" | custom-call | flops 12079595520 | tf_op jit(solution)/shard_map/attend_backward/pallas_call | solution.py:167
  703.8 38.7 %attend_backward.3 = (bf16[1536,384]{1,0:T(8,128)(2,1)}, bf16[128,2048]{1,0:T(8,128)(2,1)S(1)}, bf16[128,2048]{1,0:T(8,128)(2,1)S(1)}, bf16[256,2048]{1,0:T(8,128)(2,1)S(1)}, bf16[256,2048]{1,0:T(8,128)(2,1)S(1)}) custom-call(s32[1]{0:T(128)} %dynamic_slice.6.refs_0_, bf16[1536,768]{1,0:T(8,128)(2,1)} %project.1.refs_1_, ...), custom_call_target="tpu_custom_call" | custom-call | flops 12079595520 | tf_op jit(solution)/shard_map/attend_backward/pallas_call | solution.py:167
  750.4 29.2 %outer_pair.1 = (bf16[384,2048]{1,0:T(8,128)(2,1)}, bf16[384,2048]{1,0:T(8,128)(2,1)}, bf16[256,2048]{1,0:T(8,128)(2,1)}, bf16[256,2048]{1,0:T(8,128)(2,1)}) custom-call(bf16[1536,384]{1,0:T(8,128)(2,1)} %get-tuple-element.210.refs_0_, bf16[1536,384]{1,0:T(8,128)(2,1)} %get-tuple-element.219.refs_1_, ...), custom_call_target="tpu_custom_call" | custom-call | flops 4831838208 | tf_op jit(solution)/shard_map/outer_pair/pallas_call | solution.py:167
  800.8 8.5 ff_end.3
  814.5 35.6 %first_back.1 = (bf16[1536,2048]{1,0:T(8,128)(2,1)}, bf16[160,2048]{1,0:T(8,128)(2,1)}, bf16[160,2048]{1,0:T(8,128)(2,1)}, bf16[160,2048]{1,0:T(8,128)(2,1)}) custom-call(bf16[1536,384]{1,0:T(8,128)(2,1)} %get-tuple-element.210.refs_0_, bf16[1536,384]{1,0:T(8,128)(2,1)} %get-tuple-element.219.refs_1_, bf16[768,2048]{1,0:T(8,128)(2,1)} %copy-done.1, ...), custom_call_target="tpu_custom_call" | custom-call | flops 4831838208 | tf_op jit(solution)/shard_map/first_back/pallas_call | solution.py:167
  866.5 39.5 %move.11 = (bf16[8,12,16,1024]{3,2,1,0:T(8,128)(2,1)}, f32[8,2,2048]{2,1,0:T(2,128)}) custom-call(bf16[8,12,16,1024]{3,2,1,0:T(8,128)(2,1)} %get-tuple-element.245.refs_0_.refs_2_, f32[2,2048]{1,0:T(2,128)} %pad_maximum_fusion.3.refs_1_), custom_call_target="tpu_custom_call" | custom-call | tf_op jit(solution)/shard_map/move/pallas_call | solution.py:167
  917.8 17.2 %update_units.2 = (f32[26,1,1024,128]{3,2,1,0:T(8,128)}, f32[26,1,1024,128]{3,2,1,0:T(8,128)}, bf16[26,1,1024,128]{3,2,1,0:T(8,128)(2,1)}, f32[26,1,1024,128]{3,2,1,0:T(8,128)}, f32[26,1,1024,128]{3,2,1,0:T(8,128)}) custom-call(s32[2]{0:T(128)S(1)} %pad_add_fusion.1.refs_0_, bf16[8,12,16,1024]{3,2,1,0:T(8,128)(2,1)S(1)} %copy-done.6, ...), custom_call_target="tpu_custom_call" | custom-call | bytes 54525952 | tf_op jit(solution)/shard_map/update_units/pallas_call | solution.py:167
  934.9 19.5 %all-to-all-done.refs_1_.refs_2_ = bf16[8,14,16,1024]{3,2,1,0:T(8,128)(2,1)} async-done(((bf16[8,14,16,1024]{3,2,1,0:T(8,128)(2,1)}), bf16[8,14,16,1024]{3,2,1,0:T(8,128)(2,1)}, u32[]{:S(2)}, u32[]{:S(2)}) %all-to-all-start) | async-done | bytes 3670048 | tf_op jit(solution)/shard_map/all_to_all | solution.py:1568
  954.4 22.6 %update_units.3 = (f32[26,1,1024,128]{3,2,1,0:T(8,128)}, f32[26,1,1024,128]{3,2,1,0:T(8,128)}, bf16[26,1,1024,128]{3,2,1,0:T(8,128)(2,1)}, f32[26,1,1024,128]{3,2,1,0:T(8,128)}, f32[26,1,1024,128]{3,2,1,0:T(8,128)}) custom-call(s32[2]{0:T(128)S(1)} %pad_add_fusion.1.refs_0_, ...), custom_call_target="tpu_custom_call", output_to_operand_aliasing={{0}: (6, {}), {1}: (7, {}), {2}: (8, {}), {3}: (9, {}), {4}... | custom-call | bytes 54525952 | tf_op jit(solution)/shard_map/update_units/pallas_call | solution.py:167
  (257 shorter events, 162.4 us)
Async XLA Ops:
  7.2 146.0 %all-gather.5.cloned.1.call-start = ((), (), s32[]{:S(2)}) async-start(), calls=%async_computation.3 | async-start | bytes 7864320 | tf_op jit(solution)/shard_map/all_gather | solution.py:1289
  14.6 234.0 %all-gather.7.cloned.1.call-start = ((), (), s32[]{:S(2)}) async-start(), calls=%async_computation.4 | async-start | bytes 3932160 | tf_op jit(solution)/shard_map/all_gather | solution.py:1325
  22.3 78.5 %copy-start.72 = (s32[116]{0:T(128)S(1)}, s32[116]{0:T(128)}, u32[]{:S(2)}) copy-start(s32[116]{0:T(128)} %param.15) | copy-start | bytes 1396
  109.0 37.8 %copy-start = (bf16[928,2048]{1,0:T(8,128)(2,1)S(1)}, bf16[928,2048]{1,0:T(8,128)(2,1)}, u32[]{:S(2)}) copy-start(bf16[928,2048]{1,0:T(8,128)(2,1)} %pick_units.1.refs_0_.refs_1_.refs_2_.refs_3_) | copy-start | bytes 11403268
  109.0 37.8 %copy-start.28 = (s32[2]{0:T(128)S(1)}, s32[2]{0:T(128)}, u32[]{:S(2)}) copy-start(s32[2]{0:T(128)} %pad_add_fusion.refs_0_) | copy-start | bytes 28
  153.2 240.3 %all-gather.9.cloned.1.call-start = ((), (), s32[]{:S(2)}) async-start(), calls=%async_computation.5 | async-start | bytes 3932160 | tf_op jit(solution)/shard_map/all_gather | solution.py:1386
  154.4 10.8 %copy-start.12 = (bf16[3,64,2048]{2,1,0:T(8,128)(2,1)S(1)}, bf16[3,64,2048]{2,1,0:T(8,128)(2,1)}, u32[]{:S(2)}) copy-start(bf16[3,64,2048]{2,1,0:T(8,128)(2,1)} %get-tuple-element.136.refs_3_.refs_4_.refs_2_) | copy-start | bytes 2359300
  248.7 538.2 %all-gather.11.cloned.1.call-start = ((), (), s32[]{:S(2)}) async-start(), calls=%async_computation.7 | async-start | bytes 7864320 | tf_op jit(solution)/shard_map/all_gather | solution.py:1478
  347.5 45.6 %copy-start.35 = (f32[384,2048]{1,0:T(8,128)S(1)}, f32[384,2048]{1,0:T(8,128)}, u32[]{:S(2)}) copy-start(f32[384,2048]{1,0:T(8,128)} %get-tuple-element.143) | copy-start | bytes 9437188
  393.5 161.7 %copy-start.61 = (f32[384]{0:T(512)}, f32[384]{0:T(512)S(1)}, u32[]{:S(2)}) copy-start(f32[384]{0:T(512)S(1)} %fusion.13) | copy-start | bytes 4612
  511.8 39.5 %copy-start.50 = (f32[1,2048]{1,0:T(1,128)S(1)}, f32[1,2048]{1,0:T(1,128)}, u32[]{:S(2)}) copy-start(f32[1,2048]{1,0:T(1,128)} %get-tuple-element.274.refs_4_) | copy-start | bytes 24580
  551.4 7.8 slice-start
  559.4 4.7 copy-start.3
  614.7 238.3 %reduce-scatter.3.cloned.1.call-start = ((), (), s32[]{:S(2)}) async-start(), calls=%async_computation.6 | async-start | bytes 7864320 | tf_op jit(solution)/shard_map/reduce_scatter | solution.py:1479
  615.3 368.9 %reduce-scatter.5.cloned.1.call-start = ((), (), s32[]{:S(2)}) async-start(), calls=%async_computation.8 | async-start | bytes 7864320 | tf_op jit(solution)/shard_map/reduce_scatter | solution.py:1590
  787.0 8.2 copy-start.4
  787.0 8.2 copy-start.7
  855.1 4.5 copy-start.44
  906.1 4.9 copy-start.75
  906.1 9.8 copy-start.5
  906.1 48.3 %all-to-all-start = ((bf16[8,14,16,1024]{3,2,1,0:T(8,128)(2,1)}), bf16[8,14,16,1024]{3,2,1,0:T(8,128)(2,1)}, u32[]{:S(2)}, u32[]{:S(2)}) async-start(bf16[8,14,16,1024]{3,2,1,0:T(8,128)(2,1)} %after.15), calls=%async_computation.2 | async-start | bytes 7340032 | tf_op jit(solution)/shard_map/all_to_all | solution.py:1568
  913.1 64.0 %collective-permute-start.2 = (f32[2,2048]{1,0:T(2,128)}, f32[2,2048]{1,0:T(2,128)S(1)}, u32[]{:S(2)}, u32[]{:S(2)}) collective-permute-start(f32[2,2048]{1,0:T(2,128)} %sum_places.2.refs_1_), channel_id=1, source_target_pairs={{0,3},{1,0},{2,1},{3,2},{4,7},{5,4},{6,5},{7,6},{8,11},{9,8},{10,9... | collective-permute-start | bytes 49160 | tf_op jit(solution)/shard_map/ppermute | solution.py:1582
  913.4 64.3 %collective-permute-start.1 = (f32[2,2048]{1,0:T(2,128)}, f32[2,2048]{1,0:T(2,128)S(1)}, u32[]{:S(2)}, u32[]{:S(2)}) collective-permute-start(f32[2,2048]{1,0:T(2,128)} %sum_places.2.refs_1_), channel_id=1, source_target_pairs={{0,2},{1,3},{2,0},{3,1},{4,6},{5,7},{6,4},{7,5},{8,10},{9,11},{10,... | collective-permute-start | bytes 49160 | tf_op jit(solution)/shard_map/ppermute | solution.py:1582
  913.4 64.9 %collective-permute-start = (f32[2,2048]{1,0:T(2,128)}, f32[2,2048]{1,0:T(2,128)S(1)}, u32[]{:S(2)}, u32[]{:S(2)}) collective-permute-start(f32[2,2048]{1,0:T(2,128)} %sum_places.2.refs_1_), channel_id=1, source_target_pairs={{0,1},{1,2},{2,3},{3,0},{4,5},{5,6},{6,7},{7,4},{8,9},{9,10},{10,1... | collective-permute-start | bytes 49160 | tf_op jit(solution)/shard_map/ppermute | solution.py:1582
  (66 other events, 139.9 us)
Sparse Core Ops, SparseCore 0:
  14.7 137.9 all-gather.4
  154.9 93.3 all-gather.6
  249.9 102.6 all-gather.8
  614.8 112.6 all-gather.10
  729.7 108.9 reduce-scatter.2
  853.1 109.2 reduce-scatter.4

commit v7 on v6

--- a/solution.py
+++ b/solution.py
@@ -313,7 +313,7 @@
 def unpick_units(rows, block_of, half_of, owners, piece, unit_rows):
     slots = block_of.shape[0]
     capacity = slots // owners
-    low = capacity // 4 * 2
+    low = capacity * 5 // 16 * 2
     sizes = (low, capacity - low)
     return call(
         functools.partial(unpick_kernel, piece=piece, unit_rows=unit_rows),
@@ -667,27 +667,47 @@
     )
 
 
-def first_back_kernel(*refs):
-    groups = (len(refs) - 1) // 2
-    total = sum(dot(refs[g][...], refs[groups + g][...], 1, 0) for g in range(groups))
-    refs[-1][...] = total.astype(bf16)
-
-
-def first_back(qkv_back, w_qkv, step, deps=(), **beside):
+def first_back_kernel(*refs, groups, sums):
+    taken, weights, grads = refs[:groups], refs[groups : 2 * groups], refs[2 * groups : 3 * groups]
+    terms, outs = refs[3 * groups : -2 - sums], refs[-2 - sums :]
+    outs[0][...] = sum(dot(taken[g][...], weights[g][...], 1, 0) for g in range(groups)).astype(bf16)
+
+    @pl.when(pl.program_id(0) == 0)
+    def _():
+        outs[1][...] = sum(
+            jnp.sum(weights[g][...].astype(f32) * grads[g][...].astype(f32), axis=0, keepdims=True)
+            for g in range(groups)
+        )
+
+    each = len(terms) // sums
+    for k in range(sums):
+
+        @pl.when(pl.program_id(0) == k + 1)
+        def _(k=k):
+            parts = terms[k * each : (k + 1) * each]
+            outs[2 + k][...] = sum(part[...].astype(f32) for part in parts).astype(bf16)
+
+
+def first_back(qkv_back, w_qkv, step, grads, ends, deps=(), **beside):
     groups = len(qkv_back)
     seq_len, width = qkv_back[0].shape
-    return call(
-        first_back_kernel,
-        [*qkv_back, *([w_qkv] * groups)],
+    rows = ends[0][2].shape[0]
+    end = blocks((rows, D), lambda i: (0, 0))
+    return call(
+        functools.partial(first_back_kernel, groups=groups, sums=len(ends)),
+        [*qkv_back, *([w_qkv] * groups), *grads, *[term for terms in ends for term in terms]],
         [blocks((step, width), lambda i: (i, 0))] * groups
-        + [blocks((width, D), lambda i, g=g: (g, 0)) for g in range(groups)],
-        shaped((seq_len, D)),
-        blocks((step, D), lambda i: (i, 0)),
+        + [blocks((width, D), lambda i, g=g: (g, 0)) for g in range(groups)]
+        + [blocks((width, D), lambda i: (0, 0))] * groups
+        + [end] * sum(len(terms) for terms in ends),
+        [shaped((seq_len, D)), shaped((1, D), f32)] + [shaped((rows, D))] * len(ends),
+        [blocks((step, D), lambda i: (i, 0)), blocks((1, D), lambda i: (0, 0))]
+        + [end] * len(ends),
         grid=(seq_len // step,),
         deps=deps,
+        mib=60,
         flops=2 * seq_len * width * groups * D,
         name="first_back",
-        mib=60,
         **beside,
     )
 
@@ -1518,11 +1538,13 @@
         grad_gate[0], gate_swap, [gate_x, gate_y],
         sends=[Send(0, 0, "wide", 1)], sources=[other_attn], lands=[other_attn.shape],
     )
-    down_sum = ff_end(grad_down[0], down_swap, [down_x, down_y], (grad_qkv[0],))
-    upper_sum = ff_end(grad_upper[0], upper_swap, [upper_x, upper_y])
     met_attn = sum_entries(own_attn, attn_swap)
-    norm_one_term, *arrived = first_back(
-        qkv_back, w_qkv, row_count, (down_sum, upper_sum),
+    norm_one_term, gain_one, down_sum, upper_sum, *arrived = first_back(
+        qkv_back, w_qkv, row_count, grad_qkv,
+        [
+            [grad_down[0], down_swap, down_x, down_y],
+            [grad_upper[0], upper_swap, upper_x, upper_y],
+        ],
         sends=[Send(r - 1, r - 1, "wide", 2 * r) for r in (1, 2, 3)],
         sources=met_attn[1:],
         lands=[met_attn[0].shape] * 3,
@@ -1542,14 +1564,7 @@
         piece,
         unit_rows,
     )
-    gain_one = sum(
-        jnp.sum(
-            w_qkv[g * group_width : (g + 1) * group_width].astype(f32) * grad_qkv[g].astype(f32),
-            axis=0,
-        )
-        for g in range(groups)
-    )
-    gain_terms = jnp.stack([gain_one / norm_gains[0], gain_two])
+    gain_terms = jnp.stack([gain_one[0] / norm_gains[0], gain_two])
     owned_low, gain_others = move(
         [
             Send(

time: 1010 us -> 992 us (0.982)
  waiting for transfers between devices: 20.1 us -> 0.8 us
    all_to_all x1, waiting for transfers between devices: 19.5 us -> 0.16 us  [local(): lax.all_to_all(after(high, owned_low), 'wide', split_axis=0, concat_axis=0)]
    pallas_call x53 -> x51, Pallas kernels: 883 us -> 890 us  [call(): pl.pallas_call(wrapped, grid_spec=pltpu.PrefetchScalarGridSpec(num_scalar...]
    unnamed x158 -> x156, local copies, waits for them, and re-layouts: 31.1 us -> 33.7 us
  transfers between devices with their start and end apart: 10 -> 10, of which waited for: 1 -> 1; matrix products, arithmetic and copies ran while one was open for 2% -> 2% of each run, Pallas kernels for 67% -> 69%
where the time goes in v7:
time: 992 us; the launch traced here: 987 us
  Pallas kernels  890 us (90%)
  local copies, waits for them, and re-layouts  41.8 us (4%)
  other arithmetic  33.1 us (3%)
  between operations  15.7 us (2%)
    pallas_call x51, Pallas kernels, call(): pl.pallas_call(wrapped, grid_spec=pltpu.PrefetchScalarGridSpec(num_scalar...  890 us
    unnamed x156, local copies, waits for them, and re-layouts  33.7 us
  transfers between devices with their start and end apart: 10, of which 1 were waited for; matrix products, arithmetic and copies ran while one was open for 2% of the time, Pallas kernels for 69%

profile of v7, /device:TPU:0, one launch (start us, length us, event | category | flops | bytes accessed | tf_op | source)
XLA Modules:
  0.0 986.9 jit_solution(14645281003878110362)
XLA Ops:
  22.3 78.4 %move.6.refs_3_ = bf16[8,26,16,1024]{3,2,1,0:T(8,128)(2,1)} custom-call(bf16[8,26,16,1024]{3,2,1,0:T(8,128)(2,1)} %turn_units.1.refs_0_.refs_2_), custom_call_target="tpu_custom_call" | custom-call | tf_op jit(solution)/shard_map/move/pallas_call | solution.py:167
  109.0 37.8 %move.7 = (bf16[3,96,2048]{2,1,0:T(8,128)(2,1)}, bf16[4,96,2048]{2,1,0:T(8,128)(2,1)}, bf16[3,64,2048]{2,1,0:T(8,128)(2,1)}) custom-call(bf16[928,2048]{1,0:T(8,128)(2,1)} %pick_units.1.refs_0_.refs_1_.refs_2_.refs_3_), custom_call_target="tpu_custom_call" | custom-call | tf_op jit(solution)/shard_map/move/pallas_call | solution.py:167
  154.4 10.8 %project.1.refs_1_ = bf16[1536,768]{1,0:T(8,128)(2,1)} custom-call(bf16[1536,2048]{1,0:T(8,128)(2,1)} %all-gather.5.cloned.1.call-done.refs_1_.refs_0_.refs_2_, bf16[768,2048]{1,0:T(8,128)(2,1)} %copy-done.1, f32[1536,128]{1,0:T(8,128)} %constant.101.clone.refs_2_.refs_5_, f32[1536,128]{1,0:T(8,128)} %constant.102.clone.refs_3_.refs_6_, ...), custom_call_target="tpu_custom_call" | custom-call | flops 4831838208 | tf_op jit(solution)/shard_map/project/pallas_call | solution.py:167
  165.2 28.9 %attend_forward.1 = (bf16[1536,512]{1,0:T(8,128)(2,1)S(1)}, f32[2,8,1536]{2,1,0:T(8,128)S(1)}, bf16[4,64,2048]{2,1,0:T(8,128)(2,1)S(1)}, bf16[4,64,2048]{2,1,0:T(8,128)(2,1)S(1)}) custom-call(s32[1]{0:T(128)} %dynamic_slice.6.refs_0_, bf16[1536,768]{1,0:T(8,128)(2,1)} %project.1.refs_1_, bf16[928,2048]{1,0:T(8,128)(2,1)} %pick_units.1.refs_0_.refs_1_.refs_2_.refs_3_, ...), custom_call_target="tpu_custom_call" | custom-call | flops 9663676416 | tf_op jit(solution)/shard_map/attend_forward/pallas_call | solution.py:167
  197.2 51.5 %move.8 = (bf16[3,384,512]{2,1,0:T(8,128)(2,1)}, bf16[4,64,2048]{2,1,0:T(8,128)(2,1)}, bf16[4,4,64,2048]{3,2,1,0:T(8,128)(2,1)}, bf16[256,2048]{1,0:T(8,128)(2,1)}, bf16[256,2048]{1,0:T(8,128)(2,1)}) custom-call(bf16[1536,512]{1,0:T(8,128)(2,1)} %copy-done.7, bf16[928,2048]{1,0:T(8,128)(2,1)} %pick_units.1.refs_0_.refs_1_.refs_2_.refs_3_, ...), custom_call_target="tpu_custom_call" | custom-call | tf_op jit(solution)/shard_map/move/pallas_call | solution.py:167
  257.1 10.1 %branch.1 = (f32[384,2048]{1,0:T(8,128)}, bf16[384,2048]{1,0:T(8,128)(2,1)}) custom-call(bf16[1536,512]{1,0:T(8,128)(2,1)} %copy-done.7, bf16[3,384,512]{2,1,0:T(8,128)(2,1)} %get-tuple-element.143.refs_1_, bf16[2048,2048]{1,0:T(8,128)(2,1)} %assemble_out.1.refs_2_, bf16[384,2048]{1,0:T(8,128)(2,1)} %refs_3_.4, f32[1,2048]{1,0:T(1,128)} %get-tuple-element.278.refs_4_), custom_call_target="tpu_custom_call" | custom-call | flops 3221225472 | tf_op jit(solution)/shard_map/branch/pallas_call | solution.py:167
  267.2 80.3 %move.9 = (bf16[384,2048]{1,0:T(8,128)(2,1)}, bf16[512,2048]{1,0:T(8,128)(2,1)}, bf16[512,2048]{1,0:T(8,128)(2,1)}, bf16[768,2048]{1,0:T(8,128)(2,1)}, bf16[256,...) custom-call(bf16[384,2048]{1,0:T(8,128)(2,1)} %get-tuple-element.147, ...), custom_call_target="tpu_custom_call" | custom-call | tf_op jit(solution)/shard_map/move/pallas_call | solution.py:167
  347.5 45.6 %move.10 = (bf16[384,2048]{1,0:T(8,128)(2,1)}, bf16[128,2048]{1,0:T(8,128)(2,1)}, bf16[384,2048]{1,0:T(8,128)(2,1)}, bf16[256,2048]{1,0:T(8,128)(2,1)}, bf16[128...) custom-call(bf16[384,2048]{1,0:T(8,128)(2,1)} %get-tuple-element.153.refs_0_, ...), custom_call_target="tpu_custom_call" | custom-call | tf_op jit(solution)/shard_map/move/pallas_call | solution.py:167
  393.5 40.3 %ff_step.4 = (bf16[1536,2048]{1,0:T(8,128)(2,1)}, bf16[1536,2048]{1,0:T(8,128)(2,1)}, bf16[1536,2048]{1,0:T(8,128)(2,1)}, bf16[1536,2048]{1,0:T(8,128)(2,1)}, bf...) custom-call(bf16[384,2048]{1,0:T(8,128)(2,1)} %get-tuple-element.153, ...), custom_call_target="tpu_custom_call" | custom-call | flops 16106127360 | tf_op jit(solution)/shard_map/ff_step/pallas_call | solution.py:167
  433.8 39.5 %ff_step.5 = (bf16[1536,2048]{1,0:T(8,128)(2,1)}, bf16[1536,2048]{1,0:T(8,128)(2,1)}, bf16[1536,2048]{1,0:T(8,128)(2,1)}, bf16[1536,2048]{1,0:T(8,128)(2,1)}, bf...) custom-call(bf16[384,2048]{1,0:T(8,128)(2,1)} %get-tuple-element.164, ...), custom_call_target="tpu_custom_call", output_to_operand_aliasing={{0}: (19, {}), {1}: (20, {}), {2}: (21, {}), {3}: (22, {}),... | custom-call | flops 16106127360 | tf_op jit(solution)/shard_map/ff_step/pallas_call | solution.py:167
  473.3 38.6 %ff_step.6 = (bf16[1536,2048]{1,0:T(8,128)(2,1)}, bf16[1536,2048]{1,0:T(8,128)(2,1)}, bf16[1536,2048]{1,0:T(8,128)(2,1)}, bf16[1536,2048]{1,0:T(8,128)(2,1)}, bf...) custom-call(bf16[384,2048]{1,0:T(8,128)(2,1)} %get-tuple-element.165, ...), custom_call_target="tpu_custom_call", output_to_operand_aliasing={{0}: (19, {}), {1}: (20, {}), {2}: (21, {}), {3}: (22, {}),... | custom-call | flops 16106127360 | tf_op jit(solution)/shard_map/ff_step/pallas_call | solution.py:167
  511.9 39.4 %ff_step.7 = (bf16[1536,2048]{1,0:T(8,128)(2,1)}, bf16[1536,2048]{1,0:T(8,128)(2,1)}, bf16[1536,2048]{1,0:T(8,128)(2,1)}, bf16[1536,2048]{1,0:T(8,128)(2,1)}, bf...) custom-call(bf16[384,2048]{1,0:T(8,128)(2,1)} %get-tuple-element.147, ...), custom_call_target="tpu_custom_call", output_to_operand_aliasing={{0}: (19, {}), {1}: (20, {}), {2}: (21, {}), {3}: (22, {}),... | custom-call | flops 16106127360 | tf_op jit(solution)/shard_map/ff_step/pallas_call | solution.py:167
  565.2 23.1 %outer.4 = (bf16[1024,2048]{1,0:T(8,128)(2,1)}, bf16[1024,2048]{1,0:T(8,128)(2,1)}, bf16[384,512]{1,0:T(8,128)(2,1)}, bf16[384,512]{1,0:T(8,128)(2,1)}) custom-call(bf16[1536,2048]{1,0:T(8,128)(2,1)} %get-tuple-element.191.refs_0_, bf16[1536,2048]{1,0:T(8,128)(2,1)} %get-tuple-element.192.refs_1_, bf16[4,384,512]{2,1,0:T(8,128)(2,1)} %copy-done.26), custom_call_target="tpu_custom_call" | custom-call | flops 12884901888 | tf_op jit(solution)/shard_map/outer/pallas_call | solution.py:167
  588.3 26.3 %outer.5 = (bf16[1024,2048]{1,0:T(8,128)(2,1)}, bf16[1024,2048]{1,0:T(8,128)(2,1)}, bf16[384,512]{1,0:T(8,128)(2,1)}, bf16[1024,2048]{1,0:T(8,128)(2,1)}) custom-call(bf16[1536,2048]{1,0:T(8,128)(2,1)} %get-tuple-element.188.refs_0_, bf16[1536,2048]{1,0:T(8,128)(2,1)} %get-tuple-element.189.refs_1_, bf16[4,384,512]{2,1,0:T(8,128)(2,1)} %copy-done.26, ...), custom_call_target="tpu_custom_call" | custom-call | flops 12884901888 | tf_op jit(solution)/shard_map/outer/pallas_call | solution.py:167
  622.6 22.0 %outer.6 = (bf16[1024,2048]{1,0:T(8,128)(2,1)}, bf16[1024,2048]{1,0:T(8,128)(2,1)}, bf16[1024,2048]{1,0:T(8,128)(2,1)}, bf16[128,2048]{1,0:T(8,128)(2,1)}, bf16[128,2048]{1,0:T(8,128)(2,1)}) custom-call(bf16[1536,2048]{1,0:T(8,128)(2,1)} %get-tuple-element.198.refs_0_, bf16[1536,2048]{1,0:T(8,128)(2,1)} %get-tuple-element.189.refs_1_, ...), custom_call_target="tpu_custom_call" | custom-call | flops 12884901888 | tf_op jit(solution)/shard_map/outer/pallas_call | solution.py:167
  653.6 39.3 %attend_backward.2 = (bf16[1536,384]{1,0:T(8,128)(2,1)}, bf16[1024,2048]{1,0:T(8,128)(2,1)}, bf16[128,2048]{1,0:T(8,128)(2,1)S(1)}, bf16[128,2048]{1,0:T(8,128)(...) custom-call(s32[1]{0:T(128)} %dynamic_slice.6.refs_0_, bf16[1536,768]{1,0:T(8,128)(2,1)} %project.1.refs_1_, ...), custom_call_target="tpu_custom_call" | custom-call | flops 12079595520 | tf_op jit(solution)/shard_map/attend_backward/pallas_call | solution.py:167
  703.9 38.7 %attend_backward.3 = (bf16[1536,384]{1,0:T(8,128)(2,1)}, bf16[128,2048]{1,0:T(8,128)(2,1)S(1)}, bf16[128,2048]{1,0:T(8,128)(2,1)S(1)}, bf16[256,2048]{1,0:T(8,128)(2,1)S(1)}, bf16[256,2048]{1,0:T(8,128)(2,1)S(1)}) custom-call(s32[1]{0:T(128)} %dynamic_slice.6.refs_0_, bf16[1536,768]{1,0:T(8,128)(2,1)} %project.1.refs_1_, ...), custom_call_target="tpu_custom_call" | custom-call | flops 12079595520 | tf_op jit(solution)/shard_map/attend_backward/pallas_call | solution.py:167
  750.5 29.4 %outer_pair.1 = (bf16[384,2048]{1,0:T(8,128)(2,1)}, bf16[384,2048]{1,0:T(8,128)(2,1)}, bf16[256,2048]{1,0:T(8,128)(2,1)}, bf16[256,2048]{1,0:T(8,128)(2,1)}) custom-call(bf16[1536,384]{1,0:T(8,128)(2,1)} %get-tuple-element.213.refs_0_, bf16[1536,384]{1,0:T(8,128)(2,1)} %get-tuple-element.222.refs_1_, ...), custom_call_target="tpu_custom_call" | custom-call | flops 4831838208 | tf_op jit(solution)/shard_map/outer_pair/pallas_call | solution.py:167
  779.9 8.2 outer.7.refs_3_
  793.7 8.5 ff_end.1
  807.6 39.7 %first_back.1 = (bf16[1536,2048]{1,0:T(8,128)(2,1)}, f32[1,2048]{1,0:T(1,128)}, bf16[256,2048]{1,0:T(8,128)(2,1)}, bf16[256,2048]{1,0:T(8,128)(2,1)}, bf16[160,2...) custom-call(bf16[1536,384]{1,0:T(8,128)(2,1)} %get-tuple-element.213.refs_0_, ...), custom_call_target="tpu_custom_call" | custom-call | flops 4831838208 | tf_op jit(solution)/shard_map/first_back/pallas_call | solution.py:167
  860.9 50.9 %move.11 = (bf16[8,16,16,1024]{3,2,1,0:T(8,128)(2,1)}, f32[8,2,2048]{2,1,0:T(2,128)}) custom-call(bf16[8,16,16,1024]{3,2,1,0:T(8,128)(2,1)} %get-tuple-element.250.refs_0_.refs_2_, f32[2,2048]{1,0:T(2,128)} %pad_maximum_fusion.3.refs_1_), custom_call_target="tpu_custom_call" | custom-call | tf_op jit(solution)/shard_map/move/pallas_call | solution.py:167
  924.9 22.6 %update_units.2 = (f32[26,1,1024,128]{3,2,1,0:T(8,128)}, f32[26,1,1024,128]{3,2,1,0:T(8,128)}, bf16[26,1,1024,128]{3,2,1,0:T(8,128)(2,1)}, f32[26,1,1024,128]{3,2,1,0:T(8,128)}, f32[26,1,1024,128]{3,2,1,0:T(8,128)}) custom-call(s32[2]{0:T(128)S(1)} %pad_add_fusion.1.refs_0_, bf16[8,16,16,1024]{3,2,1,0:T(8,128)(2,1)S(1)} %copy-done.3, ...), custom_call_target="tpu_custom_call" | custom-call | bytes 54525952 | tf_op jit(solution)/shard_map/update_units/pallas_call | solution.py:167
  947.6 15.6 %update_units.3 = (f32[26,1,1024,128]{3,2,1,0:T(8,128)}, f32[26,1,1024,128]{3,2,1,0:T(8,128)}, bf16[26,1,1024,128]{3,2,1,0:T(8,128)(2,1)}, f32[26,1,1024,128]{3,2,1,0:T(8,128)}, f32[26,1,1024,128]{3,2,1,0:T(8,128)}) custom-call(s32[2]{0:T(128)S(1)} %pad_add_fusion.1.refs_0_, ...), custom_call_target="tpu_custom_call", output_to_operand_aliasing={{0}: (6, {}), {1}: (7, {}), {2}: (8, {}), {3}: (9, {}), {4}... | custom-call | bytes 54525952 | tf_op jit(solution)/shard_map/update_units/pallas_call | solution.py:167
  (251 shorter events, 145.8 us)
Async XLA Ops:
  7.2 146.0 %all-gather.5.cloned.1.call-start = ((), (), s32[]{:S(2)}) async-start(), calls=%async_computation.3 | async-start | bytes 7864320 | tf_op jit(solution)/shard_map/all_gather | solution.py:1309
  14.6 234.0 %all-gather.7.cloned.1.call-start = ((), (), s32[]{:S(2)}) async-start(), calls=%async_computation.4 | async-start | bytes 3932160 | tf_op jit(solution)/shard_map/all_gather | solution.py:1345
  22.3 78.5 %copy-start.71 = (s32[116]{0:T(128)S(1)}, s32[116]{0:T(128)}, u32[]{:S(2)}) copy-start(s32[116]{0:T(128)} %param.15) | copy-start | bytes 1396
  108.9 37.8 %copy-start = (bf16[928,2048]{1,0:T(8,128)(2,1)S(1)}, bf16[928,2048]{1,0:T(8,128)(2,1)}, u32[]{:S(2)}) copy-start(bf16[928,2048]{1,0:T(8,128)(2,1)} %pick_units.1.refs_0_.refs_1_.refs_2_.refs_3_) | copy-start | bytes 11403268
  109.0 37.8 %copy-start.27 = (s32[2]{0:T(128)S(1)}, s32[2]{0:T(128)}, u32[]{:S(2)}) copy-start(s32[2]{0:T(128)} %pad_add_fusion.refs_0_) | copy-start | bytes 28
  153.2 240.3 %all-gather.9.cloned.1.call-start = ((), (), s32[]{:S(2)}) async-start(), calls=%async_computation.5 | async-start | bytes 3932160 | tf_op jit(solution)/shard_map/all_gather | solution.py:1406
  154.4 10.8 %copy-start.11 = (bf16[3,64,2048]{2,1,0:T(8,128)(2,1)S(1)}, bf16[3,64,2048]{2,1,0:T(8,128)(2,1)}, u32[]{:S(2)}) copy-start(bf16[3,64,2048]{2,1,0:T(8,128)(2,1)} %get-tuple-element.139.refs_3_.refs_4_.refs_2_) | copy-start | bytes 2359300
  248.7 531.2 %all-gather.11.cloned.1.call-start = ((), (), s32[]{:S(2)}) async-start(), calls=%async_computation.7 | async-start | bytes 7864320 | tf_op jit(solution)/shard_map/all_gather | solution.py:1498
  347.5 45.7 %copy-start.34 = (f32[384,2048]{1,0:T(8,128)S(1)}, f32[384,2048]{1,0:T(8,128)}, u32[]{:S(2)}) copy-start(f32[384,2048]{1,0:T(8,128)} %get-tuple-element.146) | copy-start | bytes 9437188
  393.5 161.7 %copy-start.59 = (f32[384]{0:T(512)}, f32[384]{0:T(512)S(1)}, u32[]{:S(2)}) copy-start(f32[384]{0:T(512)S(1)} %fusion.13) | copy-start | bytes 4612
  511.9 39.5 %copy-start.48 = (f32[1,2048]{1,0:T(1,128)S(1)}, f32[1,2048]{1,0:T(1,128)}, u32[]{:S(2)}) copy-start(f32[1,2048]{1,0:T(1,128)} %get-tuple-element.278.refs_4_) | copy-start | bytes 24580
  551.3 7.8 slice-start
  559.4 4.7 copy-start.4
  614.7 235.3 %reduce-scatter.3.cloned.1.call-start = ((), (), s32[]{:S(2)}) async-start(), calls=%async_computation.6 | async-start | bytes 7864320 | tf_op jit(solution)/shard_map/reduce_scatter | solution.py:1499
  615.3 355.0 %reduce-scatter.5.cloned.1.call-start = ((), (), s32[]{:S(2)}) async-start(), calls=%async_computation.8 | async-start | bytes 7864320 | tf_op jit(solution)/shard_map/reduce_scatter | solution.py:1605
  779.9 8.2 copy-start.5
  779.9 8.2 copy-start.6
  855.3 4.9 copy-start.53
  855.3 4.9 copy-start.69
  911.8 35.8 %all-to-all-start = ((bf16[8,10,16,1024]{3,2,1,0:T(8,128)(2,1)}), bf16[8,10,16,1024]{3,2,1,0:T(8,128)(2,1)S(1)}, u32[]{:S(2)}, u32[]{:S(2)}) async-start(bf16[8,10,16,1024]{3,2,1,0:T(8,128)(2,1)} %after.15), calls=%async_computation.2 | async-start | bytes 5242880 | tf_op jit(solution)/shard_map/all_to_all | solution.py:1583
  917.6 45.6 %collective-permute-start.2 = (f32[2,2048]{1,0:T(2,128)}, f32[2,2048]{1,0:T(2,128)S(1)}, u32[]{:S(2)}, u32[]{:S(2)}) collective-permute-start(f32[2,2048]{1,0:T(2,128)} %sum_places.2.refs_1_), channel_id=1, source_target_pairs={{0,3},{1,0},{2,1},{3,2},{4,7},{5,4},{6,5},{7,6},{8,11},{9,8},{10,9... | collective-permute-start | bytes 49160 | tf_op jit(solution)/shard_map/ppermute | solution.py:1597
  918.9 45.0 %collective-permute-start.1 = (f32[2,2048]{1,0:T(2,128)}, f32[2,2048]{1,0:T(2,128)S(1)}, u32[]{:S(2)}, u32[]{:S(2)}) collective-permute-start(f32[2,2048]{1,0:T(2,128)} %sum_places.2.refs_1_), channel_id=1, source_target_pairs={{0,2},{1,3},{2,0},{3,1},{4,6},{5,7},{6,4},{7,5},{8,10},{9,11},{10,... | collective-permute-start | bytes 49160 | tf_op jit(solution)/shard_map/ppermute | solution.py:1597
  918.9 45.6 %collective-permute-start = (f32[2,2048]{1,0:T(2,128)}, f32[2,2048]{1,0:T(2,128)S(1)}, u32[]{:S(2)}, u32[]{:S(2)}) collective-permute-start(f32[2,2048]{1,0:T(2,128)} %sum_places.2.refs_1_), channel_id=1, source_target_pairs={{0,1},{1,2},{2,3},{3,0},{4,5},{5,6},{6,7},{7,4},{8,9},{9,10},{10,1... | collective-permute-start | bytes 49160 | tf_op jit(solution)/shard_map/ppermute | solution.py:1597
  964.5 4.4 copy-start.67
  (65 other events, 128.0 us)
Sparse Core Ops, SparseCore 0:
  14.7 138.0 all-gather.4
  154.9 93.3 all-gather.6
  249.9 102.6 all-gather.8
  614.8 112.6 all-gather.10
  729.7 108.9 reduce-scatter.2
  850.2 109.0 reduce-scatter.4

commit v8 on v7

--- a/solution.py
+++ b/solution.py
@@ -385,7 +385,7 @@
         grid=(slots // step,),
         aliases={6 + k: k for k in range(len(done))},
         moved=master.size * 16,
-        mib=40,
+        mib=60,
         deps=deps,
         name="update_units",
     )
@@ -1179,7 +1179,7 @@
         shaped((height * 8, D)),
         blocks((height * 8, D), lambda i: (0, 0)),
         grid=(1,),
-        mib=32,
+        mib=60,
         moved=height * 8 * D * 4,
         name="assemble_qkv",
     )

time: 992 us -> 994 us (level)
    unnamed x156 -> x146, local copies, waits for them, and re-layouts: 33.7 us -> 26.4 us
  transfers between devices with their start and end apart: 10 -> 10, of which waited for: 1 -> 2; matrix products, arithmetic and copies ran while one was open for 2% -> 2% of each run, Pallas kernels for 69% -> 69%
where the time goes in v8:
time: 994 us; the launch traced here: 989 us
  Pallas kernels  895 us (90%)
  local copies, waits for them, and re-layouts  34.5 us (3%)
  other arithmetic  33.7 us (3%)
  between operations  15.7 us (2%)
    pallas_call x51, Pallas kernels, call(): pl.pallas_call(wrapped, grid_spec=pltpu.PrefetchScalarGridSpec(num_scalar...  895 us
    unnamed x146, local copies, waits for them, and re-layouts  26.4 us
  transfers between devices with their start and end apart: 10, of which 2 were waited for; matrix products, arithmetic and copies ran while one was open for 2% of the time, Pallas kernels for 69%

profile of v8, /device:TPU:0, one launch (start us, length us, event | category | flops | bytes accessed | tf_op | source)
XLA Modules:
  0.0 988.7 jit_solution(14295705804705263356)
XLA Ops:
  22.2 78.4 %move.6.refs_3_ = bf16[8,26,16,1024]{3,2,1,0:T(8,128)(2,1)} custom-call(bf16[8,26,16,1024]{3,2,1,0:T(8,128)(2,1)} %turn_units.1.refs_0_.refs_2_), custom_call_target="tpu_custom_call" | custom-call | tf_op jit(solution)/shard_map/move/pallas_call | solution.py:167
  108.9 37.7 %move.7 = (bf16[3,96,2048]{2,1,0:T(8,128)(2,1)}, bf16[4,96,2048]{2,1,0:T(8,128)(2,1)}, bf16[3,64,2048]{2,1,0:T(8,128)(2,1)}) custom-call(bf16[928,2048]{1,0:T(8,128)(2,1)} %pick_units.1.refs_0_.refs_1_.refs_2_.refs_3_), custom_call_target="tpu_custom_call" | custom-call | tf_op jit(solution)/shard_map/move/pallas_call | solution.py:167
  154.0 10.8 %project.1.refs_1_ = bf16[1536,768]{1,0:T(8,128)(2,1)} custom-call(bf16[1536,2048]{1,0:T(8,128)(2,1)} %all-gather.5.cloned.1.call-done.refs_1_.refs_0_.refs_2_, bf16[768,2048]{1,0:T(8,128)(2,1)} %assemble_qkv.1.refs_2_.refs_1_.refs_3_, f32[1536,128]{1,0:T(8,128)} %constant.101.clone.refs_2_.refs_5_, f32[1536,128]{1,0:T(8,128)} %constant.102.clone.refs_3_.refs_6_, ...), custom_call_target="tpu_custom_call" | custom-call | flops 4831838208 | tf_op jit(solution)/shard_map/project/pallas_call | solution.py:167
  164.7 29.3 %attend_forward.1 = (bf16[1536,512]{1,0:T(8,128)(2,1)S(1)}, f32[2,8,1536]{2,1,0:T(8,128)S(1)}, bf16[4,64,2048]{2,1,0:T(8,128)(2,1)S(1)}, bf16[4,64,2048]{2,1,0:T(8,128)(2,1)S(1)}) custom-call(s32[1]{0:T(128)} %dynamic_slice.6.refs_0_, bf16[1536,768]{1,0:T(8,128)(2,1)} %project.1.refs_1_, bf16[928,2048]{1,0:T(8,128)(2,1)} %pick_units.1.refs_0_.refs_1_.refs_2_.refs_3_, ...), custom_call_target="tpu_custom_call" | custom-call | flops 9663676416 | tf_op jit(solution)/shard_map/attend_forward/pallas_call | solution.py:167
  197.1 50.2 %move.8 = (bf16[3,384,512]{2,1,0:T(8,128)(2,1)}, bf16[4,64,2048]{2,1,0:T(8,128)(2,1)}, bf16[4,4,64,2048]{3,2,1,0:T(8,128)(2,1)}, bf16[256,2048]{1,0:T(8,128)(2,1)}, bf16[256,2048]{1,0:T(8,128)(2,1)}) custom-call(bf16[1536,512]{1,0:T(8,128)(2,1)} %copy-done.3, bf16[928,2048]{1,0:T(8,128)(2,1)} %pick_units.1.refs_0_.refs_1_.refs_2_.refs_3_, ...), custom_call_target="tpu_custom_call" | custom-call | tf_op jit(solution)/shard_map/move/pallas_call | solution.py:167
  255.8 10.2 %branch.1 = (f32[384,2048]{1,0:T(8,128)}, bf16[384,2048]{1,0:T(8,128)(2,1)}) custom-call(bf16[1536,512]{1,0:T(8,128)(2,1)} %copy-done.3, bf16[3,384,512]{2,1,0:T(8,128)(2,1)} %get-tuple-element.143.refs_1_, bf16[2048,2048]{1,0:T(8,128)(2,1)} %assemble_out.1.refs_2_, bf16[384,2048]{1,0:T(8,128)(2,1)} %refs_3_.4, f32[1,2048]{1,0:T(1,128)} %get-tuple-element.278.refs_4_), custom_call_target="tpu_custom_call" | custom-call | flops 3221225472 | tf_op jit(solution)/shard_map/branch/pallas_call | solution.py:167
  266.0 80.2 %move.9 = (bf16[384,2048]{1,0:T(8,128)(2,1)}, bf16[512,2048]{1,0:T(8,128)(2,1)}, bf16[512,2048]{1,0:T(8,128)(2,1)}, bf16[768,2048]{1,0:T(8,128)(2,1)}, bf16[256,...) custom-call(bf16[384,2048]{1,0:T(8,128)(2,1)} %get-tuple-element.147, ...), custom_call_target="tpu_custom_call" | custom-call | tf_op jit(solution)/shard_map/move/pallas_call | solution.py:167
  346.2 45.6 %move.10 = (bf16[384,2048]{1,0:T(8,128)(2,1)}, bf16[128,2048]{1,0:T(8,128)(2,1)}, bf16[384,2048]{1,0:T(8,128)(2,1)}, bf16[256,2048]{1,0:T(8,128)(2,1)}, bf16[128...) custom-call(bf16[384,2048]{1,0:T(8,128)(2,1)} %get-tuple-element.153.refs_0_, ...), custom_call_target="tpu_custom_call" | custom-call | tf_op jit(solution)/shard_map/move/pallas_call | solution.py:167
  392.2 40.3 %ff_step.4 = (bf16[1536,2048]{1,0:T(8,128)(2,1)}, bf16[1536,2048]{1,0:T(8,128)(2,1)}, bf16[1536,2048]{1,0:T(8,128)(2,1)}, bf16[1536,2048]{1,0:T(8,128)(2,1)}, bf...) custom-call(bf16[384,2048]{1,0:T(8,128)(2,1)} %get-tuple-element.153, ...), custom_call_target="tpu_custom_call" | custom-call | flops 16106127360 | tf_op jit(solution)/shard_map/ff_step/pallas_call | solution.py:167
  432.5 39.5 %ff_step.5 = (bf16[1536,2048]{1,0:T(8,128)(2,1)}, bf16[1536,2048]{1,0:T(8,128)(2,1)}, bf16[1536,2048]{1,0:T(8,128)(2,1)}, bf16[1536,2048]{1,0:T(8,128)(2,1)}, bf...) custom-call(bf16[384,2048]{1,0:T(8,128)(2,1)} %get-tuple-element.164, ...), custom_call_target="tpu_custom_call", output_to_operand_aliasing={{0}: (19, {}), {1}: (20, {}), {2}: (21, {}), {3}: (22, {}),... | custom-call | flops 16106127360 | tf_op jit(solution)/shard_map/ff_step/pallas_call | solution.py:167
  472.0 38.6 %ff_step.6 = (bf16[1536,2048]{1,0:T(8,128)(2,1)}, bf16[1536,2048]{1,0:T(8,128)(2,1)}, bf16[1536,2048]{1,0:T(8,128)(2,1)}, bf16[1536,2048]{1,0:T(8,128)(2,1)}, bf...) custom-call(bf16[384,2048]{1,0:T(8,128)(2,1)} %get-tuple-element.165, ...), custom_call_target="tpu_custom_call", output_to_operand_aliasing={{0}: (19, {}), {1}: (20, {}), {2}: (21, {}), {3}: (22, {}),... | custom-call | flops 16106127360 | tf_op jit(solution)/shard_map/ff_step/pallas_call | solution.py:167
  510.6 39.5 %ff_step.7 = (bf16[1536,2048]{1,0:T(8,128)(2,1)}, bf16[1536,2048]{1,0:T(8,128)(2,1)}, bf16[1536,2048]{1,0:T(8,128)(2,1)}, bf16[1536,2048]{1,0:T(8,128)(2,1)}, bf...) custom-call(bf16[384,2048]{1,0:T(8,128)(2,1)} %get-tuple-element.147, ...), custom_call_target="tpu_custom_call", output_to_operand_aliasing={{0}: (19, {}), {1}: (20, {}), {2}: (21, {}), {3}: (22, {}),... | custom-call | flops 16106127360 | tf_op jit(solution)/shard_map/ff_step/pallas_call | solution.py:167
  563.9 23.1 %outer.4 = (bf16[1024,2048]{1,0:T(8,128)(2,1)}, bf16[1024,2048]{1,0:T(8,128)(2,1)}, bf16[384,512]{1,0:T(8,128)(2,1)}, bf16[384,512]{1,0:T(8,128)(2,1)}) custom-call(bf16[1536,2048]{1,0:T(8,128)(2,1)} %get-tuple-element.191.refs_0_, bf16[1536,2048]{1,0:T(8,128)(2,1)} %get-tuple-element.192.refs_1_, bf16[4,384,512]{2,1,0:T(8,128)(2,1)} %copy-done.20), custom_call_target="tpu_custom_call" | custom-call | flops 12884901888 | tf_op jit(solution)/shard_map/outer/pallas_call | solution.py:167
  587.1 26.3 %outer.5 = (bf16[1024,2048]{1,0:T(8,128)(2,1)}, bf16[1024,2048]{1,0:T(8,128)(2,1)}, bf16[384,512]{1,0:T(8,128)(2,1)}, bf16[1024,2048]{1,0:T(8,128)(2,1)}) custom-call(bf16[1536,2048]{1,0:T(8,128)(2,1)} %get-tuple-element.188.refs_0_, bf16[1536,2048]{1,0:T(8,128)(2,1)} %get-tuple-element.189.refs_1_, bf16[4,384,512]{2,1,0:T(8,128)(2,1)} %copy-done.20, ...), custom_call_target="tpu_custom_call" | custom-call | flops 12884901888 | tf_op jit(solution)/shard_map/outer/pallas_call | solution.py:167
  621.4 22.0 %outer.6 = (bf16[1024,2048]{1,0:T(8,128)(2,1)}, bf16[1024,2048]{1,0:T(8,128)(2,1)}, bf16[1024,2048]{1,0:T(8,128)(2,1)}, bf16[128,2048]{1,0:T(8,128)(2,1)}, bf16[128,2048]{1,0:T(8,128)(2,1)}) custom-call(bf16[1536,2048]{1,0:T(8,128)(2,1)} %get-tuple-element.198.refs_0_, bf16[1536,2048]{1,0:T(8,128)(2,1)} %get-tuple-element.189.refs_1_, ...), custom_call_target="tpu_custom_call" | custom-call | flops 12884901888 | tf_op jit(solution)/shard_map/outer/pallas_call | solution.py:167
  652.4 39.3 %attend_backward.2 = (bf16[1536,384]{1,0:T(8,128)(2,1)}, bf16[1024,2048]{1,0:T(8,128)(2,1)}, bf16[128,2048]{1,0:T(8,128)(2,1)S(1)}, bf16[128,2048]{1,0:T(8,128)(...) custom-call(s32[1]{0:T(128)} %dynamic_slice.6.refs_0_, bf16[1536,768]{1,0:T(8,128)(2,1)} %project.1.refs_1_, ...), custom_call_target="tpu_custom_call" | custom-call | flops 12079595520 | tf_op jit(solution)/shard_map/attend_backward/pallas_call | solution.py:167
  702.6 38.7 %attend_backward.3 = (bf16[1536,384]{1,0:T(8,128)(2,1)}, bf16[128,2048]{1,0:T(8,128)(2,1)S(1)}, bf16[128,2048]{1,0:T(8,128)(2,1)S(1)}, bf16[256,2048]{1,0:T(8,128)(2,1)S(1)}, bf16[256,2048]{1,0:T(8,128)(2,1)S(1)}) custom-call(s32[1]{0:T(128)} %dynamic_slice.6.refs_0_, bf16[1536,768]{1,0:T(8,128)(2,1)} %project.1.refs_1_, ...), custom_call_target="tpu_custom_call" | custom-call | flops 12079595520 | tf_op jit(solution)/shard_map/attend_backward/pallas_call | solution.py:167
  749.2 29.3 %outer_pair.1 = (bf16[384,2048]{1,0:T(8,128)(2,1)}, bf16[384,2048]{1,0:T(8,128)(2,1)}, bf16[256,2048]{1,0:T(8,128)(2,1)}, bf16[256,2048]{1,0:T(8,128)(2,1)}) custom-call(bf16[1536,384]{1,0:T(8,128)(2,1)} %get-tuple-element.213.refs_0_, bf16[1536,384]{1,0:T(8,128)(2,1)} %get-tuple-element.222.refs_1_, ...), custom_call_target="tpu_custom_call" | custom-call | flops 4831838208 | tf_op jit(solution)/shard_map/outer_pair/pallas_call | solution.py:167
  778.6 8.2 outer.7.refs_3_
  792.4 8.6 ff_end.1
  806.3 39.7 %first_back.1 = (bf16[1536,2048]{1,0:T(8,128)(2,1)}, f32[1,2048]{1,0:T(1,128)}, bf16[256,2048]{1,0:T(8,128)(2,1)}, bf16[256,2048]{1,0:T(8,128)(2,1)}, bf16[160,2...) custom-call(bf16[1536,384]{1,0:T(8,128)(2,1)} %get-tuple-element.213.refs_0_, ...), custom_call_target="tpu_custom_call" | custom-call | flops 4831838208 | tf_op jit(solution)/shard_map/first_back/pallas_call | solution.py:167
  859.7 50.9 %move.11 = (bf16[8,16,16,1024]{3,2,1,0:T(8,128)(2,1)}, f32[8,2,2048]{2,1,0:T(2,128)}) custom-call(bf16[8,16,16,1024]{3,2,1,0:T(8,128)(2,1)} %get-tuple-element.250.refs_0_.refs_2_, f32[2,2048]{1,0:T(2,128)} %pad_maximum_fusion.3.refs_1_), custom_call_target="tpu_custom_call" | custom-call | tf_op jit(solution)/shard_map/move/pallas_call | solution.py:167
  919.8 24.2 %update_units.2 = (f32[26,1,1024,128]{3,2,1,0:T(8,128)}, f32[26,1,1024,128]{3,2,1,0:T(8,128)}, bf16[26,1,1024,128]{3,2,1,0:T(8,128)(2,1)}, f32[26,1,1024,128]{3,2,1,0:T(8,128)}, f32[26,1,1024,128]{3,2,1,0:T(8,128)}) custom-call(s32[2]{0:T(128)} %pad_add_fusion.1.refs_0_, bf16[8,16,16,1024]{3,2,1,0:T(8,128)(2,1)} %get-tuple-element.252.refs_1_, ...), custom_call_target="tpu_custom_call" | custom-call | bytes 54525952 | tf_op jit(solution)/shard_map/update_units/pallas_call | solution.py:167
  948.1 16.9 %update_units.3 = (f32[26,1,1024,128]{3,2,1,0:T(8,128)}, f32[26,1,1024,128]{3,2,1,0:T(8,128)}, bf16[26,1,1024,128]{3,2,1,0:T(8,128)(2,1)}, f32[26,1,1024,128]{3,2,1,0:T(8,128)}, f32[26,1,1024,128]{3,2,1,0:T(8,128)}) custom-call(s32[2]{0:T(128)} %pad_add_fusion.1.refs_0_, ...), custom_call_target="tpu_custom_call", output_to_operand_aliasing={{0}: (6, {}), {1}: (7, {}), {2}: (8, {}), {3}: (9, {}), {4}... | custom-call | bytes 54525952 | tf_op jit(solution)/shard_map/update_units/pallas_call | solution.py:167
  (241 shorter events, 145.5 us)
Async XLA Ops:
  7.2 145.6 %all-gather.5.cloned.1.call-start = ((), (), s32[]{:S(2)}) async-start(), calls=%async_computation.3 | async-start | bytes 7864320 | tf_op jit(solution)/shard_map/all_gather | solution.py:1309
  14.6 232.8 %all-gather.7.cloned.1.call-start = ((), (), s32[]{:S(2)}) async-start(), calls=%async_computation.4 | async-start | bytes 3932160 | tf_op jit(solution)/shard_map/all_gather | solution.py:1345
  22.2 78.5 %copy-start.66 = (s32[116]{0:T(128)S(1)}, s32[116]{0:T(128)}, u32[]{:S(2)}) copy-start(s32[116]{0:T(128)} %param.15) | copy-start | bytes 1396
  152.8 239.5 %all-gather.9.cloned.1.call-start = ((), (), s32[]{:S(2)}) async-start(), calls=%async_computation.5 | async-start | bytes 3932160 | tf_op jit(solution)/shard_map/all_gather | solution.py:1406
  154.0 10.8 %copy-start.7 = (bf16[3,64,2048]{2,1,0:T(8,128)(2,1)S(1)}, bf16[3,64,2048]{2,1,0:T(8,128)(2,1)}, u32[]{:S(2)}) copy-start(bf16[3,64,2048]{2,1,0:T(8,128)(2,1)} %get-tuple-element.139.refs_3_.refs_4_.refs_2_) | copy-start | bytes 2359300
  247.5 531.1 %all-gather.11.cloned.1.call-start = ((), (), s32[]{:S(2)}) async-start(), calls=%async_computation.7 | async-start | bytes 7864320 | tf_op jit(solution)/shard_map/all_gather | solution.py:1498
  346.2 45.7 %copy-start.28 = (f32[384,2048]{1,0:T(8,128)S(1)}, f32[384,2048]{1,0:T(8,128)}, u32[]{:S(2)}) copy-start(f32[384,2048]{1,0:T(8,128)} %get-tuple-element.146) | copy-start | bytes 9437188
  392.2 161.7 %copy-start.54 = (f32[384]{0:T(512)}, f32[384]{0:T(512)S(1)}, u32[]{:S(2)}) copy-start(f32[384]{0:T(512)S(1)} %fusion.13) | copy-start | bytes 4612
  510.6 39.5 %copy-start.43 = (f32[1,2048]{1,0:T(1,128)S(1)}, f32[1,2048]{1,0:T(1,128)}, u32[]{:S(2)}) copy-start(f32[1,2048]{1,0:T(1,128)} %get-tuple-element.278.refs_4_) | copy-start | bytes 24580
  550.1 7.8 slice-start
  553.9 4.2 slice-start.1
  558.1 4.7 copy-start
  613.5 235.4 %reduce-scatter.3.cloned.1.call-start = ((), (), s32[]{:S(2)}) async-start(), calls=%async_computation.6 | async-start | bytes 7864320 | tf_op jit(solution)/shard_map/reduce_scatter | solution.py:1499
  614.0 358.1 %reduce-scatter.5.cloned.1.call-start = ((), (), s32[]{:S(2)}) async-start(), calls=%async_computation.8 | async-start | bytes 7864320 | tf_op jit(solution)/shard_map/reduce_scatter | solution.py:1605
  778.6 8.2 copy-start.1
  778.6 8.2 copy-start.2
  854.2 4.9 copy-start.48
  854.2 4.9 copy-start.64
  910.7 35.8 %all-to-all-start = ((bf16[8,10,16,1024]{3,2,1,0:T(8,128)(2,1)}), bf16[8,10,16,1024]{3,2,1,0:T(8,128)(2,1)S(1)}, u32[]{:S(2)}, u32[]{:S(2)}) async-start(bf16[8,10,16,1024]{3,2,1,0:T(8,128)(2,1)} %after.15), calls=%async_computation.2 | async-start | bytes 5242880 | tf_op jit(solution)/shard_map/all_to_all | solution.py:1583
  916.5 48.6 %collective-permute-start.2 = (f32[2,2048]{1,0:T(2,128)}, f32[2,2048]{1,0:T(2,128)S(1)}, u32[]{:S(2)}, u32[]{:S(2)}) collective-permute-start(f32[2,2048]{1,0:T(2,128)} %sum_places.2.refs_1_), channel_id=1, source_target_pairs={{0,3},{1,0},{2,1},{3,2},{4,7},{5,4},{6,5},{7,6},{8,11},{9,8},{10,9... | collective-permute-start | bytes 49160 | tf_op jit(solution)/shard_map/ppermute | solution.py:1597
  917.8 47.9 %collective-permute-start.1 = (f32[2,2048]{1,0:T(2,128)}, f32[2,2048]{1,0:T(2,128)S(1)}, u32[]{:S(2)}, u32[]{:S(2)}) collective-permute-start(f32[2,2048]{1,0:T(2,128)} %sum_places.2.refs_1_), channel_id=1, source_target_pairs={{0,2},{1,3},{2,0},{3,1},{4,6},{5,7},{6,4},{7,5},{8,10},{9,11},{10,... | collective-permute-start | bytes 49160 | tf_op jit(solution)/shard_map/ppermute | solution.py:1597
  917.8 48.5 %collective-permute-start = (f32[2,2048]{1,0:T(2,128)}, f32[2,2048]{1,0:T(2,128)S(1)}, u32[]{:S(2)}, u32[]{:S(2)}) collective-permute-start(f32[2,2048]{1,0:T(2,128)} %sum_places.2.refs_1_), channel_id=1, source_target_pairs={{0,1},{1,2},{2,3},{3,0},{4,5},{5,6},{6,7},{7,4},{8,9},{9,10},{10,1... | collective-permute-start | bytes 49160 | tf_op jit(solution)/shard_map/ppermute | solution.py:1597
  966.3 4.4 copy-start.62
  966.3 4.4 copy-start.63
  (60 other events, 114.8 us)
Sparse Core Ops, SparseCore 0:
  14.7 138.0 all-gather.4
  154.9 92.0 all-gather.6
  248.6 102.6 all-gather.8
  613.6 112.6 all-gather.10
  728.4 108.9 reduce-scatter.2
  849.0 109.1 reduce-scatter.4
